TPU v7x, 32 devices: a whole 2x2x4 slice. The times are simulated.
32 devices in a mesh: dp: 8 (over y, x, core), section: 4 (over z).
Axes of the slice: x: 2, y: 2, z: 4, core: 2. Of those that a mesh axis runs over, the one named last changes fastest.
Arguments:
- inputs: bfloat16 [2, 512, 1024], P(None, 'dp'), may hold values from -6 to 6
- ln_gain: float32 [4, 1024], P('section'), may hold values from 0.5 to 1.5
- w_in: bfloat16 [4, 1024, 2048], P('section'), may hold values from -0.1875 to 0.1875
- w_out: bfloat16 [4, 2048, 1024], P('section'), may hold values from -0.125 to 0.125
- layer_scale: float32 [4, 1024], P('section'), may hold values from 0.25 to 1
- out_grad: bfloat16 [2, 512, 1024], P(None, 'dp'), may hold values from -6 to 6
- owner_table: int32 [8], replicated, may hold values from 0 to 7, each once
Outputs:
- act_factor: float32 [4, 1024, 1024], P('section', 'dp')
- grad_factor: float32 [4, 2048, 2048], P('section', 'dp')
Inputs may be any that keep to these rules, and one draw needn't show every extreme that they name: owner_table holds each of 0 .. 7 once.
All inputs are finite; a program needn't handle non-finite values.
Results may differ from a plain program's by a relative error of at most 0.009.
Values may be sent and summed in bfloat16 or wider, within the bound.
No kernel may reach another device: no remote copies, remote signals or barrier semaphores. Data moves between devices by JAX's collectives and lax.ppermute only.
A program may use at most 128 MiB of HBM per device.

v0:
```python
import jax
import jax.numpy as jnp
from jax import lax
from jax.sharding import PartitionSpec as P

SQRT_HALF = 0.7071067811865476
INV_ROOT_TAU = 0.3989422804014327


def passed_along(value, axis, steps):
    count = lax.axis_size(axis)
    initial, last = (max(0, -steps), min(count, count - steps))
    return lax.ppermute(value, axis, [(source, source + steps) for source in range(initial, last)])


def gelu_exact(values):
    return 0.5 * values * (1.0 + jax.scipy.special.erf(values * SQRT_HALF))


def gelu_slope(values):
    return 0.5 * (
        1.0 + jax.scipy.special.erf(values * SQRT_HALF)
    ) + values * INV_ROOT_TAU * jnp.exp(-0.5 * values * values)


def normalize(activations, gain_row):
    floats = activations.astype(jnp.float32)
    center = floats - jnp.mean(floats, axis=-1, keepdims=True)
    inv_std = lax.rsqrt(jnp.mean(center * center, axis=-1, keepdims=True) + 1e-06)
    normed = center * inv_std
    return ((normed * gain_row).astype(jnp.bfloat16), normed, inv_std)


def forward_block(activations, gain_row, weight_in, weight_out, scales):
    normed_bf, normed, inv_std = normalize(activations, gain_row)
    hidden = jnp.dot(normed_bf, weight_in, preferred_element_type=jnp.float32)
    activated = gelu_exact(hidden).astype(jnp.bfloat16)
    branch = jnp.dot(activated, weight_out, preferred_element_type=jnp.float32)
    output = (activations.astype(jnp.float32) + scales * branch).astype(jnp.bfloat16)
    return (output, normed_bf, normed, inv_std, hidden)


def backward_block(cotangent, normed, inv_std, hidden, gain_row, weight_in, weight_out, scales):
    scaled = (cotangent.astype(jnp.float32) * scales).astype(jnp.bfloat16)
    grad_act = lax.dot_general(
        scaled, weight_out, (((1,), (1,)), ((), ())), preferred_element_type=jnp.float32
    )
    grad_hidden = (grad_act * gelu_slope(hidden)).astype(jnp.bfloat16)
    grad_normed = (
        lax.dot_general(
            grad_hidden, weight_in, (((1,), (1,)), ((), ())), preferred_element_type=jnp.float32
        )
        * gain_row
    )
    mean_one = jnp.mean(grad_normed, axis=-1, keepdims=True)
    mean_two = jnp.mean(grad_normed * normed, axis=-1, keepdims=True)
    grad_input = cotangent.astype(jnp.float32) + inv_std * (
        grad_normed - mean_one - normed * mean_two
    )
    return (grad_input.astype(jnp.bfloat16), grad_hidden)


def block_columns(data, owner_table):
    owners = owner_table.shape[0]
    row_total, col_total = data.shape
    split = data.reshape(row_total, owners, col_total // owners)
    return jnp.take(split, owner_table, axis=1).reshape(row_total, col_total)


def square_term(permuted, plain, total_rows):
    product = lax.dot_general(
        permuted, plain, (((0,), (0,)), ((), ())), preferred_element_type=jnp.float32
    )
    return product / total_rows


def slot_of(position, batch_count):
    valid = (position >= 0) & (position < batch_count)
    return jnp.where(valid, position, batch_count)


def body(inputs, ln_gain, w_in, w_out, layer_scale, out_grad, owner_table):
    gain_row = ln_gain[0]
    weight_in = w_in[0]
    weight_out = w_out[0]
    scales = layer_scale[0]
    section_count = lax.axis_size("section")
    dp_count = lax.axis_size("dp")
    section_index = lax.axis_index("section")
    batch_count, row_count, width_in = inputs.shape
    width_hidden = weight_in.shape[1]
    total_rows = batch_count * row_count * dp_count
    tick_count = batch_count + section_count - 1
    saved_bf = jnp.zeros((batch_count + 1, row_count, width_in), jnp.bfloat16)
    saved_normed = jnp.zeros((batch_count + 1, row_count, width_in), jnp.float32)
    saved_inv = jnp.zeros((batch_count + 1, row_count, 1), jnp.float32)
    saved_hidden = jnp.zeros((batch_count + 1, row_count, width_hidden), jnp.float32)
    arriving = jnp.zeros((row_count, width_in), jnp.bfloat16)
    for tick_step in range(tick_count):
        first_input = inputs[min(tick_step, batch_count - 1)]
        incoming = jnp.where(section_index == 0, first_input, arriving)
        output, normed_bf, normed, inv_std, hidden = forward_block(
            incoming, gain_row, weight_in, weight_out, scales
        )
        slot_index = slot_of(tick_step - section_index, batch_count)
        saved_bf = lax.dynamic_update_index_in_dim(saved_bf, normed_bf, slot_index, 0)
        saved_normed = lax.dynamic_update_index_in_dim(saved_normed, normed, slot_index, 0)
        saved_inv = lax.dynamic_update_index_in_dim(saved_inv, inv_std, slot_index, 0)
        saved_hidden = lax.dynamic_update_index_in_dim(saved_hidden, hidden, slot_index, 0)
        if tick_step + 1 < tick_count:
            arriving = passed_along(output, "section", 1)
    grad_saved = jnp.zeros((batch_count + 1, row_count, width_hidden), jnp.bfloat16)
    returning = jnp.zeros((row_count, width_in), jnp.bfloat16)
    for tick_step in range(tick_count):
        position = tick_step - (section_count - 1 - section_index)
        pick_index = jnp.clip(position, 0, batch_count - 1)
        top_grad = out_grad[min(tick_step, batch_count - 1)]
        cotangent = jnp.where(section_index == section_count - 1, top_grad, returning)
        normed = lax.dynamic_index_in_dim(saved_normed, pick_index, 0, keepdims=False)
        inv_std = lax.dynamic_index_in_dim(saved_inv, pick_index, 0, keepdims=False)
        hidden = lax.dynamic_index_in_dim(saved_hidden, pick_index, 0, keepdims=False)
        grad_input, grad_hidden = backward_block(
            cotangent, normed, inv_std, hidden, gain_row, weight_in, weight_out, scales
        )
        grad_saved = lax.dynamic_update_index_in_dim(
            grad_saved, grad_hidden, slot_of(position, batch_count), 0
        )
        if tick_step + 1 < tick_count:
            returning = passed_along(grad_input, "section", -1)
    act_rows = saved_bf[:batch_count].reshape(batch_count * row_count, width_in)
    grad_rows = grad_saved[:batch_count].reshape(batch_count * row_count, width_hidden)
    act_perm = block_columns(act_rows, owner_table)
    grad_perm = block_columns(grad_rows, owner_table)
    act_share = lax.psum_scatter(
        square_term(act_perm, act_rows, total_rows), "dp", scatter_dimension=0, tiled=True
    )
    grad_share = lax.psum_scatter(
        square_term(grad_perm, grad_rows, total_rows), "dp", scatter_dimension=0, tiled=True
    )
    return (act_share[None], grad_share[None])


def solution(mesh):
    placed = (
        P(None, "dp", None),
        P("section", None),
        P("section", None, None),
        P("section", None, None),
        P("section", None),
        P(None, "dp", None),
        P(),
    )
    return jax.shard_map(
        body,
        mesh=mesh,
        in_specs=placed,
        out_specs=(P("section", "dp", None), P("section", "dp", None)),
        check_vma=False,
    )
```

profile of v0, /device:TPU:9, one launch (start us, length us, event | category | flops | bytes accessed | tf_op | source)
XLA Modules:
  0.0 246.0 jit_solution(2927719133032820114)
XLA Ops:
  7.2 1.0 convert_reduce_fusion.3
  8.3 1.1 fusion.195
  9.6 3.3 %bitcast_dynamic-update-slice_fusion.3 = (f32[3,64,2048]{2,1,0:T(8,128)S(1)}, f32[64,2048]{1,0:T(8,128)S(1)}) fusion(f32[3,64,2048]{2,1,0:T(8,128)S(1)} %broadcast_in_dim.138, s32[]{:T(128)S(6)} %select_n.192, bf16[1,1024,2048]{2,1,0:T(8,128)(2,1)} %param.9, f32[1024]{0:T(1024)} %bitcast.400, f32[64]{0:T(128)S(1)} %add_rsqrt_fusion.4, ...), kind=kOutput, calls=%fused_computation.118 | convolution fusion | flops 268828672 | bytes 5379077 | tf_op jit(solution)/shard_map/dot_general | solution.py:36
  13.0 0.9 fusion.123
  13.9 3.2 %collective-permute-start = (bf16[64,1024]{1,0:T(8,128)(2,1)S(1)}, bf16[64,1024]{1,0:T(8,128)(2,1)S(1)}, u32[]{:S(2)}, u32[]{:S(2)}) collective-permute-start(bf16[64,1024]{1,0:T(8,128)(2,1)S(1)} %fusion.123), channel_id=1, source_target_pairs={{0,1},{1,2},{2,3},{4,5},{5,6},{6,7},{8,9},{9,10},{10,11},{12,13},{... | collective-permute-start | bytes 393224 | tf_op jit(solution)/shard_map/ppermute | solution.py:13
  17.1 0.6 compare_and_fusion
  18.2 1.9 collective-permute-done
  20.7 3.1 %bitcast_dynamic-update-slice_fusion.2 = (f32[3,64,2048]{2,1,0:T(8,128)S(1)}, f32[64,2048]{1,0:T(8,128)S(1)}) fusion(f32[3,64,2048]{2,1,0:T(8,128)S(1)} %get-tuple-element.22, s32[]{:T(128)S(6)} %select_n.196, bf16[1,1024,2048]{2,1,0:T(8,128)(2,1)} %param.9, bf16[64,1024]{1,0:T(8,128)(2,1)S(1)} %get-tuple-element.17, f32[1024]{0:T(1024)S(1)} %bitcast.403, ...), kind=kOutput, calls=%fused_computation.117 | convolution fusion | flops 268763136 | bytes 5379076 | tf_op jit(solution)/shard_map/dot_general | solution.py:36
  23.8 0.9 fusion.120
  24.7 3.3 %collective-permute-start.1 = (bf16[64,1024]{1,0:T(8,128)(2,1)S(1)}, bf16[64,1024]{1,0:T(8,128)(2,1)S(1)}, u32[]{:S(2)}, u32[]{:S(2)}) collective-permute-start(bf16[64,1024]{1,0:T(8,128)(2,1)S(1)} %fusion.120), channel_id=1, source_target_pairs={{0,1},{1,2},{2,3},{4,5},{5,6},{6,7},{8,9},{9,10},{10,11},{12,13},{... | collective-permute-start | bytes 393224 | tf_op jit(solution)/shard_map/ppermute | solution.py:13
  28.1 2.5 %collective-permute-done.1 = bf16[64,1024]{1,0:T(8,128)(2,1)S(1)} collective-permute-done((bf16[64,1024]{1,0:T(8,128)(2,1)S(1)}, bf16[64,1024]{1,0:T(8,128)(2,1)S(1)}, u32[]{:S(2)}, u32[]{:S(2)}) %collective-permute-start.1) | collective-permute-done | bytes 131104 | tf_op jit(solution)/shard_map/ppermute | solution.py:13
  31.1 0.9 bitcast_dynamic-update-slice_fusion.1
  32.1 0.9 fusion.117
  32.9 3.2 %collective-permute-start.2 = (bf16[64,1024]{1,0:T(8,128)(2,1)S(1)}, bf16[64,1024]{1,0:T(8,128)(2,1)S(1)}, u32[]{:S(2)}, u32[]{:S(2)}) collective-permute-start(bf16[64,1024]{1,0:T(8,128)(2,1)S(1)} %fusion.117), channel_id=1, source_target_pairs={{0,1},{1,2},{2,3},{4,5},{5,6},{6,7},{8,9},{9,10},{10,11},{12,13},{... | collective-permute-start | bytes 393224 | tf_op jit(solution)/shard_map/ppermute | solution.py:13
  36.1 2.5 %collective-permute-done.2 = bf16[64,1024]{1,0:T(8,128)(2,1)S(1)} collective-permute-done((bf16[64,1024]{1,0:T(8,128)(2,1)S(1)}, bf16[64,1024]{1,0:T(8,128)(2,1)S(1)}, u32[]{:S(2)}, u32[]{:S(2)}) %collective-permute-start.2) | collective-permute-done | bytes 131104 | tf_op jit(solution)/shard_map/ppermute | solution.py:13
  39.2 0.9 bitcast_dynamic-update-slice_fusion
  40.1 0.9 fusion.114
  41.0 3.2 %collective-permute-start.3 = (bf16[64,1024]{1,0:T(8,128)(2,1)S(1)}, bf16[64,1024]{1,0:T(8,128)(2,1)S(1)}, u32[]{:S(2)}, u32[]{:S(2)}) collective-permute-start(bf16[64,1024]{1,0:T(8,128)(2,1)S(1)} %fusion.114), channel_id=1, source_target_pairs={{0,1},{1,2},{2,3},{4,5},{5,6},{6,7},{8,9},{9,10},{10,11},{12,13},{... | collective-permute-start | bytes 393224 | tf_op jit(solution)/shard_map/ppermute | solution.py:13
  44.2 2.5 %collective-permute-done.3 = bf16[64,1024]{1,0:T(8,128)(2,1)S(1)} collective-permute-done((bf16[64,1024]{1,0:T(8,128)(2,1)S(1)}, bf16[64,1024]{1,0:T(8,128)(2,1)S(1)}, u32[]{:S(2)}, u32[]{:S(2)}) %collective-permute-start.3) | collective-permute-done | bytes 131104 | tf_op jit(solution)/shard_map/ppermute | solution.py:13
  47.2 0.9 fusion.54
  48.3 0.6 gather_fusion
  48.9 0.8 select_bitcast_fusion.1
  49.9 2.6 %convolution_multiply_fusion.1 = f32[1024,1024]{1,0:T(8,128)} fusion(bf16[128,1024]{0,1:T(8,128)(2,1)S(1)} %bitcast.398, bf16[128,1024]{1,0:T(8,128)(2,1)S(1)} %bitcast.396), kind=kOutput, calls=%fused_computation.53 | convolution fusion | flops 269484032 | bytes 4718592 | tf_op jit(solution)/shard_map/dot_general | solution.py:71
  52.7 3.8 %bitcast_dynamic-update-slice_fusion.7 = (bf16[3,64,2048]{2,1,0:T(8,128)(2,1)S(1)}, bf16[64,2048]{1,0:T(8,128)(2,1)S(1)}) fusion(bf16[3,64,2048]{2,1,0:T(8,128)(2,1)S(1)} %broadcast_in_dim.137, s32[]{:T(128)S(6)} %select_n.211, f32[3,64,2048]{2,1,0:T(8,128)S(1)} %fusion.54, s32[]{:T(128)S(6)} %min.16, bf16[1,2048,1024]{2,1,0:T(8,128)(2,1)} %param.10, ...), kind=kOutput, calls=%fused_computation.210 | convolution fusion | flops 270008320 | bytes 5378057 | tf_op jit(solution)/shard_map/dot_general | solution.py:45
  56.5 1.5 fusion.263
  58.0 0.6 fusion.241
  58.6 0.8 fusion.187
  59.4 2.1 collective-permute-start.4
  61.5 3.8 %collective-permute-done.4 = bf16[64,1024]{1,0:T(8,128)(2,1)S(1)} collective-permute-done((bf16[64,1024]{1,0:T(8,128)(2,1)}, bf16[64,1024]{1,0:T(8,128)(2,1)S(1)}, u32[]{:S(2)}, u32[]{:S(2)}) %collective-permute-start.4) | collective-permute-done | bytes 131104 | tf_op jit(solution)/shard_map/ppermute | solution.py:13
  65.3 4.1 %bitcast_dynamic-update-slice_fusion.6 = (bf16[3,64,2048]{2,1,0:T(8,128)(2,1)S(1)}, bf16[64,2048]{1,0:T(8,128)(2,1)S(1)}) fusion(bf16[3,64,2048]{2,1,0:T(8,128)(2,1)S(1)} %get-tuple-element.30, s32[]{:T(128)S(6)} %select_n.215, f32[3,64,2048]{2,1,0:T(8,128)S(1)} %fusion.54, s32[]{:T(128)S(6)} %min.17, bf16[1,2048,1024]{2,1,0:T(8,128)(2,1)} %param.10, ...), kind=kOutput, calls=%fused_computation.204 | convolution fusion | flops 270008320 | bytes 5509129 | tf_op jit(solution)/shard_map/dot_general | solution.py:45
  69.4 1.5 fusion.262
  70.9 0.8 fusion.189
  71.7 1.9 collective-permute-start.5
  73.7 4.0 %collective-permute-done.5 = bf16[64,1024]{1,0:T(8,128)(2,1)S(1)} collective-permute-done((bf16[64,1024]{1,0:T(8,128)(2,1)}, bf16[64,1024]{1,0:T(8,128)(2,1)S(1)}, u32[]{:S(2)}, u32[]{:S(2)}) %collective-permute-start.5) | collective-permute-done | bytes 131104 | tf_op jit(solution)/shard_map/ppermute | solution.py:13
  77.6 3.6 %bitcast_dynamic-update-slice_fusion.5 = (bf16[3,64,2048]{2,1,0:T(8,128)(2,1)S(1)}, bf16[64,2048]{1,0:T(8,128)(2,1)S(1)}) fusion(bf16[3,64,2048]{2,1,0:T(8,128)(2,1)S(1)} %get-tuple-element.33, s32[]{:T(128)S(6)} %select_n.218, f32[3,64,2048]{2,1,0:T(8,128)S(1)} %fusion.54, s32[]{:T(128)S(6)} %min.18, bf16[1,2048,1024]{2,1,0:T(8,128)(2,1)} %param.10, ...), kind=kOutput, calls=%fused_computation.198 | convolution fusion | flops 270008320 | bytes 5509129 | tf_op jit(solution)/shard_map/dot_general | solution.py:45
  81.3 1.5 fusion.261
  82.8 0.8 fusion.191
  83.6 1.9 collective-permute-start.6
  85.5 4.4 %collective-permute-done.6 = bf16[64,1024]{1,0:T(8,128)(2,1)S(1)} collective-permute-done((bf16[64,1024]{1,0:T(8,128)(2,1)}, bf16[64,1024]{1,0:T(8,128)(2,1)S(1)}, u32[]{:S(2)}, u32[]{:S(2)}) %collective-permute-start.6) | collective-permute-done | bytes 131104 | tf_op jit(solution)/shard_map/ppermute | solution.py:13
  89.9 3.6 %bitcast_dynamic-update-slice_fusion.4 = (bf16[3,64,2048]{2,1,0:T(8,128)(2,1)S(1)}, bf16[64,2048]{1,0:T(8,128)(2,1)S(1)}) fusion(bf16[3,64,2048]{2,1,0:T(8,128)(2,1)S(1)} %get-tuple-element.36, s32[]{:T(128)S(6)} %select_n.221, f32[3,64,2048]{2,1,0:T(8,128)S(1)} %fusion.54, s32[]{:T(128)S(6)} %min.19, bf16[1,2048,1024]{2,1,0:T(8,128)(2,1)} %param.10, ...), kind=kOutput, calls=%fused_computation.192 | convolution fusion | flops 270008320 | bytes 5509129 | tf_op jit(solution)/shard_map/dot_general | solution.py:45
  93.5 1.5 fusion.260
  95.0 0.8 fusion.193
  95.8 1.9 collective-permute-start.7
  97.7 4.0 %collective-permute-done.7 = bf16[64,1024]{1,0:T(8,128)(2,1)S(1)} collective-permute-done((bf16[64,1024]{1,0:T(8,128)(2,1)}, bf16[64,1024]{1,0:T(8,128)(2,1)S(1)}, u32[]{:S(2)}, u32[]{:S(2)}) %collective-permute-start.7) | collective-permute-done | bytes 131104 | tf_op jit(solution)/shard_map/ppermute | solution.py:13
  101.7 3.6 %fusion.75 = bf16[3,64,2048]{2,1,0:T(8,128)(2,1)S(1)} fusion(bf16[3,64,2048]{2,1,0:T(8,128)(2,1)S(1)} %get-tuple-element.39, s32[]{:T(128)S(6)} %select_n.224, bf16[1,2048,1024]{2,1,0:T(8,128)(2,1)} %param.10, f32[3,64,2048]{2,1,0:T(8,128)S(1)} %fusion.54, s32[]{:T(128)S(6)} %min.20, bf16[64,1024]{1,0:T(8,128)(2,1)S(1)} %collective-permute-done.7, ...), kind=kOutput, calls=%fused_computation.52 | convolution fusion | flops 270008320 | bytes 5246985 | tf_op jit(solution)/shard_map/dot_general | solution.py:45
  105.6 0.6 gather_fusion.1
  106.6 8.1 %convolution_multiply_fusion = f32[2048,2048]{1,0:T(8,128)} fusion(bf16[128,2048]{0,1:T(8,128)(2,1)S(1)} %bitcast.394, bf16[128,2048]{1,0:T(8,128)(2,1)S(1)} %bitcast.393), kind=kOutput, calls=%fused_computation.2 | convolution fusion | flops 1077936128 | bytes 17825792 | tf_op jit(solution)/shard_map/dot_general | solution.py:71
  114.7 124.4 %reduce-scatter.5.cloned.1.call-done = f32[256,2048]{1,0:T(8,128)} async-done(((f32[2048,2048]{1,0:T(8,128)}), f32[256,2048]{1,0:T(8,128)}) %reduce-scatter.5.cloned.1.call-update) | async-done | bytes 2097168 | tf_op jit(solution)/shard_map/reduce_scatter | solution.py:137
  (93 shorter events, 4.1 us)
Async XLA Ops:
  7.2 5.8 %copy-start.7 = (bf16[2,64,1024]{2,1,0:T(8,128)(2,1)S(1)}, bf16[2,64,1024]{2,1,0:T(8,128)(2,1)}, u32[]{:S(2)}) copy-start(bf16[2,64,1024]{2,1,0:T(8,128)(2,1)} %param.7) | copy-start | bytes 786436
  7.2 5.8 %copy-start.10 = (f32[1,1024]{1,0:T(1,128)S(1)}, f32[1,1024]{1,0:T(1,128)}, u32[]{:S(2)}) copy-start(f32[1,1024]{1,0:T(1,128)} %param.11) | copy-start | bytes 12292
  7.2 107.5 %reduce-scatter.3.cloned.1.call-start = ((), (), s32[]{:S(2)}) async-start(), calls=%async_computation.2 | async-start | bytes 4718592 | tf_op jit(solution)/shard_map/reduce_scatter | solution.py:134
  9.4 3.6 %copy-start.5 = (bf16[1,2048,1024]{2,1,0:T(8,128)(2,1)S(1)}, bf16[1,2048,1024]{2,1,0:T(8,128)(2,1)}, u32[]{:S(2)}) copy-start(bf16[1,2048,1024]{2,1,0:T(8,128)(2,1)} %param.10) | copy-start | bytes 12582916
  9.6 7.5 %copy-start.15 = (s32[8]{0:T(128)S(1)}, s32[8]{0:T(128)}, u32[]{:S(2)}) copy-start(s32[8]{0:T(128)} %param.13) | copy-start | bytes 100
  9.6 8.1 %copy-start.9 = (f32[1,1024]{1,0:T(1,128)S(1)}, f32[1,1024]{1,0:T(1,128)}, u32[]{:S(2)}) copy-start(f32[1,1024]{1,0:T(1,128)} %param.8) | copy-start | bytes 12292
  13.9 6.3 %collective-permute-start = (bf16[64,1024]{1,0:T(8,128)(2,1)S(1)}, bf16[64,1024]{1,0:T(8,128)(2,1)S(1)}, u32[]{:S(2)}, u32[]{:S(2)}) collective-permute-start(bf16[64,1024]{1,0:T(8,128)(2,1)S(1)} %fusion.123), channel_id=1, source_target_pairs={{0,1},{1,2},{2,3},{4,5},{5,6},{6,7},{8,9},{9,10},{10,11},{12,13},{... | collective-permute-start | bytes 393224 | tf_op jit(solution)/shard_map/ppermute | solution.py:13
  18.1 5.7 %copy-start.6 = (bf16[1,2048,1024]{2,1,0:T(8,128)(2,1)S(1)}, bf16[1,2048,1024]{2,1,0:T(8,128)(2,1)}, u32[]{:S(2)}) copy-start(bf16[1,2048,1024]{2,1,0:T(8,128)(2,1)} %param.10) | copy-start | bytes 12582916
  23.8 7.3 %copy-start = (bf16[1,1024,2048]{2,1,0:T(8,128)(2,1)S(1)}, bf16[1,1024,2048]{2,1,0:T(8,128)(2,1)}, u32[]{:S(2)}) copy-start(bf16[1,1024,2048]{2,1,0:T(8,128)(2,1)} %param.9) | copy-start | bytes 12582916
  24.7 5.8 %collective-permute-start.1 = (bf16[64,1024]{1,0:T(8,128)(2,1)S(1)}, bf16[64,1024]{1,0:T(8,128)(2,1)S(1)}, u32[]{:S(2)}, u32[]{:S(2)}) collective-permute-start(bf16[64,1024]{1,0:T(8,128)(2,1)S(1)} %fusion.120), channel_id=1, source_target_pairs={{0,1},{1,2},{2,3},{4,5},{5,6},{6,7},{8,9},{9,10},{10,11},{12,13},{... | collective-permute-start | bytes 393224 | tf_op jit(solution)/shard_map/ppermute | solution.py:13
  32.9 5.7 %collective-permute-start.2 = (bf16[64,1024]{1,0:T(8,128)(2,1)S(1)}, bf16[64,1024]{1,0:T(8,128)(2,1)S(1)}, u32[]{:S(2)}, u32[]{:S(2)}) collective-permute-start(bf16[64,1024]{1,0:T(8,128)(2,1)S(1)} %fusion.117), channel_id=1, source_target_pairs={{0,1},{1,2},{2,3},{4,5},{5,6},{6,7},{8,9},{9,10},{10,11},{12,13},{... | collective-permute-start | bytes 393224 | tf_op jit(solution)/shard_map/ppermute | solution.py:13
  41.0 5.7 %collective-permute-start.3 = (bf16[64,1024]{1,0:T(8,128)(2,1)S(1)}, bf16[64,1024]{1,0:T(8,128)(2,1)S(1)}, u32[]{:S(2)}, u32[]{:S(2)}) collective-permute-start(bf16[64,1024]{1,0:T(8,128)(2,1)S(1)} %fusion.114), channel_id=1, source_target_pairs={{0,1},{1,2},{2,3},{4,5},{5,6},{6,7},{8,9},{9,10},{10,11},{12,13},{... | collective-permute-start | bytes 393224 | tf_op jit(solution)/shard_map/ppermute | solution.py:13
  49.9 2.8 %copy-start.8 = (bf16[2,64,1024]{2,1,0:T(8,128)(2,1)S(1)}, bf16[2,64,1024]{2,1,0:T(8,128)(2,1)}, u32[]{:S(2)}) copy-start(bf16[2,64,1024]{2,1,0:T(8,128)(2,1)} %param.12) | copy-start | bytes 786436
  52.6 186.6 %reduce-scatter.5.cloned.1.call-start = ((), (), s32[]{:S(2)}) async-start(), calls=%async_computation.3 | async-start | bytes 18874368 | tf_op jit(solution)/shard_map/reduce_scatter | solution.py:137
  52.6 3.9 %copy-start.1 = (bf16[1,1024,2048]{2,1,0:T(8,128)(2,1)S(1)}, bf16[1,1024,2048]{2,1,0:T(8,128)(2,1)}, u32[]{:S(2)}) copy-start(bf16[1,1024,2048]{2,1,0:T(8,128)(2,1)} %param.9) | copy-start | bytes 12582916
  59.4 5.9 %collective-permute-start.4 = (bf16[64,1024]{1,0:T(8,128)(2,1)}, bf16[64,1024]{1,0:T(8,128)(2,1)S(1)}, u32[]{:S(2)}, u32[]{:S(2)}) collective-permute-start(bf16[64,1024]{1,0:T(8,128)(2,1)} %fusion.187), channel_id=1, source_target_pairs={{1,0},{2,1},{3,2},{5,4},{6,5},{7,6},{9,8},{10,9},{11,10},{13,12},{... | collective-permute-start | bytes 393224 | tf_op jit(solution)/shard_map/ppermute | solution.py:13
  61.5 7.9 %copy-start.2 = (bf16[1,1024,2048]{2,1,0:T(8,128)(2,1)S(1)}, bf16[1,1024,2048]{2,1,0:T(8,128)(2,1)}, u32[]{:S(2)}) copy-start(bf16[1,1024,2048]{2,1,0:T(8,128)(2,1)} %param.9) | copy-start | bytes 12582916
  65.3 5.6 %copy-start.14 = (f32[64]{0:T(128)S(1)}, f32[64]{0:T(128)}, u32[]{:S(2)}) copy-start(f32[64]{0:T(128)} %get-tuple-element.20) | copy-start | bytes 772
  71.7 5.9 %collective-permute-start.5 = (bf16[64,1024]{1,0:T(8,128)(2,1)}, bf16[64,1024]{1,0:T(8,128)(2,1)S(1)}, u32[]{:S(2)}, u32[]{:S(2)}) collective-permute-start(bf16[64,1024]{1,0:T(8,128)(2,1)} %fusion.189), channel_id=1, source_target_pairs={{1,0},{2,1},{3,2},{5,4},{6,5},{7,6},{9,8},{10,9},{11,10},{13,12},{... | collective-permute-start | bytes 393224 | tf_op jit(solution)/shard_map/ppermute | solution.py:13
  73.7 7.6 %copy-start.3 = (bf16[1,1024,2048]{2,1,0:T(8,128)(2,1)S(1)}, bf16[1,1024,2048]{2,1,0:T(8,128)(2,1)}, u32[]{:S(2)}) copy-start(bf16[1,1024,2048]{2,1,0:T(8,128)(2,1)} %param.9) | copy-start | bytes 12582916
  77.6 5.1 %copy-start.13 = (f32[64]{0:T(128)S(1)}, f32[64]{0:T(128)}, u32[]{:S(2)}) copy-start(f32[64]{0:T(128)} %get-tuple-element.19) | copy-start | bytes 772
  83.6 6.3 %collective-permute-start.6 = (bf16[64,1024]{1,0:T(8,128)(2,1)}, bf16[64,1024]{1,0:T(8,128)(2,1)S(1)}, u32[]{:S(2)}, u32[]{:S(2)}) collective-permute-start(bf16[64,1024]{1,0:T(8,128)(2,1)} %fusion.191), channel_id=1, source_target_pairs={{1,0},{2,1},{3,2},{5,4},{6,5},{7,6},{9,8},{10,9},{11,10},{13,12},{... | collective-permute-start | bytes 393224 | tf_op jit(solution)/shard_map/ppermute | solution.py:13
  85.5 8.0 %copy-start.4 = (bf16[1,1024,2048]{2,1,0:T(8,128)(2,1)S(1)}, bf16[1,1024,2048]{2,1,0:T(8,128)(2,1)}, u32[]{:S(2)}) copy-start(bf16[1,1024,2048]{2,1,0:T(8,128)(2,1)} %param.9) | copy-start | bytes 12582916
  89.9 5.1 %copy-start.12 = (f32[64]{0:T(128)S(1)}, f32[64]{0:T(128)}, u32[]{:S(2)}) copy-start(f32[64]{0:T(128)} %get-tuple-element.18) | copy-start | bytes 772
  95.8 5.9 %collective-permute-start.7 = (bf16[64,1024]{1,0:T(8,128)(2,1)}, bf16[64,1024]{1,0:T(8,128)(2,1)S(1)}, u32[]{:S(2)}, u32[]{:S(2)}) collective-permute-start(bf16[64,1024]{1,0:T(8,128)(2,1)} %fusion.193), channel_id=1, source_target_pairs={{1,0},{2,1},{3,2},{5,4},{6,5},{7,6},{9,8},{10,9},{11,10},{13,12},{... | collective-permute-start | bytes 393224 | tf_op jit(solution)/shard_map/ppermute | solution.py:13
  101.7 4.5 %copy-start.11 = (pred[8]{0:T(512)(128)(4,1)S(1)}, pred[8]{0:T(512)(128)(4,1)}, u32[]{:S(2)}) copy-start(pred[8]{0:T(512)(128)(4,1)} %compare_and_fusion) | copy-start | bytes 28
Sparse Core Ops, SparseCore 0:
  52.7 56.8 reduce-scatter.2
  114.8 124.2 reduce-scatter.4
where the time goes:
time: 248 us; the launch traced here: 246 us
  waiting for transfers between devices  150 us (60%)
  matrix products  47.9 us (19%)
  starting transfers between devices  20.8 us (8%)
  between operations  14.8 us (6%)
  other arithmetic  9.4 us (4%)
  local copies, waits for them, and re-layouts  3.04 us (1%)
    reduce_scatter x1, waiting for transfers between devices, body(): lax.psum_scatter(square_term(grad_perm, grad_rows, total_rows), 'dp', sca...  124 us
    ppermute x8, waiting for transfers between devices, passed_along(): lax.ppermute(value, axis, [(source, source + steps) for source in range(i...  25.5 us
    ppermute x8, starting transfers between devices, passed_along(): lax.ppermute(value, axis, [(source, source + steps) for source in range(i...  20.8 us
    dot_general x5, matrix products, backward_block(): lax.dot_general(scaled, weight_out, (((1,), (1,)), ((), ())), preferred_e...  18.7 us
    dot_general x2, matrix products, square_term(): lax.dot_general(permuted, plain, (((0,), (0,)), ((), ())), preferred_elem...  10.7 us
    dot_general x5, matrix products, forward_block(): hidden = jnp.dot(normed_bf, weight_in, preferred_element_type=jnp.float32)  9.14 us
    dot_general x4, matrix products, backward_block(): lax.dot_general(grad_hidden, weight_in, (((1,), (1,)), ((), ())), preferr...  5.99 us
  transfers between devices with their start and end apart: 10, of which 9 were waited for; matrix products, arithmetic and copies ran while one was open for 16% of the time, Pallas kernels for 0%

commit v1 on v0

v1 whole, which is shorter than its diff:
```python
import jax
import jax.numpy as jnp
from jax import lax
from jax.sharding import PartitionSpec as P

SQRT_HALF = 0.7071067811865476
INV_ROOT_TAU = 0.3989422804014327


def hop(value, source, steps):
    return lax.ppermute(value, "section", [(source, source + steps)])


def swapped(value, axis, mask):
    count = lax.axis_size(axis)
    return lax.ppermute(value, axis, [(source, source ^ mask) for source in range(count)])


def turned(value, axis, steps):
    count = lax.axis_size(axis)
    return lax.ppermute(value, axis, [(source, (source + steps) % count) for source in range(count)])


def gathered(value, axis):
    count = lax.axis_size(axis)
    if count & (count - 1):
        return [value] + [turned(value, axis, steps) for steps in range(1, count)]
    if count == 1:
        return [value]
    blocks = [value] + [swapped(value, axis, mask) for mask in range(2, count, 2)]
    return blocks + [swapped(block, axis, 1) for block in blocks]


def gelu_exact(values):
    return 0.5 * values * (1.0 + jax.scipy.special.erf(values * SQRT_HALF))


def gelu_slope(values):
    return 0.5 * (
        1.0 + jax.scipy.special.erf(values * SQRT_HALF)
    ) + values * INV_ROOT_TAU * jnp.exp(-0.5 * values * values)


def normalize(activations, gain_row):
    floats = activations.astype(jnp.float32)
    center = floats - jnp.mean(floats, axis=-1, keepdims=True)
    inv_std = lax.rsqrt(jnp.mean(center * center, axis=-1, keepdims=True) + 1e-06)
    normed = center * inv_std
    return ((normed * gain_row).astype(jnp.bfloat16), normed, inv_std)


def forward_block(activations, gain_row, weight_in, weight_out, scales):
    normed_bf, _, _ = normalize(activations, gain_row)
    hidden = jnp.dot(normed_bf, weight_in, preferred_element_type=jnp.float32)
    activated = gelu_exact(hidden).astype(jnp.bfloat16)
    branch = jnp.dot(activated, weight_out, preferred_element_type=jnp.float32)
    return (activations.astype(jnp.float32) + scales * branch).astype(jnp.bfloat16)


def hidden_grad(cotangent, slope, weight_out, scales):
    scaled = (cotangent.astype(jnp.float32) * scales).astype(jnp.bfloat16)
    grad_act = lax.dot_general(
        scaled, weight_out, (((1,), (1,)), ((), ())), preferred_element_type=jnp.float32
    )
    return (grad_act * slope).astype(jnp.bfloat16)


def input_grad(cotangent, grad_hidden, normed, inv_std, gain_row, weight_in):
    grad_normed = (
        lax.dot_general(
            grad_hidden, weight_in, (((1,), (1,)), ((), ())), preferred_element_type=jnp.float32
        )
        * gain_row
    )
    mean_one = jnp.mean(grad_normed, axis=-1, keepdims=True)
    mean_two = jnp.mean(grad_normed * normed, axis=-1, keepdims=True)
    grad_input = cotangent.astype(jnp.float32) + inv_std * (
        grad_normed - mean_one - normed * mean_two
    )
    return grad_input.astype(jnp.bfloat16)


def owned_square(blocks, owner, owners, total_rows):
    rows = jnp.concatenate(blocks, axis=0)
    width = rows.shape[1] // owners
    own = lax.dynamic_slice_in_dim(rows, owner * width, width, axis=1)
    product = lax.dot_general(
        own, rows, (((0,), (0,)), ((), ())), preferred_element_type=jnp.float32
    )
    return product / total_rows


def body(inputs, ln_gain, w_in, w_out, layer_scale, out_grad, owner_table):
    gain_row = ln_gain[0]
    weight_in = w_in[0]
    weight_out = w_out[0]
    scales = layer_scale[0]
    section_count = lax.axis_size("section")
    dp_count = lax.axis_size("dp")
    section_index = lax.axis_index("section")
    batch_count, row_count, _ = inputs.shape
    total_rows = batch_count * row_count * dp_count
    owner = owner_table[lax.axis_index("dp")]
    batches = range(batch_count)

    held = [inputs[m] for m in batches]
    for step in range(section_count - 1):
        for m in batches:
            output = forward_block(held[m], gain_row, weight_in, weight_out, scales)
            arrived = hop(output, step, 1)
            held[m] = jnp.where(section_index == step + 1, arrived, held[m])
    saved = []
    for m in batches:
        normed_bf, normed, inv_std = normalize(held[m], gain_row)
        hidden = jnp.dot(normed_bf, weight_in, preferred_element_type=jnp.float32)
        saved.append((normed_bf, normed, inv_std, gelu_slope(hidden)))

    returning = [out_grad[m] for m in batches]
    for step in range(section_count - 1, 0, -1):
        for m in batches:
            _, normed, inv_std, slope = saved[m]
            grad_hidden = hidden_grad(returning[m], slope, weight_out, scales)
            grad_input = input_grad(
                returning[m], grad_hidden, normed, inv_std, gain_row, weight_in
            )
            arrived = hop(grad_input, step, -1)
            returning[m] = jnp.where(section_index == step - 1, arrived, returning[m])
    act_blocks, grad_blocks = [], []
    for m in batches:
        act_blocks += gathered(saved[m][0], "dp")
    for m in batches:
        grad_blocks += gathered(hidden_grad(returning[m], saved[m][3], weight_out, scales), "dp")
    act_share = owned_square(act_blocks, owner, dp_count, total_rows)
    grad_share = owned_square(grad_blocks, owner, dp_count, total_rows)
    return (act_share[None], grad_share[None])


def solution(mesh):
    placed = (
        P(None, "dp", None),
        P("section", None),
        P("section", None, None),
        P("section", None, None),
        P("section", None),
        P(None, "dp", None),
        P(),
    )
    return jax.shard_map(
        body,
        mesh=mesh,
        in_specs=placed,
        out_specs=(P("section", "dp", None), P("section", "dp", None)),
        check_vma=False,
    )
```

time: 248 us -> 192 us (0.77)
  waiting for transfers between devices: 150 us -> 18.1 us
  matrix products: 47.9 us -> 90.4 us
  starting transfers between devices: 20.8 us -> 44.4 us
  other arithmetic: 9.4 us -> 23 us
  between operations: 14.8 us -> 2.62 us
  local copies, waits for them, and re-layouts: 3.04 us -> 11.6 us
    reduce_scatter x2 -> x0, waiting for transfers between devices: 124 us -> none  [the longest x1 124 us: body(): lax.psum_scatter(square_term(grad_perm, grad_rows, total_rows), 'dp', sca...]
    dot_general x4 -> x6, matrix products: 3.44 us -> 30.9 us  [forward_block(): branch = jnp.dot(activated, weight_out, preferred_element_type=jnp.float32)]
    ppermute x8 -> x40, starting transfers between devices: 20.8 us -> 44.4 us  [the longest x28 28.9 us: swapped(): lax.ppermute(value, axis, [(source, source ^ mask) for source in range(co...]
    dot_general x16 -> x12, matrix products: 44.5 us -> 59.5 us  [the longest x6 44.1 us: input_grad(): lax.dot_general(grad_hidden, weight_in, (((1,), (1,)), ((), ())), preferr...]
    unnamed x34 -> x44, local copies, waits for them, and re-layouts: 0.24 us -> 9.45 us
    ppermute x8 -> x40, waiting for transfers between devices: 25.5 us -> 18.1 us  [the longest x28 13.2 us: swapped(): lax.ppermute(value, axis, [(source, source ^ mask) for source in range(co...]
    div x7 -> x12, other arithmetic: 0.03 us -> 5.64 us  [the longest x6 3.13 us: input_grad(): mean_two = jnp.mean(grad_normed * normed, axis=-1, keepdims=True)]
    convert_element_type x4 -> x5, other arithmetic: 3.14 us -> 7.47 us  [input_grad(): return grad_input.astype(jnp.bfloat16)]
  transfers between devices with their start and end apart: 10 -> 40, of which waited for: 9 -> 9; matrix products, arithmetic and copies ran while one was open for 16% -> 50% of each run, Pallas kernels for 0% -> 0%
where the time goes in v1:
time: 192 us; the launch traced here: 190 us
  matrix products  90.4 us (47%)
  starting transfers between devices  44.4 us (23%)
  other arithmetic  23 us (12%)
  waiting for transfers between devices  18.1 us (9%)
  local copies, waits for them, and re-layouts  11.6 us (6%)
  between operations  2.62 us (1%)
    dot_general x6, matrix products, input_grad(): lax.dot_general(grad_hidden, weight_in, (((1,), (1,)), ((), ())), preferr...  44.1 us
    dot_general x6, matrix products, forward_block(): branch = jnp.dot(activated, weight_out, preferred_element_type=jnp.float32)  30.9 us
    ppermute x28, starting transfers between devices, swapped(): lax.ppermute(value, axis, [(source, source ^ mask) for source in range(co...  28.9 us
    ppermute x12, starting transfers between devices, hop(): return lax.ppermute(value, 'section', [(source, source + steps)])  15.5 us
    ppermute x28, waiting for transfers between devices, swapped(): lax.ppermute(value, axis, [(source, source ^ mask) for source in range(co...  13.2 us
    unnamed x44, local copies, waits for them, and re-layouts  9.45 us
    convert_element_type x5, other arithmetic, input_grad(): return grad_input.astype(jnp.bfloat16)  7.47 us
    dot_general x2, matrix products, body(): hidden = jnp.dot(normed_bf, weight_in, preferred_element_type=jnp.float32)  6.34 us
  transfers between devices with their start and end apart: 40, of which 9 were waited for; matrix products, arithmetic and copies ran while one was open for 50% of the time, Pallas kernels for 0%

profile of v1, /device:TPU:9, one launch (start us, length us, event | category | flops | bytes accessed | tf_op | source)
XLA Modules:
  0.0 190.1 jit_solution(15967235144704514809)
XLA Ops:
  3.0 5.3 %fusion.166 = bf16[64,1024]{1,0:T(8,128)(2,1)S(1)} fusion(bf16[1,2048,1024]{2,1,0:T(8,128)(2,1)} %param.10, bf16[1,1024,2048]{2,1,0:T(8,128)(2,1)} %param.9, f32[64]{0:T(128)S(1)} %add_rsqrt_fusion.3, f32[64]{0:T(128)S(1)} %get-tuple-element.50, f32[1024]{0:T(1024)} %bitcast.256, f32[1024]{0:T(1024)} %bitcast.270, bf16[2,64,1024]{2,1,0:T(8,128)(2,1)} %param.7), kind=kOutput, calls=%fused_computation.96 | convolution fusion | flops 538116096 | bytes 8790528 | tf_op jit(solution)/shard_map/dot_general | solution.py:56
  8.3 1.3 collective-permute-start.10
  9.6 5.1 %fusion.175 = bf16[64,1024]{1,0:T(8,128)(2,1)S(1)} fusion(bf16[1,2048,1024]{2,1,0:T(8,128)(2,1)} %param.10, bf16[1,1024,2048]{2,1,0:T(8,128)(2,1)} %param.9, f32[1024]{0:T(1024)S(1)} %bitcast.257, f32[64]{0:T(128)S(1)} %add_rsqrt_fusion.7, f32[64]{0:T(128)S(1)} %get-tuple-element.51, f32[1024]{0:T(1024)S(1)} %bitcast.271, bf16[2,64,1024]{2,1,0:T(8,128)(2,1)S(1)} %copy-done.1), kind=kOutput, calls=%fused_computation.99 | convolution fusion | flops 538116096 | bytes 8790528 | tf_op jit(solution)/shard_map/dot_general | solution.py:56
  14.8 1.3 collective-permute-start
  16.1 4.9 %collective-permute-done = bf16[64,1024]{1,0:T(8,128)(2,1)S(1)} collective-permute-done((bf16[64,1024]{1,0:T(8,128)(2,1)S(1)}, bf16[64,1024]{1,0:T(8,128)(2,1)S(1)}, u32[]{:S(2)}, u32[]{:S(2)}) %collective-permute-start) | collective-permute-done | bytes 131104 | tf_op jit(solution)/shard_map/ppermute | solution.py:11
  21.4 5.1 %fusion.172 = bf16[64,1024]{1,0:T(8,128)(2,1)S(1)} fusion(bf16[1,2048,1024]{2,1,0:T(8,128)(2,1)} %param.10, bf16[1,1024,2048]{2,1,0:T(8,128)(2,1)} %param.9, bf16[64,1024]{1,0:T(8,128)(2,1)S(1)} %get-tuple-element.39, f32[1024]{0:T(1024)S(1)} %bitcast.258, f32[64]{0:T(128)S(1)} %add_rsqrt_fusion.6, f32[64]{0:T(128)S(1)} %broadcast_multiply_fusion.18, ...), kind=kOutput, calls=%fused_computation.98 | convolution fusion | flops 538116096 | bytes 8659456 | tf_op jit(solution)/shard_map/dot_general | solution.py:56
  26.5 1.3 collective-permute-start.1
  28.1 5.1 %fusion.163 = bf16[64,1024]{1,0:T(8,128)(2,1)S(1)} fusion(bf16[1,2048,1024]{2,1,0:T(8,128)(2,1)} %param.10, bf16[1,1024,2048]{2,1,0:T(8,128)(2,1)} %param.9, bf16[64,1024]{1,0:T(8,128)(2,1)S(1)} %get-tuple-element.25, f32[64]{0:T(128)S(1)} %add_rsqrt_fusion.2, f32[64]{0:T(128)S(1)} %broadcast_multiply_fusion.14, f32[1024]{0:T(1024)S(1)} %bitcast.259, ...), kind=kOutput, calls=%fused_computation.95 | convolution fusion | flops 538116096 | bytes 8659456 | tf_op jit(solution)/shard_map/dot_general | solution.py:56
  33.2 1.3 collective-permute-start.11
  34.9 5.1 %fusion.169 = bf16[64,1024]{1,0:T(8,128)(2,1)S(1)} fusion(bf16[1,2048,1024]{2,1,0:T(8,128)(2,1)} %param.10, bf16[1,1024,2048]{2,1,0:T(8,128)(2,1)} %param.9, bf16[64,1024]{1,0:T(8,128)(2,1)S(1)} %get-tuple-element.31, f32[64]{0:T(128)S(1)} %add_rsqrt_fusion.5, f32[64]{0:T(128)S(1)} %broadcast_multiply_fusion.17, f32[1024]{0:T(1024)S(1)} %bitcast.260, ...), kind=kOutput, calls=%fused_computation.97 | convolution fusion | flops 538116096 | bytes 8659456 | tf_op jit(solution)/shard_map/dot_general | solution.py:56
  41.1 5.1 %fusion.160 = bf16[64,1024]{1,0:T(8,128)(2,1)S(1)} fusion(bf16[1,2048,1024]{2,1,0:T(8,128)(2,1)} %param.10, bf16[1,1024,2048]{2,1,0:T(8,128)(2,1)} %param.9, bf16[64,1024]{1,0:T(8,128)(2,1)S(1)} %get-tuple-element.23, f32[64]{0:T(128)S(1)} %add_rsqrt_fusion.1, f32[64]{0:T(128)S(1)} %broadcast_multiply_fusion.13, f32[1024]{0:T(1024)S(1)} %bitcast.261, ...), kind=kOutput, calls=%fused_computation.94 | convolution fusion | flops 538116096 | bytes 8659456 | tf_op jit(solution)/shard_map/dot_general | solution.py:56
  47.7 1.3 collective-permute-start.3
  50.4 2.4 %collective-permute-start.6 = (bf16[64,1024]{1,0:T(8,128)(2,1)S(1)}, bf16[64,1024]{1,0:T(8,128)(2,1)}, u32[]{:S(2)}, u32[]{:S(2)}) collective-permute-start(bf16[64,1024]{1,0:T(8,128)(2,1)S(1)} %get-tuple-element.27), channel_id=1, source_target_pairs={{0,4},{4,0},{8,12},{12,8},{16,20},{20,16},{24,28},{28,24},{1,5},{5... | collective-permute-start | bytes 393224 | tf_op jit(solution)/shard_map/ppermute | solution.py:16
  52.8 3.1 %fusion.192 = f32[64,2048]{1,0:T(8,128)S(1)} fusion(bf16[64,1024]{1,0:T(8,128)(2,1)S(1)} %get-tuple-element.27, bf16[1,1024,2048]{2,1,0:T(8,128)(2,1)} %param.9), kind=kOutput, calls=%fused_computation.104 | convolution fusion | flops 269484032 | bytes 4849664 | tf_op jit(solution)/shard_map/dot_general | solution.py:115
  56.9 6.9 %fusion.435 = (f32[64]{0:T(128)S(1)}, f32[64]{0:T(128)S(1)}, f32[64,1024]{1,0:T(8,128)}) fusion(f32[64]{0:T(128)} %copy-done.8, f32[64]{0:T(128)S(1)} %broadcast_multiply_fusion.16, bf16[64,1024]{1,0:T(8,128)(2,1)S(1)} %get-tuple-element.29, f32[1024]{0:T(1024)S(1)} %bitcast.263, bf16[1,1024,2048]{2,1,0:T(8,128)(2,1)} %param.9, ...), kind=kOutput, calls=%fused_computation.373 | convolution fusion | flops 537788288 | bytes 9446656 | tf_op jit(solution)/shard_map/dot_general | solution.py:70
  69.4 1.4 constant_dynamic-update-slice_fusion.7
  70.8 3.2 %fusion.195 = f32[64,2048]{1,0:T(8,128)S(1)} fusion(bf16[64,1024]{1,0:T(8,128)(2,1)} %get-tuple-element.19, bf16[1,1024,2048]{2,1,0:T(8,128)(2,1)} %param.9), kind=kOutput, calls=%fused_computation.107 | convolution fusion | flops 269484032 | bytes 4849664 | tf_op jit(solution)/shard_map/dot_general | solution.py:115
  74.0 7.0 %fusion.432 = (f32[64]{0:T(128)S(1)}, f32[64]{0:T(128)S(1)}, f32[64,1024]{1,0:T(8,128)}) fusion(f32[64]{0:T(128)} %add_rsqrt_fusion, f32[64]{0:T(128)S(1)} %broadcast_multiply_fusion.12, bf16[64,1024]{1,0:T(8,128)(2,1)S(1)} %get-tuple-element.21, f32[1024]{0:T(1024)S(1)} %bitcast.265, bf16[1,1024,2048]{2,1,0:T(8,128)(2,1)} %param.9, ...), kind=kOutput, calls=%fused_computation.370 | convolution fusion | flops 537788288 | bytes 9446656 | tf_op jit(solution)/shard_map/dot_general | solution.py:70
  81.0 2.0 %fusion.268 = (bf16[64,1024]{1,0:T(8,128)(2,1)}, bf16[64,1024]{1,0:T(8,128)(2,1)S(1)}) fusion(bf16[64,1024]{1,0:T(8,128)(2,1)S(1)} %get-tuple-element.21, f32[64,1024]{1,0:T(8,128)} %get-tuple-element.40, f32[64]{0:T(128)S(1)} %broadcast_multiply_fusion.4, f32[64]{0:T(128)S(1)} %broadcast_multiply_fusion.5, f32[64]{0:T(128)} %add_rsqrt_fusion, ...), kind=kLoop, calls=%fused_computation.182 | loop fusion | flops 1310720 | bytes 1312768 | tf_op jit(solution)/shard_map/convert_element_type | solution.py:80
  83.0 1.3 collective-permute-start.30
  84.3 1.3 collective-permute-start.20
  88.2 1.3 collective-permute-start.13
  90.9 1.3 collective-permute-start.16
  92.3 1.7 bitcast_select_fusion
  93.9 7.6 %fusion.434 = (f32[64]{0:T(128)}, f32[64]{0:T(128)}, f32[64,1024]{1,0:T(8,128)}) fusion(f32[64]{0:T(128)} %copy-done.8, f32[64]{0:T(128)S(1)} %broadcast_multiply_fusion.16, bf16[64,1024]{1,0:T(8,128)(2,1)S(1)} %get-tuple-element.29, f32[1024]{0:T(1024)S(1)} %bitcast.266, bf16[1,1024,2048]{2,1,0:T(8,128)(2,1)} %param.9, f32[64,2048]{1,0:T(8,128)S(1)} %fusion.192, ...), kind=kOutput, calls=%fused_computation.372 | convolution fusion | flops 537788288 | bytes 9446400 | tf_op jit(solution)/shard_map/dot_general | solution.py:70
  102.8 1.8 fusion.290
  104.5 1.3 collective-permute-start.21
  105.8 7.5 %fusion.431 = (f32[64]{0:T(128)}, f32[64]{0:T(128)}, f32[64,1024]{1,0:T(8,128)}) fusion(f32[64]{0:T(128)} %add_rsqrt_fusion, f32[64]{0:T(128)S(1)} %broadcast_multiply_fusion.12, bf16[64,1024]{1,0:T(8,128)(2,1)S(1)} %get-tuple-element.21, f32[1024]{0:T(1024)S(1)} %bitcast.267, bf16[1,1024,2048]{2,1,0:T(8,128)(2,1)} %param.9, f32[64,2048]{1,0:T(8,128)S(1)} %fusion.195, ...), kind=kOutput, calls=%fused_computation.369 | convolution fusion | flops 537788288 | bytes 9446400 | tf_op jit(solution)/shard_map/dot_general | solution.py:70
  114.7 1.8 fusion.294
  116.4 1.5 collective-permute-start.31
  123.3 7.5 %fusion.433 = (f32[64]{0:T(128)}, f32[64]{0:T(128)}, f32[64,1024]{1,0:T(8,128)}) fusion(f32[64]{0:T(128)} %copy-done.8, f32[64]{0:T(128)S(1)} %broadcast_multiply_fusion.16, bf16[64,1024]{1,0:T(8,128)(2,1)S(1)} %get-tuple-element.29, f32[1024]{0:T(1024)S(1)} %bitcast.268, bf16[1,1024,2048]{2,1,0:T(8,128)(2,1)} %param.9, f32[64,2048]{1,0:T(8,128)S(1)} %fusion.192, ...), kind=kOutput, calls=%fused_computation.371 | convolution fusion | flops 537788288 | bytes 9446400 | tf_op jit(solution)/shard_map/dot_general | solution.py:70
  132.0 1.8 fusion.292
  133.8 1.9 %collective-permute-start.22 = (bf16[64,1024]{1,0:T(8,128)(2,1)}, bf16[64,1024]{1,0:T(8,128)(2,1)}, u32[]{:S(2)}, u32[]{:S(2)}) collective-permute-start(bf16[64,1024]{1,0:T(8,128)(2,1)} %fusion.292), channel_id=1, source_target_pairs={{1,0},{5,4},{9,8},{13,12},{17,16},{21,20},{25,24},{29,28}} | collective-permute-start | bytes 393224 | tf_op jit(solution)/shard_map/ppermute | solution.py:11
  136.6 7.5 %fusion.430 = (f32[64]{0:T(128)S(1)}, f32[64]{0:T(128)}, f32[64,1024]{1,0:T(8,128)}) fusion(f32[64]{0:T(128)} %add_rsqrt_fusion, f32[64]{0:T(128)S(1)} %broadcast_multiply_fusion.12, bf16[64,1024]{1,0:T(8,128)(2,1)S(1)} %get-tuple-element.21, f32[1024]{0:T(1024)S(1)} %bitcast.269, bf16[1,1024,2048]{2,1,0:T(8,128)(2,1)} %param.9, ...), kind=kOutput, calls=%fused_computation.368 | convolution fusion | flops 537788288 | bytes 9446400 | tf_op jit(solution)/shard_map/dot_general | solution.py:70
  144.9 3.7 %constant_dynamic-update-slice_fusion.31 = (bf16[1024,2048]{1,0:T(8,128)(2,1)S(1)}, bf16[64,2048]{1,0:T(8,128)(2,1)S(1)}) fusion(f32[64,2048]{1,0:T(8,128)S(1)} %fusion.192, bf16[1,2048,1024]{2,1,0:T(8,128)(2,1)} %param.10, bf16[64,1024]{1,0:T(8,128)(2,1)} %collective-permute-done.22, bf16[64,1024]{1,0:T(8,128)(2,1)S(1)} %broadcast_select_fusion.1, ...), kind=kOutput, calls=%fused_computation.319 | convolution fusion | flops 268959744 | bytes 5509121 | tf_op jit(solution)/shard_map/dot_general | solution.py:62
  148.7 1.3 collective-permute-start.23
  150.1 1.3 collective-permute-start.32
  152.3 1.3 collective-permute-start.24
  154.8 1.3 collective-permute-done.23
  156.1 1.3 collective-permute-start.26
  157.5 7.6 %collective-permute-done.24 = bf16[64,2048]{1,0:T(8,128)(2,1)S(1)} collective-permute-done((bf16[64,2048]{1,0:T(8,128)(2,1)S(1)}, bf16[64,2048]{1,0:T(8,128)(2,1)S(1)}, u32[]{:S(2)}, u32[]{:S(2)}) %collective-permute-start.24) | collective-permute-done | bytes 262176 | tf_op jit(solution)/shard_map/ppermute | solution.py:16
  165.1 1.7 collective-permute-start.27
  168.8 1.4 constant_dynamic-update-slice_fusion.23
  171.4 1.3 collective-permute-start.34
  176.3 1.6 collective-permute-done.33
  177.9 1.8 collective-permute-start.37
  179.7 6.1 %collective-permute-start.38 = (bf16[64,2048]{1,0:T(8,128)(2,1)S(1)}, bf16[64,2048]{1,0:T(8,128)(2,1)S(1)}, u32[]{:S(2)}, u32[]{:S(2)}) collective-permute-start(bf16[64,2048]{1,0:T(8,128)(2,1)S(1)} %collective-permute-done.34), channel_id=1, source_target_pairs={{0,4},{4,0},{8,12},{12,8},{16,20},{20,16},{24,28},{28,24},{1,5},{5... | collective-permute-start | bytes 786440 | tf_op jit(solution)/shard_map/ppermute | solution.py:16
  187.5 2.6 %fusion.56 = f32[1,256,2048]{2,1,0:T(8,128)} fusion(bf16[1024,2048]{1,0:T(8,128)(2,1)S(1)} %constant_dynamic-update-slice_fusion.16, s32[]{:T(128)S(6)} %select_n.85), kind=kOutput, calls=%fused_computation.57 | convolution fusion | flops 1074266112 | bytes 6815748 | tf_op jit(solution)/shard_map/dot_general | solution.py:87
  (147 shorter events, 37.7 us)
Async XLA Ops:
  3.0 6.6 %copy-start.1 = (bf16[2,64,1024]{2,1,0:T(8,128)(2,1)S(1)}, bf16[2,64,1024]{2,1,0:T(8,128)(2,1)}, u32[]{:S(2)}) copy-start(bf16[2,64,1024]{2,1,0:T(8,128)(2,1)} %param.7) | copy-start | bytes 786436
  3.0 6.6 %copy-start.5 = (f32[1,1024]{1,0:T(1,128)S(1)}, f32[1,1024]{1,0:T(1,128)}, u32[]{:S(2)}) copy-start(f32[1,1024]{1,0:T(1,128)} %param.8) | copy-start | bytes 12292
  3.0 6.6 %copy-start.6 = (f32[1,1024]{1,0:T(1,128)S(1)}, f32[1,1024]{1,0:T(1,128)}, u32[]{:S(2)}) copy-start(f32[1,1024]{1,0:T(1,128)} %param.11) | copy-start | bytes 12292
  8.3 7.8 %collective-permute-start.10 = (bf16[64,1024]{1,0:T(8,128)(2,1)S(1)}, bf16[64,1024]{1,0:T(8,128)(2,1)S(1)}, u32[]{:S(2)}, u32[]{:S(2)}) collective-permute-start(bf16[64,1024]{1,0:T(8,128)(2,1)S(1)} %fusion.166), channel_id=1, source_target_pairs={{0,1},{4,5},{8,9},{12,13},{16,17},{20,21},{24,25},{28,29}} | collective-permute-start | bytes 393224 | tf_op jit(solution)/shard_map/ppermute | solution.py:11
  14.8 6.3 %collective-permute-start = (bf16[64,1024]{1,0:T(8,128)(2,1)S(1)}, bf16[64,1024]{1,0:T(8,128)(2,1)S(1)}, u32[]{:S(2)}, u32[]{:S(2)}) collective-permute-start(bf16[64,1024]{1,0:T(8,128)(2,1)S(1)} %fusion.175), channel_id=1, source_target_pairs={{0,1},{4,5},{8,9},{12,13},{16,17},{20,21},{24,25},{28,29}} | collective-permute-start | bytes 393224 | tf_op jit(solution)/shard_map/ppermute | solution.py:11
  26.5 8.0 %collective-permute-start.1 = (bf16[64,1024]{1,0:T(8,128)(2,1)S(1)}, bf16[64,1024]{1,0:T(8,128)(2,1)S(1)}, u32[]{:S(2)}, u32[]{:S(2)}) collective-permute-start(bf16[64,1024]{1,0:T(8,128)(2,1)S(1)} %fusion.172), channel_id=1, source_target_pairs={{1,2},{5,6},{9,10},{13,14},{17,18},{21,22},{25,26},{29,30}} | collective-permute-start | bytes 393224 | tf_op jit(solution)/shard_map/ppermute | solution.py:11
  33.2 7.5 %collective-permute-start.11 = (bf16[64,1024]{1,0:T(8,128)(2,1)S(1)}, bf16[64,1024]{1,0:T(8,128)(2,1)S(1)}, u32[]{:S(2)}, u32[]{:S(2)}) collective-permute-start(bf16[64,1024]{1,0:T(8,128)(2,1)S(1)} %fusion.163), channel_id=1, source_target_pairs={{1,2},{5,6},{9,10},{13,14},{17,18},{21,22},{25,26},{29,30}} | collective-permute-start | bytes 393224 | tf_op jit(solution)/shard_map/ppermute | solution.py:11
  40.0 7.2 %collective-permute-start.2 = (bf16[64,1024]{1,0:T(8,128)(2,1)S(1)}, bf16[64,1024]{1,0:T(8,128)(2,1)S(1)}, u32[]{:S(2)}, u32[]{:S(2)}) collective-permute-start(bf16[64,1024]{1,0:T(8,128)(2,1)S(1)} %fusion.169), channel_id=1, source_target_pairs={{2,3},{6,7},{10,11},{14,15},{18,19},{22,23},{26,27},{30,31}} | collective-permute-start | bytes 393224 | tf_op jit(solution)/shard_map/ppermute | solution.py:11
  46.2 10.7 %copy-start.2 = (bf16[2,64,1024]{2,1,0:T(8,128)(2,1)S(1)}, bf16[2,64,1024]{2,1,0:T(8,128)(2,1)}, u32[]{:S(2)}) copy-start(bf16[2,64,1024]{2,1,0:T(8,128)(2,1)} %param.12) | copy-start | bytes 786436
  46.2 9.7 %collective-permute-start.12 = (bf16[64,1024]{1,0:T(8,128)(2,1)S(1)}, bf16[64,1024]{1,0:T(8,128)(2,1)S(1)}, u32[]{:S(2)}, u32[]{:S(2)}) collective-permute-start(bf16[64,1024]{1,0:T(8,128)(2,1)S(1)} %fusion.160), channel_id=1, source_target_pairs={{2,3},{6,7},{10,11},{14,15},{18,19},{22,23},{26,27},{30,31}} | collective-permute-start | bytes 393224 | tf_op jit(solution)/shard_map/ppermute | solution.py:11
  47.6 8.5 %copy-start.8 = (f32[64]{0:T(128)}, f32[64]{0:T(128)S(1)}, u32[]{:S(2)}) copy-start(f32[64]{0:T(128)S(1)} %add_rsqrt_fusion.4) | copy-start | bytes 772
  47.7 17.2 %collective-permute-start.3 = (bf16[64,1024]{1,0:T(8,128)(2,1)S(1)}, bf16[64,1024]{1,0:T(8,128)(2,1)}, u32[]{:S(2)}, u32[]{:S(2)}) collective-permute-start(bf16[64,1024]{1,0:T(8,128)(2,1)S(1)} %get-tuple-element.27), channel_id=1, source_target_pairs={{0,8},{4,12},{8,0},{12,4},{16,24},{20,28},{24,16},{28,20},{1,9},{5... | collective-permute-start | bytes 393224 | tf_op jit(solution)/shard_map/ppermute | solution.py:16
  49.0 16.9 %collective-permute-start.4 = (bf16[64,1024]{1,0:T(8,128)(2,1)S(1)}, bf16[64,1024]{1,0:T(8,128)(2,1)}, u32[]{:S(2)}, u32[]{:S(2)}) collective-permute-start(bf16[64,1024]{1,0:T(8,128)(2,1)S(1)} %get-tuple-element.27), channel_id=1, source_target_pairs={{0,16},{4,20},{8,24},{12,28},{16,0},{20,4},{24,8},{28,12},{1,17},{... | collective-permute-start | bytes 393224 | tf_op jit(solution)/shard_map/ppermute | solution.py:16
  50.2 17.1 %collective-permute-start.5 = (bf16[64,1024]{1,0:T(8,128)(2,1)S(1)}, bf16[64,1024]{1,0:T(8,128)(2,1)}, u32[]{:S(2)}, u32[]{:S(2)}) collective-permute-start(bf16[64,1024]{1,0:T(8,128)(2,1)S(1)} %get-tuple-element.27), channel_id=1, source_target_pairs={{0,24},{4,28},{8,16},{12,20},{16,8},{20,12},{24,0},{28,4},{1,25},{... | collective-permute-start | bytes 393224 | tf_op jit(solution)/shard_map/ppermute | solution.py:16
  50.4 17.9 %collective-permute-start.6 = (bf16[64,1024]{1,0:T(8,128)(2,1)S(1)}, bf16[64,1024]{1,0:T(8,128)(2,1)}, u32[]{:S(2)}, u32[]{:S(2)}) collective-permute-start(bf16[64,1024]{1,0:T(8,128)(2,1)S(1)} %get-tuple-element.27), channel_id=1, source_target_pairs={{0,4},{4,0},{8,12},{12,8},{16,20},{20,16},{24,28},{28,24},{1,5},{5... | collective-permute-start | bytes 393224 | tf_op jit(solution)/shard_map/ppermute | solution.py:16
  64.9 4.4 %collective-permute-start.7 = (bf16[64,1024]{1,0:T(8,128)(2,1)}, bf16[64,1024]{1,0:T(8,128)(2,1)S(1)}, u32[]{:S(2)}, u32[]{:S(2)}) collective-permute-start(bf16[64,1024]{1,0:T(8,128)(2,1)} %collective-permute-done.3), channel_id=1, source_target_pairs={{0,4},{4,0},{8,12},{12,8},{16,20},{20,16},{24,28},{28,24},{1,5},{5... | collective-permute-start | bytes 393224 | tf_op jit(solution)/shard_map/ppermute | solution.py:16
  65.9 3.5 %collective-permute-start.8 = (bf16[64,1024]{1,0:T(8,128)(2,1)}, bf16[64,1024]{1,0:T(8,128)(2,1)S(1)}, u32[]{:S(2)}, u32[]{:S(2)}) collective-permute-start(bf16[64,1024]{1,0:T(8,128)(2,1)} %collective-permute-done.4), channel_id=1, source_target_pairs={{0,4},{4,0},{8,12},{12,8},{16,20},{20,16},{24,28},{28,24},{1,5},{5... | collective-permute-start | bytes 393224 | tf_op jit(solution)/shard_map/ppermute | solution.py:16
  67.4 2.0 %collective-permute-start.9 = (bf16[64,1024]{1,0:T(8,128)(2,1)}, bf16[64,1024]{1,0:T(8,128)(2,1)S(1)}, u32[]{:S(2)}, u32[]{:S(2)}) collective-permute-start(bf16[64,1024]{1,0:T(8,128)(2,1)} %collective-permute-done.5), channel_id=1, source_target_pairs={{0,4},{4,0},{8,12},{12,8},{16,20},{20,16},{24,28},{28,24},{1,5},{5... | collective-permute-start | bytes 393224 | tf_op jit(solution)/shard_map/ppermute | solution.py:16
  83.0 7.9 %collective-permute-start.30 = (bf16[64,1024]{1,0:T(8,128)(2,1)}, bf16[64,1024]{1,0:T(8,128)(2,1)}, u32[]{:S(2)}, u32[]{:S(2)}) collective-permute-start(bf16[64,1024]{1,0:T(8,128)(2,1)} %get-tuple-element.36), channel_id=1, source_target_pairs={{3,2},{7,6},{11,10},{15,14},{19,18},{23,22},{27,26},{31,30}} | collective-permute-start | bytes 393224 | tf_op jit(solution)/shard_map/ppermute | solution.py:11
  84.3 7.9 %collective-permute-start.20 = (bf16[64,1024]{1,0:T(8,128)(2,1)S(1)}, bf16[64,1024]{1,0:T(8,128)(2,1)}, u32[]{:S(2)}, u32[]{:S(2)}) collective-permute-start(bf16[64,1024]{1,0:T(8,128)(2,1)S(1)} %get-tuple-element.37), channel_id=1, source_target_pairs={{3,2},{7,6},{11,10},{15,14},{19,18},{23,22},{27,26},{31,30}} | collective-permute-start | bytes 393224 | tf_op jit(solution)/shard_map/ppermute | solution.py:11
  88.2 28.2 %collective-permute-start.13 = (bf16[64,1024]{1,0:T(8,128)(2,1)}, bf16[64,1024]{1,0:T(8,128)(2,1)}, u32[]{:S(2)}, u32[]{:S(2)}) collective-permute-start(bf16[64,1024]{1,0:T(8,128)(2,1)} %get-tuple-element.19), channel_id=1, source_target_pairs={{0,8},{4,12},{8,0},{12,4},{16,24},{20,28},{24,16},{28,20},{1,9},{5... | collective-permute-start | bytes 393224 | tf_op jit(solution)/shard_map/ppermute | solution.py:16
  89.5 29.4 %collective-permute-start.14 = (bf16[64,1024]{1,0:T(8,128)(2,1)}, bf16[64,1024]{1,0:T(8,128)(2,1)}, u32[]{:S(2)}, u32[]{:S(2)}) collective-permute-start(bf16[64,1024]{1,0:T(8,128)(2,1)} %get-tuple-element.19), channel_id=1, source_target_pairs={{0,16},{4,20},{8,24},{12,28},{16,0},{20,4},{24,8},{28,12},{1,17},{... | collective-permute-start | bytes 393224 | tf_op jit(solution)/shard_map/ppermute | solution.py:16
  90.7 29.1 %collective-permute-start.15 = (bf16[64,1024]{1,0:T(8,128)(2,1)}, bf16[64,1024]{1,0:T(8,128)(2,1)}, u32[]{:S(2)}, u32[]{:S(2)}) collective-permute-start(bf16[64,1024]{1,0:T(8,128)(2,1)} %get-tuple-element.19), channel_id=1, source_target_pairs={{0,24},{4,28},{8,16},{12,20},{16,8},{20,12},{24,0},{28,4},{1,25},{... | collective-permute-start | bytes 393224 | tf_op jit(solution)/shard_map/ppermute | solution.py:16
  90.9 30.4 %collective-permute-start.16 = (bf16[64,1024]{1,0:T(8,128)(2,1)}, bf16[64,1024]{1,0:T(8,128)(2,1)}, u32[]{:S(2)}, u32[]{:S(2)}) collective-permute-start(bf16[64,1024]{1,0:T(8,128)(2,1)} %get-tuple-element.19), channel_id=1, source_target_pairs={{0,4},{4,0},{8,12},{12,8},{16,20},{20,16},{24,28},{28,24},{1,5},{5... | collective-permute-start | bytes 393224 | tf_op jit(solution)/shard_map/ppermute | solution.py:16
  93.9 20.7 %copy-start.3 = (bf16[64,1024]{1,0:T(8,128)(2,1)}, bf16[64,1024]{1,0:T(8,128)(2,1)S(1)}, u32[]{:S(2)}) copy-start(bf16[64,1024]{1,0:T(8,128)(2,1)S(1)} %get-tuple-element.34) | copy-start | bytes 393220
  104.5 17.8 %collective-permute-start.21 = (bf16[64,1024]{1,0:T(8,128)(2,1)}, bf16[64,1024]{1,0:T(8,128)(2,1)}, u32[]{:S(2)}, u32[]{:S(2)}) collective-permute-start(bf16[64,1024]{1,0:T(8,128)(2,1)} %fusion.290), channel_id=1, source_target_pairs={{2,1},{6,5},{10,9},{14,13},{18,17},{22,21},{26,25},{30,29}} | collective-permute-start | bytes 393224 | tf_op jit(solution)/shard_map/ppermute | solution.py:11
  116.4 19.3 %collective-permute-start.31 = (bf16[64,1024]{1,0:T(8,128)(2,1)}, bf16[64,1024]{1,0:T(8,128)(2,1)}, u32[]{:S(2)}, u32[]{:S(2)}) collective-permute-start(bf16[64,1024]{1,0:T(8,128)(2,1)} %fusion.294), channel_id=1, source_target_pairs={{2,1},{6,5},{10,9},{14,13},{18,17},{22,21},{26,25},{30,29}} | collective-permute-start | bytes 393224 | tf_op jit(solution)/shard_map/ppermute | solution.py:11
  118.8 32.6 %collective-permute-start.17 = (bf16[64,1024]{1,0:T(8,128)(2,1)}, bf16[64,1024]{1,0:T(8,128)(2,1)}, u32[]{:S(2)}, u32[]{:S(2)}) collective-permute-start(bf16[64,1024]{1,0:T(8,128)(2,1)} %collective-permute-done.13), channel_id=1, source_target_pairs={{0,4},{4,0},{8,12},{12,8},{16,20},{20,16},{24,28},{28,24},{1,5},{5... | collective-permute-start | bytes 393224 | tf_op jit(solution)/shard_map/ppermute | solution.py:16
  119.9 33.8 %collective-permute-start.18 = (bf16[64,1024]{1,0:T(8,128)(2,1)}, bf16[64,1024]{1,0:T(8,128)(2,1)}, u32[]{:S(2)}, u32[]{:S(2)}) collective-permute-start(bf16[64,1024]{1,0:T(8,128)(2,1)} %collective-permute-done.14), channel_id=1, source_target_pairs={{0,4},{4,0},{8,12},{12,8},{16,20},{20,16},{24,28},{28,24},{1,5},{5... | collective-permute-start | bytes 393224 | tf_op jit(solution)/shard_map/ppermute | solution.py:16
  121.3 49.2 %collective-permute-start.19 = (bf16[64,1024]{1,0:T(8,128)(2,1)}, bf16[64,1024]{1,0:T(8,128)(2,1)}, u32[]{:S(2)}, u32[]{:S(2)}) collective-permute-start(bf16[64,1024]{1,0:T(8,128)(2,1)} %collective-permute-done.15), channel_id=1, source_target_pairs={{0,4},{4,0},{8,12},{12,8},{16,20},{20,16},{24,28},{28,24},{1,5},{5... | collective-permute-start | bytes 393224 | tf_op jit(solution)/shard_map/ppermute | solution.py:16
  133.8 11.1 %collective-permute-start.22 = (bf16[64,1024]{1,0:T(8,128)(2,1)}, bf16[64,1024]{1,0:T(8,128)(2,1)}, u32[]{:S(2)}, u32[]{:S(2)}) collective-permute-start(bf16[64,1024]{1,0:T(8,128)(2,1)} %fusion.292), channel_id=1, source_target_pairs={{1,0},{5,4},{9,8},{13,12},{17,16},{21,20},{25,24},{29,28}} | collective-permute-start | bytes 393224 | tf_op jit(solution)/shard_map/ppermute | solution.py:11
  144.2 5.8 %copy-start.7 = (f32[64]{0:T(128)S(1)}, f32[64]{0:T(128)}, u32[]{:S(2)}) copy-start(f32[64]{0:T(128)} %add_rsqrt_fusion) | copy-start | bytes 772
  144.9 23.9 %copy-start = (bf16[1,2048,1024]{2,1,0:T(8,128)(2,1)S(1)}, bf16[1,2048,1024]{2,1,0:T(8,128)(2,1)}, u32[]{:S(2)}) copy-start(bf16[1,2048,1024]{2,1,0:T(8,128)(2,1)} %param.10) | copy-start | bytes 12582916
  148.7 7.4 %collective-permute-start.23 = (bf16[64,2048]{1,0:T(8,128)(2,1)S(1)}, bf16[64,2048]{1,0:T(8,128)(2,1)S(1)}, u32[]{:S(2)}, u32[]{:S(2)}) collective-permute-start(bf16[64,2048]{1,0:T(8,128)(2,1)S(1)} %get-tuple-element.45), channel_id=1, source_target_pairs={{0,8},{4,12},{8,0},{12,4},{16,24},{20,28},{24,16},{28,20},{1,9},{5... | collective-permute-start | bytes 786440 | tf_op jit(solution)/shard_map/ppermute | solution.py:16
  150.1 18.7 %collective-permute-start.32 = (bf16[64,1024]{1,0:T(8,128)(2,1)S(1)}, bf16[64,1024]{1,0:T(8,128)(2,1)S(1)}, u32[]{:S(2)}, u32[]{:S(2)}) collective-permute-start(bf16[64,1024]{1,0:T(8,128)(2,1)S(1)} %fusion.296), channel_id=1, source_target_pairs={{1,0},{5,4},{9,8},{13,12},{17,16},{21,20},{25,24},{29,28}} | collective-permute-start | bytes 393224 | tf_op jit(solution)/shard_map/ppermute | solution.py:11
  152.3 12.7 %collective-permute-start.24 = (bf16[64,2048]{1,0:T(8,128)(2,1)S(1)}, bf16[64,2048]{1,0:T(8,128)(2,1)S(1)}, u32[]{:S(2)}, u32[]{:S(2)}) collective-permute-start(bf16[64,2048]{1,0:T(8,128)(2,1)S(1)} %get-tuple-element.45), channel_id=1, source_target_pairs={{0,16},{4,20},{8,24},{12,28},{16,0},{20,4},{24,8},{28,12},{1,17},{... | collective-permute-start | bytes 786440 | tf_op jit(solution)/shard_map/ppermute | solution.py:16
  154.6 12.2 %collective-permute-start.25 = (bf16[64,2048]{1,0:T(8,128)(2,1)S(1)}, bf16[64,2048]{1,0:T(8,128)(2,1)S(1)}, u32[]{:S(2)}, u32[]{:S(2)}) collective-permute-start(bf16[64,2048]{1,0:T(8,128)(2,1)S(1)} %get-tuple-element.45), channel_id=1, source_target_pairs={{0,24},{4,28},{8,16},{12,20},{16,8},{20,12},{24,0},{28,4},{1,25},{... | collective-permute-start | bytes 786440 | tf_op jit(solution)/shard_map/ppermute | solution.py:16
  156.1 10.8 %collective-permute-start.26 = (bf16[64,2048]{1,0:T(8,128)(2,1)S(1)}, bf16[64,2048]{1,0:T(8,128)(2,1)S(1)}, u32[]{:S(2)}, u32[]{:S(2)}) collective-permute-start(bf16[64,2048]{1,0:T(8,128)(2,1)S(1)} %get-tuple-element.45), channel_id=1, source_target_pairs={{0,4},{4,0},{8,12},{12,8},{16,20},{20,16},{24,28},{28,24},{1,5},{5... | collective-permute-start | bytes 786440 | tf_op jit(solution)/shard_map/ppermute | solution.py:16
  165.1 2.8 %collective-permute-start.27 = (bf16[64,2048]{1,0:T(8,128)(2,1)S(1)}, bf16[64,2048]{1,0:T(8,128)(2,1)S(1)}, u32[]{:S(2)}, u32[]{:S(2)}) collective-permute-start(bf16[64,2048]{1,0:T(8,128)(2,1)S(1)} %collective-permute-done.23), channel_id=1, source_target_pairs={{0,4},{4,0},{8,12},{12,8},{16,20},{20,16},{24,28},{28,24},{1,5},{5... | collective-permute-start | bytes 786440 | tf_op jit(solution)/shard_map/ppermute | solution.py:16
  166.8 1.6 collective-permute-start.28
  166.9 1.9 collective-permute-start.29
  170.2 7.7 %collective-permute-start.33 = (bf16[64,2048]{1,0:T(8,128)(2,1)S(1)}, bf16[64,2048]{1,0:T(8,128)(2,1)S(1)}, u32[]{:S(2)}, u32[]{:S(2)}) collective-permute-start(bf16[64,2048]{1,0:T(8,128)(2,1)S(1)} %get-tuple-element.49), channel_id=1, source_target_pairs={{0,8},{4,12},{8,0},{12,4},{16,24},{20,28},{24,16},{28,20},{1,9},{5... | collective-permute-start | bytes 786440 | tf_op jit(solution)/shard_map/ppermute | solution.py:16
  171.4 8.3 %collective-permute-start.34 = (bf16[64,2048]{1,0:T(8,128)(2,1)S(1)}, bf16[64,2048]{1,0:T(8,128)(2,1)S(1)}, u32[]{:S(2)}, u32[]{:S(2)}) collective-permute-start(bf16[64,2048]{1,0:T(8,128)(2,1)S(1)} %get-tuple-element.49), channel_id=1, source_target_pairs={{0,16},{4,20},{8,24},{12,28},{16,0},{20,4},{24,8},{28,12},{1,17},{... | collective-permute-start | bytes 786440 | tf_op jit(solution)/shard_map/ppermute | solution.py:16
  174.0 11.9 %collective-permute-start.35 = (bf16[64,2048]{1,0:T(8,128)(2,1)S(1)}, bf16[64,2048]{1,0:T(8,128)(2,1)S(1)}, u32[]{:S(2)}, u32[]{:S(2)}) collective-permute-start(bf16[64,2048]{1,0:T(8,128)(2,1)S(1)} %get-tuple-element.49), channel_id=1, source_target_pairs={{0,24},{4,28},{8,16},{12,20},{16,8},{20,12},{24,0},{28,4},{1,25},{... | collective-permute-start | bytes 786440 | tf_op jit(solution)/shard_map/ppermute | solution.py:16
  175.2 10.8 %collective-permute-start.36 = (bf16[64,2048]{1,0:T(8,128)(2,1)S(1)}, bf16[64,2048]{1,0:T(8,128)(2,1)S(1)}, u32[]{:S(2)}, u32[]{:S(2)}) collective-permute-start(bf16[64,2048]{1,0:T(8,128)(2,1)S(1)} %get-tuple-element.49), channel_id=1, source_target_pairs={{0,4},{4,0},{8,12},{12,8},{16,20},{20,16},{24,28},{28,24},{1,5},{5... | collective-permute-start | bytes 786440 | tf_op jit(solution)/shard_map/ppermute | solution.py:16
  177.9 8.1 %collective-permute-start.37 = (bf16[64,2048]{1,0:T(8,128)(2,1)S(1)}, bf16[64,2048]{1,0:T(8,128)(2,1)S(1)}, u32[]{:S(2)}, u32[]{:S(2)}) collective-permute-start(bf16[64,2048]{1,0:T(8,128)(2,1)S(1)} %collective-permute-done.33), channel_id=1, source_target_pairs={{0,4},{4,0},{8,12},{12,8},{16,20},{20,16},{24,28},{28,24},{1,5},{5... | collective-permute-start | bytes 786440 | tf_op jit(solution)/shard_map/ppermute | solution.py:16
  179.7 7.3 %collective-permute-start.38 = (bf16[64,2048]{1,0:T(8,128)(2,1)S(1)}, bf16[64,2048]{1,0:T(8,128)(2,1)S(1)}, u32[]{:S(2)}, u32[]{:S(2)}) collective-permute-start(bf16[64,2048]{1,0:T(8,128)(2,1)S(1)} %collective-permute-done.34), channel_id=1, source_target_pairs={{0,4},{4,0},{8,12},{12,8},{16,20},{20,16},{24,28},{28,24},{1,5},{5... | collective-permute-start | bytes 786440 | tf_op jit(solution)/shard_map/ppermute | solution.py:16
  185.9 1.6 collective-permute-start.39
  (1 other events, 5.8 us)

commit v2 on v1

v2 whole, which is shorter than its diff:
```python
import functools

import jax
import jax.numpy as jnp
from jax import lax
from jax.experimental import pallas as pl
from jax.experimental.pallas import tpu as pltpu
from jax.sharding import PartitionSpec as P

SQRT_HALF = 0.7071067811865476
INV_ROOT_TAU = 0.3989422804014327
F32 = jnp.float32
BF16 = jnp.bfloat16
IN_VMEM = pl.BlockSpec(memory_space=pltpu.VMEM)
IN_SMEM = pl.BlockSpec(memory_space=pltpu.SMEM)
TILE = 512
MIB = 2**20


def hop(value, source, steps):
    return lax.ppermute(value, "section", [(source, source + steps)])


def swapped(value, axis, mask):
    count = lax.axis_size(axis)
    return lax.ppermute(value, axis, [(source, source ^ mask) for source in range(count)])


def turned(value, axis, steps):
    count = lax.axis_size(axis)
    return lax.ppermute(value, axis, [(source, (source + steps) % count) for source in range(count)])


def gathered(value, axis):
    count = lax.axis_size(axis)
    if count & (count - 1):
        return [value] + [turned(value, axis, steps) for steps in range(1, count)]
    if count == 1:
        return [value]
    blocks = [value] + [swapped(value, axis, mask) for mask in range(2, count, 2)]
    return blocks + [swapped(block, axis, 1) for block in blocks]


def tiles(width):
    size = min(TILE, width)
    return [slice(start, min(start + size, width)) for start in range(0, width, size)]


def dot_nt(left, right):
    return lax.dot_general(left, right, (((1,), (1,)), ((), ())), preferred_element_type=F32)


def dot_tn(left, right):
    return lax.dot_general(left, right, (((0,), (0,)), ((), ())), preferred_element_type=F32)


def normalize(floats, gain_row):
    center = floats - jnp.mean(floats, axis=-1, keepdims=True)
    inv_std = lax.rsqrt(jnp.mean(center * center, axis=-1, keepdims=True) + 1e-06)
    normed = center * inv_std
    return ((normed * gain_row).astype(BF16), normed, inv_std)


def forward_kernel(here, x_ref, gain, weight_in, weight_out, scales, out, acted):
    @pl.when(here[0] == 1)
    def _():
        x = x_ref[...].astype(F32)
        normed_bf, _, _ = normalize(x, gain[...])
        for cols in tiles(weight_in.shape[1]):
            hidden = jnp.dot(normed_bf, weight_in[:, cols], preferred_element_type=F32)
            acted[:, cols] = (0.5 * hidden * (1.0 + lax.erf(hidden * SQRT_HALF))).astype(BF16)
        for cols in tiles(x.shape[1]):
            branch = jnp.dot(acted[...], weight_out[:, cols], preferred_element_type=F32)
            out[:, cols] = (x[:, cols] + scales[:, cols] * branch).astype(BF16)


def save_kernel(count, where, *refs):
    held, (gain, weight_in, normed_bf, normed, inv_std, slope, chosen) = refs[:count], refs[count:]
    for index, ref in enumerate(held):
        @pl.when(where[0] == index)
        def _():
            chosen[...] = ref[...]

    normed_bf[...], normed[...], inv_std[...] = normalize(chosen[...].astype(F32), gain[...])
    for cols in tiles(weight_in.shape[1]):
        v = jnp.dot(normed_bf[...], weight_in[:, cols], preferred_element_type=F32)
        slope[:, cols] = 0.5 * (1.0 + lax.erf(v * SQRT_HALF)) + v * INV_ROOT_TAU * jnp.exp(
            -0.5 * v * v
        )


def hidden_grad(cotangent, scales, weight_out, slope, grad_hidden):
    scaled = (cotangent * scales).astype(BF16)
    for cols in tiles(weight_out.shape[0]):
        grad_act = dot_nt(scaled, weight_out[cols, :])
        grad_hidden[:, cols] = (grad_act * slope[:, cols]).astype(BF16)


def backward_kernel(
    here, gy_ref, gain, weight_in, weight_out, scales, normed_ref, inv_std, slope, out, grad_hidden
):
    @pl.when(here[0] == 1)
    def _():
        cotangent = gy_ref[...].astype(F32)
        hidden_grad(cotangent, scales[...], weight_out, slope, grad_hidden)
        grad_normed = dot_nt(grad_hidden[...], weight_in[...]) * gain[...]
        normed = normed_ref[...]
        mean_one = jnp.mean(grad_normed, axis=-1, keepdims=True)
        mean_two = jnp.mean(grad_normed * normed, axis=-1, keepdims=True)
        out[...] = (
            cotangent + inv_std[...] * (grad_normed - mean_one - normed * mean_two)
        ).astype(BF16)


def last_kernel(count, where, *refs):
    held, (scales, weight_out, slope, grad_hidden, chosen) = refs[:count], refs[count:]
    for index, ref in enumerate(held):
        @pl.when(where[0] == index)
        def _():
            chosen[...] = ref[...]

    hidden_grad(chosen[...].astype(F32), scales[...], weight_out, slope, grad_hidden)


def square_kernel(count, factor, owner, *refs):
    blocks, (total, rows) = refs[:count], refs[count:]
    height = blocks[0].shape[0]

    @pl.when(pl.program_id(0) == 0)
    def _():
        for index, ref in enumerate(blocks):
            rows[index * height : (index + 1) * height, :] = ref[...]

    wide, tall = total.shape[1], total.shape[0]
    own = rows[:, pl.ds(pl.multiple_of(owner[0] * tall, tall), tall)]
    here = rows[:, pl.ds(pl.multiple_of(pl.program_id(0) * wide, wide), wide)]
    total[...] = dot_tn(own, here) * factor


def pinned(value):
    return pltpu.with_memory_space_constraint(value, pltpu.VMEM)


def call(kernel, scalars, arrays, outs, scratch=(), flops=0, room=24 * MIB):
    moved = sum(array.size * array.dtype.itemsize for array in arrays)
    return pl.pallas_call(
        kernel,
        in_specs=[IN_SMEM] * len(scalars) + [IN_VMEM] * len(arrays),
        out_specs=[IN_VMEM] * len(outs),
        out_shape=outs,
        scratch_shapes=list(scratch),
        compiler_params=pltpu.CompilerParams(vmem_limit_bytes=room),
        cost_estimate=pl.CostEstimate(flops=flops, bytes_accessed=moved, transcendentals=0),
    )(*scalars, *arrays)


def owned_square(blocks, owner, owners, total_rows):
    height, width = blocks[0].shape
    tall = width // owners
    wide = min(TILE, width)
    if tall % 128 or width % wide:
        rows = jnp.concatenate(blocks, axis=0)
        own = lax.dynamic_slice_in_dim(rows, owner[0] * tall, tall, axis=1)
        return dot_tn(own, rows) / total_rows
    count = len(blocks)
    depth = height * count
    return pl.pallas_call(
        functools.partial(square_kernel, count, 1.0 / total_rows),
        grid=(width // wide,),
        in_specs=[IN_SMEM] + [pl.BlockSpec((height, width), lambda step: (0, 0))] * count,
        out_specs=pl.BlockSpec((tall, wide), lambda step: (0, step)),
        out_shape=jax.ShapeDtypeStruct((tall, width), F32),
        scratch_shapes=[pltpu.VMEM((depth, width), BF16)],
        compiler_params=pltpu.CompilerParams(vmem_limit_bytes=40 * MIB),
        cost_estimate=pl.CostEstimate(
            flops=2 * depth * tall * width, bytes_accessed=2 * depth * width, transcendentals=0
        ),
    )(owner, *blocks)


def body(inputs, ln_gain, w_in, w_out, layer_scale, out_grad, owner_table):
    weight_in = pinned(w_in[0])
    weight_out = pinned(w_out[0])
    section_count = lax.axis_size("section")
    dp_count = lax.axis_size("dp")
    section_index = lax.axis_index("section")
    batch_count, row_count, width = inputs.shape
    width_hidden = w_in.shape[2]
    total_rows = batch_count * row_count * dp_count
    owner = owner_table[lax.axis_index("dp")].reshape(1)
    where = section_index.reshape(1)
    batches = range(batch_count)
    product = 2 * row_count * width * width_hidden
    block = jax.ShapeDtypeStruct((row_count, width), BF16)
    wide_scratch = pltpu.VMEM((row_count, width_hidden), BF16)

    def active(step):
        return (section_index == step).astype(jnp.int32).reshape(1)

    held = [[inputs[m]] for m in batches]
    for step in range(section_count - 1):
        for m in batches:
            (output,) = call(
                forward_kernel,
                [active(step)],
                [held[m][-1], ln_gain, weight_in, weight_out, layer_scale],
                [block],
                [wide_scratch],
                2 * product,
            )
            held[m].append(hop(output, step, 1))

    saved = [None] * batch_count
    returned = [[out_grad[m]] for m in batches]
    for step in range(section_count - 1, 0, -1):
        for m in batches:
            if saved[m] is None:
                saved[m] = call(
                    functools.partial(save_kernel, section_count),
                    [where],
                    [*held[m], ln_gain, weight_in],
                    [
                        block,
                        jax.ShapeDtypeStruct((row_count, width), F32),
                        jax.ShapeDtypeStruct((row_count, 1), F32),
                        jax.ShapeDtypeStruct((row_count, width_hidden), F32),
                    ],
                    [pltpu.VMEM((row_count, width), BF16)],
                    product,
                )
            _, normed, inv_std, slope = saved[m]
            (grad_input,) = call(
                backward_kernel,
                [active(step)],
                [
                    returned[m][0], ln_gain, weight_in, weight_out, layer_scale,
                    pinned(normed), pinned(inv_std), pinned(slope),
                ],
                [block],
                [wide_scratch],
                2 * product,
            )
            returned[m].insert(0, hop(grad_input, step, -1))

    act_blocks, grad_blocks = [], []
    for m in batches:
        act_blocks += gathered(saved[m][0], "dp")
    for m in batches:
        (grad_hidden,) = call(
            functools.partial(last_kernel, section_count),
            [where],
            [*returned[m], layer_scale, weight_out, pinned(saved[m][3])],
            [jax.ShapeDtypeStruct((row_count, width_hidden), BF16)],
            [pltpu.VMEM((row_count, width), BF16)],
            product,
        )
        grad_blocks += gathered(grad_hidden, "dp")
    act_share = owned_square(act_blocks, owner, dp_count, total_rows)
    grad_share = owned_square(grad_blocks, owner, dp_count, total_rows)
    return (act_share[None], grad_share[None])


def solution(mesh):
    placed = (
        P(None, "dp", None),
        P("section", None),
        P("section", None, None),
        P("section", None, None),
        P("section", None),
        P(None, "dp", None),
        P(),
    )
    return jax.shard_map(
        body,
        mesh=mesh,
        in_specs=placed,
        out_specs=(P("section", "dp", None), P("section", "dp", None)),
        check_vma=False,
    )
```

time: 192 us -> 127 us (0.66)
  matrix products: 90.4 us -> 0 us
  local copies, waits for them, and re-layouts: 11.6 us -> 35.7 us
  other arithmetic: 23 us -> 0 us
  Pallas kernels: 0 us -> 22 us
  starting transfers between devices: 44.4 us -> 47.3 us
  waiting for transfers between devices: 18.1 us -> 20.3 us
    dot_general x18 -> x0, matrix products: 90.4 us -> none  [the longest x6 44.1 us: input_grad(): lax.dot_general(grad_hidden, weight_in, (((1,), (1,)), ((), ())), preferr...]
    unnamed x44 -> x92, local copies, waits for them, and re-layouts: 9.45 us -> 34 us
    pallas_call x0 -> x18, Pallas kernels: none -> 22 us  [the longest x16 14.7 us: call(): pl.pallas_call(kernel, in_specs=[IN_SMEM] * len(scalars) + [IN_VMEM] * le...]
    ppermute x12, waiting for transfers between devices: 4.96 us -> 13.4 us  [hop(): return lax.ppermute(value, 'section', [(source, source + steps)])]
    convert_element_type x5 -> x0, other arithmetic: 7.47 us -> none  [input_grad(): return grad_input.astype(jnp.bfloat16)]
    ppermute x28, waiting for transfers between devices: 13.2 us -> 6.83 us  [swapped(): lax.ppermute(value, axis, [(source, source ^ mask) for source in range(co...]
    div x19 -> x0, other arithmetic: 5.68 us -> none  [the longest x6 3.13 us: input_grad(): mean_two = jnp.mean(grad_normed * normed, axis=-1, keepdims=True)]
    ppermute x28, starting transfers between devices: 28.9 us -> 33.7 us  [swapped(): lax.ppermute(value, axis, [(source, source ^ mask) for source in range(co...]
  transfers between devices with their start and end apart: 40 -> 40, of which waited for: 9 -> 6; matrix products, arithmetic and copies ran while one was open for 50% -> 0% of each run, Pallas kernels for 0% -> 13%
where the time goes in v2:
time: 127 us; the launch traced here: 126 us
  starting transfers between devices  47.3 us (37%)
  local copies, waits for them, and re-layouts  35.7 us (28%)
  Pallas kernels  22 us (17%)
  waiting for transfers between devices  20.3 us (16%)
    unnamed x92, local copies, waits for them, and re-layouts  34 us
    ppermute x28, starting transfers between devices, swapped(): lax.ppermute(value, axis, [(source, source ^ mask) for source in range(co...  33.7 us
    pallas_call x16, Pallas kernels, call(): pl.pallas_call(kernel, in_specs=[IN_SMEM] * len(scalars) + [IN_VMEM] * le...  14.7 us
    ppermute x12, starting transfers between devices, hop(): return lax.ppermute(value, 'section', [(source, source + steps)])  13.6 us
    ppermute x12, waiting for transfers between devices, hop(): return lax.ppermute(value, 'section', [(source, source + steps)])  13.4 us
    pallas_call x2, Pallas kernels, owned_square(): pl.pallas_call(functools.partial(square_kernel, count, 1.0 / total_rows),...  7.36 us
    ppermute x28, waiting for transfers between devices, swapped(): lax.ppermute(value, axis, [(source, source ^ mask) for source in range(co...  6.83 us
  transfers between devices with their start and end apart: 40, of which 6 were waited for; matrix products, arithmetic and copies ran while one was open for 0% of the time, Pallas kernels for 13%

profile of v2, /device:TPU:9, one launch (start us, length us, event | category | flops | bytes accessed | tf_op | source)
XLA Modules:
  0.0 126.4 jit_solution(12227038400085802311)
XLA Ops:
  1.6 2.2 %copy-done = bf16[1,1024,2048]{2,1,0:T(8,128)(2,1)S(1)} copy-done((bf16[1,1024,2048]{2,1,0:T(8,128)(2,1)S(1)}, bf16[1,1024,2048]{2,1,0:T(8,128)(2,1)}, u32[]{:S(2)}) %copy-start) | copy-done | bytes 4194328
  3.8 2.2 %copy-done.6 = bf16[1,2048,1024]{2,1,0:T(8,128)(2,1)S(1)} copy-done((bf16[1,2048,1024]{2,1,0:T(8,128)(2,1)S(1)}, bf16[1,2048,1024]{2,1,0:T(8,128)(2,1)}, u32[]{:S(2)}) %copy-start.6) | copy-done | bytes 4194328
  7.4 1.5 %collective-permute-start.10 = (bf16[64,1024]{1,0:T(8,128)(2,1)S(1)}, bf16[64,1024]{1,0:T(8,128)(2,1)S(1)}, u32[]{:S(2)}, u32[]{:S(2)}) collective-permute-start(bf16[64,1024]{1,0:T(8,128)(2,1)S(1)} %shard_map.90), channel_id=1, source_target_pairs={{0,1},{4,5},{8,9},{12,13},{16,17},{20,21},{24,25},{28,29}} | collective-permute-start | bytes 393224 | tf_op jit(solution)/shard_map/ppermute | solution.py:21
  9.6 1.4 %collective-permute-start = (bf16[64,1024]{1,0:T(8,128)(2,1)S(1)}, bf16[64,1024]{1,0:T(8,128)(2,1)S(1)}, u32[]{:S(2)}, u32[]{:S(2)}) collective-permute-start(bf16[64,1024]{1,0:T(8,128)(2,1)S(1)} %shard_map.86), channel_id=1, source_target_pairs={{0,1},{4,5},{8,9},{12,13},{16,17},{20,21},{24,25},{28,29}} | collective-permute-start | bytes 393224 | tf_op jit(solution)/shard_map/ppermute | solution.py:21
  11.0 2.9 %collective-permute-done.10.x_ref.refs_1_ = bf16[64,1024]{1,0:T(8,128)(2,1)S(1)} collective-permute-done((bf16[64,1024]{1,0:T(8,128)(2,1)S(1)}, bf16[64,1024]{1,0:T(8,128)(2,1)S(1)}, u32[]{:S(2)}, u32[]{:S(2)}) %collective-permute-start.10) | collective-permute-done | bytes 131104 | tf_op jit(solution)/shard_map/ppermute | solution.py:21
  13.9 2.2 %copy-done.2 = bf16[1,1024,2048]{2,1,0:T(8,128)(2,1)S(1)} copy-done((bf16[1,1024,2048]{2,1,0:T(8,128)(2,1)S(1)}, bf16[1,1024,2048]{2,1,0:T(8,128)(2,1)}, u32[]{:S(2)}) %copy-start.2) | copy-done | bytes 4194328
  16.1 2.2 %copy-done.7 = bf16[1,2048,1024]{2,1,0:T(8,128)(2,1)S(1)} copy-done((bf16[1,2048,1024]{2,1,0:T(8,128)(2,1)S(1)}, bf16[1,2048,1024]{2,1,0:T(8,128)(2,1)}, u32[]{:S(2)}) %copy-start.7) | copy-done | bytes 4194328
  18.3 1.8 %shard_map.91 = bf16[64,1024]{1,0:T(8,128)(2,1)S(1)} custom-call(s32[1]{0:T(128)} %bitcast.5.here, bf16[64,1024]{1,0:T(8,128)(2,1)S(1)} %collective-permute-done.10.x_ref.refs_1_, f32[1,1024]{1,0:T(1,128)S(1)} %copy-done.13, bf16[1024,2048]{1,0:T(8,128)(2,1)S(1)} %bitcast.19, bf16[2048,1024]{1,0:T(8,128)(2,1)S(1)} %bitcast.33, f32[1,1024]{1,0:T(1,128)S(1)} %copy-done.11), custom_call_target="tpu_custom_call" | custom-call | flops 536870912 | bytes 8527872 | tf_op jit(solution)/shard_map/pallas_call | solution.py:146
  20.1 1.3 %collective-permute-start.11 = (bf16[64,1024]{1,0:T(8,128)(2,1)S(1)}, bf16[64,1024]{1,0:T(8,128)(2,1)S(1)}, u32[]{:S(2)}, u32[]{:S(2)}) collective-permute-start(bf16[64,1024]{1,0:T(8,128)(2,1)S(1)} %shard_map.91), channel_id=1, source_target_pairs={{1,2},{5,6},{9,10},{13,14},{17,18},{21,22},{25,26},{29,30}} | collective-permute-start | bytes 393224 | tf_op jit(solution)/shard_map/ppermute | solution.py:21
  21.4 1.8 %shard_map.87 = bf16[64,1024]{1,0:T(8,128)(2,1)S(1)} custom-call(s32[1]{0:T(128)} %bitcast.5.here, bf16[64,1024]{1,0:T(8,128)(2,1)S(1)} %collective-permute-done.x_ref.refs_1_, f32[1,1024]{1,0:T(1,128)S(1)} %copy-done.13, bf16[1024,2048]{1,0:T(8,128)(2,1)S(1)} %bitcast.20, bf16[2048,1024]{1,0:T(8,128)(2,1)S(1)} %bitcast.34, f32[1,1024]{1,0:T(1,128)S(1)} %copy-done.11), custom_call_target="tpu_custom_call" | custom-call | flops 536870912 | bytes 8527872 | tf_op jit(solution)/shard_map/pallas_call | solution.py:146
  23.2 1.3 %collective-permute-start.1 = (bf16[64,1024]{1,0:T(8,128)(2,1)S(1)}, bf16[64,1024]{1,0:T(8,128)(2,1)S(1)}, u32[]{:S(2)}, u32[]{:S(2)}) collective-permute-start(bf16[64,1024]{1,0:T(8,128)(2,1)S(1)} %shard_map.87), channel_id=1, source_target_pairs={{1,2},{5,6},{9,10},{13,14},{17,18},{21,22},{25,26},{29,30}} | collective-permute-start | bytes 393224 | tf_op jit(solution)/shard_map/ppermute | solution.py:21
  24.5 2.2 %copy-done.3 = bf16[1,1024,2048]{2,1,0:T(8,128)(2,1)S(1)} copy-done((bf16[1,1024,2048]{2,1,0:T(8,128)(2,1)S(1)}, bf16[1,1024,2048]{2,1,0:T(8,128)(2,1)}, u32[]{:S(2)}) %copy-start.3) | copy-done | bytes 4194328
  26.7 2.2 %copy-done.8 = bf16[1,2048,1024]{2,1,0:T(8,128)(2,1)S(1)} copy-done((bf16[1,2048,1024]{2,1,0:T(8,128)(2,1)S(1)}, bf16[1,2048,1024]{2,1,0:T(8,128)(2,1)}, u32[]{:S(2)}) %copy-start.8) | copy-done | bytes 4194328
  30.4 2.2 %copy-done.4 = bf16[1,1024,2048]{2,1,0:T(8,128)(2,1)S(1)} copy-done((bf16[1,1024,2048]{2,1,0:T(8,128)(2,1)S(1)}, bf16[1,1024,2048]{2,1,0:T(8,128)(2,1)}, u32[]{:S(2)}) %copy-start.4) | copy-done | bytes 4194328
  32.6 1.1 shard_map.93
  33.7 1.1 copy-done.9
  35.6 1.4 %copy-done.5 = bf16[1,1024,2048]{2,1,0:T(8,128)(2,1)S(1)} copy-done((bf16[1,1024,2048]{2,1,0:T(8,128)(2,1)S(1)}, bf16[1,1024,2048]{2,1,0:T(8,128)(2,1)}, u32[]{:S(2)}) %copy-start.5) | copy-done | bytes 4194328
  37.0 1.1 shard_map.89
  39.0 1.3 %collective-permute-start.13 = (bf16[64,1024]{1,0:T(8,128)(2,1)S(1)}, bf16[64,1024]{1,0:T(8,128)(2,1)S(1)}, u32[]{:S(2)}, u32[]{:S(2)}) collective-permute-start(bf16[64,1024]{1,0:T(8,128)(2,1)S(1)} %get-tuple-element.11.refs_8_), channel_id=1, source_target_pairs={{0,8},{4,12},{8,0},{12,4},{16,24},{20,28},{24,16},{28,20},{1,9},{5... | collective-permute-start | bytes 393224 | tf_op jit(solution)/shard_map/ppermute | solution.py:26
  40.3 1.2 collective-permute-start.14
  41.7 2.4 %collective-permute-start.16 = (bf16[64,1024]{1,0:T(8,128)(2,1)S(1)}, bf16[64,1024]{1,0:T(8,128)(2,1)S(1)}, u32[]{:S(2)}, u32[]{:S(2)}) collective-permute-start(bf16[64,1024]{1,0:T(8,128)(2,1)S(1)} %get-tuple-element.11.refs_8_), channel_id=1, source_target_pairs={{0,4},{4,0},{8,12},{12,8},{16,20},{20,16},{24,28},{28,24},{1,5},{5... | collective-permute-start | bytes 393224 | tf_op jit(solution)/shard_map/ppermute | solution.py:26
  44.1 1.2 collective-permute-start.3
  45.4 1.3 %collective-permute-start.31 = (bf16[64,1024]{1,0:T(8,128)(2,1)S(1)}, bf16[64,1024]{1,0:T(8,128)(2,1)S(1)}, u32[]{:S(2)}, u32[]{:S(2)}) collective-permute-start(bf16[64,1024]{1,0:T(8,128)(2,1)S(1)} %shard_map.100), channel_id=1, source_target_pairs={{2,1},{6,5},{10,9},{14,13},{18,17},{22,21},{26,25},{30,29}} | collective-permute-start | bytes 393224 | tf_op jit(solution)/shard_map/ppermute | solution.py:21
  46.7 1.3 %collective-permute-start.4 = (bf16[64,1024]{1,0:T(8,128)(2,1)S(1)}, bf16[64,1024]{1,0:T(8,128)(2,1)S(1)}, u32[]{:S(2)}, u32[]{:S(2)}) collective-permute-start(bf16[64,1024]{1,0:T(8,128)(2,1)S(1)} %get-tuple-element.10.refs_0_), channel_id=1, source_target_pairs={{0,16},{4,20},{8,24},{12,28},{16,0},{20,4},{24,8},{28,12},{1,17},{... | collective-permute-start | bytes 393224 | tf_op jit(solution)/shard_map/ppermute | solution.py:26
  48.2 2.7 %collective-permute-start.6 = (bf16[64,1024]{1,0:T(8,128)(2,1)S(1)}, bf16[64,1024]{1,0:T(8,128)(2,1)S(1)}, u32[]{:S(2)}, u32[]{:S(2)}) collective-permute-start(bf16[64,1024]{1,0:T(8,128)(2,1)S(1)} %get-tuple-element.10.refs_0_), channel_id=1, source_target_pairs={{0,4},{4,0},{8,12},{12,8},{16,20},{20,16},{24,28},{28,24},{1,5},{5... | collective-permute-start | bytes 393224 | tf_op jit(solution)/shard_map/ppermute | solution.py:26
  50.9 1.3 %collective-permute-start.21 = (bf16[64,1024]{1,0:T(8,128)(2,1)S(1)}, bf16[64,1024]{1,0:T(8,128)(2,1)S(1)}, u32[]{:S(2)}, u32[]{:S(2)}) collective-permute-start(bf16[64,1024]{1,0:T(8,128)(2,1)S(1)} %shard_map.96), channel_id=1, source_target_pairs={{2,1},{6,5},{10,9},{14,13},{18,17},{22,21},{26,25},{30,29}} | collective-permute-start | bytes 393224 | tf_op jit(solution)/shard_map/ppermute | solution.py:21
  52.2 8.4 %collective-permute-done.31.gy_ref.refs_1_ = bf16[64,1024]{1,0:T(8,128)(2,1)S(1)} collective-permute-done((bf16[64,1024]{1,0:T(8,128)(2,1)S(1)}, bf16[64,1024]{1,0:T(8,128)(2,1)S(1)}, u32[]{:S(2)}, u32[]{:S(2)}) %collective-permute-start.31) | collective-permute-done | bytes 131104 | tf_op jit(solution)/shard_map/ppermute | solution.py:21
  60.6 3.4 %collective-permute-start.17 = (bf16[64,1024]{1,0:T(8,128)(2,1)S(1)}, bf16[64,1024]{1,0:T(8,128)(2,1)S(1)}, u32[]{:S(2)}, u32[]{:S(2)}) collective-permute-start(bf16[64,1024]{1,0:T(8,128)(2,1)S(1)} %collective-permute-done.13.refs_9_), channel_id=1, source_target_pairs={{0,4},{4,0},{8,12},{12,8},{16,20},{20,16},{24,28},{28,24},{1,5},{5... | collective-permute-start | bytes 393224 | tf_op jit(solution)/shard_map/ppermute | solution.py:26
  64.0 2.8 %shard_map.101 = bf16[64,1024]{1,0:T(8,128)(2,1)S(1)} custom-call(s32[1]{0:T(128)} %bitcast.5.here, bf16[64,1024]{1,0:T(8,128)(2,1)S(1)} %collective-permute-done.31.gy_ref.refs_1_, f32[1,1024]{1,0:T(1,128)S(1)} %copy-done.13, bf16[1024,2048]{1,0:T(8,128)(2,1)S(1)} %bitcast.29, bf16[2048,1024]{1,0:T(8,128)(2,1)S(1)} %bitcast.41, f32[1,1024]{1,0:T(1,128)S(1)} %copy-done.11, ...), custom_call_target="tpu_custom_call" | custom-call | flops 536870912 | bytes 9314560 | tf_op jit(solution)/shard_map/pallas_call | solution.py:146
  66.8 1.3 %collective-permute-start.32 = (bf16[64,1024]{1,0:T(8,128)(2,1)S(1)}, bf16[64,1024]{1,0:T(8,128)(2,1)S(1)}, u32[]{:S(2)}, u32[]{:S(2)}) collective-permute-start(bf16[64,1024]{1,0:T(8,128)(2,1)S(1)} %shard_map.101), channel_id=1, source_target_pairs={{1,0},{5,4},{9,8},{13,12},{17,16},{21,20},{25,24},{29,28}} | collective-permute-start | bytes 393224 | tf_op jit(solution)/shard_map/ppermute | solution.py:21
  68.8 2.1 %collective-permute-done.21.gy_ref.refs_1_ = bf16[64,1024]{1,0:T(8,128)(2,1)S(1)} collective-permute-done((bf16[64,1024]{1,0:T(8,128)(2,1)S(1)}, bf16[64,1024]{1,0:T(8,128)(2,1)S(1)}, u32[]{:S(2)}, u32[]{:S(2)}) %collective-permute-start.21) | collective-permute-done | bytes 131104 | tf_op jit(solution)/shard_map/ppermute | solution.py:21
  71.6 2.8 %shard_map.97 = bf16[64,1024]{1,0:T(8,128)(2,1)S(1)} custom-call(s32[1]{0:T(128)} %bitcast.5.here, bf16[64,1024]{1,0:T(8,128)(2,1)S(1)} %collective-permute-done.21.gy_ref.refs_1_, f32[1,1024]{1,0:T(1,128)S(1)} %copy-done.13, bf16[1024,2048]{1,0:T(8,128)(2,1)S(1)} %bitcast.30, bf16[2048,1024]{1,0:T(8,128)(2,1)S(1)} %bitcast.42, f32[1,1024]{1,0:T(1,128)S(1)} %copy-done.11, ...), custom_call_target="tpu_custom_call" | custom-call | flops 536870912 | bytes 9314560 | tf_op jit(solution)/shard_map/pallas_call | solution.py:146
  74.5 1.3 %collective-permute-start.22 = (bf16[64,1024]{1,0:T(8,128)(2,1)S(1)}, bf16[64,1024]{1,0:T(8,128)(2,1)S(1)}, u32[]{:S(2)}, u32[]{:S(2)}) collective-permute-start(bf16[64,1024]{1,0:T(8,128)(2,1)S(1)} %shard_map.97), channel_id=1, source_target_pairs={{1,0},{5,4},{9,8},{13,12},{17,16},{21,20},{25,24},{29,28}} | collective-permute-start | bytes 393224 | tf_op jit(solution)/shard_map/ppermute | solution.py:21
  75.8 1.4 %shard_map.102.refs_8_ = bf16[64,2048]{1,0:T(8,128)(2,1)S(1)} custom-call(s32[1]{0:T(128)} %bitcast.where, bf16[64,1024]{1,0:T(8,128)(2,1)S(1)} %collective-permute-done.32.refs_0_, bf16[64,1024]{1,0:T(8,128)(2,1)S(1)} %collective-permute-done.31.gy_ref.refs_1_, bf16[64,1024]{1,0:T(8,128)(2,1)S(1)} %collective-permute-done.30.gy_ref.refs_2_, ...), custom_call_target="tpu_custom_call" | custom-call | flops 268435456 | bytes 5246976 | tf_op jit(solution)/shard_map/pallas_call | solution.py:146
  77.3 1.3 %collective-permute-start.33 = (bf16[64,2048]{1,0:T(8,128)(2,1)S(1)}, bf16[64,2048]{1,0:T(8,128)(2,1)S(1)}, u32[]{:S(2)}, u32[]{:S(2)}) collective-permute-start(bf16[64,2048]{1,0:T(8,128)(2,1)S(1)} %shard_map.102.refs_8_), channel_id=1, source_target_pairs={{0,8},{4,12},{8,0},{12,4},{16,24},{20,28},{24,16},{28,20},{1,9},{5... | collective-permute-start | bytes 786440 | tf_op jit(solution)/shard_map/ppermute | solution.py:26
  78.5 1.2 collective-permute-start.34
  80.0 1.3 %collective-permute-start.36 = (bf16[64,2048]{1,0:T(8,128)(2,1)S(1)}, bf16[64,2048]{1,0:T(8,128)(2,1)S(1)}, u32[]{:S(2)}, u32[]{:S(2)}) collective-permute-start(bf16[64,2048]{1,0:T(8,128)(2,1)S(1)} %shard_map.102.refs_8_), channel_id=1, source_target_pairs={{0,4},{4,0},{8,12},{12,8},{16,20},{20,16},{24,28},{28,24},{1,5},{5... | collective-permute-start | bytes 786440 | tf_op jit(solution)/shard_map/ppermute | solution.py:26
  81.3 1.6 %shard_map.98.refs_0_ = bf16[64,2048]{1,0:T(8,128)(2,1)S(1)} custom-call(s32[1]{0:T(128)} %bitcast.where, bf16[64,1024]{1,0:T(8,128)(2,1)S(1)} %collective-permute-done.22.refs_0_, bf16[64,1024]{1,0:T(8,128)(2,1)S(1)} %collective-permute-done.21.gy_ref.refs_1_, bf16[64,1024]{1,0:T(8,128)(2,1)S(1)} %collective-permute-done.20.gy_ref.refs_2_, ...), custom_call_target="tpu_custom_call" | custom-call | flops 268435456 | bytes 5246976 | tf_op jit(solution)/shard_map/pallas_call | solution.py:146
  83.6 1.2 collective-permute-start.23
  84.8 1.2 collective-permute-start.24
  86.1 1.1 collective-permute-start.25
  87.2 4.2 %collective-permute-done.35.refs_11_ = bf16[64,2048]{1,0:T(8,128)(2,1)S(1)} collective-permute-done((bf16[64,2048]{1,0:T(8,128)(2,1)S(1)}, bf16[64,2048]{1,0:T(8,128)(2,1)S(1)}, u32[]{:S(2)}, u32[]{:S(2)}) %collective-permute-start.35) | collective-permute-done | bytes 262176 | tf_op jit(solution)/shard_map/ppermute | solution.py:26
  91.4 2.7 %collective-permute-start.26 = (bf16[64,2048]{1,0:T(8,128)(2,1)S(1)}, bf16[64,2048]{1,0:T(8,128)(2,1)S(1)}, u32[]{:S(2)}, u32[]{:S(2)}) collective-permute-start(bf16[64,2048]{1,0:T(8,128)(2,1)S(1)} %shard_map.98.refs_0_), channel_id=1, source_target_pairs={{0,4},{4,0},{8,12},{12,8},{16,20},{20,16},{24,28},{28,24},{1,5},{5... | collective-permute-start | bytes 786440 | tf_op jit(solution)/shard_map/ppermute | solution.py:26
  94.2 1.9 %collective-permute-done.23.refs_1_ = bf16[64,2048]{1,0:T(8,128)(2,1)S(1)} collective-permute-done((bf16[64,2048]{1,0:T(8,128)(2,1)S(1)}, bf16[64,2048]{1,0:T(8,128)(2,1)S(1)}, u32[]{:S(2)}, u32[]{:S(2)}) %collective-permute-start.23) | collective-permute-done | bytes 262176 | tf_op jit(solution)/shard_map/ppermute | solution.py:26
  96.0 2.2 %collective-permute-start.38 = (bf16[64,2048]{1,0:T(8,128)(2,1)S(1)}, bf16[64,2048]{1,0:T(8,128)(2,1)S(1)}, u32[]{:S(2)}, u32[]{:S(2)}) collective-permute-start(bf16[64,2048]{1,0:T(8,128)(2,1)S(1)} %collective-permute-done.34.refs_10_), channel_id=1, source_target_pairs={{0,4},{4,0},{8,12},{12,8},{16,20},{20,16},{24,28},{28,24},{1,5},{5... | collective-permute-start | bytes 786440 | tf_op jit(solution)/shard_map/ppermute | solution.py:26
  98.9 5.2 %collective-permute-start.39 = (bf16[64,2048]{1,0:T(8,128)(2,1)S(1)}, bf16[64,2048]{1,0:T(8,128)(2,1)S(1)}, u32[]{:S(2)}, u32[]{:S(2)}) collective-permute-start(bf16[64,2048]{1,0:T(8,128)(2,1)S(1)} %collective-permute-done.35.refs_11_), channel_id=1, source_target_pairs={{0,4},{4,0},{8,12},{12,8},{16,20},{20,16},{24,28},{28,24},{1,5},{5... | collective-permute-start | bytes 786440 | tf_op jit(solution)/shard_map/ppermute | solution.py:26
  119.0 2.2 %shard_map.94 = f32[128,1024]{1,0:T(8,128)} custom-call(s32[1]{0:T(128)} %dynamic_slice.3.owner, bf16[64,1024]{1,0:T(8,128)(2,1)S(1)} %copy-done.15, bf16[64,1024]{1,0:T(8,128)(2,1)S(1)} %copy-done.25, bf16[64,1024]{1,0:T(8,128)(2,1)S(1)} %copy-done.27, bf16[64,1024]{1,0:T(8,128)(2,1)S(1)} %copy-done.29, bf16[64,1024]{1,0:T(8,128)(2,1)S(1)} %copy-done.31, ...), custom_call_target="tpu_custom_call" | custom-call | flops 268435456 | bytes 2097152 | tf_op jit(solution)/shard_map/pallas_call | solution.py:167
  121.2 5.1 %shard_map.103 = f32[256,2048]{1,0:T(8,128)} custom-call(s32[1]{0:T(128)} %dynamic_slice.3.owner, bf16[64,2048]{1,0:T(8,128)(2,1)S(1)} %shard_map.98.refs_0_, bf16[64,2048]{1,0:T(8,128)(2,1)S(1)} %collective-permute-done.23.refs_1_, bf16[64,2048]{1,0:T(8,128)(2,1)S(1)} %collective-permute-done.24.refs_2_, ...), custom_call_target="tpu_custom_call" | custom-call | flops 1073741824 | bytes 4194304 | tf_op jit(solution)/shard_map/pallas_call | solution.py:167
  (145 shorter events, 24.5 us)
Async XLA Ops:
  7.4 6.5 %collective-permute-start.10 = (bf16[64,1024]{1,0:T(8,128)(2,1)S(1)}, bf16[64,1024]{1,0:T(8,128)(2,1)S(1)}, u32[]{:S(2)}, u32[]{:S(2)}) collective-permute-start(bf16[64,1024]{1,0:T(8,128)(2,1)S(1)} %shard_map.90), channel_id=1, source_target_pairs={{0,1},{4,5},{8,9},{12,13},{16,17},{20,21},{24,25},{28,29}} | collective-permute-start | bytes 393224 | tf_op jit(solution)/shard_map/ppermute | solution.py:21
  9.6 11.8 %collective-permute-start = (bf16[64,1024]{1,0:T(8,128)(2,1)S(1)}, bf16[64,1024]{1,0:T(8,128)(2,1)S(1)}, u32[]{:S(2)}, u32[]{:S(2)}) collective-permute-start(bf16[64,1024]{1,0:T(8,128)(2,1)S(1)} %shard_map.86), channel_id=1, source_target_pairs={{0,1},{4,5},{8,9},{12,13},{16,17},{20,21},{24,25},{28,29}} | collective-permute-start | bytes 393224 | tf_op jit(solution)/shard_map/ppermute | solution.py:21
  20.1 4.4 %collective-permute-start.11 = (bf16[64,1024]{1,0:T(8,128)(2,1)S(1)}, bf16[64,1024]{1,0:T(8,128)(2,1)S(1)}, u32[]{:S(2)}, u32[]{:S(2)}) collective-permute-start(bf16[64,1024]{1,0:T(8,128)(2,1)S(1)} %shard_map.91), channel_id=1, source_target_pairs={{1,2},{5,6},{9,10},{13,14},{17,18},{21,22},{25,26},{29,30}} | collective-permute-start | bytes 393224 | tf_op jit(solution)/shard_map/ppermute | solution.py:21
  23.2 6.5 %collective-permute-start.1 = (bf16[64,1024]{1,0:T(8,128)(2,1)S(1)}, bf16[64,1024]{1,0:T(8,128)(2,1)S(1)}, u32[]{:S(2)}, u32[]{:S(2)}) collective-permute-start(bf16[64,1024]{1,0:T(8,128)(2,1)S(1)} %shard_map.87), channel_id=1, source_target_pairs={{1,2},{5,6},{9,10},{13,14},{17,18},{21,22},{25,26},{29,30}} | collective-permute-start | bytes 393224 | tf_op jit(solution)/shard_map/ppermute | solution.py:21
  28.9 1.5 %collective-permute-start.12 = (bf16[64,1024]{1,0:T(8,128)(2,1)S(1)}, bf16[64,1024]{1,0:T(8,128)(2,1)S(1)}, u32[]{:S(2)}, u32[]{:S(2)}) collective-permute-start(bf16[64,1024]{1,0:T(8,128)(2,1)S(1)} %shard_map.92), channel_id=1, source_target_pairs={{2,3},{6,7},{10,11},{14,15},{18,19},{22,23},{26,27},{30,31}} | collective-permute-start | bytes 393224 | tf_op jit(solution)/shard_map/ppermute | solution.py:21
  29.7 5.9 %collective-permute-start.2 = (bf16[64,1024]{1,0:T(8,128)(2,1)S(1)}, bf16[64,1024]{1,0:T(8,128)(2,1)S(1)}, u32[]{:S(2)}, u32[]{:S(2)}) collective-permute-start(bf16[64,1024]{1,0:T(8,128)(2,1)S(1)} %shard_map.88), channel_id=1, source_target_pairs={{2,3},{6,7},{10,11},{14,15},{18,19},{22,23},{26,27},{30,31}} | collective-permute-start | bytes 393224 | tf_op jit(solution)/shard_map/ppermute | solution.py:21
  34.8 6.9 %collective-permute-start.30 = (bf16[64,1024]{1,0:T(8,128)(2,1)S(1)}, bf16[64,1024]{1,0:T(8,128)(2,1)S(1)}, u32[]{:S(2)}, u32[]{:S(2)}) collective-permute-start(bf16[64,1024]{1,0:T(8,128)(2,1)S(1)} %shard_map.99), channel_id=1, source_target_pairs={{3,2},{7,6},{11,10},{15,14},{19,18},{23,22},{27,26},{31,30}} | collective-permute-start | bytes 393224 | tf_op jit(solution)/shard_map/ppermute | solution.py:21
  38.3 5.8 %collective-permute-start.20 = (bf16[64,1024]{1,0:T(8,128)(2,1)S(1)}, bf16[64,1024]{1,0:T(8,128)(2,1)S(1)}, u32[]{:S(2)}, u32[]{:S(2)}) collective-permute-start(bf16[64,1024]{1,0:T(8,128)(2,1)S(1)} %shard_map.95), channel_id=1, source_target_pairs={{3,2},{7,6},{11,10},{15,14},{19,18},{23,22},{27,26},{31,30}} | collective-permute-start | bytes 393224 | tf_op jit(solution)/shard_map/ppermute | solution.py:21
  39.0 6.3 %collective-permute-start.13 = (bf16[64,1024]{1,0:T(8,128)(2,1)S(1)}, bf16[64,1024]{1,0:T(8,128)(2,1)S(1)}, u32[]{:S(2)}, u32[]{:S(2)}) collective-permute-start(bf16[64,1024]{1,0:T(8,128)(2,1)S(1)} %get-tuple-element.11.refs_8_), channel_id=1, source_target_pairs={{0,8},{4,12},{8,0},{12,4},{16,24},{20,28},{24,16},{28,20},{1,9},{5... | collective-permute-start | bytes 393224 | tf_op jit(solution)/shard_map/ppermute | solution.py:26
  40.3 6.4 %collective-permute-start.14 = (bf16[64,1024]{1,0:T(8,128)(2,1)S(1)}, bf16[64,1024]{1,0:T(8,128)(2,1)S(1)}, u32[]{:S(2)}, u32[]{:S(2)}) collective-permute-start(bf16[64,1024]{1,0:T(8,128)(2,1)S(1)} %get-tuple-element.11.refs_8_), channel_id=1, source_target_pairs={{0,16},{4,20},{8,24},{12,28},{16,0},{20,4},{24,8},{28,12},{1,17},{... | collective-permute-start | bytes 393224 | tf_op jit(solution)/shard_map/ppermute | solution.py:26
  41.5 6.4 %collective-permute-start.15 = (bf16[64,1024]{1,0:T(8,128)(2,1)S(1)}, bf16[64,1024]{1,0:T(8,128)(2,1)S(1)}, u32[]{:S(2)}, u32[]{:S(2)}) collective-permute-start(bf16[64,1024]{1,0:T(8,128)(2,1)S(1)} %get-tuple-element.11.refs_8_), channel_id=1, source_target_pairs={{0,24},{4,28},{8,16},{12,20},{16,8},{20,12},{24,0},{28,4},{1,25},{... | collective-permute-start | bytes 393224 | tf_op jit(solution)/shard_map/ppermute | solution.py:26
  41.7 6.4 %collective-permute-start.16 = (bf16[64,1024]{1,0:T(8,128)(2,1)S(1)}, bf16[64,1024]{1,0:T(8,128)(2,1)S(1)}, u32[]{:S(2)}, u32[]{:S(2)}) collective-permute-start(bf16[64,1024]{1,0:T(8,128)(2,1)S(1)} %get-tuple-element.11.refs_8_), channel_id=1, source_target_pairs={{0,4},{4,0},{8,12},{12,8},{16,20},{20,16},{24,28},{28,24},{1,5},{5... | collective-permute-start | bytes 393224 | tf_op jit(solution)/shard_map/ppermute | solution.py:26
  44.1 6.8 %collective-permute-start.3 = (bf16[64,1024]{1,0:T(8,128)(2,1)S(1)}, bf16[64,1024]{1,0:T(8,128)(2,1)S(1)}, u32[]{:S(2)}, u32[]{:S(2)}) collective-permute-start(bf16[64,1024]{1,0:T(8,128)(2,1)S(1)} %get-tuple-element.10.refs_0_), channel_id=1, source_target_pairs={{0,8},{4,12},{8,0},{12,4},{16,24},{20,28},{24,16},{28,20},{1,9},{5... | collective-permute-start | bytes 393224 | tf_op jit(solution)/shard_map/ppermute | solution.py:26
  45.4 15.2 %collective-permute-start.31 = (bf16[64,1024]{1,0:T(8,128)(2,1)S(1)}, bf16[64,1024]{1,0:T(8,128)(2,1)S(1)}, u32[]{:S(2)}, u32[]{:S(2)}) collective-permute-start(bf16[64,1024]{1,0:T(8,128)(2,1)S(1)} %shard_map.100), channel_id=1, source_target_pairs={{2,1},{6,5},{10,9},{14,13},{18,17},{22,21},{26,25},{30,29}} | collective-permute-start | bytes 393224 | tf_op jit(solution)/shard_map/ppermute | solution.py:21
  46.7 21.5 %copy-start.18 = (bf16[64,1024]{1,0:T(8,128)(2,1)}, bf16[64,1024]{1,0:T(8,128)(2,1)S(1)}, u32[]{:S(2)}) copy-start(bf16[64,1024]{1,0:T(8,128)(2,1)S(1)} %collective-permute-done.14.refs_10_) | copy-start | bytes 393220
  46.7 20.1 %collective-permute-start.4 = (bf16[64,1024]{1,0:T(8,128)(2,1)S(1)}, bf16[64,1024]{1,0:T(8,128)(2,1)S(1)}, u32[]{:S(2)}, u32[]{:S(2)}) collective-permute-start(bf16[64,1024]{1,0:T(8,128)(2,1)S(1)} %get-tuple-element.10.refs_0_), channel_id=1, source_target_pairs={{0,16},{4,20},{8,24},{12,28},{16,0},{20,4},{24,8},{28,12},{1,17},{... | collective-permute-start | bytes 393224 | tf_op jit(solution)/shard_map/ppermute | solution.py:26
  48.0 20.3 %copy-start.20 = (bf16[64,1024]{1,0:T(8,128)(2,1)}, bf16[64,1024]{1,0:T(8,128)(2,1)S(1)}, u32[]{:S(2)}) copy-start(bf16[64,1024]{1,0:T(8,128)(2,1)S(1)} %collective-permute-done.15.refs_11_) | copy-start | bytes 393220
  48.0 20.2 %collective-permute-start.5 = (bf16[64,1024]{1,0:T(8,128)(2,1)S(1)}, bf16[64,1024]{1,0:T(8,128)(2,1)S(1)}, u32[]{:S(2)}, u32[]{:S(2)}) collective-permute-start(bf16[64,1024]{1,0:T(8,128)(2,1)S(1)} %get-tuple-element.10.refs_0_), channel_id=1, source_target_pairs={{0,24},{4,28},{8,16},{12,20},{16,8},{20,12},{24,0},{28,4},{1,25},{... | collective-permute-start | bytes 393224 | tf_op jit(solution)/shard_map/ppermute | solution.py:26
  48.2 20.0 %collective-permute-start.6 = (bf16[64,1024]{1,0:T(8,128)(2,1)S(1)}, bf16[64,1024]{1,0:T(8,128)(2,1)S(1)}, u32[]{:S(2)}, u32[]{:S(2)}) collective-permute-start(bf16[64,1024]{1,0:T(8,128)(2,1)S(1)} %get-tuple-element.10.refs_0_), channel_id=1, source_target_pairs={{0,4},{4,0},{8,12},{12,8},{16,20},{20,16},{24,28},{28,24},{1,5},{5... | collective-permute-start | bytes 393224 | tf_op jit(solution)/shard_map/ppermute | solution.py:26
  50.9 20.0 %copy-start.24 = (bf16[64,1024]{1,0:T(8,128)(2,1)}, bf16[64,1024]{1,0:T(8,128)(2,1)S(1)}, u32[]{:S(2)}) copy-start(bf16[64,1024]{1,0:T(8,128)(2,1)S(1)} %collective-permute-done.3.refs_1_) | copy-start | bytes 393220
  50.9 20.0 %collective-permute-start.21 = (bf16[64,1024]{1,0:T(8,128)(2,1)S(1)}, bf16[64,1024]{1,0:T(8,128)(2,1)S(1)}, u32[]{:S(2)}, u32[]{:S(2)}) collective-permute-start(bf16[64,1024]{1,0:T(8,128)(2,1)S(1)} %shard_map.96), channel_id=1, source_target_pairs={{2,1},{6,5},{10,9},{14,13},{18,17},{22,21},{26,25},{30,29}} | collective-permute-start | bytes 393224 | tf_op jit(solution)/shard_map/ppermute | solution.py:21
  60.6 11.0 %collective-permute-start.17 = (bf16[64,1024]{1,0:T(8,128)(2,1)S(1)}, bf16[64,1024]{1,0:T(8,128)(2,1)S(1)}, u32[]{:S(2)}, u32[]{:S(2)}) collective-permute-start(bf16[64,1024]{1,0:T(8,128)(2,1)S(1)} %collective-permute-done.13.refs_9_), channel_id=1, source_target_pairs={{0,4},{4,0},{8,12},{12,8},{16,20},{20,16},{24,28},{28,24},{1,5},{5... | collective-permute-start | bytes 393224 | tf_op jit(solution)/shard_map/ppermute | solution.py:26
  66.8 7.7 %collective-permute-start.32 = (bf16[64,1024]{1,0:T(8,128)(2,1)S(1)}, bf16[64,1024]{1,0:T(8,128)(2,1)S(1)}, u32[]{:S(2)}, u32[]{:S(2)}) collective-permute-start(bf16[64,1024]{1,0:T(8,128)(2,1)S(1)} %shard_map.101), channel_id=1, source_target_pairs={{1,0},{5,4},{9,8},{13,12},{17,16},{21,20},{25,24},{29,28}} | collective-permute-start | bytes 393224 | tf_op jit(solution)/shard_map/ppermute | solution.py:21
  68.1 9.1 %collective-permute-start.18 = (bf16[64,1024]{1,0:T(8,128)(2,1)S(1)}, bf16[64,1024]{1,0:T(8,128)(2,1)S(1)}, u32[]{:S(2)}, u32[]{:S(2)}) collective-permute-start(bf16[64,1024]{1,0:T(8,128)(2,1)S(1)} %collective-permute-done.14.refs_10_), channel_id=1, source_target_pairs={{0,4},{4,0},{8,12},{12,8},{16,20},{20,16},{24,28},{28,24},{1,5},{5... | collective-permute-start | bytes 393224 | tf_op jit(solution)/shard_map/ppermute | solution.py:26
  68.3 10.3 %collective-permute-start.19 = (bf16[64,1024]{1,0:T(8,128)(2,1)S(1)}, bf16[64,1024]{1,0:T(8,128)(2,1)S(1)}, u32[]{:S(2)}, u32[]{:S(2)}) collective-permute-start(bf16[64,1024]{1,0:T(8,128)(2,1)S(1)} %collective-permute-done.15.refs_11_), channel_id=1, source_target_pairs={{0,4},{4,0},{8,12},{12,8},{16,20},{20,16},{24,28},{28,24},{1,5},{5... | collective-permute-start | bytes 393224 | tf_op jit(solution)/shard_map/ppermute | solution.py:26
  70.9 8.8 %collective-permute-start.7 = (bf16[64,1024]{1,0:T(8,128)(2,1)S(1)}, bf16[64,1024]{1,0:T(8,128)(2,1)S(1)}, u32[]{:S(2)}, u32[]{:S(2)}) collective-permute-start(bf16[64,1024]{1,0:T(8,128)(2,1)S(1)} %collective-permute-done.3.refs_1_), channel_id=1, source_target_pairs={{0,4},{4,0},{8,12},{12,8},{16,20},{20,16},{24,28},{28,24},{1,5},{5... | collective-permute-start | bytes 393224 | tf_op jit(solution)/shard_map/ppermute | solution.py:26
  71.6 8.4 %collective-permute-start.8 = (bf16[64,1024]{1,0:T(8,128)(2,1)S(1)}, bf16[64,1024]{1,0:T(8,128)(2,1)S(1)}, u32[]{:S(2)}, u32[]{:S(2)}) collective-permute-start(bf16[64,1024]{1,0:T(8,128)(2,1)S(1)} %collective-permute-done.4.refs_2_), channel_id=1, source_target_pairs={{0,4},{4,0},{8,12},{12,8},{16,20},{20,16},{24,28},{28,24},{1,5},{5... | collective-permute-start | bytes 393224 | tf_op jit(solution)/shard_map/ppermute | solution.py:26
  74.5 30.3 %copy-start.45 = (s32[8]{0:T(128)S(1)}, s32[8]{0:T(128)}, u32[]{:S(2)}) copy-start(s32[8]{0:T(128)} %param.13) | copy-start | bytes 100
  74.5 6.8 %collective-permute-start.22 = (bf16[64,1024]{1,0:T(8,128)(2,1)S(1)}, bf16[64,1024]{1,0:T(8,128)(2,1)S(1)}, u32[]{:S(2)}, u32[]{:S(2)}) collective-permute-start(bf16[64,1024]{1,0:T(8,128)(2,1)S(1)} %shard_map.97), channel_id=1, source_target_pairs={{1,0},{5,4},{9,8},{13,12},{17,16},{21,20},{25,24},{29,28}} | collective-permute-start | bytes 393224 | tf_op jit(solution)/shard_map/ppermute | solution.py:21
  77.2 27.4 %copy-start.34 = (bf16[64,1024]{1,0:T(8,128)(2,1)}, bf16[64,1024]{1,0:T(8,128)(2,1)S(1)}, u32[]{:S(2)}) copy-start(bf16[64,1024]{1,0:T(8,128)(2,1)S(1)} %collective-permute-done.18.refs_14_) | copy-start | bytes 393220
  77.3 7.6 %collective-permute-start.33 = (bf16[64,2048]{1,0:T(8,128)(2,1)S(1)}, bf16[64,2048]{1,0:T(8,128)(2,1)S(1)}, u32[]{:S(2)}, u32[]{:S(2)}) collective-permute-start(bf16[64,2048]{1,0:T(8,128)(2,1)S(1)} %shard_map.102.refs_8_), channel_id=1, source_target_pairs={{0,8},{4,12},{8,0},{12,4},{16,24},{20,28},{24,16},{28,20},{1,9},{5... | collective-permute-start | bytes 786440 | tf_op jit(solution)/shard_map/ppermute | solution.py:26
  78.5 26.1 %copy-start.36 = (bf16[64,1024]{1,0:T(8,128)(2,1)}, bf16[64,1024]{1,0:T(8,128)(2,1)S(1)}, u32[]{:S(2)}) copy-start(bf16[64,1024]{1,0:T(8,128)(2,1)S(1)} %collective-permute-done.19.refs_15_) | copy-start | bytes 393220
  78.5 7.6 %collective-permute-start.34 = (bf16[64,2048]{1,0:T(8,128)(2,1)S(1)}, bf16[64,2048]{1,0:T(8,128)(2,1)S(1)}, u32[]{:S(2)}, u32[]{:S(2)}) collective-permute-start(bf16[64,2048]{1,0:T(8,128)(2,1)S(1)} %shard_map.102.refs_8_), channel_id=1, source_target_pairs={{0,16},{4,20},{8,24},{12,28},{16,0},{20,4},{24,8},{28,12},{1,17},{... | collective-permute-start | bytes 786440 | tf_op jit(solution)/shard_map/ppermute | solution.py:26
  79.8 24.9 %copy-start.38 = (bf16[64,1024]{1,0:T(8,128)(2,1)}, bf16[64,1024]{1,0:T(8,128)(2,1)S(1)}, u32[]{:S(2)}) copy-start(bf16[64,1024]{1,0:T(8,128)(2,1)S(1)} %collective-permute-done.7.refs_5_) | copy-start | bytes 393220
  79.8 11.6 %collective-permute-start.35 = (bf16[64,2048]{1,0:T(8,128)(2,1)S(1)}, bf16[64,2048]{1,0:T(8,128)(2,1)S(1)}, u32[]{:S(2)}, u32[]{:S(2)}) collective-permute-start(bf16[64,2048]{1,0:T(8,128)(2,1)S(1)} %shard_map.102.refs_8_), channel_id=1, source_target_pairs={{0,24},{4,28},{8,16},{12,20},{16,8},{20,12},{24,0},{28,4},{1,25},{... | collective-permute-start | bytes 786440 | tf_op jit(solution)/shard_map/ppermute | solution.py:26
  80.0 24.7 %copy-start.40 = (bf16[64,1024]{1,0:T(8,128)(2,1)}, bf16[64,1024]{1,0:T(8,128)(2,1)S(1)}, u32[]{:S(2)}) copy-start(bf16[64,1024]{1,0:T(8,128)(2,1)S(1)} %collective-permute-done.8.refs_6_) | copy-start | bytes 393220
  80.0 14.1 %collective-permute-start.36 = (bf16[64,2048]{1,0:T(8,128)(2,1)S(1)}, bf16[64,2048]{1,0:T(8,128)(2,1)S(1)}, u32[]{:S(2)}, u32[]{:S(2)}) collective-permute-start(bf16[64,2048]{1,0:T(8,128)(2,1)S(1)} %shard_map.102.refs_8_), channel_id=1, source_target_pairs={{0,4},{4,0},{8,12},{12,8},{16,20},{20,16},{24,28},{28,24},{1,5},{5... | collective-permute-start | bytes 786440 | tf_op jit(solution)/shard_map/ppermute | solution.py:26
  81.3 1.7 %collective-permute-start.9 = (bf16[64,1024]{1,0:T(8,128)(2,1)S(1)}, bf16[64,1024]{1,0:T(8,128)(2,1)S(1)}, u32[]{:S(2)}, u32[]{:S(2)}) collective-permute-start(bf16[64,1024]{1,0:T(8,128)(2,1)S(1)} %collective-permute-done.5.refs_3_), channel_id=1, source_target_pairs={{0,4},{4,0},{8,12},{12,8},{16,20},{20,16},{24,28},{28,24},{1,5},{5... | collective-permute-start | bytes 393224 | tf_op jit(solution)/shard_map/ppermute | solution.py:26
  83.6 12.4 %collective-permute-start.23 = (bf16[64,2048]{1,0:T(8,128)(2,1)S(1)}, bf16[64,2048]{1,0:T(8,128)(2,1)S(1)}, u32[]{:S(2)}, u32[]{:S(2)}) collective-permute-start(bf16[64,2048]{1,0:T(8,128)(2,1)S(1)} %shard_map.98.refs_0_), channel_id=1, source_target_pairs={{0,8},{4,12},{8,0},{12,4},{16,24},{20,28},{24,16},{28,20},{1,9},{5... | collective-permute-start | bytes 786440 | tf_op jit(solution)/shard_map/ppermute | solution.py:26
  84.8 14.0 %collective-permute-start.24 = (bf16[64,2048]{1,0:T(8,128)(2,1)S(1)}, bf16[64,2048]{1,0:T(8,128)(2,1)S(1)}, u32[]{:S(2)}, u32[]{:S(2)}) collective-permute-start(bf16[64,2048]{1,0:T(8,128)(2,1)S(1)} %shard_map.98.refs_0_), channel_id=1, source_target_pairs={{0,16},{4,20},{8,24},{12,28},{16,0},{20,4},{24,8},{28,12},{1,17},{... | collective-permute-start | bytes 786440 | tf_op jit(solution)/shard_map/ppermute | solution.py:26
  86.1 18.0 %collective-permute-start.25 = (bf16[64,2048]{1,0:T(8,128)(2,1)S(1)}, bf16[64,2048]{1,0:T(8,128)(2,1)S(1)}, u32[]{:S(2)}, u32[]{:S(2)}) collective-permute-start(bf16[64,2048]{1,0:T(8,128)(2,1)S(1)} %shard_map.98.refs_0_), channel_id=1, source_target_pairs={{0,24},{4,28},{8,16},{12,20},{16,8},{20,12},{24,0},{28,4},{1,25},{... | collective-permute-start | bytes 786440 | tf_op jit(solution)/shard_map/ppermute | solution.py:26
  91.4 12.7 %collective-permute-start.26 = (bf16[64,2048]{1,0:T(8,128)(2,1)S(1)}, bf16[64,2048]{1,0:T(8,128)(2,1)S(1)}, u32[]{:S(2)}, u32[]{:S(2)}) collective-permute-start(bf16[64,2048]{1,0:T(8,128)(2,1)S(1)} %shard_map.98.refs_0_), channel_id=1, source_target_pairs={{0,4},{4,0},{8,12},{12,8},{16,20},{20,16},{24,28},{28,24},{1,5},{5... | collective-permute-start | bytes 786440 | tf_op jit(solution)/shard_map/ppermute | solution.py:26
  94.1 10.5 %collective-permute-start.37 = (bf16[64,2048]{1,0:T(8,128)(2,1)S(1)}, bf16[64,2048]{1,0:T(8,128)(2,1)S(1)}, u32[]{:S(2)}, u32[]{:S(2)}) collective-permute-start(bf16[64,2048]{1,0:T(8,128)(2,1)S(1)} %collective-permute-done.33.refs_9_), channel_id=1, source_target_pairs={{0,4},{4,0},{8,12},{12,8},{16,20},{20,16},{24,28},{28,24},{1,5},{5... | collective-permute-start | bytes 786440 | tf_op jit(solution)/shard_map/ppermute | solution.py:26
  96.0 25.2 %collective-permute-start.38 = (bf16[64,2048]{1,0:T(8,128)(2,1)S(1)}, bf16[64,2048]{1,0:T(8,128)(2,1)S(1)}, u32[]{:S(2)}, u32[]{:S(2)}) collective-permute-start(bf16[64,2048]{1,0:T(8,128)(2,1)S(1)} %collective-permute-done.34.refs_10_), channel_id=1, source_target_pairs={{0,4},{4,0},{8,12},{12,8},{16,20},{20,16},{24,28},{28,24},{1,5},{5... | collective-permute-start | bytes 786440 | tf_op jit(solution)/shard_map/ppermute | solution.py:26
  98.9 22.4 %collective-permute-start.39 = (bf16[64,2048]{1,0:T(8,128)(2,1)S(1)}, bf16[64,2048]{1,0:T(8,128)(2,1)S(1)}, u32[]{:S(2)}, u32[]{:S(2)}) collective-permute-start(bf16[64,2048]{1,0:T(8,128)(2,1)S(1)} %collective-permute-done.35.refs_11_), channel_id=1, source_target_pairs={{0,4},{4,0},{8,12},{12,8},{16,20},{20,16},{24,28},{28,24},{1,5},{5... | collective-permute-start | bytes 786440 | tf_op jit(solution)/shard_map/ppermute | solution.py:26
  104.1 17.1 %collective-permute-start.27 = (bf16[64,2048]{1,0:T(8,128)(2,1)S(1)}, bf16[64,2048]{1,0:T(8,128)(2,1)}, u32[]{:S(2)}, u32[]{:S(2)}) collective-permute-start(bf16[64,2048]{1,0:T(8,128)(2,1)S(1)} %collective-permute-done.23.refs_1_), channel_id=1, source_target_pairs={{0,4},{4,0},{8,12},{12,8},{16,20},{20,16},{24,28},{28,24},{1,5},{5... | collective-permute-start | bytes 786440 | tf_op jit(solution)/shard_map/ppermute | solution.py:26
  104.1 17.1 %collective-permute-start.28 = (bf16[64,2048]{1,0:T(8,128)(2,1)S(1)}, bf16[64,2048]{1,0:T(8,128)(2,1)}, u32[]{:S(2)}, u32[]{:S(2)}) collective-permute-start(bf16[64,2048]{1,0:T(8,128)(2,1)S(1)} %collective-permute-done.24.refs_2_), channel_id=1, source_target_pairs={{0,4},{4,0},{8,12},{12,8},{16,20},{20,16},{24,28},{28,24},{1,5},{5... | collective-permute-start | bytes 786440 | tf_op jit(solution)/shard_map/ppermute | solution.py:26
  104.7 16.6 %collective-permute-start.29 = (bf16[64,2048]{1,0:T(8,128)(2,1)S(1)}, bf16[64,2048]{1,0:T(8,128)(2,1)}, u32[]{:S(2)}, u32[]{:S(2)}) collective-permute-start(bf16[64,2048]{1,0:T(8,128)(2,1)S(1)} %collective-permute-done.25.refs_3_), channel_id=1, source_target_pairs={{0,4},{4,0},{8,12},{12,8},{16,20},{20,16},{24,28},{28,24},{1,5},{5... | collective-permute-start | bytes 786440 | tf_op jit(solution)/shard_map/ppermute | solution.py:26
  (38 other events, 121.4 us)

commit v3 on v2

v3 whole, which is shorter than its diff:
```python
import functools

import jax
import jax.numpy as jnp
from jax import lax
from jax.experimental import pallas as pl
from jax.experimental.pallas import tpu as pltpu
from jax.sharding import PartitionSpec as P

SQRT_HALF = 0.7071067811865476
INV_ROOT_TAU = 0.3989422804014327
F32 = jnp.float32
BF16 = jnp.bfloat16
IN_VMEM = pl.BlockSpec(memory_space=pltpu.VMEM)
IN_SMEM = pl.BlockSpec(memory_space=pltpu.SMEM)
ANYWHERE = pl.BlockSpec(memory_space=pl.ANY)
TILE = 512
MIB = 2**20
ROOM = 24 * MIB


def hop(value, source, steps):
    return lax.ppermute(value, "section", [(source, source + steps)])


def swapped(value, axis, mask):
    count = lax.axis_size(axis)
    return lax.ppermute(value, axis, [(source, source ^ mask) for source in range(count)])


def tiles(width, most=TILE):
    size = min(most, width)
    return [slice(start, min(start + size, width)) for start in range(0, width, size)]


def dot(left, right):
    return jnp.dot(left, right, preferred_element_type=F32)


def dot_tn(left, right):
    return lax.dot_general(left, right, (((0,), (0,)), ((), ())), preferred_element_type=F32)


def normalize(floats, gain_row):
    center = floats - jnp.mean(floats, axis=-1, keepdims=True)
    inv_std = lax.rsqrt(jnp.mean(center * center, axis=-1, keepdims=True) + 1e-06)
    normed = center * inv_std
    return ((normed * gain_row).astype(BF16), normed, inv_std)


def gelu(v):
    return 0.5 * v * (1.0 + lax.erf(v * SQRT_HALF))


def gelu_slope(v):
    return 0.5 * (1.0 + lax.erf(v * SQRT_HALF)) + v * INV_ROOT_TAU * jnp.exp(-0.5 * v * v)


def first_kernel(*refs):
    far, near, (out, acted, arrived) = refs[:6], refs[6:12], refs[12:]
    gain, x_all, weight_in, weight_out, scales, _ = near
    in_tiles, out_tiles = tiles(weight_in.shape[1]), tiles(weight_out.shape[0])
    pairs = [(far[0], gain), (far[1], x_all)]
    pairs += [(far[2].at[0, :, cols], weight_in.at[:, cols]) for cols in in_tiles]
    pairs += [(far[3].at[0, rows, :], weight_out.at[rows, :]) for rows in out_tiles]
    pairs += [(far[4], scales), (far[5], near[5])]
    copies = [
        pltpu.make_async_copy(source, target, arrived.at[index])
        for index, (source, target) in enumerate(pairs)
    ]
    for copy in copies:
        copy.start()
    mine = lax.axis_index("section") == 0
    copies[0].wait()
    copies[1].wait()
    x = x_all[0].astype(F32)
    normed_bf, _, _ = normalize(x, gain[...])
    for copy, cols in zip(copies[2:], in_tiles):
        copy.wait()

        @pl.when(mine)
        def _():
            acted[:, cols] = gelu(dot(normed_bf, weight_in[:, cols])).astype(BF16)

    for copy in copies[2 + len(in_tiles) :]:
        copy.wait()

    @pl.when(mine)
    def _():
        for cols in tiles(x.shape[1]):
            branch = dot(acted[...], weight_out[:, cols])
            out[:, cols] = (x[:, cols] + scales[:, cols] * branch).astype(BF16)


def turn_kernel(weight_in, weight_out, turned_in, turned_out):
    for ref, turned in ((weight_in, turned_in), (weight_out, turned_out)):
        for rows in tiles(ref.shape[0]):
            for cols in tiles(ref.shape[1]):
                turned[cols, rows] = ref[rows, cols].T


def forward_kernel(step, batch, x_ref, gain, weight_in, weight_out, scales, *refs):
    out, acted = refs[-2:]
    @pl.when(lax.axis_index("section") == step)
    def _():
        x = (x_ref[...] if batch is None else x_ref[batch]).astype(F32)
        normed_bf, _, _ = normalize(x, gain[...])
        for cols in tiles(weight_in.shape[1]):
            acted[:, cols] = gelu(dot(normed_bf, weight_in[:, cols])).astype(BF16)
        for cols in tiles(x.shape[1]):
            branch = dot(acted[...], weight_out[:, cols])
            out[:, cols] = (x[:, cols] + scales[:, cols] * branch).astype(BF16)


def choose(whole, batch, place, later, chosen):
    section = lax.axis_index("section")

    @pl.when(section == place)
    def _():
        chosen[...] = whole[batch]

    for index, ref in later:
        @pl.when(section == index)
        def _():
            chosen[...] = ref[...]


def save_kernel(batch, sections, *refs):
    whole, later, refs = refs[0], refs[1:sections], refs[sections:]
    gain, weight_in, normed_bf, normed, inv_std, slope, chosen = refs
    choose(whole, batch, 0, list(enumerate(later, 1)), chosen)
    normed_bf[...], normed[...], inv_std[...] = normalize(chosen[...].astype(F32), gain[...])
    for cols in tiles(weight_in.shape[1]):
        slope[:, cols] = gelu_slope(dot(normed_bf[...], weight_in[:, cols]))


def backward_kernel(
    step, batch, merged, gy_ref, gain, turned_in, turned_out, scales, normed_ref, inv_std, slope, *refs
):
    parts, out, grad_hidden = refs[:merged], refs[-2], refs[-1]
    if merged:
        out, whole = refs[merged], refs[merged + 1]
        height = whole.shape[0] // merged
        for index, part in enumerate(parts):
            whole[index * height : (index + 1) * height, :] = part[...]

    @pl.when(lax.axis_index("section") == step)
    def _():
        cotangent = (gy_ref[...] if batch is None else gy_ref[batch]).astype(F32)
        scaled = (cotangent * scales[...]).astype(BF16)
        for cols in tiles(turned_out.shape[1]):
            grad_act = dot(scaled, turned_out[:, cols])
            grad_hidden[:, cols] = (grad_act * slope[:, cols]).astype(BF16)
        grad_normed = dot(grad_hidden[...], turned_in[...]) * gain[...]
        normed = normed_ref[...]
        mean_one = jnp.mean(grad_normed, axis=-1, keepdims=True)
        mean_two = jnp.mean(grad_normed * normed, axis=-1, keepdims=True)
        out[...] = (
            cotangent + inv_std[...] * (grad_normed - mean_one - normed * mean_two)
        ).astype(BF16)


def pick_kernel(batch, sections, *refs):
    whole, later, chosen = refs[0], refs[1:sections], refs[-1]
    choose(whole, batch, sections - 1, list(enumerate(later)), chosen)


def slopes_kernel(count, batches, *refs):
    blocks, (weight_in, _, rows), slopes = refs[:count], refs[count : count + 3], refs[count + 3 :]
    height = blocks[0].shape[0]
    part = height // batches
    for batch in range(batches):
        for index, block in enumerate(blocks):
            start = (batch * count + index) * part
            rows[start : start + part, :] = block[batch * part : (batch + 1) * part, :]
    for batch, slope in enumerate(slopes):
        size = count * part
        for high in tiles(size, 256):
            mine = rows[batch * size + high.start : batch * size + high.stop, :]
            for cols in tiles(weight_in.shape[1], 256):
                slope[high, cols] = gelu_slope(dot(mine, weight_in[:, cols]))


def hidden_kernel(count, *refs):
    blocks, (scales, turned_out, slope, grad_hidden, scaled) = refs[:count], refs[count:]
    part = blocks[0].shape[0]
    for index, block in enumerate(blocks):
        scaled[index * part : (index + 1) * part, :] = (
            block[...].astype(F32) * scales[...]
        ).astype(BF16)
    for cols in tiles(turned_out.shape[1], 256):
        grad_act = dot(scaled[...], turned_out[:, cols])
        grad_hidden[:, cols] = (grad_act * slope[:, cols]).astype(BF16)


def square_kernel(count, factor, summed, owner_table, *refs):
    blocks, earlier, (total, stage, left) = refs[:count], refs[count:-3], refs[-3:]
    tall, width = stage.shape
    mine = pl.ds(pl.multiple_of(owner_table[lax.axis_index("dp")] * tall, tall), tall)
    pieces = tiles(width)
    copies = [
        pltpu.make_async_copy(stage.at[:, cols], total.at[:, cols], left.at[index])
        for index, cols in enumerate(pieces)
    ]
    own = [block[:, mine].T for block in blocks]
    for copy, cols in zip(copies, pieces):
        value = earlier[0][:, cols] if summed else None
        for mine_turned, block in zip(own, blocks):
            term = dot(mine_turned, block[:, cols])
            value = term if value is None else value + term
        stage[:, cols] = value * factor
        copy.start()
    for copy in copies:
        copy.wait()


def partial_kernel(count, owner_table, *refs):
    blocks, total = refs[:count], refs[-1]
    tall = total.shape[0]
    mine = pl.ds(pl.multiple_of(owner_table[lax.axis_index("dp")] * tall, tall), tall)
    own = [block[:, mine].T for block in blocks]
    for cols in tiles(total.shape[1]):
        value = None
        for mine_turned, block in zip(own, blocks):
            term = dot(mine_turned, block[:, cols])
            value = term if value is None else value + term
        total[:, cols] = value


def pinned(value):
    return pltpu.with_memory_space_constraint(value, pltpu.VMEM)


def shape(dims, dtype=BF16):
    return jax.ShapeDtypeStruct(dims, dtype)


def call(kernel, arrays, outs, scratch=(), flops=0, specs=None, name=None):
    return pl.pallas_call(
        kernel,
        in_specs=specs or [IN_VMEM] * len(arrays),
        out_specs=[IN_VMEM] * len(outs),
        out_shape=outs,
        scratch_shapes=list(scratch),
        compiler_params=pltpu.CompilerParams(vmem_limit_bytes=ROOM),
        cost_estimate=pl.CostEstimate(flops=flops, bytes_accessed=8 * MIB, transcendentals=0),
        name=name,
    )(*arrays)


def owned_square(blocks, owner_table, owners, factor, earlier=None, extra=()):
    width = blocks[0].shape[1]
    tall = width // owners
    depth = sum(block.shape[0] for block in blocks)
    before = [] if earlier is None else [pinned(earlier)]
    count = len(blocks)
    flops = 2 * depth * tall * width
    specs = [IN_SMEM] + [IN_VMEM] * (count + len(before)) + [ANYWHERE] * len(extra)
    arrays = [owner_table, *[pinned(block) for block in blocks], *before, *extra]
    if factor is None:
        return call(
            functools.partial(partial_kernel, count),
            arrays,
            [shape((tall, width), F32)],
            flops=flops,
            specs=specs,
            name="partial",
        )[0]
    return pl.pallas_call(
        functools.partial(square_kernel, count, factor, bool(before)),
        in_specs=specs,
        out_specs=pl.BlockSpec(memory_space=pltpu.HBM),
        out_shape=shape((tall, width), F32),
        scratch_shapes=[
            pltpu.VMEM((tall, width), F32),
            pltpu.SemaphoreType.DMA((len(tiles(width)),)),
        ],
        compiler_params=pltpu.CompilerParams(vmem_limit_bytes=ROOM),
        cost_estimate=pl.CostEstimate(
            flops=flops, bytes_accessed=4 * tall * width, transcendentals=0
        ),
        name="square",
    )(*arrays)


def plain_square(rows, owner_table, owners, total_rows):
    everything = lax.all_gather(rows, "dp", axis=0, tiled=True)
    tall = rows.shape[1] // owners
    start = owner_table[lax.axis_index("dp")] * tall
    own = lax.dynamic_slice_in_dim(everything, start, tall, axis=1)
    return dot_tn(own, everything) / total_rows


def body(inputs, ln_gain, w_in, w_out, layer_scale, out_grad, owner_table):
    sections = lax.axis_size("section")
    owners = lax.axis_size("dp")
    batch_count, row_count, width = inputs.shape
    width_hidden = w_in.shape[2]
    total_rows = batch_count * row_count * owners
    batches = range(batch_count)
    product = 2 * row_count * width * width_hidden
    block = shape((row_count, width))
    wide = pltpu.VMEM((row_count, width_hidden), BF16)
    flat = pltpu.VMEM((row_count, width), BF16)
    far = [ln_gain, inputs, w_in, w_out, layer_scale, out_grad]
    sizes = [ln_gain.shape, inputs.shape, w_in.shape[1:], w_out.shape[1:], ln_gain.shape, inputs.shape]
    *near, output = call(
        first_kernel,
        [pltpu.with_memory_space_constraint(value, pltpu.HBM) for value in far],
        [pltpu.VMEM(size, value.dtype) for size, value in zip(sizes, far)] + [block],
        [wide, pltpu.SemaphoreType.DMA((4 + 2 * len(tiles(width_hidden)),))],
        2 * product,
        [pl.BlockSpec(memory_space=pltpu.HBM)] * len(far),
        "first",
    )
    paired = owners in (2, 4, 8) and not (width // owners % 128 or width_hidden // owners % 128)
    masks = range(2, owners, 2)
    gain, given, weight_in, weight_out, scales, asked = [pinned(value) for value in near]
    arrived, after = [[] for m in batches], []
    for step in range(sections - 1):
        for m in batches:
            if step or m:
                (output,) = call(
                    functools.partial(forward_kernel, step, None if step else m),
                    [arrived[m][-1] if step else given, gain, weight_in, weight_out, scales, *after],
                    [block],
                    [wide],
                    2 * product,
                    [IN_VMEM] * 5 + [ANYWHERE] * len(after),
                    "forward",
                )
            arrived[m].append(pinned(hop(output, step, 1)))
        if step == 0:
            turned_in, turned_out = call(
                turn_kernel,
                [weight_in, weight_out],
                [pltpu.VMEM((width_hidden, width), BF16), pltpu.VMEM((width, width_hidden), BF16)],
                name="turn",
            )
            turned_in, turned_out = pinned(turned_in), pinned(turned_out)
            after = [turned_in]

    saved, returned, gathered = [], [[] for m in batches], None
    for step in range(sections - 1, 0, -1):
        for m in batches:
            if len(saved) <= m:
                values = call(
                    functools.partial(save_kernel, m, sections),
                    [given, *arrived[m], gain, weight_in],
                    [
                        block,
                        shape((row_count, width), F32),
                        shape((row_count, 1), F32),
                        shape((row_count, width_hidden), F32),
                    ],
                    [flat],
                    product,
                    name="save",
                )
                saved.append([pinned(value) for value in values])
            merge = [saved[n][0] for n in batches] if step == sections - 1 and m == batches[-1] else []
            outs = [block] + ([shape((batch_count * row_count, width))] if merge else [])
            grad_input, *rest = call(
                functools.partial(
                    backward_kernel, step, m if step == sections - 1 else None, len(merge)
                ),
                [
                    asked if step == sections - 1 else returned[m][0],
                    gain, turned_in, turned_out, scales, *saved[m][1:], *merge,
                ],
                outs,
                [wide],
                2 * product,
                name="backward",
            )
            returned[m].insert(0, pinned(hop(grad_input, step, -1)))
        if rest:
            merged = rest[0]
        if rest and paired:
            gathered = [merged] + [swapped(merged, "dp", mask) for mask in masks]
        if paired and step == max(sections - 2, 1):
            count = len(gathered)
            rows, *slopes = call(
                functools.partial(slopes_kernel, count, batch_count),
                [*[pinned(x) for x in gathered], weight_in, grad_input],
                [shape((count * batch_count * row_count, width))]
                + [shape((count * row_count, width_hidden), F32)] * batch_count,
                flops=product * count * batch_count,
                specs=[IN_VMEM] * (count + 1) + [ANYWHERE],
                name="slopes",
            )
            act_blocks = [rows, swapped(rows, "dp", 1)]

    cotangents = [
        call(
            functools.partial(pick_kernel, m, sections),
            [asked, *returned[m], *([pinned(slopes[m])] if paired else [])],
            [block],
            specs=[IN_VMEM] * sections + [ANYWHERE] * paired,
            name="pick",
        )[0]
        for m in batches
    ]
    hidden_blocks = []
    for m in batches:
        near = [cotangents[m]] + [swapped(cotangents[m], "dp", mask) for mask in masks if paired]
        count = len(near)
        (grad_hidden,) = call(
            functools.partial(hidden_kernel, count),
            [*[pinned(x) for x in near], scales, turned_out, pinned(slopes[m]) if paired else saved[m][3]],
            [shape((count * row_count, width_hidden))],
            [pltpu.VMEM((count * row_count, width), BF16)],
            product * count,
            name="hidden",
        )
        hidden_blocks += [grad_hidden] + ([swapped(grad_hidden, "dp", 1)] if paired else [])
    if not paired:
        grad_rows = jnp.concatenate(hidden_blocks, axis=0)
        return (
            plain_square(merged, owner_table, owners, total_rows)[None],
            plain_square(grad_rows, owner_table, owners, total_rows)[None],
        )
    factor = 1.0 / total_rows
    act_share = owned_square(act_blocks, owner_table, owners, factor, extra=hidden_blocks[:1])
    earlier = owned_square(hidden_blocks[:-1], owner_table, owners, None)
    grad_share = owned_square(hidden_blocks[-1:], owner_table, owners, factor, earlier)
    return (act_share[None], grad_share[None])


def solution(mesh):
    placed = (
        P(None, "dp", None),
        P("section", None),
        P("section", None, None),
        P("section", None, None),
        P("section", None),
        P(None, "dp", None),
        P(),
    )
    return jax.shard_map(
        body,
        mesh=mesh,
        in_specs=placed,
        out_specs=(P("section", "dp", None), P("section", "dp", None)),
        check_vma=False,
    )
```

time: 127 us -> 73.7 us (0.58)
  local copies, waits for them, and re-layouts: 35.7 us -> 0.01 us
  starting transfers between devices: 47.3 us -> 30.5 us
  waiting for transfers between devices: 20.3 us -> 14.4 us
  Pallas kernels: 22 us -> 27.3 us
    unnamed x92 -> x2, local copies, waits for them, and re-layouts: 34 us -> 0.01 us
    ppermute x28 -> x12, starting transfers between devices: 33.7 us -> 17.5 us  [swapped(): lax.ppermute(value, axis, [(source, source ^ mask) for source in range(co...]
    ppermute x28 -> x12, waiting for transfers between devices: 6.83 us -> 0.1 us  [swapped(): lax.ppermute(value, axis, [(source, source ^ mask) for source in range(co...]
    pallas_call x18 -> x23, Pallas kernels: 22 us -> 27.3 us  [the longest x21 23.4 us: call(): pl.pallas_call(kernel, in_specs=specs or [IN_VMEM] * len(arrays), out_spe...]
  transfers between devices with their start and end apart: 40 -> 24, of which waited for: 6 -> 5; matrix products, arithmetic and copies ran while one was open for 0% -> 0% of each run, Pallas kernels for 13% -> 29%
where the time goes in v3:
time: 73.7 us; the launch traced here: 73.4 us
  starting transfers between devices  30.5 us (41%)
  Pallas kernels  27.3 us (37%)
  waiting for transfers between devices  14.4 us (20%)
  between operations  1.2 us (2%)
    pallas_call x21, Pallas kernels, call(): pl.pallas_call(kernel, in_specs=specs or [IN_VMEM] * len(arrays), out_spe...  23.4 us
    ppermute x12, starting transfers between devices, swapped(): lax.ppermute(value, axis, [(source, source ^ mask) for source in range(co...  17.5 us
    ppermute x12, waiting for transfers between devices, hop(): return lax.ppermute(value, 'section', [(source, source + steps)])  14.3 us
    ppermute x12, starting transfers between devices, hop(): return lax.ppermute(value, 'section', [(source, source + steps)])  13 us
    pallas_call x2, Pallas kernels, owned_square(): pl.pallas_call(functools.partial(square_kernel, count, factor, bool(befor...  3.92 us
  transfers between devices with their start and end apart: 24, of which 5 were waited for; matrix products, arithmetic and copies ran while one was open for 0% of the time, Pallas kernels for 29%

profile of v3, /device:TPU:9, one launch (start us, length us, event | category | flops | bytes accessed | tf_op | source)
XLA Modules:
  0.0 73.4 jit_solution(2430618371903425858)
XLA Ops:
  0.6 3.7 %first.1 = (f32[1,1024]{1,0:T(1,128)S(1)}, bf16[2,64,1024]{2,1,0:T(8,128)(2,1)S(1)}, bf16[1024,2048]{1,0:T(8,128)(2,1)S(1)}, bf16[2048,1024]{1,0:T(8,128)(2,1)S(...) custom-call(f32[1,1024]{1,0:T(1,128)} %refs_0_.1, ...), custom_call_target="tpu_custom_call" | custom-call | flops 536870912 | bytes 8388608 | tf_op jit(solution)/shard_map/first/pallas_call | solution.py:239
  4.3 1.3 %collective-permute-start.3 = (bf16[64,1024]{1,0:T(8,128)(2,1)S(1)}, bf16[64,1024]{1,0:T(8,128)(2,1)S(1)}, u32[]{:S(2)}, u32[]{:S(2)}) collective-permute-start(bf16[64,1024]{1,0:T(8,128)(2,1)S(1)} %get-tuple-element.35), channel_id=1, source_target_pairs={{0,1},{4,5},{8,9},{12,13},{16,17},{20,21},{24,25},{28,29}} | collective-permute-start | bytes 393224 | tf_op jit(solution)/shard_map/ppermute | solution.py:23
  5.6 1.3 %collective-permute-start = (bf16[64,1024]{1,0:T(8,128)(2,1)S(1)}, bf16[64,1024]{1,0:T(8,128)(2,1)S(1)}, u32[]{:S(2)}, u32[]{:S(2)}) collective-permute-start(bf16[64,1024]{1,0:T(8,128)(2,1)S(1)} %forward.5), channel_id=1, source_target_pairs={{0,1},{4,5},{8,9},{12,13},{16,17},{20,21},{24,25},{28,29}} | collective-permute-start | bytes 393224 | tf_op jit(solution)/shard_map/ppermute | solution.py:23
  6.9 2.4 %turn.1 = (bf16[2048,1024]{1,0:T(8,128)(2,1)S(1)}, bf16[1024,2048]{1,0:T(8,128)(2,1)S(1)}) custom-call(bf16[1024,2048]{1,0:T(8,128)(2,1)S(1)} %get-tuple-element.26.weight_in.refs_5_.refs_4_, bf16[2048,1024]{1,0:T(8,128)(2,1)S(1)} %get-tuple-element.27.weight_out), custom_call_target="tpu_custom_call" | custom-call | bytes 8388608 | tf_op jit(solution)/shard_map/turn/pallas_call | solution.py:239
  9.3 1.2 %collective-permute-done.3.x_ref.refs_1_ = bf16[64,1024]{1,0:T(8,128)(2,1)S(1)} collective-permute-done((bf16[64,1024]{1,0:T(8,128)(2,1)S(1)}, bf16[64,1024]{1,0:T(8,128)(2,1)S(1)}, u32[]{:S(2)}, u32[]{:S(2)}) %collective-permute-start.3) | collective-permute-done | bytes 131104 | tf_op jit(solution)/shard_map/ppermute | solution.py:23
  10.6 1.8 %forward.8 = bf16[64,1024]{1,0:T(8,128)(2,1)S(1)} custom-call(bf16[64,1024]{1,0:T(8,128)(2,1)S(1)} %collective-permute-done.3.x_ref.refs_1_, f32[1,1024]{1,0:T(1,128)S(1)} %get-tuple-element.25.gain.refs_4_, bf16[1024,2048]{1,0:T(8,128)(2,1)S(1)} %get-tuple-element.26.weight_in.refs_5_.refs_4_, bf16[2048,1024]{1,0:T(8,128)(2,1)S(1)} %get-tuple-element.27.weight_out, ...), custom_call_target="tpu_custom_call" | custom-call | flops 536870912 | bytes 8388608 | tf_op jit(solution)/shard_map/forward/pallas_call | solution.py:239
  12.3 1.3 %collective-permute-start.4 = (bf16[64,1024]{1,0:T(8,128)(2,1)S(1)}, bf16[64,1024]{1,0:T(8,128)(2,1)S(1)}, u32[]{:S(2)}, u32[]{:S(2)}) collective-permute-start(bf16[64,1024]{1,0:T(8,128)(2,1)S(1)} %forward.8), channel_id=1, source_target_pairs={{1,2},{5,6},{9,10},{13,14},{17,18},{21,22},{25,26},{29,30}} | collective-permute-start | bytes 393224 | tf_op jit(solution)/shard_map/ppermute | solution.py:23
  13.6 0.0 collective-permute-done.x_ref.refs_1_
  13.6 1.8 %forward.6 = bf16[64,1024]{1,0:T(8,128)(2,1)S(1)} custom-call(bf16[64,1024]{1,0:T(8,128)(2,1)S(1)} %collective-permute-done.x_ref.refs_1_, f32[1,1024]{1,0:T(1,128)S(1)} %get-tuple-element.25.gain.refs_4_, bf16[1024,2048]{1,0:T(8,128)(2,1)S(1)} %get-tuple-element.26.weight_in.refs_5_.refs_4_, bf16[2048,1024]{1,0:T(8,128)(2,1)S(1)} %get-tuple-element.27.weight_out, ...), custom_call_target="tpu_custom_call" | custom-call | flops 536870912 | bytes 8388608 | tf_op jit(solution)/shard_map/forward/pallas_call | solution.py:239
  15.4 1.3 %collective-permute-start.1 = (bf16[64,1024]{1,0:T(8,128)(2,1)S(1)}, bf16[64,1024]{1,0:T(8,128)(2,1)S(1)}, u32[]{:S(2)}, u32[]{:S(2)}) collective-permute-start(bf16[64,1024]{1,0:T(8,128)(2,1)S(1)} %forward.6), channel_id=1, source_target_pairs={{1,2},{5,6},{9,10},{13,14},{17,18},{21,22},{25,26},{29,30}} | collective-permute-start | bytes 393224 | tf_op jit(solution)/shard_map/ppermute | solution.py:23
  16.7 0.0 collective-permute-done.4.x_ref.refs_2_
  16.7 0.7 collective-permute-start.5
  17.4 1.2 %collective-permute-done.1.x_ref.refs_2_ = bf16[64,1024]{1,0:T(8,128)(2,1)S(1)} collective-permute-done((bf16[64,1024]{1,0:T(8,128)(2,1)S(1)}, bf16[64,1024]{1,0:T(8,128)(2,1)S(1)}, u32[]{:S(2)}, u32[]{:S(2)}) %collective-permute-start.1) | collective-permute-done | bytes 131104 | tf_op jit(solution)/shard_map/ppermute | solution.py:23
  18.6 0.7 collective-permute-start.2
  19.3 1.1 %save.3 = (bf16[64,1024]{1,0:T(8,128)(2,1)S(1)}, f32[64,1024]{1,0:T(8,128)S(1)}, f32[64,1]{1,0:T(8,128)S(1)}, f32[64,2048]{1,0:T(8,128)S(1)}) custom-call(bf16[2,64,1024]{2,1,0:T(8,128)(2,1)S(1)} %get-tuple-element.31.x_ref.refs_0_, bf16[64,1024]{1,0:T(8,128)(2,1)S(1)} %collective-permute-done.3.x_ref.refs_1_, ...), custom_call_target="tpu_custom_call" | custom-call | flops 268435456 | bytes 8388608 | tf_op jit(solution)/shard_map/save/pallas_call | solution.py:239
  20.5 0.7 collective-permute-start.11
  21.2 1.3 %save.2 = (bf16[64,1024]{1,0:T(8,128)(2,1)S(1)}, f32[64,1024]{1,0:T(8,128)S(1)}, f32[64,1]{1,0:T(8,128)S(1)}, f32[64,2048]{1,0:T(8,128)S(1)}) custom-call(bf16[2,64,1024]{2,1,0:T(8,128)(2,1)S(1)} %get-tuple-element.31.x_ref.refs_0_, bf16[64,1024]{1,0:T(8,128)(2,1)S(1)} %collective-permute-done.x_ref.refs_1_, ...), custom_call_target="tpu_custom_call" | custom-call | flops 268435456 | bytes 8388608 | tf_op jit(solution)/shard_map/save/pallas_call | solution.py:239
  22.5 0.7 collective-permute-start.9
  23.2 2.2 %collective-permute-start.8 = (bf16[128,1024]{1,0:T(8,128)(2,1)S(1)}, bf16[128,1024]{1,0:T(8,128)(2,1)S(1)}, u32[]{:S(2)}, u32[]{:S(2)}) collective-permute-start(bf16[128,1024]{1,0:T(8,128)(2,1)S(1)} %get-tuple-element.38.refs_0_), channel_id=1, source_target_pairs={{0,24},{4,28},{8,16},{12,20},{16,8},{20,12},{24,0},{28,4},{1,25},{... | collective-permute-start | bytes 786440 | tf_op jit(solution)/shard_map/ppermute | solution.py:28
  25.4 0.2 collective-permute-start.7
  25.6 0.3 collective-permute-start.6
  25.9 1.3 %collective-permute-start.12 = (bf16[64,1024]{1,0:T(8,128)(2,1)S(1)}, bf16[64,1024]{1,0:T(8,128)(2,1)S(1)}, u32[]{:S(2)}, u32[]{:S(2)}) collective-permute-start(bf16[64,1024]{1,0:T(8,128)(2,1)S(1)} %backward.9), channel_id=1, source_target_pairs={{2,1},{6,5},{10,9},{14,13},{18,17},{22,21},{26,25},{30,29}} | collective-permute-start | bytes 393224 | tf_op jit(solution)/shard_map/ppermute | solution.py:23
  27.2 0.0 collective-permute-done.9.gy_ref.refs_3_
  27.2 1.3 %collective-permute-start.17 = (bf16[64,1024]{1,0:T(8,128)(2,1)S(1)}, bf16[64,1024]{1,0:T(8,128)(2,1)S(1)}, u32[]{:S(2)}, u32[]{:S(2)}) collective-permute-start(bf16[64,1024]{1,0:T(8,128)(2,1)S(1)} %backward.7.refs_5_), channel_id=1, source_target_pairs={{2,1},{6,5},{10,9},{14,13},{18,17},{22,21},{26,25},{30,29}} | collective-permute-start | bytes 393224 | tf_op jit(solution)/shard_map/ppermute | solution.py:23
  28.5 8.9 %collective-permute-done.12.gy_ref.refs_2_ = bf16[64,1024]{1,0:T(8,128)(2,1)S(1)} collective-permute-done((bf16[64,1024]{1,0:T(8,128)(2,1)S(1)}, bf16[64,1024]{1,0:T(8,128)(2,1)S(1)}, u32[]{:S(2)}, u32[]{:S(2)}) %collective-permute-start.12) | collective-permute-done | bytes 131104 | tf_op jit(solution)/shard_map/ppermute | solution.py:23
  37.4 1.7 %backward.10 = bf16[64,1024]{1,0:T(8,128)(2,1)S(1)} custom-call(bf16[64,1024]{1,0:T(8,128)(2,1)S(1)} %collective-permute-done.12.gy_ref.refs_2_, f32[1,1024]{1,0:T(1,128)S(1)} %get-tuple-element.25.gain.refs_4_, bf16[2048,1024]{1,0:T(8,128)(2,1)S(1)} %get-tuple-element.28.refs_0_.turned_in, bf16[1024,2048]{1,0:T(8,128)(2,1)S(1)} %get-tuple-element.29.turned_out.refs_5_, ...), custom_call_target="tpu_custom_call" | custom-call | flops 536870912 | bytes 8388608 | tf_op jit(solution)/shard_map/backward/pallas_call | solution.py:239
  39.1 1.3 %collective-permute-start.13 = (bf16[64,1024]{1,0:T(8,128)(2,1)S(1)}, bf16[64,1024]{1,0:T(8,128)(2,1)S(1)}, u32[]{:S(2)}, u32[]{:S(2)}) collective-permute-start(bf16[64,1024]{1,0:T(8,128)(2,1)S(1)} %backward.10), channel_id=1, source_target_pairs={{1,0},{5,4},{9,8},{13,12},{17,16},{21,20},{25,24},{29,28}} | collective-permute-start | bytes 393224 | tf_op jit(solution)/shard_map/ppermute | solution.py:23
  40.4 2.9 %collective-permute-done.17.gy_ref.refs_2_ = bf16[64,1024]{1,0:T(8,128)(2,1)S(1)} collective-permute-done((bf16[64,1024]{1,0:T(8,128)(2,1)S(1)}, bf16[64,1024]{1,0:T(8,128)(2,1)S(1)}, u32[]{:S(2)}, u32[]{:S(2)}) %collective-permute-start.17) | collective-permute-done | bytes 131104 | tf_op jit(solution)/shard_map/ppermute | solution.py:23
  43.4 1.7 %backward.11 = bf16[64,1024]{1,0:T(8,128)(2,1)S(1)} custom-call(bf16[64,1024]{1,0:T(8,128)(2,1)S(1)} %collective-permute-done.17.gy_ref.refs_2_, f32[1,1024]{1,0:T(1,128)S(1)} %get-tuple-element.25.gain.refs_4_, bf16[2048,1024]{1,0:T(8,128)(2,1)S(1)} %get-tuple-element.28.refs_0_.turned_in, bf16[1024,2048]{1,0:T(8,128)(2,1)S(1)} %get-tuple-element.29.turned_out.refs_5_, ...), custom_call_target="tpu_custom_call" | custom-call | flops 536870912 | bytes 8388608 | tf_op jit(solution)/shard_map/backward/pallas_call | solution.py:239
  45.1 1.3 %collective-permute-start.18 = (bf16[64,1024]{1,0:T(8,128)(2,1)S(1)}, bf16[64,1024]{1,0:T(8,128)(2,1)S(1)}, u32[]{:S(2)}, u32[]{:S(2)}) collective-permute-start(bf16[64,1024]{1,0:T(8,128)(2,1)S(1)} %backward.11), channel_id=1, source_target_pairs={{1,0},{5,4},{9,8},{13,12},{17,16},{21,20},{25,24},{29,28}} | collective-permute-start | bytes 393224 | tf_op jit(solution)/shard_map/ppermute | solution.py:23
  46.4 3.4 %slopes.1 = (bf16[512,1024]{1,0:T(8,128)(2,1)S(1)}, f32[256,2048]{1,0:T(8,128)S(1)}, f32[256,2048]{1,0:T(8,128)S(1)}) custom-call(bf16[128,1024]{1,0:T(8,128)(2,1)S(1)} %get-tuple-element.38.refs_0_, bf16[128,1024]{1,0:T(8,128)(2,1)S(1)} %collective-permute-done.6.refs_1_, bf16[128,1024]{1,0:T(8,128)(2,1)S(1)} %collective-permute-done.7.refs_2_, ...), custom_call_target="tpu_custom_call" | custom-call | flops 2147483648 | bytes 8388608 | tf_op jit(solution)/shard_map/slopes/pallas_call | solution.py:239
  49.9 2.3 %collective-permute-start.16 = (bf16[64,1024]{1,0:T(8,128)(2,1)S(1)}, bf16[64,1024]{1,0:T(8,128)(2,1)S(1)}, u32[]{:S(2)}, u32[]{:S(2)}) collective-permute-start(bf16[64,1024]{1,0:T(8,128)(2,1)S(1)} %pick.2.refs_0_), channel_id=1, source_target_pairs={{0,24},{4,28},{8,16},{12,20},{16,8},{20,12},{24,0},{28,4},{1,25},{... | collective-permute-start | bytes 393224 | tf_op jit(solution)/shard_map/ppermute | solution.py:28
  52.2 0.2 collective-permute-start.15
  52.4 0.2 collective-permute-start.14
  52.6 0.2 pick.3.refs_0_
  52.9 2.3 %collective-permute-start.21 = (bf16[64,1024]{1,0:T(8,128)(2,1)S(1)}, bf16[64,1024]{1,0:T(8,128)(2,1)S(1)}, u32[]{:S(2)}, u32[]{:S(2)}) collective-permute-start(bf16[64,1024]{1,0:T(8,128)(2,1)S(1)} %pick.3.refs_0_), channel_id=1, source_target_pairs={{0,24},{4,28},{8,16},{12,20},{16,8},{20,12},{24,0},{28,4},{1,25},{... | collective-permute-start | bytes 393224 | tf_op jit(solution)/shard_map/ppermute | solution.py:28
  55.1 0.2 collective-permute-start.20
  55.3 0.7 collective-permute-start.19
  56.0 0.1 collective-permute-done.15.refs_2_
  56.1 7.4 %collective-permute-start.10 = (bf16[512,1024]{1,0:T(8,128)(2,1)S(1)}, bf16[512,1024]{1,0:T(8,128)(2,1)S(1)}, u32[]{:S(2)}, u32[]{:S(2)}) collective-permute-start(bf16[512,1024]{1,0:T(8,128)(2,1)S(1)} %get-tuple-element.40.refs_0_), channel_id=1, source_target_pairs={{0,4},{4,0},{8,12},{12,8},{16,20},{20,16},{24,28},{28,24},{1,5},{5... | collective-permute-start | bytes 3145736 | tf_op jit(solution)/shard_map/ppermute | solution.py:28
  63.5 1.3 %hidden.2.refs_2_.refs_0_ = bf16[256,2048]{1,0:T(8,128)(2,1)S(1)} custom-call(bf16[64,1024]{1,0:T(8,128)(2,1)S(1)} %pick.2.refs_0_, bf16[64,1024]{1,0:T(8,128)(2,1)S(1)} %collective-permute-done.14.refs_1_, bf16[64,1024]{1,0:T(8,128)(2,1)S(1)} %collective-permute-done.15.refs_2_, bf16[64,1024]{1,0:T(8,128)(2,1)S(1)} %collective-permute-done.16.refs_3_, ...), custom_call_target="tpu_custom_call" | custom-call | flops 1073741824 | bytes 8388608 | tf_op jit(solution)/shard_map/hidden/pallas_call | solution.py:239
  64.8 0.0 copy-start
  64.8 0.1 collective-permute-start.23
  64.9 1.3 %hidden.3.refs_2_ = bf16[256,2048]{1,0:T(8,128)(2,1)S(1)} custom-call(bf16[64,1024]{1,0:T(8,128)(2,1)S(1)} %pick.3.refs_0_, bf16[64,1024]{1,0:T(8,128)(2,1)S(1)} %collective-permute-done.19.refs_1_, bf16[64,1024]{1,0:T(8,128)(2,1)S(1)} %collective-permute-done.20.refs_2_, bf16[64,1024]{1,0:T(8,128)(2,1)S(1)} %collective-permute-done.21.refs_3_, ...), custom_call_target="tpu_custom_call" | custom-call | flops 1073741824 | bytes 8388608 | tf_op jit(solution)/shard_map/hidden/pallas_call | solution.py:239
  66.2 1.5 %collective-permute-start.22 = (bf16[256,2048]{1,0:T(8,128)(2,1)S(1)}, bf16[256,2048]{1,0:T(8,128)(2,1)S(1)}, u32[]{:S(2)}, u32[]{:S(2)}) collective-permute-start(bf16[256,2048]{1,0:T(8,128)(2,1)S(1)} %hidden.3.refs_2_), channel_id=1, source_target_pairs={{0,4},{4,0},{8,12},{12,8},{16,20},{20,16},{24,28},{28,24},{1,5},{5... | collective-permute-start | bytes 3145736 | tf_op jit(solution)/shard_map/ppermute | solution.py:28
  67.7 1.8 %square.2 = f32[128,1024]{1,0:T(8,128)} custom-call(s32[8]{0:T(128)S(1)} %copy-done, bf16[512,1024]{1,0:T(8,128)(2,1)S(1)} %get-tuple-element.40.refs_0_, bf16[512,1024]{1,0:T(8,128)(2,1)S(1)} %collective-permute-done.10.refs_1_, bf16[256,2048]{1,0:T(8,128)(2,1)S(1)} %hidden.2.refs_2_.refs_0_), custom_call_target="tpu_custom_call" | custom-call | flops 268435456 | bytes 524288 | tf_op jit(solution)/shard_map/square/pallas_call | solution.py:269
  69.5 1.6 %partial.1.refs_1_ = f32[256,2048]{1,0:T(8,128)S(1)} custom-call(s32[8]{0:T(128)S(1)} %copy-done, bf16[256,2048]{1,0:T(8,128)(2,1)S(1)} %hidden.2.refs_2_.refs_0_, bf16[256,2048]{1,0:T(8,128)(2,1)S(1)} %collective-permute-done.23.refs_1_, bf16[256,2048]{1,0:T(8,128)(2,1)S(1)} %hidden.3.refs_2_), custom_call_target="tpu_custom_call" | custom-call | flops 805306368 | bytes 8388608 | tf_op jit(solution)/shard_map/partial/pallas_call | solution.py:239
  71.0 2.2 %square.3 = f32[256,2048]{1,0:T(8,128)} custom-call(s32[8]{0:T(128)S(1)} %copy-done, bf16[256,2048]{1,0:T(8,128)(2,1)S(1)} %collective-permute-done.22.refs_0_, f32[256,2048]{1,0:T(8,128)S(1)} %partial.1.refs_1_), custom_call_target="tpu_custom_call" | custom-call | flops 268435456 | bytes 2097152 | tf_op jit(solution)/shard_map/square/pallas_call | solution.py:269
  (25 shorter events, 0.2 us)
Async XLA Ops:
  4.3 6.3 %collective-permute-start.3 = (bf16[64,1024]{1,0:T(8,128)(2,1)S(1)}, bf16[64,1024]{1,0:T(8,128)(2,1)S(1)}, u32[]{:S(2)}, u32[]{:S(2)}) collective-permute-start(bf16[64,1024]{1,0:T(8,128)(2,1)S(1)} %get-tuple-element.35), channel_id=1, source_target_pairs={{0,1},{4,5},{8,9},{12,13},{16,17},{20,21},{24,25},{28,29}} | collective-permute-start | bytes 393224 | tf_op jit(solution)/shard_map/ppermute | solution.py:23
  5.6 8.0 %collective-permute-start = (bf16[64,1024]{1,0:T(8,128)(2,1)S(1)}, bf16[64,1024]{1,0:T(8,128)(2,1)S(1)}, u32[]{:S(2)}, u32[]{:S(2)}) collective-permute-start(bf16[64,1024]{1,0:T(8,128)(2,1)S(1)} %forward.5), channel_id=1, source_target_pairs={{0,1},{4,5},{8,9},{12,13},{16,17},{20,21},{24,25},{28,29}} | collective-permute-start | bytes 393224 | tf_op jit(solution)/shard_map/ppermute | solution.py:23
  12.3 4.4 %collective-permute-start.4 = (bf16[64,1024]{1,0:T(8,128)(2,1)S(1)}, bf16[64,1024]{1,0:T(8,128)(2,1)S(1)}, u32[]{:S(2)}, u32[]{:S(2)}) collective-permute-start(bf16[64,1024]{1,0:T(8,128)(2,1)S(1)} %forward.8), channel_id=1, source_target_pairs={{1,2},{5,6},{9,10},{13,14},{17,18},{21,22},{25,26},{29,30}} | collective-permute-start | bytes 393224 | tf_op jit(solution)/shard_map/ppermute | solution.py:23
  15.4 3.2 %collective-permute-start.1 = (bf16[64,1024]{1,0:T(8,128)(2,1)S(1)}, bf16[64,1024]{1,0:T(8,128)(2,1)S(1)}, u32[]{:S(2)}, u32[]{:S(2)}) collective-permute-start(bf16[64,1024]{1,0:T(8,128)(2,1)S(1)} %forward.6), channel_id=1, source_target_pairs={{1,2},{5,6},{9,10},{13,14},{17,18},{21,22},{25,26},{29,30}} | collective-permute-start | bytes 393224 | tf_op jit(solution)/shard_map/ppermute | solution.py:23
  16.7 2.6 %collective-permute-start.5 = (bf16[64,1024]{1,0:T(8,128)(2,1)S(1)}, bf16[64,1024]{1,0:T(8,128)(2,1)S(1)}, u32[]{:S(2)}, u32[]{:S(2)}) collective-permute-start(bf16[64,1024]{1,0:T(8,128)(2,1)S(1)} %forward.9), channel_id=1, source_target_pairs={{2,3},{6,7},{10,11},{14,15},{18,19},{22,23},{26,27},{30,31}} | collective-permute-start | bytes 393224 | tf_op jit(solution)/shard_map/ppermute | solution.py:23
  18.6 2.5 %collective-permute-start.2 = (bf16[64,1024]{1,0:T(8,128)(2,1)S(1)}, bf16[64,1024]{1,0:T(8,128)(2,1)S(1)}, u32[]{:S(2)}, u32[]{:S(2)}) collective-permute-start(bf16[64,1024]{1,0:T(8,128)(2,1)S(1)} %forward.7), channel_id=1, source_target_pairs={{2,3},{6,7},{10,11},{14,15},{18,19},{22,23},{26,27},{30,31}} | collective-permute-start | bytes 393224 | tf_op jit(solution)/shard_map/ppermute | solution.py:23
  20.5 5.4 %collective-permute-start.11 = (bf16[64,1024]{1,0:T(8,128)(2,1)S(1)}, bf16[64,1024]{1,0:T(8,128)(2,1)S(1)}, u32[]{:S(2)}, u32[]{:S(2)}) collective-permute-start(bf16[64,1024]{1,0:T(8,128)(2,1)S(1)} %backward.8), channel_id=1, source_target_pairs={{3,2},{7,6},{11,10},{15,14},{19,18},{23,22},{27,26},{31,30}} | collective-permute-start | bytes 393224 | tf_op jit(solution)/shard_map/ppermute | solution.py:23
  22.5 4.7 %collective-permute-start.9 = (bf16[64,1024]{1,0:T(8,128)(2,1)S(1)}, bf16[64,1024]{1,0:T(8,128)(2,1)S(1)}, u32[]{:S(2)}, u32[]{:S(2)}) collective-permute-start(bf16[64,1024]{1,0:T(8,128)(2,1)S(1)} %get-tuple-element.39), channel_id=1, source_target_pairs={{3,2},{7,6},{11,10},{15,14},{19,18},{23,22},{27,26},{31,30}} | collective-permute-start | bytes 393224 | tf_op jit(solution)/shard_map/ppermute | solution.py:23
  23.2 23.2 %collective-permute-start.8 = (bf16[128,1024]{1,0:T(8,128)(2,1)S(1)}, bf16[128,1024]{1,0:T(8,128)(2,1)S(1)}, u32[]{:S(2)}, u32[]{:S(2)}) collective-permute-start(bf16[128,1024]{1,0:T(8,128)(2,1)S(1)} %get-tuple-element.38.refs_0_), channel_id=1, source_target_pairs={{0,24},{4,28},{8,16},{12,20},{16,8},{20,12},{24,0},{28,4},{1,25},{... | collective-permute-start | bytes 786440 | tf_op jit(solution)/shard_map/ppermute | solution.py:28
  25.4 21.0 %collective-permute-start.7 = (bf16[128,1024]{1,0:T(8,128)(2,1)S(1)}, bf16[128,1024]{1,0:T(8,128)(2,1)S(1)}, u32[]{:S(2)}, u32[]{:S(2)}) collective-permute-start(bf16[128,1024]{1,0:T(8,128)(2,1)S(1)} %get-tuple-element.38.refs_0_), channel_id=1, source_target_pairs={{0,16},{4,20},{8,24},{12,28},{16,0},{20,4},{24,8},{28,12},{1,17},{... | collective-permute-start | bytes 786440 | tf_op jit(solution)/shard_map/ppermute | solution.py:28
  25.6 20.8 %collective-permute-start.6 = (bf16[128,1024]{1,0:T(8,128)(2,1)S(1)}, bf16[128,1024]{1,0:T(8,128)(2,1)S(1)}, u32[]{:S(2)}, u32[]{:S(2)}) collective-permute-start(bf16[128,1024]{1,0:T(8,128)(2,1)S(1)} %get-tuple-element.38.refs_0_), channel_id=1, source_target_pairs={{0,8},{4,12},{8,0},{12,4},{16,24},{20,28},{24,16},{28,20},{1,9},{5... | collective-permute-start | bytes 786440 | tf_op jit(solution)/shard_map/ppermute | solution.py:28
  25.9 11.5 %collective-permute-start.12 = (bf16[64,1024]{1,0:T(8,128)(2,1)S(1)}, bf16[64,1024]{1,0:T(8,128)(2,1)S(1)}, u32[]{:S(2)}, u32[]{:S(2)}) collective-permute-start(bf16[64,1024]{1,0:T(8,128)(2,1)S(1)} %backward.9), channel_id=1, source_target_pairs={{2,1},{6,5},{10,9},{14,13},{18,17},{22,21},{26,25},{30,29}} | collective-permute-start | bytes 393224 | tf_op jit(solution)/shard_map/ppermute | solution.py:23
  27.2 16.1 %collective-permute-start.17 = (bf16[64,1024]{1,0:T(8,128)(2,1)S(1)}, bf16[64,1024]{1,0:T(8,128)(2,1)S(1)}, u32[]{:S(2)}, u32[]{:S(2)}) collective-permute-start(bf16[64,1024]{1,0:T(8,128)(2,1)S(1)} %backward.7.refs_5_), channel_id=1, source_target_pairs={{2,1},{6,5},{10,9},{14,13},{18,17},{22,21},{26,25},{30,29}} | collective-permute-start | bytes 393224 | tf_op jit(solution)/shard_map/ppermute | solution.py:23
  39.1 10.7 %collective-permute-start.13 = (bf16[64,1024]{1,0:T(8,128)(2,1)S(1)}, bf16[64,1024]{1,0:T(8,128)(2,1)S(1)}, u32[]{:S(2)}, u32[]{:S(2)}) collective-permute-start(bf16[64,1024]{1,0:T(8,128)(2,1)S(1)} %backward.10), channel_id=1, source_target_pairs={{1,0},{5,4},{9,8},{13,12},{17,16},{21,20},{25,24},{29,28}} | collective-permute-start | bytes 393224 | tf_op jit(solution)/shard_map/ppermute | solution.py:23
  45.1 7.5 %collective-permute-start.18 = (bf16[64,1024]{1,0:T(8,128)(2,1)S(1)}, bf16[64,1024]{1,0:T(8,128)(2,1)S(1)}, u32[]{:S(2)}, u32[]{:S(2)}) collective-permute-start(bf16[64,1024]{1,0:T(8,128)(2,1)S(1)} %backward.11), channel_id=1, source_target_pairs={{1,0},{5,4},{9,8},{13,12},{17,16},{21,20},{25,24},{29,28}} | collective-permute-start | bytes 393224 | tf_op jit(solution)/shard_map/ppermute | solution.py:23
  49.9 5.4 %collective-permute-start.16 = (bf16[64,1024]{1,0:T(8,128)(2,1)S(1)}, bf16[64,1024]{1,0:T(8,128)(2,1)S(1)}, u32[]{:S(2)}, u32[]{:S(2)}) collective-permute-start(bf16[64,1024]{1,0:T(8,128)(2,1)S(1)} %pick.2.refs_0_), channel_id=1, source_target_pairs={{0,24},{4,28},{8,16},{12,20},{16,8},{20,12},{24,0},{28,4},{1,25},{... | collective-permute-start | bytes 393224 | tf_op jit(solution)/shard_map/ppermute | solution.py:28
  52.2 3.9 %collective-permute-start.15 = (bf16[64,1024]{1,0:T(8,128)(2,1)S(1)}, bf16[64,1024]{1,0:T(8,128)(2,1)S(1)}, u32[]{:S(2)}, u32[]{:S(2)}) collective-permute-start(bf16[64,1024]{1,0:T(8,128)(2,1)S(1)} %pick.2.refs_0_), channel_id=1, source_target_pairs={{0,16},{4,20},{8,24},{12,28},{16,0},{20,4},{24,8},{28,12},{1,17},{... | collective-permute-start | bytes 393224 | tf_op jit(solution)/shard_map/ppermute | solution.py:28
  52.4 11.1 %collective-permute-start.14 = (bf16[64,1024]{1,0:T(8,128)(2,1)S(1)}, bf16[64,1024]{1,0:T(8,128)(2,1)S(1)}, u32[]{:S(2)}, u32[]{:S(2)}) collective-permute-start(bf16[64,1024]{1,0:T(8,128)(2,1)S(1)} %pick.2.refs_0_), channel_id=1, source_target_pairs={{0,8},{4,12},{8,0},{12,4},{16,24},{20,28},{24,16},{28,20},{1,9},{5... | collective-permute-start | bytes 393224 | tf_op jit(solution)/shard_map/ppermute | solution.py:28
  52.9 12.0 %collective-permute-start.21 = (bf16[64,1024]{1,0:T(8,128)(2,1)S(1)}, bf16[64,1024]{1,0:T(8,128)(2,1)S(1)}, u32[]{:S(2)}, u32[]{:S(2)}) collective-permute-start(bf16[64,1024]{1,0:T(8,128)(2,1)S(1)} %pick.3.refs_0_), channel_id=1, source_target_pairs={{0,24},{4,28},{8,16},{12,20},{16,8},{20,12},{24,0},{28,4},{1,25},{... | collective-permute-start | bytes 393224 | tf_op jit(solution)/shard_map/ppermute | solution.py:28
  55.1 9.8 %collective-permute-start.20 = (bf16[64,1024]{1,0:T(8,128)(2,1)S(1)}, bf16[64,1024]{1,0:T(8,128)(2,1)S(1)}, u32[]{:S(2)}, u32[]{:S(2)}) collective-permute-start(bf16[64,1024]{1,0:T(8,128)(2,1)S(1)} %pick.3.refs_0_), channel_id=1, source_target_pairs={{0,16},{4,20},{8,24},{12,28},{16,0},{20,4},{24,8},{28,12},{1,17},{... | collective-permute-start | bytes 393224 | tf_op jit(solution)/shard_map/ppermute | solution.py:28
  55.3 9.5 %collective-permute-start.19 = (bf16[64,1024]{1,0:T(8,128)(2,1)S(1)}, bf16[64,1024]{1,0:T(8,128)(2,1)S(1)}, u32[]{:S(2)}, u32[]{:S(2)}) collective-permute-start(bf16[64,1024]{1,0:T(8,128)(2,1)S(1)} %pick.3.refs_0_), channel_id=1, source_target_pairs={{0,8},{4,12},{8,0},{12,4},{16,24},{20,28},{24,16},{28,20},{1,9},{5... | collective-permute-start | bytes 393224 | tf_op jit(solution)/shard_map/ppermute | solution.py:28
  56.1 11.6 %collective-permute-start.10 = (bf16[512,1024]{1,0:T(8,128)(2,1)S(1)}, bf16[512,1024]{1,0:T(8,128)(2,1)S(1)}, u32[]{:S(2)}, u32[]{:S(2)}) collective-permute-start(bf16[512,1024]{1,0:T(8,128)(2,1)S(1)} %get-tuple-element.40.refs_0_), channel_id=1, source_target_pairs={{0,4},{4,0},{8,12},{12,8},{16,20},{20,16},{24,28},{28,24},{1,5},{5... | collective-permute-start | bytes 3145736 | tf_op jit(solution)/shard_map/ppermute | solution.py:28
  64.8 2.9 %copy-start = (s32[8]{0:T(128)S(1)}, s32[8]{0:T(128)}, u32[]{:S(2)}) copy-start(s32[8]{0:T(128)} %owner_table.5) | copy-start | bytes 100
  64.8 4.7 %collective-permute-start.23 = (bf16[256,2048]{1,0:T(8,128)(2,1)S(1)}, bf16[256,2048]{1,0:T(8,128)(2,1)S(1)}, u32[]{:S(2)}, u32[]{:S(2)}) collective-permute-start(bf16[256,2048]{1,0:T(8,128)(2,1)S(1)} %hidden.2.refs_2_.refs_0_), channel_id=1, source_target_pairs={{0,4},{4,0},{8,12},{12,8},{16,20},{20,16},{24,28},{28,24},{1,5},{5... | collective-permute-start | bytes 3145736 | tf_op jit(solution)/shard_map/ppermute | solution.py:28
  66.2 4.9 %collective-permute-start.22 = (bf16[256,2048]{1,0:T(8,128)(2,1)S(1)}, bf16[256,2048]{1,0:T(8,128)(2,1)S(1)}, u32[]{:S(2)}, u32[]{:S(2)}) collective-permute-start(bf16[256,2048]{1,0:T(8,128)(2,1)S(1)} %hidden.3.refs_2_), channel_id=1, source_target_pairs={{0,4},{4,0},{8,12},{12,8},{16,20},{20,16},{24,28},{28,24},{1,5},{5... | collective-permute-start | bytes 3145736 | tf_op jit(solution)/shard_map/ppermute | solution.py:28

commit v4 on v3

v4 whole, which is shorter than its diff:
```python
import functools

import jax
import jax.numpy as jnp
from jax import lax
from jax.experimental import pallas as pl
from jax.experimental.pallas import tpu as pltpu
from jax.sharding import PartitionSpec as P

SQRT_HALF = 0.7071067811865476
INV_ROOT_TAU = 0.3989422804014327
F32 = jnp.float32
BF16 = jnp.bfloat16
IN_VMEM = pl.BlockSpec(memory_space=pltpu.VMEM)
IN_SMEM = pl.BlockSpec(memory_space=pltpu.SMEM)
TILE = 512
MIB = 2**20
ROOM = 24 * MIB


def hop(value, source, steps):
    return lax.ppermute(value, "section", [(source, source + steps)])


def swapped(value, axis, mask):
    count = lax.axis_size(axis)
    return lax.ppermute(value, axis, [(source, source ^ mask) for source in range(count)])


def tiles(width, most=TILE):
    size = min(most, width)
    return [slice(start, min(start + size, width)) for start in range(0, width, size)]


def dot(left, right):
    return jnp.dot(left, right, preferred_element_type=F32)


def dot_tn(left, right):
    return lax.dot_general(left, right, (((0,), (0,)), ((), ())), preferred_element_type=F32)


def normalize(floats, gain_row):
    center = floats - jnp.mean(floats, axis=-1, keepdims=True)
    inv_std = lax.rsqrt(jnp.mean(center * center, axis=-1, keepdims=True) + 1e-06)
    normed = center * inv_std
    return ((normed * gain_row).astype(BF16), normed, inv_std)


def gelu(v):
    return 0.5 * v * (1.0 + lax.erf(v * SQRT_HALF))


def gelu_slope(v):
    return 0.5 * (1.0 + lax.erf(v * SQRT_HALF)) + v * INV_ROOT_TAU * jnp.exp(-0.5 * v * v)


def arrivals(far, near, arrived):
    gain, x_all, weight_in, weight_out, scales, asked = near
    pairs = [(far[0], gain), (far[1], x_all)]
    pairs += [(far[2].at[0, :, cols], weight_in.at[:, cols]) for cols in tiles(weight_in.shape[1])]
    pairs += [(far[3].at[0, rows, :], weight_out.at[rows, :]) for rows in tiles(weight_out.shape[0])]
    pairs += [(far[4], scales), (far[5], asked)]
    return [
        pltpu.make_async_copy(source, target, arrived.at[index])
        for index, (source, target) in enumerate(pairs)
    ]


def first_kernel(*refs):
    far, near, (out, acted, arrived) = refs[:6], refs[6:12], refs[12:]
    gain, x_all, weight_in, weight_out, scales, _ = near

    @pl.when(lax.axis_index("section") == 0)
    def _():
        copies = arrivals(far, near, arrived)
        for copy in copies:
            copy.start()
        copies[0].wait()
        copies[1].wait()
        x = x_all[0].astype(F32)
        normed_bf, _, _ = normalize(x, gain[...])
        in_tiles = tiles(weight_in.shape[1])
        for copy, cols in zip(copies[2:], in_tiles):
            copy.wait()
            acted[:, cols] = gelu(dot(normed_bf, weight_in[:, cols])).astype(BF16)
        for copy in copies[2 + len(in_tiles) :]:
            copy.wait()
        for cols in tiles(x.shape[1]):
            branch = dot(acted[...], weight_out[:, cols])
            out[:, cols] = (x[:, cols] + scales[:, cols] * branch).astype(BF16)


def load_kernel(*refs):
    far, near, arrived = refs[:6], refs[12:18], refs[18]

    @pl.when(lax.axis_index("section") != 0)
    def _():
        copies = arrivals(far, near, arrived)
        for copy in copies:
            copy.start()
        for copy in copies:
            copy.wait()


def turn_kernel(last, owner_table, weight_in, weight_out, scales, asked, turned_in, turned_out, owned, *ahead):
    device = lax.axis_index("dp")
    owned[0] = owner_table[device]
    owned[1] = owner_table[lax.min(device + 1 - 2 * lax.rem(device, 2), owner_table.shape[0] - 1)]
    for ref, turned in ((weight_in, turned_in), (weight_out, turned_out)):
        for rows in tiles(ref.shape[0]):
            for cols in tiles(ref.shape[1]):
                turned[cols, rows] = ref[rows, cols].T

    @pl.when(lax.axis_index("section") == last)
    def _():
        for batch, grad_act in enumerate(ahead):
            scaled = (asked[batch].astype(F32) * scales[...]).astype(BF16)
            for cols in tiles(turned_out.shape[1]):
                grad_act[:, cols] = dot(scaled, turned_out[:, cols])


def forward_kernel(step, batch, x_ref, gain, weight_in, weight_out, scales, out, acted):
    @pl.when(lax.axis_index("section") == step)
    def _():
        x = (x_ref[...] if batch is None else x_ref[batch]).astype(F32)
        normed_bf, _, _ = normalize(x, gain[...])
        for cols in tiles(weight_in.shape[1]):
            acted[:, cols] = gelu(dot(normed_bf, weight_in[:, cols])).astype(BF16)
        for cols in tiles(x.shape[1]):
            branch = dot(acted[...], weight_out[:, cols])
            out[:, cols] = (x[:, cols] + scales[:, cols] * branch).astype(BF16)


def choose(whole, batch, place, later, chosen):
    section = lax.axis_index("section")

    @pl.when(section == place)
    def _():
        chosen[...] = whole[batch]

    for index, ref in later:
        @pl.when(section == index)
        def _():
            chosen[...] = ref[...]


def save_kernel(batch, sections, *refs):
    whole, later, refs = refs[0], refs[1:sections], refs[sections:]
    gain, weight_in, normed_bf, normed, inv_std, slope, chosen = refs
    choose(whole, batch, 0, list(enumerate(later, 1)), chosen)
    normed_bf[...], normed[...], inv_std[...] = normalize(chosen[...].astype(F32), gain[...])
    for cols in tiles(weight_in.shape[1]):
        slope[:, cols] = gelu_slope(dot(normed_bf[...], weight_in[:, cols]))


def backward_kernel(
    step, batch, gy_ref, gain, turned_in, turned_out, scales, normed_ref, inv_std, slope, *refs
):
    *ahead, out, grad_hidden = refs

    @pl.when(lax.axis_index("section") == step)
    def _():
        cotangent = (gy_ref[...] if batch is None else gy_ref[batch]).astype(F32)
        scaled = (cotangent * scales[...]).astype(BF16)
        for cols in tiles(turned_out.shape[1]):
            grad_act = ahead[0][:, cols] if ahead else dot(scaled, turned_out[:, cols])
            grad_hidden[:, cols] = (grad_act * slope[:, cols]).astype(BF16)
        grad_normed = dot(grad_hidden[...], turned_in[...]) * gain[...]
        normed = normed_ref[...]
        mean_one = jnp.mean(grad_normed, axis=-1, keepdims=True)
        mean_two = jnp.mean(grad_normed * normed, axis=-1, keepdims=True)
        out[...] = (
            cotangent + inv_std[...] * (grad_normed - mean_one - normed * mean_two)
        ).astype(BF16)


def pick_kernel(batch, sections, *refs):
    whole, later, chosen = refs[0], refs[1:sections], refs[-1]
    choose(whole, batch, sections - 1, list(enumerate(later)), chosen)


def slopes_kernel(count, batches, owned, *refs):
    blocks, weight_in, known, refs = refs[:count], refs[count], refs[count + 1 :][:batches], refs[count + 1 + batches :]
    sums, slopes, rows = refs[:2], refs[2:-1], refs[-1]
    part = known[0].shape[0]
    for batch, slope in enumerate(slopes):
        slope[:part, :] = known[batch][...]
        others = jnp.concatenate([block[batch * part : (batch + 1) * part, :] for block in blocks[1:]], axis=0)
        for cols in tiles(weight_in.shape[1], 256):
            slope[part:, cols] = gelu_slope(dot(others, weight_in[:, cols]))
    height = blocks[0].shape[0]
    for index, block in enumerate(blocks):
        rows[index * height : (index + 1) * height, :] = block[...]
    for which, total in enumerate(sums):
        for cols, value in products([[rows]], owned[which], total.shape[0], tiles(total.shape[1])):
            total[:, cols] = value


def arrived_kernel(*refs):
    pass


def stack_kernel(*refs):
    *blocks, whole = refs
    height = blocks[0].shape[0]
    for index, block in enumerate(blocks):
        whole[index * height : (index + 1) * height, :] = block[...]


def hidden_kernel(count, columns, *refs):
    blocks, (scales, turned_out, slope, grad_hidden, scaled) = refs[:count], refs[count:]
    first = columns.start
    part = blocks[0].shape[0]
    for index, block in enumerate(blocks):
        scaled[index * part : (index + 1) * part, :] = (
            block[...].astype(F32) * scales[...]
        ).astype(BF16)
    for cols in tiles(columns.stop - first, 256):
        there = slice(first + cols.start, first + cols.stop)
        grad_act = dot(scaled[...], turned_out[:, there])
        grad_hidden[:, cols] = (grad_act * slope[:, there]).astype(BF16)


def products(blocks, owner, tall, pieces, earlier=None):
    own = []
    for parts in blocks:
        each = parts[0].shape[1] // tall
        mine = pl.ds(pl.multiple_of(lax.rem(owner, each) * tall, tall), tall)
        value = parts[0][:, mine].T
        for index, part in enumerate(parts[1:], 1):
            value = jnp.where(lax.div(owner, each) == index, part[:, mine].T, value)
        own.append(value)
    for cols in pieces:
        value = None if earlier is None else earlier[:, cols]
        for mine_turned, parts in zip(own, blocks):
            width = parts[0].shape[1]
            first = cols.start // width
            there = slice(cols.start - first * width, cols.stop - first * width)
            term = dot(mine_turned, parts[first][:, there])
            value = term if value is None else value + term
        yield cols, value


def grouped(counts, refs):
    blocks = []
    for count in counts:
        blocks.append(refs[:count])
        refs = refs[count:]
    return blocks, refs


def square_kernel(counts, factor, owned, *refs):
    blocks, (earlier, total, stage, left) = grouped(counts, refs)
    tall, width = stage.shape
    copies = []
    for cols, value in products(blocks, owned[0], tall, tiles(width, 256), earlier):
        stage[:, cols] = value * factor
        copies.append(pltpu.make_async_copy(stage.at[:, cols], total.at[:, cols], left.at[len(copies)]))
        copies[-1].start()
    for copy in copies:
        copy.wait()


def partial_kernel(counts, factor, owned, *refs):
    blocks, (mine, other, total, act_share, stage, left) = grouped(counts, refs)
    stage[...] = (mine[...] + other[...]) * factor
    copy = pltpu.make_async_copy(stage, act_share, left.at[0])
    copy.start()
    for cols, value in products(blocks, owned[0], total.shape[0], tiles(total.shape[1], 256)):
        total[:, cols] = value
    copy.wait()


def pinned(value):
    return pltpu.with_memory_space_constraint(value, pltpu.VMEM)


def shape(dims, dtype=BF16):
    return jax.ShapeDtypeStruct(dims, dtype)


class Order:
    def __init__(self):
        self.token = []

    def __call__(
        self, kernel, arrays, outs, scratch=(), flops=0, specs=None, name=None, aliases=None, out_specs=None, ordered=True, free=False
    ):
        count, before = len(arrays), [] if free else self.token

        def body(*refs):
            given, rest = refs[:count], refs[count + len(before) :]
            kernel(*given, *rest[: len(outs)], *rest[len(outs) + ordered :])

        results = pl.pallas_call(
            body,
            in_specs=(specs or [IN_VMEM] * count) + [IN_VMEM] * len(before),
            out_specs=(out_specs or [IN_VMEM] * len(outs)) + [IN_VMEM] * ordered,
            out_shape=[*outs] + [pltpu.VMEM((8, 128), F32)] * ordered,
            scratch_shapes=list(scratch),
            input_output_aliases=aliases or {},
            compiler_params=pltpu.CompilerParams(vmem_limit_bytes=ROOM),
            cost_estimate=pl.CostEstimate(flops=flops, bytes_accessed=8 * MIB, transcendentals=0),
            name=name,
        )(*arrays, *before)
        if ordered:
            self.token = [pinned(results[-1])]
            return results[:-1]
        return results


def stack(call, blocks):
    height, width = blocks[0].shape
    outs = [shape((height * len(blocks), width), blocks[0].dtype)]
    return call(stack_kernel, [pinned(block) for block in blocks], outs, name="stack", ordered=False, free=True)[0]


def owned_partial(call, blocks, owned, owners, factor, act_parts):
    width = sum(part.shape[1] for part in blocks[0])
    parts = [pinned(part) for block in blocks for part in block]
    act = shape(act_parts[0].shape, F32)
    return call(
        functools.partial(partial_kernel, [len(block) for block in blocks], factor),
        [owned, *parts, *[pinned(value) for value in act_parts]],
        [shape((width // owners, width), F32), act],
        [pltpu.VMEM(act.shape, F32), pltpu.SemaphoreType.DMA((1,))],
        specs=[IN_SMEM] + [IN_VMEM] * (len(parts) + 2),
        name="partial",
        out_specs=[IN_VMEM, pl.BlockSpec(memory_space=pltpu.HBM)],
        ordered=False,
    )


def owned_square(call, blocks, owned, owners, factor, earlier):
    width = sum(part.shape[1] for part in blocks[0])
    tall = width // owners
    parts = [pinned(part) for block in blocks for part in block]
    return call(
        functools.partial(square_kernel, [len(block) for block in blocks], factor),
        [owned, *parts, pinned(earlier)],
        [shape((tall, width), F32)],
        [pltpu.VMEM((tall, width), F32), pltpu.SemaphoreType.DMA((len(tiles(width, 256)),))],
        specs=[IN_SMEM] + [IN_VMEM] * (len(parts) + 1),
        name="square",
        out_specs=[pl.BlockSpec(memory_space=pltpu.HBM)],
        ordered=False,
    )[0]


def plain_square(rows, owner_table, owners, total_rows):
    everything = lax.all_gather(rows, "dp", axis=0, tiled=True)
    tall = rows.shape[1] // owners
    start = owner_table[lax.axis_index("dp")] * tall
    own = lax.dynamic_slice_in_dim(everything, start, tall, axis=1)
    return dot_tn(own, everything) / total_rows


def body(inputs, ln_gain, w_in, w_out, layer_scale, out_grad, owner_table):
    sections = lax.axis_size("section")
    owners = lax.axis_size("dp")
    batch_count, row_count, width = inputs.shape
    width_hidden = w_in.shape[2]
    total_rows = batch_count * row_count * owners
    batches = range(batch_count)
    product = 2 * row_count * width * width_hidden
    block = shape((row_count, width))
    wide = pltpu.VMEM((row_count, width_hidden), BF16)
    flat = pltpu.VMEM((row_count, width), BF16)
    far = [ln_gain, inputs, w_in, w_out, layer_scale, out_grad]
    sizes = [ln_gain.shape, inputs.shape, w_in.shape[1:], w_out.shape[1:], ln_gain.shape, inputs.shape]
    homes = [pltpu.VMEM(size, value.dtype) for size, value in zip(sizes, far)]
    far = [pltpu.with_memory_space_constraint(value, pltpu.HBM) for value in far]
    far_specs = [pl.BlockSpec(memory_space=pltpu.HBM)] * len(far)
    flags = pltpu.SemaphoreType.DMA((4 + 2 * len(tiles(width_hidden)),))
    call = Order()
    *near, output = call(
        first_kernel, far, homes + [block], [wide, flags], 2 * product, far_specs, "first"
    )
    arrived = [[pinned(hop(output, 0, 1))]] + [[] for m in batches[1:]]
    near = call(
        load_kernel,
        far + [pinned(value) for value in near],
        homes,
        [flags],
        specs=far_specs + [IN_VMEM] * len(near),
        name="load",
        aliases={len(far) + index: index for index in range(len(far))},
    )
    paired = owners in (2, 4, 8) and not (width // owners % 128 or width_hidden // owners % 128)
    masks = range(2, owners, 2)
    gain, given, weight_in, weight_out, scales, asked = [pinned(value) for value in near]
    for step in range(sections - 1):
        for m in batches:
            if not (step or m):
                continue
            (output,) = call(
                functools.partial(forward_kernel, step, None if step else m),
                [arrived[m][-1] if step else given, gain, weight_in, weight_out, scales],
                [block],
                [wide],
                2 * product,
                name="forward",
            )
            arrived[m].append(pinned(hop(output, step, 1)))
        if step == 0:
            turned_in, turned_out, owned, *ahead = call(
                functools.partial(turn_kernel, sections - 1),
                [owner_table, weight_in, weight_out, scales, asked],
                [
                    pltpu.VMEM((width_hidden, width), BF16),
                    pltpu.VMEM((width, width_hidden), BF16),
                    pltpu.SMEM((2,), jnp.int32),
                ]
                + [shape((row_count, width_hidden), F32)] * batch_count,
                name="turn",
                specs=[IN_SMEM] + [IN_VMEM] * 4,
                out_specs=[IN_VMEM, IN_VMEM, IN_SMEM] + [IN_VMEM] * batch_count,
            )
            owned = pltpu.with_memory_space_constraint(owned, pltpu.SMEM)
            turned_in, turned_out = pinned(turned_in), pinned(turned_out)

    saved, returned = [], [[] for m in batches]
    for step in range(sections - 1, 0, -1):
        for m in batches:
            if paired and step == 1 and m == batches[-1]:
                call(arrived_kernel, [pinned(x) for x in gathered], [], name="arrived")
            if len(saved) <= m:
                values = call(
                    functools.partial(save_kernel, m, sections),
                    [given, *arrived[m], gain, weight_in],
                    [
                        block,
                        shape((row_count, width), F32),
                        shape((row_count, 1), F32),
                        shape((row_count, width_hidden), F32),
                    ],
                    [flat],
                    product,
                    name="save",
                )
                saved.append([pinned(value) for value in values])
            (grad_input,) = call(
                functools.partial(backward_kernel, step, m if step == sections - 1 else None),
                [
                    asked if step == sections - 1 else returned[m][0],
                    gain, turned_in, turned_out, scales, *saved[m][1:],
                    *([pinned(ahead[m])] if step == sections - 1 else []),
                ],
                [block],
                [wide],
                2 * product,
                name="backward",
            )
            returned[m].insert(0, pinned(hop(grad_input, step, -1)))
        if step == sections - 1:
            merged = stack(call, [saved[m][0] for m in batches])
            if paired:
                gathered = [merged] + [swapped(merged, "dp", mask) for mask in masks]
                count = len(gathered)
    factor = 1.0 / total_rows
    if paired:
        tall = width // owners
        sums = [shape((tall, width), F32)] * 2
        own, other, *slopes = call(
            functools.partial(slopes_kernel, count, batch_count),
            [owned, *[pinned(x) for x in gathered], weight_in, *[saved[m][3] for m in batches]],
            [*sums, *[shape((count * row_count, width_hidden), F32)] * batch_count],
            [pltpu.VMEM((count * batch_count * row_count, width), BF16)],
            specs=[IN_SMEM] + [IN_VMEM] * (count + 1 + batch_count),
            name="slopes",
        )
        other = swapped(other, "dp", 1)
    hidden_blocks, cotangents = [], []
    for m in batches:
        (cotangent,) = call(
            functools.partial(pick_kernel, m, sections),
            [asked, *returned[m]],
            [block],
            name="pick",
            ordered=False,
        )
        cotangents.append(cotangent)
    for m in batches:
        cotangent = cotangents[m]
        near = [cotangent] + [swapped(cotangent, "dp", mask) for mask in masks if paired]
        count = len(near)
        parts = tiles(width_hidden, width_hidden // 2 if paired else width_hidden)
        made = [
            call(
                functools.partial(hidden_kernel, count, columns),
                [*[pinned(x) for x in near], scales, turned_out, pinned(slopes[m]) if paired else saved[m][3]],
                [shape((count * row_count, columns.stop - columns.start))],
                [pltpu.VMEM((count * row_count, width), BF16)],
                product * count // len(parts),
                name="hidden",
                ordered=False,
            )[0]
            for columns in parts
        ]
        hidden_blocks.append(made)
        if paired:
            hidden_blocks.append([swapped(part, "dp", 1) for part in made])
    if not paired:
        grad_rows = jnp.concatenate([made[0] for made in hidden_blocks], axis=0)
        return (
            plain_square(merged, owner_table, owners, total_rows)[None],
            plain_square(grad_rows, owner_table, owners, total_rows)[None],
        )
    earlier, act_share = owned_partial(call, hidden_blocks[:-1], owned, owners, factor, [own, other])
    grad_share = owned_square(call, hidden_blocks[-1:], owned, owners, factor, earlier)
    return (act_share[None], grad_share[None])


def solution(mesh):
    placed = (
        P(None, "dp", None),
        P("section", None),
        P("section", None, None),
        P("section", None, None),
        P("section", None),
        P(None, "dp", None),
        P(),
    )
    return jax.shard_map(
        body,
        mesh=mesh,
        in_specs=placed,
        out_specs=(P("section", "dp", None), P("section", "dp", None)),
        check_vma=False,
    )
```

time: 73.7 us -> 69.4 us (0.942)
  waiting for transfers between devices: 14.4 us -> 11.1 us
  Pallas kernels: 27.3 us -> 26.3 us
    ppermute x12, waiting for transfers between devices: 14.3 us -> 10.9 us  [hop(): return lax.ppermute(value, 'section', [(source, source + steps)])]
    pallas_call x23 -> x27, Pallas kernels: 27.3 us -> 26.3 us  [__call__(): pl.pallas_call(body, in_specs=(specs or [IN_VMEM] * count) + [IN_VMEM] *...]
    ppermute x12 -> x14, starting transfers between devices: 17.5 us -> 17.4 us  [swapped(): lax.ppermute(value, axis, [(source, source ^ mask) for source in range(co...]
  transfers between devices with their start and end apart: 24 -> 26, of which waited for: 5 -> 4; matrix products, arithmetic and copies ran while one was open for 0% -> 0% of each run, Pallas kernels for 29% -> 35%
where the time goes in v4:
time: 69.4 us; the launch traced here: 69 us
  starting transfers between devices  30.4 us (44%)
  Pallas kernels  26.3 us (38%)
  waiting for transfers between devices  11.1 us (16%)
  between operations  1.25 us (2%)
    pallas_call x27, Pallas kernels, __call__(): pl.pallas_call(body, in_specs=(specs or [IN_VMEM] * count) + [IN_VMEM] *...  26.3 us
    ppermute x14, starting transfers between devices, swapped(): lax.ppermute(value, axis, [(source, source ^ mask) for source in range(co...  17.4 us
    ppermute x12, starting transfers between devices, hop(): return lax.ppermute(value, 'section', [(source, source + steps)])  13 us
    ppermute x12, waiting for transfers between devices, hop(): return lax.ppermute(value, 'section', [(source, source + steps)])  10.9 us
  transfers between devices with their start and end apart: 26, of which 4 were waited for; matrix products, arithmetic and copies ran while one was open for 0% of the time, Pallas kernels for 35%

profile of v4, /device:TPU:9, one launch (start us, length us, event | category | flops | bytes accessed | tf_op | source)
XLA Modules:
  0.0 69.0 jit_solution(10467310905639389425)
XLA Ops:
  0.6 0.1 first.1
  0.8 1.3 %collective-permute-start = (bf16[64,1024]{1,0:T(8,128)(2,1)S(1)}, bf16[64,1024]{1,0:T(8,128)(2,1)S(1)}, u32[]{:S(2)}, u32[]{:S(2)}) collective-permute-start(bf16[64,1024]{1,0:T(8,128)(2,1)S(1)} %get-tuple-element.80), channel_id=1, source_target_pairs={{0,1},{4,5},{8,9},{12,13},{16,17},{20,21},{24,25},{28,29}} | collective-permute-start | bytes 393224 | tf_op jit(solution)/shard_map/ppermute | solution.py:22
  2.1 3.7 %load.1 = (f32[1,1024]{1,0:T(1,128)S(1)}, bf16[2,64,1024]{2,1,0:T(8,128)(2,1)S(1)}, bf16[1024,2048]{1,0:T(8,128)(2,1)S(1)}, bf16[2048,1024]{1,0:T(8,128)(2,1)S(1...) custom-call(f32[1,1024]{1,0:T(1,128)} %refs_0_.4, ...), custom_call_target="tpu_custom_call", output_to_operand_aliasing={{0}: (6, {}), {1}: (7, {}), {2}: (8, {}), {3}: (9, {}), {4}... | custom-call | bytes 8388608 | tf_op jit(solution)/shard_map/load/pallas_call | solution.py:296
  5.8 1.3 %collective-permute-start.2 = (bf16[64,1024]{1,0:T(8,128)(2,1)S(1)}, bf16[64,1024]{1,0:T(8,128)(2,1)S(1)}, u32[]{:S(2)}, u32[]{:S(2)}) collective-permute-start(bf16[64,1024]{1,0:T(8,128)(2,1)S(1)} %get-tuple-element.83), channel_id=1, source_target_pairs={{0,1},{4,5},{8,9},{12,13},{16,17},{20,21},{24,25},{28,29}} | collective-permute-start | bytes 393224 | tf_op jit(solution)/shard_map/ppermute | solution.py:22
  7.1 3.0 %turn.1 = (bf16[2048,1024]{1,0:T(8,128)(2,1)S(1)}, bf16[1024,2048]{1,0:T(8,128)(2,1)S(1)}, s32[2]{0:T(128)S(4)}, f32[64,2048]{1,0:T(8,128)S(1)}, f32[64,2048]{1,0:T(8,128)S(1)}, /*index=5*/f32[8,128]{1,0:T(8,128)S(1)}) custom-call(s32[8]{0:T(128)S(1)} %copy-done, bf16[1024,2048]{1,0:T(8,128)(2,1)S(1)} %get-tuple-element.69.refs_2_.refs_1_.refs_5_, ...), custom_call_target="tpu_custom_call" | custom-call | bytes 8388608 | tf_op jit(solution)/shard_map/turn/pallas_call | solution.py:296
  10.1 1.8 %forward.6 = (bf16[64,1024]{1,0:T(8,128)(2,1)S(1)}, f32[8,128]{1,0:T(8,128)S(1)}) custom-call(bf16[64,1024]{1,0:T(8,128)(2,1)S(1)} %collective-permute-done.refs_0_.refs_1_, f32[1,1024]{1,0:T(1,128)S(1)} %get-tuple-element.74.refs_1_.refs_4_, bf16[1024,2048]{1,0:T(8,128)(2,1)S(1)} %get-tuple-element.69.refs_2_.refs_1_.refs_5_, ...), custom_call_target="tpu_custom_call" | custom-call | flops 536870912 | bytes 8388608 | tf_op jit(solution)/shard_map/forward/pallas_call | solution.py:296
  11.8 1.3 %collective-permute-start.1 = (bf16[64,1024]{1,0:T(8,128)(2,1)S(1)}, bf16[64,1024]{1,0:T(8,128)(2,1)S(1)}, u32[]{:S(2)}, u32[]{:S(2)}) collective-permute-start(bf16[64,1024]{1,0:T(8,128)(2,1)S(1)} %get-tuple-element.82), channel_id=1, source_target_pairs={{1,2},{5,6},{9,10},{13,14},{17,18},{21,22},{25,26},{29,30}} | collective-permute-start | bytes 393224 | tf_op jit(solution)/shard_map/ppermute | solution.py:22
  13.1 1.8 %forward.7 = (bf16[64,1024]{1,0:T(8,128)(2,1)S(1)}, f32[8,128]{1,0:T(8,128)S(1)}) custom-call(bf16[64,1024]{1,0:T(8,128)(2,1)S(1)} %collective-permute-done.2.refs_0_.refs_1_, f32[1,1024]{1,0:T(1,128)S(1)} %get-tuple-element.74.refs_1_.refs_4_, bf16[1024,2048]{1,0:T(8,128)(2,1)S(1)} %get-tuple-element.69.refs_2_.refs_1_.refs_5_, ...), custom_call_target="tpu_custom_call" | custom-call | flops 536870912 | bytes 8388608 | tf_op jit(solution)/shard_map/forward/pallas_call | solution.py:296
  14.9 1.3 %collective-permute-start.4 = (bf16[64,1024]{1,0:T(8,128)(2,1)S(1)}, bf16[64,1024]{1,0:T(8,128)(2,1)S(1)}, u32[]{:S(2)}, u32[]{:S(2)}) collective-permute-start(bf16[64,1024]{1,0:T(8,128)(2,1)S(1)} %get-tuple-element.87), channel_id=1, source_target_pairs={{1,2},{5,6},{9,10},{13,14},{17,18},{21,22},{25,26},{29,30}} | collective-permute-start | bytes 393224 | tf_op jit(solution)/shard_map/ppermute | solution.py:22
  16.3 0.7 collective-permute-start.3
  16.9 1.7 %collective-permute-done.4.refs_0_.refs_2_ = bf16[64,1024]{1,0:T(8,128)(2,1)S(1)} collective-permute-done((bf16[64,1024]{1,0:T(8,128)(2,1)S(1)}, bf16[64,1024]{1,0:T(8,128)(2,1)S(1)}, u32[]{:S(2)}, u32[]{:S(2)}) %collective-permute-start.4) | collective-permute-done | bytes 131104 | tf_op jit(solution)/shard_map/ppermute | solution.py:22
  18.7 0.7 collective-permute-start.6
  19.4 1.1 %save.2 = (bf16[64,1024]{1,0:T(8,128)(2,1)S(1)}, f32[64,1024]{1,0:T(8,128)S(1)}, f32[64,1]{1,0:T(8,128)S(1)}, f32[64,2048]{1,0:T(8,128)S(1)}, f32[8,128]{1,0:T(8,128)S(1)}) custom-call(bf16[2,64,1024]{2,1,0:T(8,128)(2,1)S(1)} %get-tuple-element.73.refs_0_, bf16[64,1024]{1,0:T(8,128)(2,1)S(1)} %collective-permute-done.refs_0_.refs_1_, ...), custom_call_target="tpu_custom_call" | custom-call | flops 268435456 | bytes 8388608 | tf_op jit(solution)/shard_map/save/pallas_call | solution.py:296
  20.5 0.2 backward.6
  20.7 0.7 collective-permute-start.5
  21.4 1.1 %save.3 = (bf16[64,1024]{1,0:T(8,128)(2,1)S(1)}, f32[64,1024]{1,0:T(8,128)S(1)}, f32[64,1]{1,0:T(8,128)S(1)}, f32[64,2048]{1,0:T(8,128)S(1)}, f32[8,128]{1,0:T(8,128)S(1)}) custom-call(bf16[2,64,1024]{2,1,0:T(8,128)(2,1)S(1)} %get-tuple-element.73.refs_0_, bf16[64,1024]{1,0:T(8,128)(2,1)S(1)} %collective-permute-done.2.refs_0_.refs_1_, ...), custom_call_target="tpu_custom_call" | custom-call | flops 268435456 | bytes 8388608 | tf_op jit(solution)/shard_map/save/pallas_call | solution.py:296
  22.5 0.7 collective-permute-start.8
  23.2 1.7 %collective-permute-start.12 = (bf16[128,1024]{1,0:T(8,128)(2,1)S(1)}, bf16[128,1024]{1,0:T(8,128)(2,1)S(1)}, u32[]{:S(2)}, u32[]{:S(2)}) collective-permute-start(bf16[128,1024]{1,0:T(8,128)(2,1)S(1)} %stack.1.refs_0_.refs_1_), channel_id=1, source_target_pairs={{0,24},{4,28},{8,16},{12,20},{16,8},{20,12},{24,0},{28,4},{1,25},{... | collective-permute-start | bytes 786440 | tf_op jit(solution)/shard_map/ppermute | solution.py:27
  24.9 0.2 collective-permute-start.11
  25.1 0.8 %collective-permute-start.10 = (bf16[128,1024]{1,0:T(8,128)(2,1)S(1)}, bf16[128,1024]{1,0:T(8,128)(2,1)S(1)}, u32[]{:S(2)}, u32[]{:S(2)}) collective-permute-start(bf16[128,1024]{1,0:T(8,128)(2,1)S(1)} %stack.1.refs_0_.refs_1_), channel_id=1, source_target_pairs={{0,8},{4,12},{8,0},{12,4},{16,24},{20,28},{24,16},{28,20},{1,9},{5... | collective-permute-start | bytes 786440 | tf_op jit(solution)/shard_map/ppermute | solution.py:27
  25.9 1.3 %collective-permute-start.7 = (bf16[64,1024]{1,0:T(8,128)(2,1)S(1)}, bf16[64,1024]{1,0:T(8,128)(2,1)S(1)}, u32[]{:S(2)}, u32[]{:S(2)}) collective-permute-start(bf16[64,1024]{1,0:T(8,128)(2,1)S(1)} %get-tuple-element.104), channel_id=1, source_target_pairs={{2,1},{6,5},{10,9},{14,13},{18,17},{22,21},{26,25},{30,29}} | collective-permute-start | bytes 393224 | tf_op jit(solution)/shard_map/ppermute | solution.py:22
  27.3 1.3 %collective-permute-start.13 = (bf16[64,1024]{1,0:T(8,128)(2,1)S(1)}, bf16[64,1024]{1,0:T(8,128)(2,1)S(1)}, u32[]{:S(2)}, u32[]{:S(2)}) collective-permute-start(bf16[64,1024]{1,0:T(8,128)(2,1)S(1)} %get-tuple-element.111), channel_id=1, source_target_pairs={{2,1},{6,5},{10,9},{14,13},{18,17},{22,21},{26,25},{30,29}} | collective-permute-start | bytes 393224 | tf_op jit(solution)/shard_map/ppermute | solution.py:22
  28.6 8.9 %collective-permute-done.7.refs_0_.refs_2_ = bf16[64,1024]{1,0:T(8,128)(2,1)S(1)} collective-permute-done((bf16[64,1024]{1,0:T(8,128)(2,1)S(1)}, bf16[64,1024]{1,0:T(8,128)(2,1)S(1)}, u32[]{:S(2)}, u32[]{:S(2)}) %collective-permute-start.7) | collective-permute-done | bytes 131104 | tf_op jit(solution)/shard_map/ppermute | solution.py:22
  37.5 1.7 %backward.10 = (bf16[64,1024]{1,0:T(8,128)(2,1)S(1)}, f32[8,128]{1,0:T(8,128)S(1)}) custom-call(bf16[64,1024]{1,0:T(8,128)(2,1)S(1)} %collective-permute-done.7.refs_0_.refs_2_, f32[1,1024]{1,0:T(1,128)S(1)} %get-tuple-element.74.refs_1_.refs_4_, bf16[2048,1024]{1,0:T(8,128)(2,1)S(1)} %get-tuple-element.78.refs_2_, ...), custom_call_target="tpu_custom_call" | custom-call | flops 536870912 | bytes 8388608 | tf_op jit(solution)/shard_map/backward/pallas_call | solution.py:296
  39.2 1.3 %collective-permute-start.9 = (bf16[64,1024]{1,0:T(8,128)(2,1)S(1)}, bf16[64,1024]{1,0:T(8,128)(2,1)S(1)}, u32[]{:S(2)}, u32[]{:S(2)}) collective-permute-start(bf16[64,1024]{1,0:T(8,128)(2,1)S(1)} %get-tuple-element.108), channel_id=1, source_target_pairs={{1,0},{5,4},{9,8},{13,12},{17,16},{21,20},{25,24},{29,28}} | collective-permute-start | bytes 393224 | tf_op jit(solution)/shard_map/ppermute | solution.py:22
  40.6 0.3 collective-permute-done.13.refs_0_.refs_2_
  40.8 1.7 %backward.11 = (bf16[64,1024]{1,0:T(8,128)(2,1)S(1)}, f32[8,128]{1,0:T(8,128)S(1)}) custom-call(bf16[64,1024]{1,0:T(8,128)(2,1)S(1)} %collective-permute-done.13.refs_0_.refs_2_, f32[1,1024]{1,0:T(1,128)S(1)} %get-tuple-element.74.refs_1_.refs_4_, bf16[2048,1024]{1,0:T(8,128)(2,1)S(1)} %get-tuple-element.78.refs_2_, ...), custom_call_target="tpu_custom_call" | custom-call | flops 536870912 | bytes 8388608 | tf_op jit(solution)/shard_map/backward/pallas_call | solution.py:296
  42.6 1.3 %collective-permute-start.19 = (bf16[64,1024]{1,0:T(8,128)(2,1)S(1)}, bf16[64,1024]{1,0:T(8,128)(2,1)S(1)}, u32[]{:S(2)}, u32[]{:S(2)}) collective-permute-start(bf16[64,1024]{1,0:T(8,128)(2,1)S(1)} %get-tuple-element.116), channel_id=1, source_target_pairs={{1,0},{5,4},{9,8},{13,12},{17,16},{21,20},{25,24},{29,28}} | collective-permute-start | bytes 393224 | tf_op jit(solution)/shard_map/ppermute | solution.py:22
  43.9 3.2 %slopes.1 = (f32[128,1024]{1,0:T(8,128)S(1)}, f32[128,1024]{1,0:T(8,128)S(1)}, f32[256,2048]{1,0:T(8,128)S(1)}, f32[256,2048]{1,0:T(8,128)S(1)}, f32[8,128]{1,0:T(8,128)S(1)}) custom-call(s32[2]{0:T(128)S(4)} %get-tuple-element.77.refs_0_, bf16[128,1024]{1,0:T(8,128)(2,1)S(1)} %stack.1.refs_0_.refs_1_, ...), custom_call_target="tpu_custom_call" | custom-call | bytes 8388608 | tf_op jit(solution)/shard_map/slopes/pallas_call | solution.py:296
  47.2 2.2 %collective-permute-start.16 = (bf16[64,1024]{1,0:T(8,128)(2,1)S(1)}, bf16[64,1024]{1,0:T(8,128)(2,1)S(1)}, u32[]{:S(2)}, u32[]{:S(2)}) collective-permute-start(bf16[64,1024]{1,0:T(8,128)(2,1)S(1)} %pick.2.refs_0_), channel_id=1, source_target_pairs={{0,24},{4,28},{8,16},{12,20},{16,8},{20,12},{24,0},{28,4},{1,25},{... | collective-permute-start | bytes 393224 | tf_op jit(solution)/shard_map/ppermute | solution.py:27
  49.4 0.2 collective-permute-start.15
  49.6 0.2 collective-permute-start.14
  49.9 0.2 pick.3.refs_0_
  50.1 2.2 %collective-permute-start.22 = (bf16[64,1024]{1,0:T(8,128)(2,1)S(1)}, bf16[64,1024]{1,0:T(8,128)(2,1)S(1)}, u32[]{:S(2)}, u32[]{:S(2)}) collective-permute-start(bf16[64,1024]{1,0:T(8,128)(2,1)S(1)} %pick.3.refs_0_), channel_id=1, source_target_pairs={{0,24},{4,28},{8,16},{12,20},{16,8},{20,12},{24,0},{28,4},{1,25},{... | collective-permute-start | bytes 393224 | tf_op jit(solution)/shard_map/ppermute | solution.py:27
  52.4 0.2 collective-permute-start.21
  52.6 0.7 collective-permute-start.20
  53.3 0.1 collective-permute-done.15.refs_2_
  53.3 7.3 %collective-permute-start.23 = (f32[128,1024]{1,0:T(8,128)S(1)}, f32[128,1024]{1,0:T(8,128)S(1)}, u32[]{:S(2)}, u32[]{:S(2)}) collective-permute-start(f32[128,1024]{1,0:T(8,128)S(1)} %get-tuple-element.119), channel_id=1, source_target_pairs={{0,4},{4,0},{8,12},{12,8},{16,20},{20,16},{24,28},{28,24},{1,5},{5... | collective-permute-start | bytes 1572872 | tf_op jit(solution)/shard_map/ppermute | solution.py:27
  60.7 0.7 %hidden.4.refs_1_ = bf16[256,1024]{1,0:T(8,128)(2,1)S(1)} custom-call(bf16[64,1024]{1,0:T(8,128)(2,1)S(1)} %pick.2.refs_0_, bf16[64,1024]{1,0:T(8,128)(2,1)S(1)} %collective-permute-done.14.refs_1_, bf16[64,1024]{1,0:T(8,128)(2,1)S(1)} %collective-permute-done.15.refs_2_, bf16[64,1024]{1,0:T(8,128)(2,1)S(1)} %collective-permute-done.16.refs_3_, ...), custom_call_target="tpu_custom_call" | custom-call | flops 536870912 | bytes 8388608 | tf_op jit(solution)/shard_map/hidden/pallas_call | solution.py:296
  61.4 0.1 collective-permute-start.17
  61.5 0.7 %hidden.5.refs_2_ = bf16[256,1024]{1,0:T(8,128)(2,1)S(1)} custom-call(bf16[64,1024]{1,0:T(8,128)(2,1)S(1)} %pick.2.refs_0_, bf16[64,1024]{1,0:T(8,128)(2,1)S(1)} %collective-permute-done.14.refs_1_, bf16[64,1024]{1,0:T(8,128)(2,1)S(1)} %collective-permute-done.15.refs_2_, bf16[64,1024]{1,0:T(8,128)(2,1)S(1)} %collective-permute-done.16.refs_3_, ...), custom_call_target="tpu_custom_call" | custom-call | flops 536870912 | bytes 8388608 | tf_op jit(solution)/shard_map/hidden/pallas_call | solution.py:296
  62.3 0.6 collective-permute-start.18
  62.8 0.7 %hidden.6.refs_5_ = bf16[256,1024]{1,0:T(8,128)(2,1)S(1)} custom-call(bf16[64,1024]{1,0:T(8,128)(2,1)S(1)} %pick.3.refs_0_, bf16[64,1024]{1,0:T(8,128)(2,1)S(1)} %collective-permute-done.20.refs_1_, bf16[64,1024]{1,0:T(8,128)(2,1)S(1)} %collective-permute-done.21.refs_2_, bf16[64,1024]{1,0:T(8,128)(2,1)S(1)} %collective-permute-done.22.refs_3_, ...), custom_call_target="tpu_custom_call" | custom-call | flops 536870912 | bytes 8388608 | tf_op jit(solution)/shard_map/hidden/pallas_call | solution.py:296
  63.6 0.7 %collective-permute-start.24 = (bf16[256,1024]{1,0:T(8,128)(2,1)S(1)}, bf16[256,1024]{1,0:T(8,128)(2,1)S(1)}, u32[]{:S(2)}, u32[]{:S(2)}) collective-permute-start(bf16[256,1024]{1,0:T(8,128)(2,1)S(1)} %hidden.6.refs_5_), channel_id=1, source_target_pairs={{0,4},{4,0},{8,12},{12,8},{16,20},{20,16},{24,28},{28,24},{1,5},{5... | collective-permute-start | bytes 1572872 | tf_op jit(solution)/shard_map/ppermute | solution.py:27
  64.3 0.7 %hidden.7.refs_6_ = bf16[256,1024]{1,0:T(8,128)(2,1)S(1)} custom-call(bf16[64,1024]{1,0:T(8,128)(2,1)S(1)} %pick.3.refs_0_, bf16[64,1024]{1,0:T(8,128)(2,1)S(1)} %collective-permute-done.20.refs_1_, bf16[64,1024]{1,0:T(8,128)(2,1)S(1)} %collective-permute-done.21.refs_2_, bf16[64,1024]{1,0:T(8,128)(2,1)S(1)} %collective-permute-done.22.refs_3_, ...), custom_call_target="tpu_custom_call" | custom-call | flops 536870912 | bytes 8388608 | tf_op jit(solution)/shard_map/hidden/pallas_call | solution.py:296
  65.0 0.1 collective-permute-start.25
  65.2 1.9 %partial.1 = (f32[256,2048]{1,0:T(8,128)S(1)}, f32[128,1024]{1,0:T(8,128)}) custom-call(s32[2]{0:T(128)S(4)} %get-tuple-element.77.refs_0_, bf16[256,1024]{1,0:T(8,128)(2,1)S(1)} %hidden.4.refs_1_, bf16[256,1024]{1,0:T(8,128)(2,1)S(1)} %hidden.5.refs_2_, bf16[256,1024]{1,0:T(8,128)(2,1)S(1)} %collective-permute-done.17.refs_3_, ...), custom_call_target="tpu_custom_call" | custom-call | bytes 8388608 | tf_op jit(solution)/shard_map/partial/pallas_call | solution.py:296
  67.1 1.7 %square.1 = f32[256,2048]{1,0:T(8,128)} custom-call(s32[2]{0:T(128)S(4)} %get-tuple-element.77.refs_0_, bf16[256,1024]{1,0:T(8,128)(2,1)S(1)} %collective-permute-done.24.refs_1_, bf16[256,1024]{1,0:T(8,128)(2,1)S(1)} %collective-permute-done.25.refs_2_, f32[256,2048]{1,0:T(8,128)S(1)} %get-tuple-element.121.refs_3_, ...), custom_call_target="tpu_custom_call" | custom-call | bytes 8388608 | tf_op jit(solution)/shard_map/square/pallas_call | solution.py:296
  (33 shorter events, 0.2 us)
Async XLA Ops:
  0.8 9.3 %collective-permute-start = (bf16[64,1024]{1,0:T(8,128)(2,1)S(1)}, bf16[64,1024]{1,0:T(8,128)(2,1)S(1)}, u32[]{:S(2)}, u32[]{:S(2)}) collective-permute-start(bf16[64,1024]{1,0:T(8,128)(2,1)S(1)} %get-tuple-element.80), channel_id=1, source_target_pairs={{0,1},{4,5},{8,9},{12,13},{16,17},{20,21},{24,25},{28,29}} | collective-permute-start | bytes 393224 | tf_op jit(solution)/shard_map/ppermute | solution.py:22
  5.7 1.3 %copy-start = (s32[8]{0:T(128)S(1)}, s32[8]{0:T(128)}, u32[]{:S(2)}) copy-start(s32[8]{0:T(128)} %refs_0_.5) | copy-start | bytes 100
  5.8 7.4 %collective-permute-start.2 = (bf16[64,1024]{1,0:T(8,128)(2,1)S(1)}, bf16[64,1024]{1,0:T(8,128)(2,1)S(1)}, u32[]{:S(2)}, u32[]{:S(2)}) collective-permute-start(bf16[64,1024]{1,0:T(8,128)(2,1)S(1)} %get-tuple-element.83), channel_id=1, source_target_pairs={{0,1},{4,5},{8,9},{12,13},{16,17},{20,21},{24,25},{28,29}} | collective-permute-start | bytes 393224 | tf_op jit(solution)/shard_map/ppermute | solution.py:22
  11.8 4.4 %collective-permute-start.1 = (bf16[64,1024]{1,0:T(8,128)(2,1)S(1)}, bf16[64,1024]{1,0:T(8,128)(2,1)S(1)}, u32[]{:S(2)}, u32[]{:S(2)}) collective-permute-start(bf16[64,1024]{1,0:T(8,128)(2,1)S(1)} %get-tuple-element.82), channel_id=1, source_target_pairs={{1,2},{5,6},{9,10},{13,14},{17,18},{21,22},{25,26},{29,30}} | collective-permute-start | bytes 393224 | tf_op jit(solution)/shard_map/ppermute | solution.py:22
  14.9 3.8 %collective-permute-start.4 = (bf16[64,1024]{1,0:T(8,128)(2,1)S(1)}, bf16[64,1024]{1,0:T(8,128)(2,1)S(1)}, u32[]{:S(2)}, u32[]{:S(2)}) collective-permute-start(bf16[64,1024]{1,0:T(8,128)(2,1)S(1)} %get-tuple-element.87), channel_id=1, source_target_pairs={{1,2},{5,6},{9,10},{13,14},{17,18},{21,22},{25,26},{29,30}} | collective-permute-start | bytes 393224 | tf_op jit(solution)/shard_map/ppermute | solution.py:22
  16.3 3.1 %collective-permute-start.3 = (bf16[64,1024]{1,0:T(8,128)(2,1)S(1)}, bf16[64,1024]{1,0:T(8,128)(2,1)S(1)}, u32[]{:S(2)}, u32[]{:S(2)}) collective-permute-start(bf16[64,1024]{1,0:T(8,128)(2,1)S(1)} %get-tuple-element.86), channel_id=1, source_target_pairs={{2,3},{6,7},{10,11},{14,15},{18,19},{22,23},{26,27},{30,31}} | collective-permute-start | bytes 393224 | tf_op jit(solution)/shard_map/ppermute | solution.py:22
  18.7 2.7 %collective-permute-start.6 = (bf16[64,1024]{1,0:T(8,128)(2,1)S(1)}, bf16[64,1024]{1,0:T(8,128)(2,1)S(1)}, u32[]{:S(2)}, u32[]{:S(2)}) collective-permute-start(bf16[64,1024]{1,0:T(8,128)(2,1)S(1)} %get-tuple-element.96), channel_id=1, source_target_pairs={{2,3},{6,7},{10,11},{14,15},{18,19},{22,23},{26,27},{30,31}} | collective-permute-start | bytes 393224 | tf_op jit(solution)/shard_map/ppermute | solution.py:22
  20.7 5.3 %collective-permute-start.5 = (bf16[64,1024]{1,0:T(8,128)(2,1)S(1)}, bf16[64,1024]{1,0:T(8,128)(2,1)S(1)}, u32[]{:S(2)}, u32[]{:S(2)}) collective-permute-start(bf16[64,1024]{1,0:T(8,128)(2,1)S(1)} %get-tuple-element.95), channel_id=1, source_target_pairs={{3,2},{7,6},{11,10},{15,14},{19,18},{23,22},{27,26},{31,30}} | collective-permute-start | bytes 393224 | tf_op jit(solution)/shard_map/ppermute | solution.py:22
  22.5 4.7 %collective-permute-start.8 = (bf16[64,1024]{1,0:T(8,128)(2,1)S(1)}, bf16[64,1024]{1,0:T(8,128)(2,1)S(1)}, u32[]{:S(2)}, u32[]{:S(2)}) collective-permute-start(bf16[64,1024]{1,0:T(8,128)(2,1)S(1)} %get-tuple-element.105), channel_id=1, source_target_pairs={{3,2},{7,6},{11,10},{15,14},{19,18},{23,22},{27,26},{31,30}} | collective-permute-start | bytes 393224 | tf_op jit(solution)/shard_map/ppermute | solution.py:22
  23.2 17.3 %collective-permute-start.12 = (bf16[128,1024]{1,0:T(8,128)(2,1)S(1)}, bf16[128,1024]{1,0:T(8,128)(2,1)S(1)}, u32[]{:S(2)}, u32[]{:S(2)}) collective-permute-start(bf16[128,1024]{1,0:T(8,128)(2,1)S(1)} %stack.1.refs_0_.refs_1_), channel_id=1, source_target_pairs={{0,24},{4,28},{8,16},{12,20},{16,8},{20,12},{24,0},{28,4},{1,25},{... | collective-permute-start | bytes 786440 | tf_op jit(solution)/shard_map/ppermute | solution.py:27
  24.9 15.6 %collective-permute-start.11 = (bf16[128,1024]{1,0:T(8,128)(2,1)S(1)}, bf16[128,1024]{1,0:T(8,128)(2,1)S(1)}, u32[]{:S(2)}, u32[]{:S(2)}) collective-permute-start(bf16[128,1024]{1,0:T(8,128)(2,1)S(1)} %stack.1.refs_0_.refs_1_), channel_id=1, source_target_pairs={{0,16},{4,20},{8,24},{12,28},{16,0},{20,4},{24,8},{28,12},{1,17},{... | collective-permute-start | bytes 786440 | tf_op jit(solution)/shard_map/ppermute | solution.py:27
  25.1 15.4 %collective-permute-start.10 = (bf16[128,1024]{1,0:T(8,128)(2,1)S(1)}, bf16[128,1024]{1,0:T(8,128)(2,1)S(1)}, u32[]{:S(2)}, u32[]{:S(2)}) collective-permute-start(bf16[128,1024]{1,0:T(8,128)(2,1)S(1)} %stack.1.refs_0_.refs_1_), channel_id=1, source_target_pairs={{0,8},{4,12},{8,0},{12,4},{16,24},{20,28},{24,16},{28,20},{1,9},{5... | collective-permute-start | bytes 786440 | tf_op jit(solution)/shard_map/ppermute | solution.py:27
  25.9 11.5 %collective-permute-start.7 = (bf16[64,1024]{1,0:T(8,128)(2,1)S(1)}, bf16[64,1024]{1,0:T(8,128)(2,1)S(1)}, u32[]{:S(2)}, u32[]{:S(2)}) collective-permute-start(bf16[64,1024]{1,0:T(8,128)(2,1)S(1)} %get-tuple-element.104), channel_id=1, source_target_pairs={{2,1},{6,5},{10,9},{14,13},{18,17},{22,21},{26,25},{30,29}} | collective-permute-start | bytes 393224 | tf_op jit(solution)/shard_map/ppermute | solution.py:22
  27.3 13.6 %collective-permute-start.13 = (bf16[64,1024]{1,0:T(8,128)(2,1)S(1)}, bf16[64,1024]{1,0:T(8,128)(2,1)S(1)}, u32[]{:S(2)}, u32[]{:S(2)}) collective-permute-start(bf16[64,1024]{1,0:T(8,128)(2,1)S(1)} %get-tuple-element.111), channel_id=1, source_target_pairs={{2,1},{6,5},{10,9},{14,13},{18,17},{22,21},{26,25},{30,29}} | collective-permute-start | bytes 393224 | tf_op jit(solution)/shard_map/ppermute | solution.py:22
  39.2 7.9 %collective-permute-start.9 = (bf16[64,1024]{1,0:T(8,128)(2,1)S(1)}, bf16[64,1024]{1,0:T(8,128)(2,1)S(1)}, u32[]{:S(2)}, u32[]{:S(2)}) collective-permute-start(bf16[64,1024]{1,0:T(8,128)(2,1)S(1)} %get-tuple-element.108), channel_id=1, source_target_pairs={{1,0},{5,4},{9,8},{13,12},{17,16},{21,20},{25,24},{29,28}} | collective-permute-start | bytes 393224 | tf_op jit(solution)/shard_map/ppermute | solution.py:22
  42.6 7.3 %collective-permute-start.19 = (bf16[64,1024]{1,0:T(8,128)(2,1)S(1)}, bf16[64,1024]{1,0:T(8,128)(2,1)S(1)}, u32[]{:S(2)}, u32[]{:S(2)}) collective-permute-start(bf16[64,1024]{1,0:T(8,128)(2,1)S(1)} %get-tuple-element.116), channel_id=1, source_target_pairs={{1,0},{5,4},{9,8},{13,12},{17,16},{21,20},{25,24},{29,28}} | collective-permute-start | bytes 393224 | tf_op jit(solution)/shard_map/ppermute | solution.py:22
  47.2 5.4 %collective-permute-start.16 = (bf16[64,1024]{1,0:T(8,128)(2,1)S(1)}, bf16[64,1024]{1,0:T(8,128)(2,1)S(1)}, u32[]{:S(2)}, u32[]{:S(2)}) collective-permute-start(bf16[64,1024]{1,0:T(8,128)(2,1)S(1)} %pick.2.refs_0_), channel_id=1, source_target_pairs={{0,24},{4,28},{8,16},{12,20},{16,8},{20,12},{24,0},{28,4},{1,25},{... | collective-permute-start | bytes 393224 | tf_op jit(solution)/shard_map/ppermute | solution.py:27
  49.4 4.0 %collective-permute-start.15 = (bf16[64,1024]{1,0:T(8,128)(2,1)S(1)}, bf16[64,1024]{1,0:T(8,128)(2,1)S(1)}, u32[]{:S(2)}, u32[]{:S(2)}) collective-permute-start(bf16[64,1024]{1,0:T(8,128)(2,1)S(1)} %pick.2.refs_0_), channel_id=1, source_target_pairs={{0,16},{4,20},{8,24},{12,28},{16,0},{20,4},{24,8},{28,12},{1,17},{... | collective-permute-start | bytes 393224 | tf_op jit(solution)/shard_map/ppermute | solution.py:27
  49.6 11.1 %collective-permute-start.14 = (bf16[64,1024]{1,0:T(8,128)(2,1)S(1)}, bf16[64,1024]{1,0:T(8,128)(2,1)S(1)}, u32[]{:S(2)}, u32[]{:S(2)}) collective-permute-start(bf16[64,1024]{1,0:T(8,128)(2,1)S(1)} %pick.2.refs_0_), channel_id=1, source_target_pairs={{0,8},{4,12},{8,0},{12,4},{16,24},{20,28},{24,16},{28,20},{1,9},{5... | collective-permute-start | bytes 393224 | tf_op jit(solution)/shard_map/ppermute | solution.py:27
  50.1 12.1 %collective-permute-start.22 = (bf16[64,1024]{1,0:T(8,128)(2,1)S(1)}, bf16[64,1024]{1,0:T(8,128)(2,1)S(1)}, u32[]{:S(2)}, u32[]{:S(2)}) collective-permute-start(bf16[64,1024]{1,0:T(8,128)(2,1)S(1)} %pick.3.refs_0_), channel_id=1, source_target_pairs={{0,24},{4,28},{8,16},{12,20},{16,8},{20,12},{24,0},{28,4},{1,25},{... | collective-permute-start | bytes 393224 | tf_op jit(solution)/shard_map/ppermute | solution.py:27
  52.4 10.5 %collective-permute-start.21 = (bf16[64,1024]{1,0:T(8,128)(2,1)S(1)}, bf16[64,1024]{1,0:T(8,128)(2,1)S(1)}, u32[]{:S(2)}, u32[]{:S(2)}) collective-permute-start(bf16[64,1024]{1,0:T(8,128)(2,1)S(1)} %pick.3.refs_0_), channel_id=1, source_target_pairs={{0,16},{4,20},{8,24},{12,28},{16,0},{20,4},{24,8},{28,12},{1,17},{... | collective-permute-start | bytes 393224 | tf_op jit(solution)/shard_map/ppermute | solution.py:27
  52.6 10.2 %collective-permute-start.20 = (bf16[64,1024]{1,0:T(8,128)(2,1)S(1)}, bf16[64,1024]{1,0:T(8,128)(2,1)S(1)}, u32[]{:S(2)}, u32[]{:S(2)}) collective-permute-start(bf16[64,1024]{1,0:T(8,128)(2,1)S(1)} %pick.3.refs_0_), channel_id=1, source_target_pairs={{0,8},{4,12},{8,0},{12,4},{16,24},{20,28},{24,16},{28,20},{1,9},{5... | collective-permute-start | bytes 393224 | tf_op jit(solution)/shard_map/ppermute | solution.py:27
  53.3 11.8 %collective-permute-start.23 = (f32[128,1024]{1,0:T(8,128)S(1)}, f32[128,1024]{1,0:T(8,128)S(1)}, u32[]{:S(2)}, u32[]{:S(2)}) collective-permute-start(f32[128,1024]{1,0:T(8,128)S(1)} %get-tuple-element.119), channel_id=1, source_target_pairs={{0,4},{4,0},{8,12},{12,8},{16,20},{20,16},{24,28},{28,24},{1,5},{5... | collective-permute-start | bytes 1572872 | tf_op jit(solution)/shard_map/ppermute | solution.py:27
  61.4 3.7 %collective-permute-start.17 = (bf16[256,1024]{1,0:T(8,128)(2,1)S(1)}, bf16[256,1024]{1,0:T(8,128)(2,1)S(1)}, u32[]{:S(2)}, u32[]{:S(2)}) collective-permute-start(bf16[256,1024]{1,0:T(8,128)(2,1)S(1)} %hidden.4.refs_1_), channel_id=1, source_target_pairs={{0,4},{4,0},{8,12},{12,8},{16,20},{20,16},{24,28},{28,24},{1,5},{5... | collective-permute-start | bytes 1572872 | tf_op jit(solution)/shard_map/ppermute | solution.py:27
  62.3 2.9 %collective-permute-start.18 = (bf16[256,1024]{1,0:T(8,128)(2,1)S(1)}, bf16[256,1024]{1,0:T(8,128)(2,1)S(1)}, u32[]{:S(2)}, u32[]{:S(2)}) collective-permute-start(bf16[256,1024]{1,0:T(8,128)(2,1)S(1)} %hidden.5.refs_2_), channel_id=1, source_target_pairs={{0,4},{4,0},{8,12},{12,8},{16,20},{20,16},{24,28},{28,24},{1,5},{5... | collective-permute-start | bytes 1572872 | tf_op jit(solution)/shard_map/ppermute | solution.py:27
  63.6 3.5 %collective-permute-start.24 = (bf16[256,1024]{1,0:T(8,128)(2,1)S(1)}, bf16[256,1024]{1,0:T(8,128)(2,1)S(1)}, u32[]{:S(2)}, u32[]{:S(2)}) collective-permute-start(bf16[256,1024]{1,0:T(8,128)(2,1)S(1)} %hidden.6.refs_5_), channel_id=1, source_target_pairs={{0,4},{4,0},{8,12},{12,8},{16,20},{20,16},{24,28},{28,24},{1,5},{5... | collective-permute-start | bytes 1572872 | tf_op jit(solution)/shard_map/ppermute | solution.py:27
  65.0 2.1 %collective-permute-start.25 = (bf16[256,1024]{1,0:T(8,128)(2,1)S(1)}, bf16[256,1024]{1,0:T(8,128)(2,1)S(1)}, u32[]{:S(2)}, u32[]{:S(2)}) collective-permute-start(bf16[256,1024]{1,0:T(8,128)(2,1)S(1)} %hidden.7.refs_6_), channel_id=1, source_target_pairs={{0,4},{4,0},{8,12},{12,8},{16,20},{20,16},{24,28},{28,24},{1,5},{5... | collective-permute-start | bytes 1572872 | tf_op jit(solution)/shard_map/ppermute | solution.py:27

commit v5 on v4

--- a/solution.py
+++ b/solution.py
@@ -84,11 +84,14 @@
         for copy, cols in zip(copies[2:], in_tiles):
             copy.wait()
             acted[:, cols] = gelu(dot(normed_bf, weight_in[:, cols])).astype(BF16)
-        for copy in copies[2 + len(in_tiles) :]:
+        branch = None
+        for copy, rows in zip(copies[2 + len(in_tiles) :], tiles(weight_out.shape[0])):
             copy.wait()
-        for cols in tiles(x.shape[1]):
-            branch = dot(acted[...], weight_out[:, cols])
-            out[:, cols] = (x[:, cols] + scales[:, cols] * branch).astype(BF16)
+            term = dot(acted[:, rows], weight_out[rows, :])
+            branch = term if branch is None else branch + term
+        for copy in copies[-2:]:
+            copy.wait()
+        out[...] = (x + scales[...] * branch).astype(BF16)
 
 
 def load_kernel(*refs):
@@ -180,21 +183,38 @@
     choose(whole, batch, sections - 1, list(enumerate(later)), chosen)
 
 
-def slopes_kernel(count, batches, owned, *refs):
-    blocks, weight_in, known, refs = refs[:count], refs[count], refs[count + 1 :][:batches], refs[count + 1 + batches :]
-    sums, slopes, rows = refs[:2], refs[2:-1], refs[-1]
+def take_slopes(section, count, *refs):
+    batches = (len(refs) - count - 1) // 2
+    blocks, weight_in, known, slopes = refs[:count], refs[count], refs[count + 1 : -batches], refs[-batches:]
     part = known[0].shape[0]
-    for batch, slope in enumerate(slopes):
-        slope[:part, :] = known[batch][...]
-        others = jnp.concatenate([block[batch * part : (batch + 1) * part, :] for block in blocks[1:]], axis=0)
+
+    @pl.when(section(lax.axis_index("section")))
+    def _():
+        size = (count - 1) * part
+        others = [block[batch * part : (batch + 1) * part, :] for batch in range(batches) for block in blocks[1:]]
+        others = jnp.concatenate(others, axis=0)
         for cols in tiles(weight_in.shape[1], 256):
-            slope[part:, cols] = gelu_slope(dot(others, weight_in[:, cols]))
+            values = gelu_slope(dot(others, weight_in[:, cols]))
+            for batch, slope in enumerate(slopes):
+                slope[part:, cols] = values[batch * size : (batch + 1) * size, :]
+        for batch, slope in enumerate(slopes):
+            slope[:part, :] = known[batch][...]
+
+
+def slopes_kernel(count, batches, late, owned, *refs):
+    sums, slopes, rows = refs[count + 1 + batches :][:2], refs[-1 - batches : -1], refs[-1]
+    take_slopes(lambda section: section != late, count, *refs[: count + 1 + batches], *slopes)
+    blocks = refs[:count]
     height = blocks[0].shape[0]
     for index, block in enumerate(blocks):
         rows[index * height : (index + 1) * height, :] = block[...]
     for which, total in enumerate(sums):
-        for cols, value in products([[rows]], owned[which], total.shape[0], tiles(total.shape[1])):
+        for cols, value in products([rows], owned[which], total.shape[0], tiles(total.shape[1])):
             total[:, cols] = value
+
+
+def late_kernel(count, batches, late, *refs):
+    take_slopes(lambda section: section == late, count, *refs[: count + 1 + batches], *refs[-batches:])
 
 
 def arrived_kernel(*refs):
@@ -208,53 +228,35 @@
         whole[index * height : (index + 1) * height, :] = block[...]
 
 
-def hidden_kernel(count, columns, *refs):
+def hidden_kernel(places, *refs):
+    count = len(places)
     blocks, (scales, turned_out, slope, grad_hidden, scaled) = refs[:count], refs[count:]
-    first = columns.start
     part = blocks[0].shape[0]
     for index, block in enumerate(blocks):
         scaled[index * part : (index + 1) * part, :] = (
             block[...].astype(F32) * scales[...]
         ).astype(BF16)
-    for cols in tiles(columns.stop - first, 256):
-        there = slice(first + cols.start, first + cols.stop)
-        grad_act = dot(scaled[...], turned_out[:, there])
-        grad_hidden[:, cols] = (grad_act * slope[:, there]).astype(BF16)
+    for cols in tiles(turned_out.shape[1], 256):
+        grad_act = dot(scaled[...], turned_out[:, cols])
+        for index, place in enumerate(places):
+            rows = slice(index * part, (index + 1) * part)
+            there = slope[place * part : (place + 1) * part, cols]
+            grad_hidden[rows, cols] = (grad_act[rows, :] * there).astype(BF16)
 
 
 def products(blocks, owner, tall, pieces, earlier=None):
-    own = []
-    for parts in blocks:
-        each = parts[0].shape[1] // tall
-        mine = pl.ds(pl.multiple_of(lax.rem(owner, each) * tall, tall), tall)
-        value = parts[0][:, mine].T
-        for index, part in enumerate(parts[1:], 1):
-            value = jnp.where(lax.div(owner, each) == index, part[:, mine].T, value)
-        own.append(value)
+    mine = pl.ds(pl.multiple_of(owner * tall, tall), tall)
     for cols in pieces:
-        value = None if earlier is None else earlier[:, cols]
-        for mine_turned, parts in zip(own, blocks):
-            width = parts[0].shape[1]
-            first = cols.start // width
-            there = slice(cols.start - first * width, cols.stop - first * width)
-            term = dot(mine_turned, parts[first][:, there])
-            value = term if value is None else value + term
-        yield cols, value
-
-
-def grouped(counts, refs):
-    blocks = []
-    for count in counts:
-        blocks.append(refs[:count])
-        refs = refs[count:]
-    return blocks, refs
-
-
-def square_kernel(counts, factor, owned, *refs):
-    blocks, (earlier, total, stage, left) = grouped(counts, refs)
+        own = jnp.concatenate([block[:, mine] for block in blocks], axis=0)
+        value = dot_tn(own, jnp.concatenate([block[:, cols] for block in blocks], axis=0))
+        yield cols, value if earlier is None else earlier[:, cols] + value
+
+
+def square_kernel(count, factor, owned, *refs):
+    blocks, (earlier, total, stage, left) = refs[:count], refs[count:]
     tall, width = stage.shape
     copies = []
-    for cols, value in products(blocks, owned[0], tall, tiles(width, 256), earlier):
+    for cols, value in products(blocks, owned[0], tall, tiles(width), earlier):
         stage[:, cols] = value * factor
         copies.append(pltpu.make_async_copy(stage.at[:, cols], total.at[:, cols], left.at[len(copies)]))
         copies[-1].start()
@@ -262,12 +264,12 @@
         copy.wait()
 
 
-def partial_kernel(counts, factor, owned, *refs):
-    blocks, (mine, other, total, act_share, stage, left) = grouped(counts, refs)
+def partial_kernel(count, factor, owned, *refs):
+    blocks, (mine, other, total, act_share, stage, left) = refs[:count], refs[count:]
     stage[...] = (mine[...] + other[...]) * factor
     copy = pltpu.make_async_copy(stage, act_share, left.at[0])
     copy.start()
-    for cols, value in products(blocks, owned[0], total.shape[0], tiles(total.shape[1], 256)):
+    for cols, value in products(blocks, owned[0], total.shape[0], tiles(total.shape[1])):
         total[:, cols] = value
     copy.wait()
 
@@ -317,15 +319,14 @@
 
 
 def owned_partial(call, blocks, owned, owners, factor, act_parts):
-    width = sum(part.shape[1] for part in blocks[0])
-    parts = [pinned(part) for block in blocks for part in block]
+    width = blocks[0].shape[1]
     act = shape(act_parts[0].shape, F32)
     return call(
-        functools.partial(partial_kernel, [len(block) for block in blocks], factor),
-        [owned, *parts, *[pinned(value) for value in act_parts]],
+        functools.partial(partial_kernel, len(blocks), factor),
+        [owned, *[pinned(value) for value in [*blocks, *act_parts]]],
         [shape((width // owners, width), F32), act],
         [pltpu.VMEM(act.shape, F32), pltpu.SemaphoreType.DMA((1,))],
-        specs=[IN_SMEM] + [IN_VMEM] * (len(parts) + 2),
+        specs=[IN_SMEM] + [IN_VMEM] * (len(blocks) + 2),
         name="partial",
         out_specs=[IN_VMEM, pl.BlockSpec(memory_space=pltpu.HBM)],
         ordered=False,
@@ -333,15 +334,14 @@
 
 
 def owned_square(call, blocks, owned, owners, factor, earlier):
-    width = sum(part.shape[1] for part in blocks[0])
+    width = blocks[0].shape[1]
     tall = width // owners
-    parts = [pinned(part) for block in blocks for part in block]
     return call(
-        functools.partial(square_kernel, [len(block) for block in blocks], factor),
-        [owned, *parts, pinned(earlier)],
+        functools.partial(square_kernel, len(blocks), factor),
+        [owned, *[pinned(value) for value in [*blocks, earlier]]],
         [shape((tall, width), F32)],
         [pltpu.VMEM((tall, width), F32), pltpu.SemaphoreType.DMA((len(tiles(width, 256)),))],
-        specs=[IN_SMEM] + [IN_VMEM] * (len(parts) + 1),
+        specs=[IN_SMEM] + [IN_VMEM] * (len(blocks) + 1),
         name="square",
         out_specs=[pl.BlockSpec(memory_space=pltpu.HBM)],
         ordered=False,
@@ -403,7 +403,7 @@
                 name="forward",
             )
             arrived[m].append(pinned(hop(output, step, 1)))
-        if step == 0:
+        if step == min(1, sections - 2):
             turned_in, turned_out, owned, *ahead = call(
                 functools.partial(turn_kernel, sections - 1),
                 [owner_table, weight_in, weight_out, scales, asked],
@@ -462,9 +462,10 @@
     if paired:
         tall = width // owners
         sums = [shape((tall, width), F32)] * 2
+        to_slopes = [*[pinned(x) for x in gathered], weight_in, *[saved[m][3] for m in batches]]
         own, other, *slopes = call(
-            functools.partial(slopes_kernel, count, batch_count),
-            [owned, *[pinned(x) for x in gathered], weight_in, *[saved[m][3] for m in batches]],
+            functools.partial(slopes_kernel, count, batch_count, 1),
+            [owned, *to_slopes],
             [*sums, *[shape((count * row_count, width_hidden), F32)] * batch_count],
             [pltpu.VMEM((count * batch_count * row_count, width), BF16)],
             specs=[IN_SMEM] + [IN_VMEM] * (count + 1 + batch_count),
@@ -478,37 +479,51 @@
             [asked, *returned[m]],
             [block],
             name="pick",
-            ordered=False,
+            ordered=m == 0,
         )
         cotangents.append(cotangent)
+        if paired and m == 0:
+            slopes = call(
+                functools.partial(late_kernel, count, batch_count, 1),
+                [*to_slopes, *[pinned(value) for value in slopes]],
+                [shape((count * row_count, width_hidden), F32)] * batch_count,
+                name="late",
+                aliases={len(to_slopes) + n: n for n in batches},
+                )
     for m in batches:
         cotangent = cotangents[m]
-        near = [cotangent] + [swapped(cotangent, "dp", mask) for mask in masks if paired]
+        order = [mask for mask in masks if paired]
+        sent = {mask: swapped(cotangent, "dp", mask) for mask in (order if m else reversed(order))}
+        near = [cotangent] + [sent[mask] for mask in order]
         count = len(near)
-        parts = tiles(width_hidden, width_hidden // 2 if paired else width_hidden)
+        places = [[0, *range(3, count)], list(range(1, min(count, 3)))] if count > 1 else [[0]]
         made = [
             call(
-                functools.partial(hidden_kernel, count, columns),
-                [*[pinned(x) for x in near], scales, turned_out, pinned(slopes[m]) if paired else saved[m][3]],
-                [shape((count * row_count, columns.stop - columns.start))],
-                [pltpu.VMEM((count * row_count, width), BF16)],
-                product * count // len(parts),
+                functools.partial(hidden_kernel, part),
+                [
+                    *[pinned(near[place]) for place in part],
+                    scales, turned_out, pinned(slopes[m]) if paired else saved[m][3],
+                ],
+                [shape((len(part) * row_count, width_hidden))],
+                [pltpu.VMEM((len(part) * row_count, width), BF16)],
                 name="hidden",
                 ordered=False,
             )[0]
-            for columns in parts
+            for part in places
         ]
-        hidden_blocks.append(made)
+        hidden_blocks += made
         if paired:
-            hidden_blocks.append([swapped(part, "dp", 1) for part in made])
+            crossed = [swapped(part, "dp", 1) for part in made]
+            hidden_blocks += crossed
     if not paired:
-        grad_rows = jnp.concatenate([made[0] for made in hidden_blocks], axis=0)
+        grad_rows = jnp.concatenate(hidden_blocks, axis=0)
         return (
             plain_square(merged, owner_table, owners, total_rows)[None],
             plain_square(grad_rows, owner_table, owners, total_rows)[None],
         )
-    earlier, act_share = owned_partial(call, hidden_blocks[:-1], owned, owners, factor, [own, other])
-    grad_share = owned_square(call, hidden_blocks[-1:], owned, owners, factor, earlier)
+    late = len(crossed)
+    earlier, act_share = owned_partial(call, hidden_blocks[:-late], owned, owners, factor, [own, other])
+    grad_share = owned_square(call, hidden_blocks[-late:], owned, owners, factor, earlier)
     return (act_share[None], grad_share[None])
 
 

time: 69.4 us -> 68.6 us (0.988)
  waiting for transfers between devices: 11.1 us -> 10 us
    ppermute x12, waiting for transfers between devices: 10.9 us -> 9.97 us  [hop(): return lax.ppermute(value, 'section', [(source, source + steps)])]
    pallas_call x27 -> x28, Pallas kernels: 26.3 us -> 26 us  [__call__(): pl.pallas_call(body, in_specs=(specs or [IN_VMEM] * count) + [IN_VMEM] *...]
  transfers between devices with their start and end apart: 26 -> 26, of which waited for: 4 -> 3; matrix products, arithmetic and copies ran while one was open for 0% -> 0% of each run, Pallas kernels for 35% -> 36%
where the time goes in v5:
time: 68.6 us; the launch traced here: 68.3 us
  starting transfers between devices  31 us (45%)
  Pallas kernels  26 us (38%)
  waiting for transfers between devices  10 us (15%)
  between operations  1.25 us (2%)
    pallas_call x28, Pallas kernels, __call__(): pl.pallas_call(body, in_specs=(specs or [IN_VMEM] * count) + [IN_VMEM] *...  26 us
    ppermute x14, starting transfers between devices, swapped(): lax.ppermute(value, axis, [(source, source ^ mask) for source in range(co...  18 us
    ppermute x12, starting transfers between devices, hop(): return lax.ppermute(value, 'section', [(source, source + steps)])  13 us
    ppermute x12, waiting for transfers between devices, hop(): return lax.ppermute(value, 'section', [(source, source + steps)])  9.97 us
  transfers between devices with their start and end apart: 26, of which 3 were waited for; matrix products, arithmetic and copies ran while one was open for 0% of the time, Pallas kernels for 36%

profile of v5, /device:TPU:9, one launch (start us, length us, event | category | flops | bytes accessed | tf_op | source)
XLA Modules:
  0.0 68.3 jit_solution(620951236277036783)
XLA Ops:
  0.6 0.1 first.1
  0.8 1.3 %collective-permute-start.1 = (bf16[64,1024]{1,0:T(8,128)(2,1)S(1)}, bf16[64,1024]{1,0:T(8,128)(2,1)S(1)}, u32[]{:S(2)}, u32[]{:S(2)}) collective-permute-start(bf16[64,1024]{1,0:T(8,128)(2,1)S(1)} %get-tuple-element.82), channel_id=1, source_target_pairs={{0,1},{4,5},{8,9},{12,13},{16,17},{20,21},{24,25},{28,29}} | collective-permute-start | bytes 393224 | tf_op jit(solution)/shard_map/ppermute | solution.py:22
  2.1 3.7 %load.1 = (f32[1,1024]{1,0:T(1,128)S(1)}, bf16[2,64,1024]{2,1,0:T(8,128)(2,1)S(1)}, bf16[1024,2048]{1,0:T(8,128)(2,1)S(1)}, bf16[2048,1024]{1,0:T(8,128)(2,1)S(1...) custom-call(f32[1,1024]{1,0:T(1,128)} %refs_0_.4, ...), custom_call_target="tpu_custom_call", output_to_operand_aliasing={{0}: (6, {}), {1}: (7, {}), {2}: (8, {}), {3}: (9, {}), {4}... | custom-call | bytes 8388608 | tf_op jit(solution)/shard_map/load/pallas_call | solution.py:298
  5.8 1.3 %collective-permute-start = (bf16[64,1024]{1,0:T(8,128)(2,1)S(1)}, bf16[64,1024]{1,0:T(8,128)(2,1)S(1)}, u32[]{:S(2)}, u32[]{:S(2)}) collective-permute-start(bf16[64,1024]{1,0:T(8,128)(2,1)S(1)} %get-tuple-element.81), channel_id=1, source_target_pairs={{0,1},{4,5},{8,9},{12,13},{16,17},{20,21},{24,25},{28,29}} | collective-permute-start | bytes 393224 | tf_op jit(solution)/shard_map/ppermute | solution.py:22
  7.1 2.0 %collective-permute-done.1.refs_0_.refs_1_ = bf16[64,1024]{1,0:T(8,128)(2,1)S(1)} collective-permute-done((bf16[64,1024]{1,0:T(8,128)(2,1)S(1)}, bf16[64,1024]{1,0:T(8,128)(2,1)S(1)}, u32[]{:S(2)}, u32[]{:S(2)}) %collective-permute-start.1) | collective-permute-done | bytes 131104 | tf_op jit(solution)/shard_map/ppermute | solution.py:22
  9.0 1.8 %forward.6 = (bf16[64,1024]{1,0:T(8,128)(2,1)S(1)}, f32[8,128]{1,0:T(8,128)S(1)}) custom-call(bf16[64,1024]{1,0:T(8,128)(2,1)S(1)} %collective-permute-done.1.refs_0_.refs_1_, f32[1,1024]{1,0:T(1,128)S(1)} %get-tuple-element.79.refs_1_.refs_4_, bf16[1024,2048]{1,0:T(8,128)(2,1)S(1)} %get-tuple-element.74.refs_2_.refs_1_.refs_5_.refs_4_, ...), custom_call_target="tpu_custom_call" | custom-call | flops 536870912 | bytes 8388608 | tf_op jit(solution)/shard_map/forward/pallas_call | solution.py:298
  10.8 1.3 %collective-permute-start.2 = (bf16[64,1024]{1,0:T(8,128)(2,1)S(1)}, bf16[64,1024]{1,0:T(8,128)(2,1)S(1)}, u32[]{:S(2)}, u32[]{:S(2)}) collective-permute-start(bf16[64,1024]{1,0:T(8,128)(2,1)S(1)} %get-tuple-element.89), channel_id=1, source_target_pairs={{1,2},{5,6},{9,10},{13,14},{17,18},{21,22},{25,26},{29,30}} | collective-permute-start | bytes 393224 | tf_op jit(solution)/shard_map/ppermute | solution.py:22
  12.1 0.0 copy-start
  12.1 1.8 %forward.7 = (bf16[64,1024]{1,0:T(8,128)(2,1)S(1)}, f32[8,128]{1,0:T(8,128)S(1)}) custom-call(bf16[64,1024]{1,0:T(8,128)(2,1)S(1)} %collective-permute-done.refs_0_.refs_1_, f32[1,1024]{1,0:T(1,128)S(1)} %get-tuple-element.79.refs_1_.refs_4_, bf16[1024,2048]{1,0:T(8,128)(2,1)S(1)} %get-tuple-element.74.refs_2_.refs_1_.refs_5_.refs_4_, ...), custom_call_target="tpu_custom_call" | custom-call | flops 536870912 | bytes 8388608 | tf_op jit(solution)/shard_map/forward/pallas_call | solution.py:298
  13.9 1.3 %collective-permute-start.4 = (bf16[64,1024]{1,0:T(8,128)(2,1)S(1)}, bf16[64,1024]{1,0:T(8,128)(2,1)S(1)}, u32[]{:S(2)}, u32[]{:S(2)}) collective-permute-start(bf16[64,1024]{1,0:T(8,128)(2,1)S(1)} %get-tuple-element.92), channel_id=1, source_target_pairs={{1,2},{5,6},{9,10},{13,14},{17,18},{21,22},{25,26},{29,30}} | collective-permute-start | bytes 393224 | tf_op jit(solution)/shard_map/ppermute | solution.py:22
  15.2 3.0 %turn.1 = (bf16[2048,1024]{1,0:T(8,128)(2,1)S(1)}, bf16[1024,2048]{1,0:T(8,128)(2,1)S(1)}, s32[2]{0:T(128)S(4)}, f32[64,2048]{1,0:T(8,128)S(1)}, f32[64,2048]{1,0:T(8,128)S(1)}, /*index=5*/f32[8,128]{1,0:T(8,128)S(1)}) custom-call(s32[8]{0:T(128)S(1)} %copy-done, bf16[1024,2048]{1,0:T(8,128)(2,1)S(1)} %get-tuple-element.74.refs_2_.refs_1_.refs_5_.refs_4_, ...), custom_call_target="tpu_custom_call" | custom-call | bytes 8388608 | tf_op jit(solution)/shard_map/turn/pallas_call | solution.py:298
  18.2 0.7 collective-permute-start.3
  18.9 0.7 collective-permute-start.6
  19.6 1.1 %save.2 = (bf16[64,1024]{1,0:T(8,128)(2,1)S(1)}, f32[64,1024]{1,0:T(8,128)S(1)}, f32[64,1]{1,0:T(8,128)S(1)}, f32[64,2048]{1,0:T(8,128)S(1)}, f32[8,128]{1,0:T(8,128)S(1)}) custom-call(bf16[2,64,1024]{2,1,0:T(8,128)(2,1)S(1)} %get-tuple-element.78.refs_0_, bf16[64,1024]{1,0:T(8,128)(2,1)S(1)} %collective-permute-done.1.refs_0_.refs_1_, ...), custom_call_target="tpu_custom_call" | custom-call | flops 268435456 | bytes 8388608 | tf_op jit(solution)/shard_map/save/pallas_call | solution.py:298
  20.7 0.2 backward.6
  20.9 0.7 collective-permute-start.5
  21.6 1.1 %save.3 = (bf16[64,1024]{1,0:T(8,128)(2,1)S(1)}, f32[64,1024]{1,0:T(8,128)S(1)}, f32[64,1]{1,0:T(8,128)S(1)}, f32[64,2048]{1,0:T(8,128)S(1)}, f32[8,128]{1,0:T(8,128)S(1)}) custom-call(bf16[2,64,1024]{2,1,0:T(8,128)(2,1)S(1)} %get-tuple-element.78.refs_0_, bf16[64,1024]{1,0:T(8,128)(2,1)S(1)} %collective-permute-done.refs_0_.refs_1_, ...), custom_call_target="tpu_custom_call" | custom-call | flops 268435456 | bytes 8388608 | tf_op jit(solution)/shard_map/save/pallas_call | solution.py:298
  22.8 0.7 collective-permute-start.8
  23.5 2.5 %collective-permute-start.12 = (bf16[128,1024]{1,0:T(8,128)(2,1)S(1)}, bf16[128,1024]{1,0:T(8,128)(2,1)S(1)}, u32[]{:S(2)}, u32[]{:S(2)}) collective-permute-start(bf16[128,1024]{1,0:T(8,128)(2,1)S(1)} %stack.1.refs_0_.refs_1_), channel_id=1, source_target_pairs={{0,24},{4,28},{8,16},{12,20},{16,8},{20,12},{24,0},{28,4},{1,25},{... | collective-permute-start | bytes 786440 | tf_op jit(solution)/shard_map/ppermute | solution.py:27
  26.0 0.2 collective-permute-start.11
  26.2 0.1 collective-permute-start.10
  26.3 1.3 %collective-permute-start.7 = (bf16[64,1024]{1,0:T(8,128)(2,1)S(1)}, bf16[64,1024]{1,0:T(8,128)(2,1)S(1)}, u32[]{:S(2)}, u32[]{:S(2)}) collective-permute-start(bf16[64,1024]{1,0:T(8,128)(2,1)S(1)} %get-tuple-element.109), channel_id=1, source_target_pairs={{2,1},{6,5},{10,9},{14,13},{18,17},{22,21},{26,25},{30,29}} | collective-permute-start | bytes 393224 | tf_op jit(solution)/shard_map/ppermute | solution.py:22
  27.7 1.3 %collective-permute-start.13 = (bf16[64,1024]{1,0:T(8,128)(2,1)S(1)}, bf16[64,1024]{1,0:T(8,128)(2,1)S(1)}, u32[]{:S(2)}, u32[]{:S(2)}) collective-permute-start(bf16[64,1024]{1,0:T(8,128)(2,1)S(1)} %get-tuple-element.116), channel_id=1, source_target_pairs={{2,1},{6,5},{10,9},{14,13},{18,17},{22,21},{26,25},{30,29}} | collective-permute-start | bytes 393224 | tf_op jit(solution)/shard_map/ppermute | solution.py:22
  29.0 7.5 %collective-permute-done.7.refs_0_.refs_2_ = bf16[64,1024]{1,0:T(8,128)(2,1)S(1)} collective-permute-done((bf16[64,1024]{1,0:T(8,128)(2,1)S(1)}, bf16[64,1024]{1,0:T(8,128)(2,1)S(1)}, u32[]{:S(2)}, u32[]{:S(2)}) %collective-permute-start.7) | collective-permute-done | bytes 131104 | tf_op jit(solution)/shard_map/ppermute | solution.py:22
  36.5 1.7 %backward.10 = (bf16[64,1024]{1,0:T(8,128)(2,1)S(1)}, f32[8,128]{1,0:T(8,128)S(1)}) custom-call(bf16[64,1024]{1,0:T(8,128)(2,1)S(1)} %collective-permute-done.7.refs_0_.refs_2_, f32[1,1024]{1,0:T(1,128)S(1)} %get-tuple-element.79.refs_1_.refs_4_, bf16[2048,1024]{1,0:T(8,128)(2,1)S(1)} %get-tuple-element.87.refs_2_, ...), custom_call_target="tpu_custom_call" | custom-call | flops 536870912 | bytes 8388608 | tf_op jit(solution)/shard_map/backward/pallas_call | solution.py:298
  38.2 1.3 %collective-permute-start.9 = (bf16[64,1024]{1,0:T(8,128)(2,1)S(1)}, bf16[64,1024]{1,0:T(8,128)(2,1)S(1)}, u32[]{:S(2)}, u32[]{:S(2)}) collective-permute-start(bf16[64,1024]{1,0:T(8,128)(2,1)S(1)} %get-tuple-element.113), channel_id=1, source_target_pairs={{1,0},{5,4},{9,8},{13,12},{17,16},{21,20},{25,24},{29,28}} | collective-permute-start | bytes 393224 | tf_op jit(solution)/shard_map/ppermute | solution.py:22
  39.6 0.4 collective-permute-done.13.refs_0_.refs_2_
  40.0 1.7 %backward.11 = (bf16[64,1024]{1,0:T(8,128)(2,1)S(1)}, f32[8,128]{1,0:T(8,128)S(1)}) custom-call(bf16[64,1024]{1,0:T(8,128)(2,1)S(1)} %collective-permute-done.13.refs_0_.refs_2_, f32[1,1024]{1,0:T(1,128)S(1)} %get-tuple-element.79.refs_1_.refs_4_, bf16[2048,1024]{1,0:T(8,128)(2,1)S(1)} %get-tuple-element.87.refs_2_, ...), custom_call_target="tpu_custom_call" | custom-call | flops 536870912 | bytes 8388608 | tf_op jit(solution)/shard_map/backward/pallas_call | solution.py:298
  41.7 1.3 %collective-permute-start.19 = (bf16[64,1024]{1,0:T(8,128)(2,1)S(1)}, bf16[64,1024]{1,0:T(8,128)(2,1)S(1)}, u32[]{:S(2)}, u32[]{:S(2)}) collective-permute-start(bf16[64,1024]{1,0:T(8,128)(2,1)S(1)} %get-tuple-element.126), channel_id=1, source_target_pairs={{1,0},{5,4},{9,8},{13,12},{17,16},{21,20},{25,24},{29,28}} | collective-permute-start | bytes 393224 | tf_op jit(solution)/shard_map/ppermute | solution.py:22
  43.0 0.6 slopes.1
  43.7 2.4 %collective-permute-start.16 = (bf16[64,1024]{1,0:T(8,128)(2,1)S(1)}, bf16[64,1024]{1,0:T(8,128)(2,1)S(1)}, u32[]{:S(2)}, u32[]{:S(2)}) collective-permute-start(bf16[64,1024]{1,0:T(8,128)(2,1)S(1)} %get-tuple-element.120.refs_0_), channel_id=1, source_target_pairs={{0,16},{4,20},{8,24},{12,28},{16,0},{20,4},{24,8},{28,12},{1,17},{... | collective-permute-start | bytes 393224 | tf_op jit(solution)/shard_map/ppermute | solution.py:27
  46.1 1.2 %collective-permute-start.15 = (bf16[64,1024]{1,0:T(8,128)(2,1)S(1)}, bf16[64,1024]{1,0:T(8,128)(2,1)S(1)}, u32[]{:S(2)}, u32[]{:S(2)}) collective-permute-start(bf16[64,1024]{1,0:T(8,128)(2,1)S(1)} %get-tuple-element.120.refs_0_), channel_id=1, source_target_pairs={{0,8},{4,12},{8,0},{12,4},{16,24},{20,28},{24,16},{28,20},{1,9},{5... | collective-permute-start | bytes 393224 | tf_op jit(solution)/shard_map/ppermute | solution.py:27
  47.3 0.1 collective-permute-start.14
  47.3 2.5 %late.1 = (f32[256,2048]{1,0:T(8,128)S(1)}, f32[256,2048]{1,0:T(8,128)S(1)}, f32[8,128]{1,0:T(8,128)S(1)}) custom-call(bf16[128,1024]{1,0:T(8,128)(2,1)S(1)} %stack.1.refs_0_.refs_1_, bf16[128,1024]{1,0:T(8,128)(2,1)S(1)} %collective-permute-done.10.refs_1_.refs_2_, ...), custom_call_target="tpu_custom_call", output_to_operand_aliasing={{0}: (7, {}), {1}: (8, {})} | custom-call | bytes 8388608 | tf_op jit(solution)/shard_map/late/pallas_call | solution.py:298
  50.0 1.5 %collective-permute-start.22 = (bf16[64,1024]{1,0:T(8,128)(2,1)S(1)}, bf16[64,1024]{1,0:T(8,128)(2,1)S(1)}, u32[]{:S(2)}, u32[]{:S(2)}) collective-permute-start(bf16[64,1024]{1,0:T(8,128)(2,1)S(1)} %pick.3.refs_0_), channel_id=1, source_target_pairs={{0,16},{4,20},{8,24},{12,28},{16,0},{20,4},{24,8},{28,12},{1,17},{... | collective-permute-start | bytes 393224 | tf_op jit(solution)/shard_map/ppermute | solution.py:27
  51.4 1.2 %collective-permute-start.21 = (bf16[64,1024]{1,0:T(8,128)(2,1)S(1)}, bf16[64,1024]{1,0:T(8,128)(2,1)S(1)}, u32[]{:S(2)}, u32[]{:S(2)}) collective-permute-start(bf16[64,1024]{1,0:T(8,128)(2,1)S(1)} %pick.3.refs_0_), channel_id=1, source_target_pairs={{0,8},{4,12},{8,0},{12,4},{16,24},{20,28},{24,16},{28,20},{1,9},{5... | collective-permute-start | bytes 393224 | tf_op jit(solution)/shard_map/ppermute | solution.py:27
  52.6 0.1 collective-permute-start.20
  52.7 5.3 %collective-permute-start.23 = (f32[128,1024]{1,0:T(8,128)S(1)}, f32[128,1024]{1,0:T(8,128)S(1)}, u32[]{:S(2)}, u32[]{:S(2)}) collective-permute-start(f32[128,1024]{1,0:T(8,128)S(1)} %get-tuple-element.129), channel_id=1, source_target_pairs={{0,4},{4,0},{8,12},{12,8},{16,20},{20,16},{24,28},{28,24},{1,5},{5... | collective-permute-start | bytes 1572872 | tf_op jit(solution)/shard_map/ppermute | solution.py:27
  57.9 0.8 %hidden.5.refs_2_ = bf16[128,2048]{1,0:T(8,128)(2,1)S(1)} custom-call(bf16[64,1024]{1,0:T(8,128)(2,1)S(1)} %collective-permute-done.15.refs_0_, bf16[64,1024]{1,0:T(8,128)(2,1)S(1)} %collective-permute-done.16.refs_1_, f32[1,1024]{1,0:T(1,128)S(1)} %get-tuple-element.76.refs_4_.refs_3_.refs_2_, bf16[1024,2048]{1,0:T(8,128)(2,1)S(1)} %get-tuple-element.88.refs_3_, ...), custom_call_target="tpu_custom_call" | custom-call | bytes 8388608 | tf_op jit(solution)/shard_map/hidden/pallas_call | solution.py:298
  58.7 0.1 collective-permute-start.18
  58.8 0.8 %hidden.4.refs_1_ = bf16[128,2048]{1,0:T(8,128)(2,1)S(1)} custom-call(bf16[64,1024]{1,0:T(8,128)(2,1)S(1)} %get-tuple-element.120.refs_0_, bf16[64,1024]{1,0:T(8,128)(2,1)S(1)} %collective-permute-done.14.refs_1_, f32[1,1024]{1,0:T(1,128)S(1)} %get-tuple-element.76.refs_4_.refs_3_.refs_2_, bf16[1024,2048]{1,0:T(8,128)(2,1)S(1)} %get-tuple-element.88.refs_3_, ...), custom_call_target="tpu_custom_call" | custom-call | bytes 8388608 | tf_op jit(solution)/shard_map/hidden/pallas_call | solution.py:298
  59.6 0.8 %collective-permute-start.17 = (bf16[128,2048]{1,0:T(8,128)(2,1)S(1)}, bf16[128,2048]{1,0:T(8,128)(2,1)S(1)}, u32[]{:S(2)}, u32[]{:S(2)}) collective-permute-start(bf16[128,2048]{1,0:T(8,128)(2,1)S(1)} %hidden.4.refs_1_), channel_id=1, source_target_pairs={{0,4},{4,0},{8,12},{12,8},{16,20},{20,16},{24,28},{28,24},{1,5},{5... | collective-permute-start | bytes 1572872 | tf_op jit(solution)/shard_map/ppermute | solution.py:27
  60.4 0.7 %hidden.7.refs_6_ = bf16[128,2048]{1,0:T(8,128)(2,1)S(1)} custom-call(bf16[64,1024]{1,0:T(8,128)(2,1)S(1)} %collective-permute-done.21.refs_0_, bf16[64,1024]{1,0:T(8,128)(2,1)S(1)} %collective-permute-done.22.refs_1_, f32[1,1024]{1,0:T(1,128)S(1)} %get-tuple-element.76.refs_4_.refs_3_.refs_2_, bf16[1024,2048]{1,0:T(8,128)(2,1)S(1)} %get-tuple-element.88.refs_3_, ...), custom_call_target="tpu_custom_call" | custom-call | bytes 8388608 | tf_op jit(solution)/shard_map/hidden/pallas_call | solution.py:298
  61.1 1.0 %collective-permute-start.25 = (bf16[128,2048]{1,0:T(8,128)(2,1)S(1)}, bf16[128,2048]{1,0:T(8,128)(2,1)S(1)}, u32[]{:S(2)}, u32[]{:S(2)}) collective-permute-start(bf16[128,2048]{1,0:T(8,128)(2,1)S(1)} %hidden.7.refs_6_), channel_id=1, source_target_pairs={{0,4},{4,0},{8,12},{12,8},{16,20},{20,16},{24,28},{28,24},{1,5},{5... | collective-permute-start | bytes 1572872 | tf_op jit(solution)/shard_map/ppermute | solution.py:27
  62.1 0.8 %hidden.6.refs_5_ = bf16[128,2048]{1,0:T(8,128)(2,1)S(1)} custom-call(bf16[64,1024]{1,0:T(8,128)(2,1)S(1)} %pick.3.refs_0_, bf16[64,1024]{1,0:T(8,128)(2,1)S(1)} %collective-permute-done.20.refs_1_, f32[1,1024]{1,0:T(1,128)S(1)} %get-tuple-element.76.refs_4_.refs_3_.refs_2_, bf16[1024,2048]{1,0:T(8,128)(2,1)S(1)} %get-tuple-element.88.refs_3_, ...), custom_call_target="tpu_custom_call" | custom-call | bytes 8388608 | tf_op jit(solution)/shard_map/hidden/pallas_call | solution.py:298
  62.9 1.7 %collective-permute-start.24 = (bf16[128,2048]{1,0:T(8,128)(2,1)S(1)}, bf16[128,2048]{1,0:T(8,128)(2,1)S(1)}, u32[]{:S(2)}, u32[]{:S(2)}) collective-permute-start(bf16[128,2048]{1,0:T(8,128)(2,1)S(1)} %hidden.6.refs_5_), channel_id=1, source_target_pairs={{0,4},{4,0},{8,12},{12,8},{16,20},{20,16},{24,28},{28,24},{1,5},{5... | collective-permute-start | bytes 1572872 | tf_op jit(solution)/shard_map/ppermute | solution.py:27
  64.6 1.9 %partial.1 = (f32[256,2048]{1,0:T(8,128)S(1)}, f32[128,1024]{1,0:T(8,128)}) custom-call(s32[2]{0:T(128)S(4)} %get-tuple-element.86.refs_0_, bf16[128,2048]{1,0:T(8,128)(2,1)S(1)} %hidden.4.refs_1_, bf16[128,2048]{1,0:T(8,128)(2,1)S(1)} %hidden.5.refs_2_, bf16[128,2048]{1,0:T(8,128)(2,1)S(1)} %collective-permute-done.17.refs_3_, ...), custom_call_target="tpu_custom_call" | custom-call | bytes 8388608 | tf_op jit(solution)/shard_map/partial/pallas_call | solution.py:298
  66.5 1.7 %square.1 = f32[256,2048]{1,0:T(8,128)} custom-call(s32[2]{0:T(128)S(4)} %get-tuple-element.86.refs_0_, bf16[128,2048]{1,0:T(8,128)(2,1)S(1)} %collective-permute-done.24.refs_1_, bf16[128,2048]{1,0:T(8,128)(2,1)S(1)} %collective-permute-done.25.refs_2_, f32[256,2048]{1,0:T(8,128)S(1)} %get-tuple-element.131.refs_3_, ...), custom_call_target="tpu_custom_call" | custom-call | bytes 8388608 | tf_op jit(solution)/shard_map/square/pallas_call | solution.py:298
  (34 shorter events, 0.2 us)
Async XLA Ops:
  0.8 8.3 %collective-permute-start.1 = (bf16[64,1024]{1,0:T(8,128)(2,1)S(1)}, bf16[64,1024]{1,0:T(8,128)(2,1)S(1)}, u32[]{:S(2)}, u32[]{:S(2)}) collective-permute-start(bf16[64,1024]{1,0:T(8,128)(2,1)S(1)} %get-tuple-element.82), channel_id=1, source_target_pairs={{0,1},{4,5},{8,9},{12,13},{16,17},{20,21},{24,25},{28,29}} | collective-permute-start | bytes 393224 | tf_op jit(solution)/shard_map/ppermute | solution.py:22
  5.8 6.4 %collective-permute-start = (bf16[64,1024]{1,0:T(8,128)(2,1)S(1)}, bf16[64,1024]{1,0:T(8,128)(2,1)S(1)}, u32[]{:S(2)}, u32[]{:S(2)}) collective-permute-start(bf16[64,1024]{1,0:T(8,128)(2,1)S(1)} %get-tuple-element.81), channel_id=1, source_target_pairs={{0,1},{4,5},{8,9},{12,13},{16,17},{20,21},{24,25},{28,29}} | collective-permute-start | bytes 393224 | tf_op jit(solution)/shard_map/ppermute | solution.py:22
  10.8 7.4 %collective-permute-start.2 = (bf16[64,1024]{1,0:T(8,128)(2,1)S(1)}, bf16[64,1024]{1,0:T(8,128)(2,1)S(1)}, u32[]{:S(2)}, u32[]{:S(2)}) collective-permute-start(bf16[64,1024]{1,0:T(8,128)(2,1)S(1)} %get-tuple-element.89), channel_id=1, source_target_pairs={{1,2},{5,6},{9,10},{13,14},{17,18},{21,22},{25,26},{29,30}} | collective-permute-start | bytes 393224 | tf_op jit(solution)/shard_map/ppermute | solution.py:22
  12.1 3.1 %copy-start = (s32[8]{0:T(128)S(1)}, s32[8]{0:T(128)}, u32[]{:S(2)}) copy-start(s32[8]{0:T(128)} %refs_0_.5) | copy-start | bytes 100
  13.9 5.0 %collective-permute-start.4 = (bf16[64,1024]{1,0:T(8,128)(2,1)S(1)}, bf16[64,1024]{1,0:T(8,128)(2,1)S(1)}, u32[]{:S(2)}, u32[]{:S(2)}) collective-permute-start(bf16[64,1024]{1,0:T(8,128)(2,1)S(1)} %get-tuple-element.92), channel_id=1, source_target_pairs={{1,2},{5,6},{9,10},{13,14},{17,18},{21,22},{25,26},{29,30}} | collective-permute-start | bytes 393224 | tf_op jit(solution)/shard_map/ppermute | solution.py:22
  18.2 1.4 %collective-permute-start.3 = (bf16[64,1024]{1,0:T(8,128)(2,1)S(1)}, bf16[64,1024]{1,0:T(8,128)(2,1)S(1)}, u32[]{:S(2)}, u32[]{:S(2)}) collective-permute-start(bf16[64,1024]{1,0:T(8,128)(2,1)S(1)} %get-tuple-element.91), channel_id=1, source_target_pairs={{2,3},{6,7},{10,11},{14,15},{18,19},{22,23},{26,27},{30,31}} | collective-permute-start | bytes 393224 | tf_op jit(solution)/shard_map/ppermute | solution.py:22
  18.9 2.7 %collective-permute-start.6 = (bf16[64,1024]{1,0:T(8,128)(2,1)S(1)}, bf16[64,1024]{1,0:T(8,128)(2,1)S(1)}, u32[]{:S(2)}, u32[]{:S(2)}) collective-permute-start(bf16[64,1024]{1,0:T(8,128)(2,1)S(1)} %get-tuple-element.101), channel_id=1, source_target_pairs={{2,3},{6,7},{10,11},{14,15},{18,19},{22,23},{26,27},{30,31}} | collective-permute-start | bytes 393224 | tf_op jit(solution)/shard_map/ppermute | solution.py:22
  20.9 5.4 %collective-permute-start.5 = (bf16[64,1024]{1,0:T(8,128)(2,1)S(1)}, bf16[64,1024]{1,0:T(8,128)(2,1)S(1)}, u32[]{:S(2)}, u32[]{:S(2)}) collective-permute-start(bf16[64,1024]{1,0:T(8,128)(2,1)S(1)} %get-tuple-element.100), channel_id=1, source_target_pairs={{3,2},{7,6},{11,10},{15,14},{19,18},{23,22},{27,26},{31,30}} | collective-permute-start | bytes 393224 | tf_op jit(solution)/shard_map/ppermute | solution.py:22
  22.8 4.9 %collective-permute-start.8 = (bf16[64,1024]{1,0:T(8,128)(2,1)S(1)}, bf16[64,1024]{1,0:T(8,128)(2,1)S(1)}, u32[]{:S(2)}, u32[]{:S(2)}) collective-permute-start(bf16[64,1024]{1,0:T(8,128)(2,1)S(1)} %get-tuple-element.110), channel_id=1, source_target_pairs={{3,2},{7,6},{11,10},{15,14},{19,18},{23,22},{27,26},{31,30}} | collective-permute-start | bytes 393224 | tf_op jit(solution)/shard_map/ppermute | solution.py:22
  23.5 16.1 %collective-permute-start.12 = (bf16[128,1024]{1,0:T(8,128)(2,1)S(1)}, bf16[128,1024]{1,0:T(8,128)(2,1)S(1)}, u32[]{:S(2)}, u32[]{:S(2)}) collective-permute-start(bf16[128,1024]{1,0:T(8,128)(2,1)S(1)} %stack.1.refs_0_.refs_1_), channel_id=1, source_target_pairs={{0,24},{4,28},{8,16},{12,20},{16,8},{20,12},{24,0},{28,4},{1,25},{... | collective-permute-start | bytes 786440 | tf_op jit(solution)/shard_map/ppermute | solution.py:27
  26.0 13.6 %collective-permute-start.11 = (bf16[128,1024]{1,0:T(8,128)(2,1)S(1)}, bf16[128,1024]{1,0:T(8,128)(2,1)S(1)}, u32[]{:S(2)}, u32[]{:S(2)}) collective-permute-start(bf16[128,1024]{1,0:T(8,128)(2,1)S(1)} %stack.1.refs_0_.refs_1_), channel_id=1, source_target_pairs={{0,16},{4,20},{8,24},{12,28},{16,0},{20,4},{24,8},{28,12},{1,17},{... | collective-permute-start | bytes 786440 | tf_op jit(solution)/shard_map/ppermute | solution.py:27
  26.2 13.4 %collective-permute-start.10 = (bf16[128,1024]{1,0:T(8,128)(2,1)S(1)}, bf16[128,1024]{1,0:T(8,128)(2,1)S(1)}, u32[]{:S(2)}, u32[]{:S(2)}) collective-permute-start(bf16[128,1024]{1,0:T(8,128)(2,1)S(1)} %stack.1.refs_0_.refs_1_), channel_id=1, source_target_pairs={{0,8},{4,12},{8,0},{12,4},{16,24},{20,28},{24,16},{28,20},{1,9},{5... | collective-permute-start | bytes 786440 | tf_op jit(solution)/shard_map/ppermute | solution.py:27
  26.3 10.2 %collective-permute-start.7 = (bf16[64,1024]{1,0:T(8,128)(2,1)S(1)}, bf16[64,1024]{1,0:T(8,128)(2,1)S(1)}, u32[]{:S(2)}, u32[]{:S(2)}) collective-permute-start(bf16[64,1024]{1,0:T(8,128)(2,1)S(1)} %get-tuple-element.109), channel_id=1, source_target_pairs={{2,1},{6,5},{10,9},{14,13},{18,17},{22,21},{26,25},{30,29}} | collective-permute-start | bytes 393224 | tf_op jit(solution)/shard_map/ppermute | solution.py:22
  27.7 12.3 %collective-permute-start.13 = (bf16[64,1024]{1,0:T(8,128)(2,1)S(1)}, bf16[64,1024]{1,0:T(8,128)(2,1)S(1)}, u32[]{:S(2)}, u32[]{:S(2)}) collective-permute-start(bf16[64,1024]{1,0:T(8,128)(2,1)S(1)} %get-tuple-element.116), channel_id=1, source_target_pairs={{2,1},{6,5},{10,9},{14,13},{18,17},{22,21},{26,25},{30,29}} | collective-permute-start | bytes 393224 | tf_op jit(solution)/shard_map/ppermute | solution.py:22
  38.2 5.4 %collective-permute-start.9 = (bf16[64,1024]{1,0:T(8,128)(2,1)S(1)}, bf16[64,1024]{1,0:T(8,128)(2,1)S(1)}, u32[]{:S(2)}, u32[]{:S(2)}) collective-permute-start(bf16[64,1024]{1,0:T(8,128)(2,1)S(1)} %get-tuple-element.113), channel_id=1, source_target_pairs={{1,0},{5,4},{9,8},{13,12},{17,16},{21,20},{25,24},{29,28}} | collective-permute-start | bytes 393224 | tf_op jit(solution)/shard_map/ppermute | solution.py:22
  41.7 8.2 %collective-permute-start.19 = (bf16[64,1024]{1,0:T(8,128)(2,1)S(1)}, bf16[64,1024]{1,0:T(8,128)(2,1)S(1)}, u32[]{:S(2)}, u32[]{:S(2)}) collective-permute-start(bf16[64,1024]{1,0:T(8,128)(2,1)S(1)} %get-tuple-element.126), channel_id=1, source_target_pairs={{1,0},{5,4},{9,8},{13,12},{17,16},{21,20},{25,24},{29,28}} | collective-permute-start | bytes 393224 | tf_op jit(solution)/shard_map/ppermute | solution.py:22
  43.7 9.0 %collective-permute-start.16 = (bf16[64,1024]{1,0:T(8,128)(2,1)S(1)}, bf16[64,1024]{1,0:T(8,128)(2,1)S(1)}, u32[]{:S(2)}, u32[]{:S(2)}) collective-permute-start(bf16[64,1024]{1,0:T(8,128)(2,1)S(1)} %get-tuple-element.120.refs_0_), channel_id=1, source_target_pairs={{0,16},{4,20},{8,24},{12,28},{16,0},{20,4},{24,8},{28,12},{1,17},{... | collective-permute-start | bytes 393224 | tf_op jit(solution)/shard_map/ppermute | solution.py:27
  46.1 6.6 %collective-permute-start.15 = (bf16[64,1024]{1,0:T(8,128)(2,1)S(1)}, bf16[64,1024]{1,0:T(8,128)(2,1)S(1)}, u32[]{:S(2)}, u32[]{:S(2)}) collective-permute-start(bf16[64,1024]{1,0:T(8,128)(2,1)S(1)} %get-tuple-element.120.refs_0_), channel_id=1, source_target_pairs={{0,8},{4,12},{8,0},{12,4},{16,24},{20,28},{24,16},{28,20},{1,9},{5... | collective-permute-start | bytes 393224 | tf_op jit(solution)/shard_map/ppermute | solution.py:27
  47.3 11.4 %collective-permute-start.14 = (bf16[64,1024]{1,0:T(8,128)(2,1)S(1)}, bf16[64,1024]{1,0:T(8,128)(2,1)S(1)}, u32[]{:S(2)}, u32[]{:S(2)}) collective-permute-start(bf16[64,1024]{1,0:T(8,128)(2,1)S(1)} %get-tuple-element.120.refs_0_), channel_id=1, source_target_pairs={{0,24},{4,28},{8,16},{12,20},{16,8},{20,12},{24,0},{28,4},{1,25},{... | collective-permute-start | bytes 393224 | tf_op jit(solution)/shard_map/ppermute | solution.py:27
  50.0 9.6 %collective-permute-start.22 = (bf16[64,1024]{1,0:T(8,128)(2,1)S(1)}, bf16[64,1024]{1,0:T(8,128)(2,1)S(1)}, u32[]{:S(2)}, u32[]{:S(2)}) collective-permute-start(bf16[64,1024]{1,0:T(8,128)(2,1)S(1)} %pick.3.refs_0_), channel_id=1, source_target_pairs={{0,16},{4,20},{8,24},{12,28},{16,0},{20,4},{24,8},{28,12},{1,17},{... | collective-permute-start | bytes 393224 | tf_op jit(solution)/shard_map/ppermute | solution.py:27
  51.4 9.0 %collective-permute-start.21 = (bf16[64,1024]{1,0:T(8,128)(2,1)S(1)}, bf16[64,1024]{1,0:T(8,128)(2,1)S(1)}, u32[]{:S(2)}, u32[]{:S(2)}) collective-permute-start(bf16[64,1024]{1,0:T(8,128)(2,1)S(1)} %pick.3.refs_0_), channel_id=1, source_target_pairs={{0,8},{4,12},{8,0},{12,4},{16,24},{20,28},{24,16},{28,20},{1,9},{5... | collective-permute-start | bytes 393224 | tf_op jit(solution)/shard_map/ppermute | solution.py:27
  52.6 9.5 %collective-permute-start.20 = (bf16[64,1024]{1,0:T(8,128)(2,1)S(1)}, bf16[64,1024]{1,0:T(8,128)(2,1)S(1)}, u32[]{:S(2)}, u32[]{:S(2)}) collective-permute-start(bf16[64,1024]{1,0:T(8,128)(2,1)S(1)} %pick.3.refs_0_), channel_id=1, source_target_pairs={{0,24},{4,28},{8,16},{12,20},{16,8},{20,12},{24,0},{28,4},{1,25},{... | collective-permute-start | bytes 393224 | tf_op jit(solution)/shard_map/ppermute | solution.py:27
  52.7 11.9 %collective-permute-start.23 = (f32[128,1024]{1,0:T(8,128)S(1)}, f32[128,1024]{1,0:T(8,128)S(1)}, u32[]{:S(2)}, u32[]{:S(2)}) collective-permute-start(f32[128,1024]{1,0:T(8,128)S(1)} %get-tuple-element.129), channel_id=1, source_target_pairs={{0,4},{4,0},{8,12},{12,8},{16,20},{20,16},{24,28},{28,24},{1,5},{5... | collective-permute-start | bytes 1572872 | tf_op jit(solution)/shard_map/ppermute | solution.py:27
  58.7 5.8 %collective-permute-start.18 = (bf16[128,2048]{1,0:T(8,128)(2,1)S(1)}, bf16[128,2048]{1,0:T(8,128)(2,1)S(1)}, u32[]{:S(2)}, u32[]{:S(2)}) collective-permute-start(bf16[128,2048]{1,0:T(8,128)(2,1)S(1)} %hidden.5.refs_2_), channel_id=1, source_target_pairs={{0,4},{4,0},{8,12},{12,8},{16,20},{20,16},{24,28},{28,24},{1,5},{5... | collective-permute-start | bytes 1572872 | tf_op jit(solution)/shard_map/ppermute | solution.py:27
  59.6 5.0 %collective-permute-start.17 = (bf16[128,2048]{1,0:T(8,128)(2,1)S(1)}, bf16[128,2048]{1,0:T(8,128)(2,1)S(1)}, u32[]{:S(2)}, u32[]{:S(2)}) collective-permute-start(bf16[128,2048]{1,0:T(8,128)(2,1)S(1)} %hidden.4.refs_1_), channel_id=1, source_target_pairs={{0,4},{4,0},{8,12},{12,8},{16,20},{20,16},{24,28},{28,24},{1,5},{5... | collective-permute-start | bytes 1572872 | tf_op jit(solution)/shard_map/ppermute | solution.py:27
  61.1 5.4 %collective-permute-start.25 = (bf16[128,2048]{1,0:T(8,128)(2,1)S(1)}, bf16[128,2048]{1,0:T(8,128)(2,1)S(1)}, u32[]{:S(2)}, u32[]{:S(2)}) collective-permute-start(bf16[128,2048]{1,0:T(8,128)(2,1)S(1)} %hidden.7.refs_6_), channel_id=1, source_target_pairs={{0,4},{4,0},{8,12},{12,8},{16,20},{20,16},{24,28},{28,24},{1,5},{5... | collective-permute-start | bytes 1572872 | tf_op jit(solution)/shard_map/ppermute | solution.py:27
  62.9 3.6 %collective-permute-start.24 = (bf16[128,2048]{1,0:T(8,128)(2,1)S(1)}, bf16[128,2048]{1,0:T(8,128)(2,1)S(1)}, u32[]{:S(2)}, u32[]{:S(2)}) collective-permute-start(bf16[128,2048]{1,0:T(8,128)(2,1)S(1)} %hidden.6.refs_5_), channel_id=1, source_target_pairs={{0,4},{4,0},{8,12},{12,8},{16,20},{20,16},{24,28},{28,24},{1,5},{5... | collective-permute-start | bytes 1572872 | tf_op jit(solution)/shard_map/ppermute | solution.py:27

commit v6 on v5

--- a/solution.py
+++ b/solution.py
@@ -388,7 +388,7 @@
         aliases={len(far) + index: index for index in range(len(far))},
     )
     paired = owners in (2, 4, 8) and not (width // owners % 128 or width_hidden // owners % 128)
-    masks = range(2, owners, 2)
+    masks = range(owners - 2, 0, -2)
     gain, given, weight_in, weight_out, scales, asked = [pinned(value) for value in near]
     for step in range(sections - 1):
         for m in batches:

time: 68.6 us -> 68.1 us (level)
  starting transfers between devices: 31 us -> 30.3 us
    ppermute x14, starting transfers between devices: 18 us -> 17.3 us  [swapped(): lax.ppermute(value, axis, [(source, source ^ mask) for source in range(co...]
where the time goes in v6:
time: 68.1 us; the launch traced here: 67.7 us
  starting transfers between devices  30.3 us (44%)
  Pallas kernels  26 us (38%)
  waiting for transfers between devices  10.1 us (15%)
  between operations  1.27 us (2%)
    pallas_call x28, Pallas kernels, __call__(): pl.pallas_call(body, in_specs=(specs or [IN_VMEM] * count) + [IN_VMEM] *...  26 us
    ppermute x14, starting transfers between devices, swapped(): lax.ppermute(value, axis, [(source, source ^ mask) for source in range(co...  17.3 us
    ppermute x12, starting transfers between devices, hop(): return lax.ppermute(value, 'section', [(source, source + steps)])  13 us
    ppermute x12, waiting for transfers between devices, hop(): return lax.ppermute(value, 'section', [(source, source + steps)])  10 us
  transfers between devices with their start and end apart: 26, of which 3 were waited for; matrix products, arithmetic and copies ran while one was open for 0% of the time, Pallas kernels for 36%

profile of v6, /device:TPU:9, one launch (start us, length us, event | category | flops | bytes accessed | tf_op | source)
XLA Modules:
  0.0 67.7 jit_solution(16351796186666477230)
XLA Ops:
  0.6 0.1 first.1
  0.8 1.3 %collective-permute-start.1 = (bf16[64,1024]{1,0:T(8,128)(2,1)S(1)}, bf16[64,1024]{1,0:T(8,128)(2,1)S(1)}, u32[]{:S(2)}, u32[]{:S(2)}) collective-permute-start(bf16[64,1024]{1,0:T(8,128)(2,1)S(1)} %get-tuple-element.82), channel_id=1, source_target_pairs={{0,1},{4,5},{8,9},{12,13},{16,17},{20,21},{24,25},{28,29}} | collective-permute-start | bytes 393224 | tf_op jit(solution)/shard_map/ppermute | solution.py:22
  2.1 3.7 %load.1 = (f32[1,1024]{1,0:T(1,128)S(1)}, bf16[2,64,1024]{2,1,0:T(8,128)(2,1)S(1)}, bf16[1024,2048]{1,0:T(8,128)(2,1)S(1)}, bf16[2048,1024]{1,0:T(8,128)(2,1)S(1...) custom-call(f32[1,1024]{1,0:T(1,128)} %refs_0_.4, ...), custom_call_target="tpu_custom_call", output_to_operand_aliasing={{0}: (6, {}), {1}: (7, {}), {2}: (8, {}), {3}: (9, {}), {4}... | custom-call | bytes 8388608 | tf_op jit(solution)/shard_map/load/pallas_call | solution.py:298
  5.8 1.3 %collective-permute-start = (bf16[64,1024]{1,0:T(8,128)(2,1)S(1)}, bf16[64,1024]{1,0:T(8,128)(2,1)S(1)}, u32[]{:S(2)}, u32[]{:S(2)}) collective-permute-start(bf16[64,1024]{1,0:T(8,128)(2,1)S(1)} %get-tuple-element.81), channel_id=1, source_target_pairs={{0,1},{4,5},{8,9},{12,13},{16,17},{20,21},{24,25},{28,29}} | collective-permute-start | bytes 393224 | tf_op jit(solution)/shard_map/ppermute | solution.py:22
  7.1 2.0 %collective-permute-done.1.refs_0_.refs_1_ = bf16[64,1024]{1,0:T(8,128)(2,1)S(1)} collective-permute-done((bf16[64,1024]{1,0:T(8,128)(2,1)S(1)}, bf16[64,1024]{1,0:T(8,128)(2,1)S(1)}, u32[]{:S(2)}, u32[]{:S(2)}) %collective-permute-start.1) | collective-permute-done | bytes 131104 | tf_op jit(solution)/shard_map/ppermute | solution.py:22
  9.0 1.8 %forward.6 = (bf16[64,1024]{1,0:T(8,128)(2,1)S(1)}, f32[8,128]{1,0:T(8,128)S(1)}) custom-call(bf16[64,1024]{1,0:T(8,128)(2,1)S(1)} %collective-permute-done.1.refs_0_.refs_1_, f32[1,1024]{1,0:T(1,128)S(1)} %get-tuple-element.79.refs_1_.refs_4_, bf16[1024,2048]{1,0:T(8,128)(2,1)S(1)} %get-tuple-element.74.refs_2_.refs_1_.refs_5_.refs_4_, ...), custom_call_target="tpu_custom_call" | custom-call | flops 536870912 | bytes 8388608 | tf_op jit(solution)/shard_map/forward/pallas_call | solution.py:298
  10.8 1.3 %collective-permute-start.2 = (bf16[64,1024]{1,0:T(8,128)(2,1)S(1)}, bf16[64,1024]{1,0:T(8,128)(2,1)S(1)}, u32[]{:S(2)}, u32[]{:S(2)}) collective-permute-start(bf16[64,1024]{1,0:T(8,128)(2,1)S(1)} %get-tuple-element.89), channel_id=1, source_target_pairs={{1,2},{5,6},{9,10},{13,14},{17,18},{21,22},{25,26},{29,30}} | collective-permute-start | bytes 393224 | tf_op jit(solution)/shard_map/ppermute | solution.py:22
  12.1 0.0 copy-start
  12.1 1.8 %forward.7 = (bf16[64,1024]{1,0:T(8,128)(2,1)S(1)}, f32[8,128]{1,0:T(8,128)S(1)}) custom-call(bf16[64,1024]{1,0:T(8,128)(2,1)S(1)} %collective-permute-done.refs_0_.refs_1_, f32[1,1024]{1,0:T(1,128)S(1)} %get-tuple-element.79.refs_1_.refs_4_, bf16[1024,2048]{1,0:T(8,128)(2,1)S(1)} %get-tuple-element.74.refs_2_.refs_1_.refs_5_.refs_4_, ...), custom_call_target="tpu_custom_call" | custom-call | flops 536870912 | bytes 8388608 | tf_op jit(solution)/shard_map/forward/pallas_call | solution.py:298
  13.9 1.3 %collective-permute-start.4 = (bf16[64,1024]{1,0:T(8,128)(2,1)S(1)}, bf16[64,1024]{1,0:T(8,128)(2,1)S(1)}, u32[]{:S(2)}, u32[]{:S(2)}) collective-permute-start(bf16[64,1024]{1,0:T(8,128)(2,1)S(1)} %get-tuple-element.92), channel_id=1, source_target_pairs={{1,2},{5,6},{9,10},{13,14},{17,18},{21,22},{25,26},{29,30}} | collective-permute-start | bytes 393224 | tf_op jit(solution)/shard_map/ppermute | solution.py:22
  15.2 3.0 %turn.1 = (bf16[2048,1024]{1,0:T(8,128)(2,1)S(1)}, bf16[1024,2048]{1,0:T(8,128)(2,1)S(1)}, s32[2]{0:T(128)S(4)}, f32[64,2048]{1,0:T(8,128)S(1)}, f32[64,2048]{1,0:T(8,128)S(1)}, /*index=5*/f32[8,128]{1,0:T(8,128)S(1)}) custom-call(s32[8]{0:T(128)S(1)} %copy-done, bf16[1024,2048]{1,0:T(8,128)(2,1)S(1)} %get-tuple-element.74.refs_2_.refs_1_.refs_5_.refs_4_, ...), custom_call_target="tpu_custom_call" | custom-call | bytes 8388608 | tf_op jit(solution)/shard_map/turn/pallas_call | solution.py:298
  18.2 0.7 collective-permute-start.3
  18.9 0.7 collective-permute-start.6
  19.6 1.1 %save.2 = (bf16[64,1024]{1,0:T(8,128)(2,1)S(1)}, f32[64,1024]{1,0:T(8,128)S(1)}, f32[64,1]{1,0:T(8,128)S(1)}, f32[64,2048]{1,0:T(8,128)S(1)}, f32[8,128]{1,0:T(8,128)S(1)}) custom-call(bf16[2,64,1024]{2,1,0:T(8,128)(2,1)S(1)} %get-tuple-element.78.refs_0_, bf16[64,1024]{1,0:T(8,128)(2,1)S(1)} %collective-permute-done.1.refs_0_.refs_1_, ...), custom_call_target="tpu_custom_call" | custom-call | flops 268435456 | bytes 8388608 | tf_op jit(solution)/shard_map/save/pallas_call | solution.py:298
  20.7 0.2 backward.6
  20.9 0.7 collective-permute-start.5
  21.6 1.1 %save.3 = (bf16[64,1024]{1,0:T(8,128)(2,1)S(1)}, f32[64,1024]{1,0:T(8,128)S(1)}, f32[64,1]{1,0:T(8,128)S(1)}, f32[64,2048]{1,0:T(8,128)S(1)}, f32[8,128]{1,0:T(8,128)S(1)}) custom-call(bf16[2,64,1024]{2,1,0:T(8,128)(2,1)S(1)} %get-tuple-element.78.refs_0_, bf16[64,1024]{1,0:T(8,128)(2,1)S(1)} %collective-permute-done.refs_0_.refs_1_, ...), custom_call_target="tpu_custom_call" | custom-call | flops 268435456 | bytes 8388608 | tf_op jit(solution)/shard_map/save/pallas_call | solution.py:298
  22.8 0.7 collective-permute-start.8
  23.5 1.5 %collective-permute-start.12 = (bf16[128,1024]{1,0:T(8,128)(2,1)S(1)}, bf16[128,1024]{1,0:T(8,128)(2,1)S(1)}, u32[]{:S(2)}, u32[]{:S(2)}) collective-permute-start(bf16[128,1024]{1,0:T(8,128)(2,1)S(1)} %stack.1.refs_0_.refs_1_), channel_id=1, source_target_pairs={{0,8},{4,12},{8,0},{12,4},{16,24},{20,28},{24,16},{28,20},{1,9},{5... | collective-permute-start | bytes 786440 | tf_op jit(solution)/shard_map/ppermute | solution.py:27
  25.0 1.2 %collective-permute-start.11 = (bf16[128,1024]{1,0:T(8,128)(2,1)S(1)}, bf16[128,1024]{1,0:T(8,128)(2,1)S(1)}, u32[]{:S(2)}, u32[]{:S(2)}) collective-permute-start(bf16[128,1024]{1,0:T(8,128)(2,1)S(1)} %stack.1.refs_0_.refs_1_), channel_id=1, source_target_pairs={{0,16},{4,20},{8,24},{12,28},{16,0},{20,4},{24,8},{28,12},{1,17},{... | collective-permute-start | bytes 786440 | tf_op jit(solution)/shard_map/ppermute | solution.py:27
  26.3 0.0 collective-permute-start.10
  26.3 1.3 %collective-permute-start.7 = (bf16[64,1024]{1,0:T(8,128)(2,1)S(1)}, bf16[64,1024]{1,0:T(8,128)(2,1)S(1)}, u32[]{:S(2)}, u32[]{:S(2)}) collective-permute-start(bf16[64,1024]{1,0:T(8,128)(2,1)S(1)} %get-tuple-element.109), channel_id=1, source_target_pairs={{2,1},{6,5},{10,9},{14,13},{18,17},{22,21},{26,25},{30,29}} | collective-permute-start | bytes 393224 | tf_op jit(solution)/shard_map/ppermute | solution.py:22
  27.6 1.3 %collective-permute-start.13 = (bf16[64,1024]{1,0:T(8,128)(2,1)S(1)}, bf16[64,1024]{1,0:T(8,128)(2,1)S(1)}, u32[]{:S(2)}, u32[]{:S(2)}) collective-permute-start(bf16[64,1024]{1,0:T(8,128)(2,1)S(1)} %get-tuple-element.116), channel_id=1, source_target_pairs={{2,1},{6,5},{10,9},{14,13},{18,17},{22,21},{26,25},{30,29}} | collective-permute-start | bytes 393224 | tf_op jit(solution)/shard_map/ppermute | solution.py:22
  28.9 7.6 %collective-permute-done.7.refs_0_.refs_2_ = bf16[64,1024]{1,0:T(8,128)(2,1)S(1)} collective-permute-done((bf16[64,1024]{1,0:T(8,128)(2,1)S(1)}, bf16[64,1024]{1,0:T(8,128)(2,1)S(1)}, u32[]{:S(2)}, u32[]{:S(2)}) %collective-permute-start.7) | collective-permute-done | bytes 131104 | tf_op jit(solution)/shard_map/ppermute | solution.py:22
  36.5 1.7 %backward.10 = (bf16[64,1024]{1,0:T(8,128)(2,1)S(1)}, f32[8,128]{1,0:T(8,128)S(1)}) custom-call(bf16[64,1024]{1,0:T(8,128)(2,1)S(1)} %collective-permute-done.7.refs_0_.refs_2_, f32[1,1024]{1,0:T(1,128)S(1)} %get-tuple-element.79.refs_1_.refs_4_, bf16[2048,1024]{1,0:T(8,128)(2,1)S(1)} %get-tuple-element.87.refs_2_, ...), custom_call_target="tpu_custom_call" | custom-call | flops 536870912 | bytes 8388608 | tf_op jit(solution)/shard_map/backward/pallas_call | solution.py:298
  38.2 1.3 %collective-permute-start.9 = (bf16[64,1024]{1,0:T(8,128)(2,1)S(1)}, bf16[64,1024]{1,0:T(8,128)(2,1)S(1)}, u32[]{:S(2)}, u32[]{:S(2)}) collective-permute-start(bf16[64,1024]{1,0:T(8,128)(2,1)S(1)} %get-tuple-element.113), channel_id=1, source_target_pairs={{1,0},{5,4},{9,8},{13,12},{17,16},{21,20},{25,24},{29,28}} | collective-permute-start | bytes 393224 | tf_op jit(solution)/shard_map/ppermute | solution.py:22
  39.6 0.4 collective-permute-done.13.refs_0_.refs_2_
  40.0 1.7 %backward.11 = (bf16[64,1024]{1,0:T(8,128)(2,1)S(1)}, f32[8,128]{1,0:T(8,128)S(1)}) custom-call(bf16[64,1024]{1,0:T(8,128)(2,1)S(1)} %collective-permute-done.13.refs_0_.refs_2_, f32[1,1024]{1,0:T(1,128)S(1)} %get-tuple-element.79.refs_1_.refs_4_, bf16[2048,1024]{1,0:T(8,128)(2,1)S(1)} %get-tuple-element.87.refs_2_, ...), custom_call_target="tpu_custom_call" | custom-call | flops 536870912 | bytes 8388608 | tf_op jit(solution)/shard_map/backward/pallas_call | solution.py:298
  41.7 1.3 %collective-permute-start.19 = (bf16[64,1024]{1,0:T(8,128)(2,1)S(1)}, bf16[64,1024]{1,0:T(8,128)(2,1)S(1)}, u32[]{:S(2)}, u32[]{:S(2)}) collective-permute-start(bf16[64,1024]{1,0:T(8,128)(2,1)S(1)} %get-tuple-element.126), channel_id=1, source_target_pairs={{1,0},{5,4},{9,8},{13,12},{17,16},{21,20},{25,24},{29,28}} | collective-permute-start | bytes 393224 | tf_op jit(solution)/shard_map/ppermute | solution.py:22
  43.0 0.6 slopes.1
  43.7 2.5 %collective-permute-start.16 = (bf16[64,1024]{1,0:T(8,128)(2,1)S(1)}, bf16[64,1024]{1,0:T(8,128)(2,1)S(1)}, u32[]{:S(2)}, u32[]{:S(2)}) collective-permute-start(bf16[64,1024]{1,0:T(8,128)(2,1)S(1)} %get-tuple-element.120.refs_0_), channel_id=1, source_target_pairs={{0,16},{4,20},{8,24},{12,28},{16,0},{20,4},{24,8},{28,12},{1,17},{... | collective-permute-start | bytes 393224 | tf_op jit(solution)/shard_map/ppermute | solution.py:27
  46.1 1.1 %collective-permute-start.15 = (bf16[64,1024]{1,0:T(8,128)(2,1)S(1)}, bf16[64,1024]{1,0:T(8,128)(2,1)S(1)}, u32[]{:S(2)}, u32[]{:S(2)}) collective-permute-start(bf16[64,1024]{1,0:T(8,128)(2,1)S(1)} %get-tuple-element.120.refs_0_), channel_id=1, source_target_pairs={{0,24},{4,28},{8,16},{12,20},{16,8},{20,12},{24,0},{28,4},{1,25},{... | collective-permute-start | bytes 393224 | tf_op jit(solution)/shard_map/ppermute | solution.py:27
  47.2 0.2 collective-permute-start.14
  47.4 2.5 %late.1 = (f32[256,2048]{1,0:T(8,128)S(1)}, f32[256,2048]{1,0:T(8,128)S(1)}, f32[8,128]{1,0:T(8,128)S(1)}) custom-call(bf16[128,1024]{1,0:T(8,128)(2,1)S(1)} %stack.1.refs_0_.refs_1_, bf16[128,1024]{1,0:T(8,128)(2,1)S(1)} %collective-permute-done.10.refs_1_.refs_2_, ...), custom_call_target="tpu_custom_call", output_to_operand_aliasing={{0}: (7, {}), {1}: (8, {})} | custom-call | bytes 8388608 | tf_op jit(solution)/shard_map/late/pallas_call | solution.py:298
  50.0 1.5 %collective-permute-start.22 = (bf16[64,1024]{1,0:T(8,128)(2,1)S(1)}, bf16[64,1024]{1,0:T(8,128)(2,1)S(1)}, u32[]{:S(2)}, u32[]{:S(2)}) collective-permute-start(bf16[64,1024]{1,0:T(8,128)(2,1)S(1)} %pick.3.refs_0_), channel_id=1, source_target_pairs={{0,16},{4,20},{8,24},{12,28},{16,0},{20,4},{24,8},{28,12},{1,17},{... | collective-permute-start | bytes 393224 | tf_op jit(solution)/shard_map/ppermute | solution.py:27
  51.4 1.1 %collective-permute-start.21 = (bf16[64,1024]{1,0:T(8,128)(2,1)S(1)}, bf16[64,1024]{1,0:T(8,128)(2,1)S(1)}, u32[]{:S(2)}, u32[]{:S(2)}) collective-permute-start(bf16[64,1024]{1,0:T(8,128)(2,1)S(1)} %pick.3.refs_0_), channel_id=1, source_target_pairs={{0,24},{4,28},{8,16},{12,20},{16,8},{20,12},{24,0},{28,4},{1,25},{... | collective-permute-start | bytes 393224 | tf_op jit(solution)/shard_map/ppermute | solution.py:27
  52.6 0.1 collective-permute-start.20
  52.7 5.2 %collective-permute-start.23 = (f32[128,1024]{1,0:T(8,128)S(1)}, f32[128,1024]{1,0:T(8,128)S(1)}, u32[]{:S(2)}, u32[]{:S(2)}) collective-permute-start(f32[128,1024]{1,0:T(8,128)S(1)} %get-tuple-element.129), channel_id=1, source_target_pairs={{0,4},{4,0},{8,12},{12,8},{16,20},{20,16},{24,28},{28,24},{1,5},{5... | collective-permute-start | bytes 1572872 | tf_op jit(solution)/shard_map/ppermute | solution.py:27
  57.9 0.8 %hidden.5.refs_2_ = bf16[128,2048]{1,0:T(8,128)(2,1)S(1)} custom-call(bf16[64,1024]{1,0:T(8,128)(2,1)S(1)} %collective-permute-done.15.refs_0_, bf16[64,1024]{1,0:T(8,128)(2,1)S(1)} %collective-permute-done.16.refs_1_, f32[1,1024]{1,0:T(1,128)S(1)} %get-tuple-element.76.refs_4_.refs_3_.refs_2_, bf16[1024,2048]{1,0:T(8,128)(2,1)S(1)} %get-tuple-element.88.refs_3_, ...), custom_call_target="tpu_custom_call" | custom-call | bytes 8388608 | tf_op jit(solution)/shard_map/hidden/pallas_call | solution.py:298
  58.7 0.1 collective-permute-start.18
  58.8 0.8 %hidden.4.refs_1_ = bf16[128,2048]{1,0:T(8,128)(2,1)S(1)} custom-call(bf16[64,1024]{1,0:T(8,128)(2,1)S(1)} %get-tuple-element.120.refs_0_, bf16[64,1024]{1,0:T(8,128)(2,1)S(1)} %collective-permute-done.14.refs_1_, f32[1,1024]{1,0:T(1,128)S(1)} %get-tuple-element.76.refs_4_.refs_3_.refs_2_, bf16[1024,2048]{1,0:T(8,128)(2,1)S(1)} %get-tuple-element.88.refs_3_, ...), custom_call_target="tpu_custom_call" | custom-call | bytes 8388608 | tf_op jit(solution)/shard_map/hidden/pallas_call | solution.py:298
  59.6 0.7 %collective-permute-start.17 = (bf16[128,2048]{1,0:T(8,128)(2,1)S(1)}, bf16[128,2048]{1,0:T(8,128)(2,1)S(1)}, u32[]{:S(2)}, u32[]{:S(2)}) collective-permute-start(bf16[128,2048]{1,0:T(8,128)(2,1)S(1)} %hidden.4.refs_1_), channel_id=1, source_target_pairs={{0,4},{4,0},{8,12},{12,8},{16,20},{20,16},{24,28},{28,24},{1,5},{5... | collective-permute-start | bytes 1572872 | tf_op jit(solution)/shard_map/ppermute | solution.py:27
  60.3 0.7 %hidden.7.refs_6_ = bf16[128,2048]{1,0:T(8,128)(2,1)S(1)} custom-call(bf16[64,1024]{1,0:T(8,128)(2,1)S(1)} %collective-permute-done.21.refs_0_, bf16[64,1024]{1,0:T(8,128)(2,1)S(1)} %collective-permute-done.22.refs_1_, f32[1,1024]{1,0:T(1,128)S(1)} %get-tuple-element.76.refs_4_.refs_3_.refs_2_, bf16[1024,2048]{1,0:T(8,128)(2,1)S(1)} %get-tuple-element.88.refs_3_, ...), custom_call_target="tpu_custom_call" | custom-call | bytes 8388608 | tf_op jit(solution)/shard_map/hidden/pallas_call | solution.py:298
  61.0 2.0 %collective-permute-start.25 = (bf16[128,2048]{1,0:T(8,128)(2,1)S(1)}, bf16[128,2048]{1,0:T(8,128)(2,1)S(1)}, u32[]{:S(2)}, u32[]{:S(2)}) collective-permute-start(bf16[128,2048]{1,0:T(8,128)(2,1)S(1)} %hidden.7.refs_6_), channel_id=1, source_target_pairs={{0,4},{4,0},{8,12},{12,8},{16,20},{20,16},{24,28},{28,24},{1,5},{5... | collective-permute-start | bytes 1572872 | tf_op jit(solution)/shard_map/ppermute | solution.py:27
  63.1 0.8 %hidden.6.refs_5_ = bf16[128,2048]{1,0:T(8,128)(2,1)S(1)} custom-call(bf16[64,1024]{1,0:T(8,128)(2,1)S(1)} %pick.3.refs_0_, bf16[64,1024]{1,0:T(8,128)(2,1)S(1)} %collective-permute-done.20.refs_1_, f32[1,1024]{1,0:T(1,128)S(1)} %get-tuple-element.76.refs_4_.refs_3_.refs_2_, bf16[1024,2048]{1,0:T(8,128)(2,1)S(1)} %get-tuple-element.88.refs_3_, ...), custom_call_target="tpu_custom_call" | custom-call | bytes 8388608 | tf_op jit(solution)/shard_map/hidden/pallas_call | solution.py:298
  63.8 0.1 collective-permute-start.24
  63.9 1.9 %partial.1 = (f32[256,2048]{1,0:T(8,128)S(1)}, f32[128,1024]{1,0:T(8,128)}) custom-call(s32[2]{0:T(128)S(4)} %get-tuple-element.86.refs_0_, bf16[128,2048]{1,0:T(8,128)(2,1)S(1)} %hidden.4.refs_1_, bf16[128,2048]{1,0:T(8,128)(2,1)S(1)} %hidden.5.refs_2_, bf16[128,2048]{1,0:T(8,128)(2,1)S(1)} %collective-permute-done.17.refs_3_, ...), custom_call_target="tpu_custom_call" | custom-call | bytes 8388608 | tf_op jit(solution)/shard_map/partial/pallas_call | solution.py:298
  65.8 1.7 %square.1 = f32[256,2048]{1,0:T(8,128)} custom-call(s32[2]{0:T(128)S(4)} %get-tuple-element.86.refs_0_, bf16[128,2048]{1,0:T(8,128)(2,1)S(1)} %collective-permute-done.24.refs_1_, bf16[128,2048]{1,0:T(8,128)(2,1)S(1)} %collective-permute-done.25.refs_2_, f32[256,2048]{1,0:T(8,128)S(1)} %get-tuple-element.131.refs_3_, ...), custom_call_target="tpu_custom_call" | custom-call | bytes 8388608 | tf_op jit(solution)/shard_map/square/pallas_call | solution.py:298
  (34 shorter events, 0.2 us)
Async XLA Ops:
  0.8 8.3 %collective-permute-start.1 = (bf16[64,1024]{1,0:T(8,128)(2,1)S(1)}, bf16[64,1024]{1,0:T(8,128)(2,1)S(1)}, u32[]{:S(2)}, u32[]{:S(2)}) collective-permute-start(bf16[64,1024]{1,0:T(8,128)(2,1)S(1)} %get-tuple-element.82), channel_id=1, source_target_pairs={{0,1},{4,5},{8,9},{12,13},{16,17},{20,21},{24,25},{28,29}} | collective-permute-start | bytes 393224 | tf_op jit(solution)/shard_map/ppermute | solution.py:22
  5.8 6.4 %collective-permute-start = (bf16[64,1024]{1,0:T(8,128)(2,1)S(1)}, bf16[64,1024]{1,0:T(8,128)(2,1)S(1)}, u32[]{:S(2)}, u32[]{:S(2)}) collective-permute-start(bf16[64,1024]{1,0:T(8,128)(2,1)S(1)} %get-tuple-element.81), channel_id=1, source_target_pairs={{0,1},{4,5},{8,9},{12,13},{16,17},{20,21},{24,25},{28,29}} | collective-permute-start | bytes 393224 | tf_op jit(solution)/shard_map/ppermute | solution.py:22
  10.8 7.4 %collective-permute-start.2 = (bf16[64,1024]{1,0:T(8,128)(2,1)S(1)}, bf16[64,1024]{1,0:T(8,128)(2,1)S(1)}, u32[]{:S(2)}, u32[]{:S(2)}) collective-permute-start(bf16[64,1024]{1,0:T(8,128)(2,1)S(1)} %get-tuple-element.89), channel_id=1, source_target_pairs={{1,2},{5,6},{9,10},{13,14},{17,18},{21,22},{25,26},{29,30}} | collective-permute-start | bytes 393224 | tf_op jit(solution)/shard_map/ppermute | solution.py:22
  12.1 3.1 %copy-start = (s32[8]{0:T(128)S(1)}, s32[8]{0:T(128)}, u32[]{:S(2)}) copy-start(s32[8]{0:T(128)} %refs_0_.5) | copy-start | bytes 100
  13.9 5.0 %collective-permute-start.4 = (bf16[64,1024]{1,0:T(8,128)(2,1)S(1)}, bf16[64,1024]{1,0:T(8,128)(2,1)S(1)}, u32[]{:S(2)}, u32[]{:S(2)}) collective-permute-start(bf16[64,1024]{1,0:T(8,128)(2,1)S(1)} %get-tuple-element.92), channel_id=1, source_target_pairs={{1,2},{5,6},{9,10},{13,14},{17,18},{21,22},{25,26},{29,30}} | collective-permute-start | bytes 393224 | tf_op jit(solution)/shard_map/ppermute | solution.py:22
  18.2 1.4 %collective-permute-start.3 = (bf16[64,1024]{1,0:T(8,128)(2,1)S(1)}, bf16[64,1024]{1,0:T(8,128)(2,1)S(1)}, u32[]{:S(2)}, u32[]{:S(2)}) collective-permute-start(bf16[64,1024]{1,0:T(8,128)(2,1)S(1)} %get-tuple-element.91), channel_id=1, source_target_pairs={{2,3},{6,7},{10,11},{14,15},{18,19},{22,23},{26,27},{30,31}} | collective-permute-start | bytes 393224 | tf_op jit(solution)/shard_map/ppermute | solution.py:22
  18.9 2.7 %collective-permute-start.6 = (bf16[64,1024]{1,0:T(8,128)(2,1)S(1)}, bf16[64,1024]{1,0:T(8,128)(2,1)S(1)}, u32[]{:S(2)}, u32[]{:S(2)}) collective-permute-start(bf16[64,1024]{1,0:T(8,128)(2,1)S(1)} %get-tuple-element.101), channel_id=1, source_target_pairs={{2,3},{6,7},{10,11},{14,15},{18,19},{22,23},{26,27},{30,31}} | collective-permute-start | bytes 393224 | tf_op jit(solution)/shard_map/ppermute | solution.py:22
  20.9 5.3 %collective-permute-start.5 = (bf16[64,1024]{1,0:T(8,128)(2,1)S(1)}, bf16[64,1024]{1,0:T(8,128)(2,1)S(1)}, u32[]{:S(2)}, u32[]{:S(2)}) collective-permute-start(bf16[64,1024]{1,0:T(8,128)(2,1)S(1)} %get-tuple-element.100), channel_id=1, source_target_pairs={{3,2},{7,6},{11,10},{15,14},{19,18},{23,22},{27,26},{31,30}} | collective-permute-start | bytes 393224 | tf_op jit(solution)/shard_map/ppermute | solution.py:22
  22.8 4.8 %collective-permute-start.8 = (bf16[64,1024]{1,0:T(8,128)(2,1)S(1)}, bf16[64,1024]{1,0:T(8,128)(2,1)S(1)}, u32[]{:S(2)}, u32[]{:S(2)}) collective-permute-start(bf16[64,1024]{1,0:T(8,128)(2,1)S(1)} %get-tuple-element.110), channel_id=1, source_target_pairs={{3,2},{7,6},{11,10},{15,14},{19,18},{23,22},{27,26},{31,30}} | collective-permute-start | bytes 393224 | tf_op jit(solution)/shard_map/ppermute | solution.py:22
  23.5 16.1 %collective-permute-start.12 = (bf16[128,1024]{1,0:T(8,128)(2,1)S(1)}, bf16[128,1024]{1,0:T(8,128)(2,1)S(1)}, u32[]{:S(2)}, u32[]{:S(2)}) collective-permute-start(bf16[128,1024]{1,0:T(8,128)(2,1)S(1)} %stack.1.refs_0_.refs_1_), channel_id=1, source_target_pairs={{0,8},{4,12},{8,0},{12,4},{16,24},{20,28},{24,16},{28,20},{1,9},{5... | collective-permute-start | bytes 786440 | tf_op jit(solution)/shard_map/ppermute | solution.py:27
  25.0 14.5 %collective-permute-start.11 = (bf16[128,1024]{1,0:T(8,128)(2,1)S(1)}, bf16[128,1024]{1,0:T(8,128)(2,1)S(1)}, u32[]{:S(2)}, u32[]{:S(2)}) collective-permute-start(bf16[128,1024]{1,0:T(8,128)(2,1)S(1)} %stack.1.refs_0_.refs_1_), channel_id=1, source_target_pairs={{0,16},{4,20},{8,24},{12,28},{16,0},{20,4},{24,8},{28,12},{1,17},{... | collective-permute-start | bytes 786440 | tf_op jit(solution)/shard_map/ppermute | solution.py:27
  26.3 13.3 %collective-permute-start.10 = (bf16[128,1024]{1,0:T(8,128)(2,1)S(1)}, bf16[128,1024]{1,0:T(8,128)(2,1)S(1)}, u32[]{:S(2)}, u32[]{:S(2)}) collective-permute-start(bf16[128,1024]{1,0:T(8,128)(2,1)S(1)} %stack.1.refs_0_.refs_1_), channel_id=1, source_target_pairs={{0,24},{4,28},{8,16},{12,20},{16,8},{20,12},{24,0},{28,4},{1,25},{... | collective-permute-start | bytes 786440 | tf_op jit(solution)/shard_map/ppermute | solution.py:27
  26.3 10.2 %collective-permute-start.7 = (bf16[64,1024]{1,0:T(8,128)(2,1)S(1)}, bf16[64,1024]{1,0:T(8,128)(2,1)S(1)}, u32[]{:S(2)}, u32[]{:S(2)}) collective-permute-start(bf16[64,1024]{1,0:T(8,128)(2,1)S(1)} %get-tuple-element.109), channel_id=1, source_target_pairs={{2,1},{6,5},{10,9},{14,13},{18,17},{22,21},{26,25},{30,29}} | collective-permute-start | bytes 393224 | tf_op jit(solution)/shard_map/ppermute | solution.py:22
  27.6 12.4 %collective-permute-start.13 = (bf16[64,1024]{1,0:T(8,128)(2,1)S(1)}, bf16[64,1024]{1,0:T(8,128)(2,1)S(1)}, u32[]{:S(2)}, u32[]{:S(2)}) collective-permute-start(bf16[64,1024]{1,0:T(8,128)(2,1)S(1)} %get-tuple-element.116), channel_id=1, source_target_pairs={{2,1},{6,5},{10,9},{14,13},{18,17},{22,21},{26,25},{30,29}} | collective-permute-start | bytes 393224 | tf_op jit(solution)/shard_map/ppermute | solution.py:22
  38.2 5.4 %collective-permute-start.9 = (bf16[64,1024]{1,0:T(8,128)(2,1)S(1)}, bf16[64,1024]{1,0:T(8,128)(2,1)S(1)}, u32[]{:S(2)}, u32[]{:S(2)}) collective-permute-start(bf16[64,1024]{1,0:T(8,128)(2,1)S(1)} %get-tuple-element.113), channel_id=1, source_target_pairs={{1,0},{5,4},{9,8},{13,12},{17,16},{21,20},{25,24},{29,28}} | collective-permute-start | bytes 393224 | tf_op jit(solution)/shard_map/ppermute | solution.py:22
  41.7 8.2 %collective-permute-start.19 = (bf16[64,1024]{1,0:T(8,128)(2,1)S(1)}, bf16[64,1024]{1,0:T(8,128)(2,1)S(1)}, u32[]{:S(2)}, u32[]{:S(2)}) collective-permute-start(bf16[64,1024]{1,0:T(8,128)(2,1)S(1)} %get-tuple-element.126), channel_id=1, source_target_pairs={{1,0},{5,4},{9,8},{13,12},{17,16},{21,20},{25,24},{29,28}} | collective-permute-start | bytes 393224 | tf_op jit(solution)/shard_map/ppermute | solution.py:22
  43.7 8.9 %collective-permute-start.16 = (bf16[64,1024]{1,0:T(8,128)(2,1)S(1)}, bf16[64,1024]{1,0:T(8,128)(2,1)S(1)}, u32[]{:S(2)}, u32[]{:S(2)}) collective-permute-start(bf16[64,1024]{1,0:T(8,128)(2,1)S(1)} %get-tuple-element.120.refs_0_), channel_id=1, source_target_pairs={{0,16},{4,20},{8,24},{12,28},{16,0},{20,4},{24,8},{28,12},{1,17},{... | collective-permute-start | bytes 393224 | tf_op jit(solution)/shard_map/ppermute | solution.py:27
  46.1 6.6 %collective-permute-start.15 = (bf16[64,1024]{1,0:T(8,128)(2,1)S(1)}, bf16[64,1024]{1,0:T(8,128)(2,1)S(1)}, u32[]{:S(2)}, u32[]{:S(2)}) collective-permute-start(bf16[64,1024]{1,0:T(8,128)(2,1)S(1)} %get-tuple-element.120.refs_0_), channel_id=1, source_target_pairs={{0,24},{4,28},{8,16},{12,20},{16,8},{20,12},{24,0},{28,4},{1,25},{... | collective-permute-start | bytes 393224 | tf_op jit(solution)/shard_map/ppermute | solution.py:27
  47.2 11.5 %collective-permute-start.14 = (bf16[64,1024]{1,0:T(8,128)(2,1)S(1)}, bf16[64,1024]{1,0:T(8,128)(2,1)S(1)}, u32[]{:S(2)}, u32[]{:S(2)}) collective-permute-start(bf16[64,1024]{1,0:T(8,128)(2,1)S(1)} %get-tuple-element.120.refs_0_), channel_id=1, source_target_pairs={{0,8},{4,12},{8,0},{12,4},{16,24},{20,28},{24,16},{28,20},{1,9},{5... | collective-permute-start | bytes 393224 | tf_op jit(solution)/shard_map/ppermute | solution.py:27
  50.0 9.6 %collective-permute-start.22 = (bf16[64,1024]{1,0:T(8,128)(2,1)S(1)}, bf16[64,1024]{1,0:T(8,128)(2,1)S(1)}, u32[]{:S(2)}, u32[]{:S(2)}) collective-permute-start(bf16[64,1024]{1,0:T(8,128)(2,1)S(1)} %pick.3.refs_0_), channel_id=1, source_target_pairs={{0,16},{4,20},{8,24},{12,28},{16,0},{20,4},{24,8},{28,12},{1,17},{... | collective-permute-start | bytes 393224 | tf_op jit(solution)/shard_map/ppermute | solution.py:27
  51.4 8.9 %collective-permute-start.21 = (bf16[64,1024]{1,0:T(8,128)(2,1)S(1)}, bf16[64,1024]{1,0:T(8,128)(2,1)S(1)}, u32[]{:S(2)}, u32[]{:S(2)}) collective-permute-start(bf16[64,1024]{1,0:T(8,128)(2,1)S(1)} %pick.3.refs_0_), channel_id=1, source_target_pairs={{0,24},{4,28},{8,16},{12,20},{16,8},{20,12},{24,0},{28,4},{1,25},{... | collective-permute-start | bytes 393224 | tf_op jit(solution)/shard_map/ppermute | solution.py:27
  52.6 10.5 %collective-permute-start.20 = (bf16[64,1024]{1,0:T(8,128)(2,1)S(1)}, bf16[64,1024]{1,0:T(8,128)(2,1)S(1)}, u32[]{:S(2)}, u32[]{:S(2)}) collective-permute-start(bf16[64,1024]{1,0:T(8,128)(2,1)S(1)} %pick.3.refs_0_), channel_id=1, source_target_pairs={{0,8},{4,12},{8,0},{12,4},{16,24},{20,28},{24,16},{28,20},{1,9},{5... | collective-permute-start | bytes 393224 | tf_op jit(solution)/shard_map/ppermute | solution.py:27
  52.7 11.2 %collective-permute-start.23 = (f32[128,1024]{1,0:T(8,128)S(1)}, f32[128,1024]{1,0:T(8,128)S(1)}, u32[]{:S(2)}, u32[]{:S(2)}) collective-permute-start(f32[128,1024]{1,0:T(8,128)S(1)} %get-tuple-element.129), channel_id=1, source_target_pairs={{0,4},{4,0},{8,12},{12,8},{16,20},{20,16},{24,28},{28,24},{1,5},{5... | collective-permute-start | bytes 1572872 | tf_op jit(solution)/shard_map/ppermute | solution.py:27
  58.7 5.2 %collective-permute-start.18 = (bf16[128,2048]{1,0:T(8,128)(2,1)S(1)}, bf16[128,2048]{1,0:T(8,128)(2,1)S(1)}, u32[]{:S(2)}, u32[]{:S(2)}) collective-permute-start(bf16[128,2048]{1,0:T(8,128)(2,1)S(1)} %hidden.5.refs_2_), channel_id=1, source_target_pairs={{0,4},{4,0},{8,12},{12,8},{16,20},{20,16},{24,28},{28,24},{1,5},{5... | collective-permute-start | bytes 1572872 | tf_op jit(solution)/shard_map/ppermute | solution.py:27
  59.6 4.3 %collective-permute-start.17 = (bf16[128,2048]{1,0:T(8,128)(2,1)S(1)}, bf16[128,2048]{1,0:T(8,128)(2,1)S(1)}, u32[]{:S(2)}, u32[]{:S(2)}) collective-permute-start(bf16[128,2048]{1,0:T(8,128)(2,1)S(1)} %hidden.4.refs_1_), channel_id=1, source_target_pairs={{0,4},{4,0},{8,12},{12,8},{16,20},{20,16},{24,28},{28,24},{1,5},{5... | collective-permute-start | bytes 1572872 | tf_op jit(solution)/shard_map/ppermute | solution.py:27
  61.0 4.8 %collective-permute-start.25 = (bf16[128,2048]{1,0:T(8,128)(2,1)S(1)}, bf16[128,2048]{1,0:T(8,128)(2,1)S(1)}, u32[]{:S(2)}, u32[]{:S(2)}) collective-permute-start(bf16[128,2048]{1,0:T(8,128)(2,1)S(1)} %hidden.7.refs_6_), channel_id=1, source_target_pairs={{0,4},{4,0},{8,12},{12,8},{16,20},{20,16},{24,28},{28,24},{1,5},{5... | collective-permute-start | bytes 1572872 | tf_op jit(solution)/shard_map/ppermute | solution.py:27
  63.8 2.0 %collective-permute-start.24 = (bf16[128,2048]{1,0:T(8,128)(2,1)S(1)}, bf16[128,2048]{1,0:T(8,128)(2,1)S(1)}, u32[]{:S(2)}, u32[]{:S(2)}) collective-permute-start(bf16[128,2048]{1,0:T(8,128)(2,1)S(1)} %hidden.6.refs_5_), channel_id=1, source_target_pairs={{0,4},{4,0},{8,12},{12,8},{16,20},{20,16},{24,28},{28,24},{1,5},{5... | collective-permute-start | bytes 1572872 | tf_op jit(solution)/shard_map/ppermute | solution.py:27

commit v7 on v6

--- a/solution.py
+++ b/solution.py
@@ -73,7 +73,7 @@
 
     @pl.when(lax.axis_index("section") == 0)
     def _():
-        copies = arrivals(far, near, arrived)
+        copies = arrivals(far, near, arrived)[:-1]
         for copy in copies:
             copy.start()
         copies[0].wait()
@@ -89,8 +89,7 @@
             copy.wait()
             term = dot(acted[:, rows], weight_out[rows, :])
             branch = term if branch is None else branch + term
-        for copy in copies[-2:]:
-            copy.wait()
+        copies[-1].wait()
         out[...] = (x + scales[...] * branch).astype(BF16)
 
 

time: 68.1 us -> 68.1 us (level)
  no operation moved by 1% of the time
where the time goes in v7:
time: 68.1 us; the launch traced here: 67.7 us
  starting transfers between devices  30.3 us (44%)
  Pallas kernels  26.1 us (38%)
  waiting for transfers between devices  10.1 us (15%)
  between operations  1.28 us (2%)
    pallas_call x28, Pallas kernels, __call__(): pl.pallas_call(body, in_specs=(specs or [IN_VMEM] * count) + [IN_VMEM] *...  26.1 us
    ppermute x14, starting transfers between devices, swapped(): lax.ppermute(value, axis, [(source, source ^ mask) for source in range(co...  17.3 us
    ppermute x12, starting transfers between devices, hop(): return lax.ppermute(value, 'section', [(source, source + steps)])  13 us
    ppermute x12, waiting for transfers between devices, hop(): return lax.ppermute(value, 'section', [(source, source + steps)])  10 us
  transfers between devices with their start and end apart: 26, of which 3 were waited for; matrix products, arithmetic and copies ran while one was open for 0% of the time, Pallas kernels for 36%

profile of v7, /device:TPU:9, one launch (start us, length us, event | category | flops | bytes accessed | tf_op | source)
XLA Modules:
  0.0 67.7 jit_solution(6763797733685473287)
XLA Ops:
  0.6 0.1 first.1
  0.8 1.3 %collective-permute-start.1 = (bf16[64,1024]{1,0:T(8,128)(2,1)S(1)}, bf16[64,1024]{1,0:T(8,128)(2,1)S(1)}, u32[]{:S(2)}, u32[]{:S(2)}) collective-permute-start(bf16[64,1024]{1,0:T(8,128)(2,1)S(1)} %get-tuple-element.82), channel_id=1, source_target_pairs={{0,1},{4,5},{8,9},{12,13},{16,17},{20,21},{24,25},{28,29}} | collective-permute-start | bytes 393224 | tf_op jit(solution)/shard_map/ppermute | solution.py:22
  2.1 3.7 %load.1 = (f32[1,1024]{1,0:T(1,128)S(1)}, bf16[2,64,1024]{2,1,0:T(8,128)(2,1)S(1)}, bf16[1024,2048]{1,0:T(8,128)(2,1)S(1)}, bf16[2048,1024]{1,0:T(8,128)(2,1)S(1...) custom-call(f32[1,1024]{1,0:T(1,128)} %refs_0_.4, ...), custom_call_target="tpu_custom_call", output_to_operand_aliasing={{0}: (6, {}), {1}: (7, {}), {2}: (8, {}), {3}: (9, {}), {4}... | custom-call | bytes 8388608 | tf_op jit(solution)/shard_map/load/pallas_call | solution.py:297
  5.8 1.3 %collective-permute-start = (bf16[64,1024]{1,0:T(8,128)(2,1)S(1)}, bf16[64,1024]{1,0:T(8,128)(2,1)S(1)}, u32[]{:S(2)}, u32[]{:S(2)}) collective-permute-start(bf16[64,1024]{1,0:T(8,128)(2,1)S(1)} %get-tuple-element.81), channel_id=1, source_target_pairs={{0,1},{4,5},{8,9},{12,13},{16,17},{20,21},{24,25},{28,29}} | collective-permute-start | bytes 393224 | tf_op jit(solution)/shard_map/ppermute | solution.py:22
  7.1 2.0 %collective-permute-done.1.refs_0_.refs_1_ = bf16[64,1024]{1,0:T(8,128)(2,1)S(1)} collective-permute-done((bf16[64,1024]{1,0:T(8,128)(2,1)S(1)}, bf16[64,1024]{1,0:T(8,128)(2,1)S(1)}, u32[]{:S(2)}, u32[]{:S(2)}) %collective-permute-start.1) | collective-permute-done | bytes 131104 | tf_op jit(solution)/shard_map/ppermute | solution.py:22
  9.0 1.8 %forward.6 = (bf16[64,1024]{1,0:T(8,128)(2,1)S(1)}, f32[8,128]{1,0:T(8,128)S(1)}) custom-call(bf16[64,1024]{1,0:T(8,128)(2,1)S(1)} %collective-permute-done.1.refs_0_.refs_1_, f32[1,1024]{1,0:T(1,128)S(1)} %get-tuple-element.79.refs_1_.refs_4_, bf16[1024,2048]{1,0:T(8,128)(2,1)S(1)} %get-tuple-element.74.refs_2_.refs_1_.refs_5_.refs_4_, ...), custom_call_target="tpu_custom_call" | custom-call | flops 536870912 | bytes 8388608 | tf_op jit(solution)/shard_map/forward/pallas_call | solution.py:297
  10.8 1.3 %collective-permute-start.2 = (bf16[64,1024]{1,0:T(8,128)(2,1)S(1)}, bf16[64,1024]{1,0:T(8,128)(2,1)S(1)}, u32[]{:S(2)}, u32[]{:S(2)}) collective-permute-start(bf16[64,1024]{1,0:T(8,128)(2,1)S(1)} %get-tuple-element.89), channel_id=1, source_target_pairs={{1,2},{5,6},{9,10},{13,14},{17,18},{21,22},{25,26},{29,30}} | collective-permute-start | bytes 393224 | tf_op jit(solution)/shard_map/ppermute | solution.py:22
  12.1 0.0 copy-start
  12.1 1.8 %forward.7 = (bf16[64,1024]{1,0:T(8,128)(2,1)S(1)}, f32[8,128]{1,0:T(8,128)S(1)}) custom-call(bf16[64,1024]{1,0:T(8,128)(2,1)S(1)} %collective-permute-done.refs_0_.refs_1_, f32[1,1024]{1,0:T(1,128)S(1)} %get-tuple-element.79.refs_1_.refs_4_, bf16[1024,2048]{1,0:T(8,128)(2,1)S(1)} %get-tuple-element.74.refs_2_.refs_1_.refs_5_.refs_4_, ...), custom_call_target="tpu_custom_call" | custom-call | flops 536870912 | bytes 8388608 | tf_op jit(solution)/shard_map/forward/pallas_call | solution.py:297
  13.9 1.3 %collective-permute-start.4 = (bf16[64,1024]{1,0:T(8,128)(2,1)S(1)}, bf16[64,1024]{1,0:T(8,128)(2,1)S(1)}, u32[]{:S(2)}, u32[]{:S(2)}) collective-permute-start(bf16[64,1024]{1,0:T(8,128)(2,1)S(1)} %get-tuple-element.92), channel_id=1, source_target_pairs={{1,2},{5,6},{9,10},{13,14},{17,18},{21,22},{25,26},{29,30}} | collective-permute-start | bytes 393224 | tf_op jit(solution)/shard_map/ppermute | solution.py:22
  15.2 3.0 %turn.1 = (bf16[2048,1024]{1,0:T(8,128)(2,1)S(1)}, bf16[1024,2048]{1,0:T(8,128)(2,1)S(1)}, s32[2]{0:T(128)S(4)}, f32[64,2048]{1,0:T(8,128)S(1)}, f32[64,2048]{1,0:T(8,128)S(1)}, /*index=5*/f32[8,128]{1,0:T(8,128)S(1)}) custom-call(s32[8]{0:T(128)S(1)} %copy-done, bf16[1024,2048]{1,0:T(8,128)(2,1)S(1)} %get-tuple-element.74.refs_2_.refs_1_.refs_5_.refs_4_, ...), custom_call_target="tpu_custom_call" | custom-call | bytes 8388608 | tf_op jit(solution)/shard_map/turn/pallas_call | solution.py:297
  18.2 0.7 collective-permute-start.3
  18.9 0.7 collective-permute-start.6
  19.6 1.1 %save.2 = (bf16[64,1024]{1,0:T(8,128)(2,1)S(1)}, f32[64,1024]{1,0:T(8,128)S(1)}, f32[64,1]{1,0:T(8,128)S(1)}, f32[64,2048]{1,0:T(8,128)S(1)}, f32[8,128]{1,0:T(8,128)S(1)}) custom-call(bf16[2,64,1024]{2,1,0:T(8,128)(2,1)S(1)} %get-tuple-element.78.refs_0_, bf16[64,1024]{1,0:T(8,128)(2,1)S(1)} %collective-permute-done.1.refs_0_.refs_1_, ...), custom_call_target="tpu_custom_call" | custom-call | flops 268435456 | bytes 8388608 | tf_op jit(solution)/shard_map/save/pallas_call | solution.py:297
  20.7 0.2 backward.6
  20.9 0.7 collective-permute-start.5
  21.6 1.1 %save.3 = (bf16[64,1024]{1,0:T(8,128)(2,1)S(1)}, f32[64,1024]{1,0:T(8,128)S(1)}, f32[64,1]{1,0:T(8,128)S(1)}, f32[64,2048]{1,0:T(8,128)S(1)}, f32[8,128]{1,0:T(8,128)S(1)}) custom-call(bf16[2,64,1024]{2,1,0:T(8,128)(2,1)S(1)} %get-tuple-element.78.refs_0_, bf16[64,1024]{1,0:T(8,128)(2,1)S(1)} %collective-permute-done.refs_0_.refs_1_, ...), custom_call_target="tpu_custom_call" | custom-call | flops 268435456 | bytes 8388608 | tf_op jit(solution)/shard_map/save/pallas_call | solution.py:297
  22.8 0.7 collective-permute-start.8
  23.5 1.5 %collective-permute-start.12 = (bf16[128,1024]{1,0:T(8,128)(2,1)S(1)}, bf16[128,1024]{1,0:T(8,128)(2,1)S(1)}, u32[]{:S(2)}, u32[]{:S(2)}) collective-permute-start(bf16[128,1024]{1,0:T(8,128)(2,1)S(1)} %stack.1.refs_0_.refs_1_), channel_id=1, source_target_pairs={{0,8},{4,12},{8,0},{12,4},{16,24},{20,28},{24,16},{28,20},{1,9},{5... | collective-permute-start | bytes 786440 | tf_op jit(solution)/shard_map/ppermute | solution.py:27
  25.0 1.2 %collective-permute-start.11 = (bf16[128,1024]{1,0:T(8,128)(2,1)S(1)}, bf16[128,1024]{1,0:T(8,128)(2,1)S(1)}, u32[]{:S(2)}, u32[]{:S(2)}) collective-permute-start(bf16[128,1024]{1,0:T(8,128)(2,1)S(1)} %stack.1.refs_0_.refs_1_), channel_id=1, source_target_pairs={{0,16},{4,20},{8,24},{12,28},{16,0},{20,4},{24,8},{28,12},{1,17},{... | collective-permute-start | bytes 786440 | tf_op jit(solution)/shard_map/ppermute | solution.py:27
  26.3 0.0 collective-permute-start.10
  26.3 1.3 %collective-permute-start.7 = (bf16[64,1024]{1,0:T(8,128)(2,1)S(1)}, bf16[64,1024]{1,0:T(8,128)(2,1)S(1)}, u32[]{:S(2)}, u32[]{:S(2)}) collective-permute-start(bf16[64,1024]{1,0:T(8,128)(2,1)S(1)} %get-tuple-element.109), channel_id=1, source_target_pairs={{2,1},{6,5},{10,9},{14,13},{18,17},{22,21},{26,25},{30,29}} | collective-permute-start | bytes 393224 | tf_op jit(solution)/shard_map/ppermute | solution.py:22
  27.6 1.3 %collective-permute-start.13 = (bf16[64,1024]{1,0:T(8,128)(2,1)S(1)}, bf16[64,1024]{1,0:T(8,128)(2,1)S(1)}, u32[]{:S(2)}, u32[]{:S(2)}) collective-permute-start(bf16[64,1024]{1,0:T(8,128)(2,1)S(1)} %get-tuple-element.116), channel_id=1, source_target_pairs={{2,1},{6,5},{10,9},{14,13},{18,17},{22,21},{26,25},{30,29}} | collective-permute-start | bytes 393224 | tf_op jit(solution)/shard_map/ppermute | solution.py:22
  28.9 7.6 %collective-permute-done.7.refs_0_.refs_2_ = bf16[64,1024]{1,0:T(8,128)(2,1)S(1)} collective-permute-done((bf16[64,1024]{1,0:T(8,128)(2,1)S(1)}, bf16[64,1024]{1,0:T(8,128)(2,1)S(1)}, u32[]{:S(2)}, u32[]{:S(2)}) %collective-permute-start.7) | collective-permute-done | bytes 131104 | tf_op jit(solution)/shard_map/ppermute | solution.py:22
  36.5 1.7 %backward.10 = (bf16[64,1024]{1,0:T(8,128)(2,1)S(1)}, f32[8,128]{1,0:T(8,128)S(1)}) custom-call(bf16[64,1024]{1,0:T(8,128)(2,1)S(1)} %collective-permute-done.7.refs_0_.refs_2_, f32[1,1024]{1,0:T(1,128)S(1)} %get-tuple-element.79.refs_1_.refs_4_, bf16[2048,1024]{1,0:T(8,128)(2,1)S(1)} %get-tuple-element.87.refs_2_, ...), custom_call_target="tpu_custom_call" | custom-call | flops 536870912 | bytes 8388608 | tf_op jit(solution)/shard_map/backward/pallas_call | solution.py:297
  38.2 1.3 %collective-permute-start.9 = (bf16[64,1024]{1,0:T(8,128)(2,1)S(1)}, bf16[64,1024]{1,0:T(8,128)(2,1)S(1)}, u32[]{:S(2)}, u32[]{:S(2)}) collective-permute-start(bf16[64,1024]{1,0:T(8,128)(2,1)S(1)} %get-tuple-element.113), channel_id=1, source_target_pairs={{1,0},{5,4},{9,8},{13,12},{17,16},{21,20},{25,24},{29,28}} | collective-permute-start | bytes 393224 | tf_op jit(solution)/shard_map/ppermute | solution.py:22
  39.6 0.4 collective-permute-done.13.refs_0_.refs_2_
  40.0 1.7 %backward.11 = (bf16[64,1024]{1,0:T(8,128)(2,1)S(1)}, f32[8,128]{1,0:T(8,128)S(1)}) custom-call(bf16[64,1024]{1,0:T(8,128)(2,1)S(1)} %collective-permute-done.13.refs_0_.refs_2_, f32[1,1024]{1,0:T(1,128)S(1)} %get-tuple-element.79.refs_1_.refs_4_, bf16[2048,1024]{1,0:T(8,128)(2,1)S(1)} %get-tuple-element.87.refs_2_, ...), custom_call_target="tpu_custom_call" | custom-call | flops 536870912 | bytes 8388608 | tf_op jit(solution)/shard_map/backward/pallas_call | solution.py:297
  41.7 1.3 %collective-permute-start.19 = (bf16[64,1024]{1,0:T(8,128)(2,1)S(1)}, bf16[64,1024]{1,0:T(8,128)(2,1)S(1)}, u32[]{:S(2)}, u32[]{:S(2)}) collective-permute-start(bf16[64,1024]{1,0:T(8,128)(2,1)S(1)} %get-tuple-element.126), channel_id=1, source_target_pairs={{1,0},{5,4},{9,8},{13,12},{17,16},{21,20},{25,24},{29,28}} | collective-permute-start | bytes 393224 | tf_op jit(solution)/shard_map/ppermute | solution.py:22
  43.0 0.6 slopes.1
  43.7 2.4 %collective-permute-start.16 = (bf16[64,1024]{1,0:T(8,128)(2,1)S(1)}, bf16[64,1024]{1,0:T(8,128)(2,1)S(1)}, u32[]{:S(2)}, u32[]{:S(2)}) collective-permute-start(bf16[64,1024]{1,0:T(8,128)(2,1)S(1)} %get-tuple-element.120.refs_0_), channel_id=1, source_target_pairs={{0,16},{4,20},{8,24},{12,28},{16,0},{20,4},{24,8},{28,12},{1,17},{... | collective-permute-start | bytes 393224 | tf_op jit(solution)/shard_map/ppermute | solution.py:27
  46.1 1.2 %collective-permute-start.15 = (bf16[64,1024]{1,0:T(8,128)(2,1)S(1)}, bf16[64,1024]{1,0:T(8,128)(2,1)S(1)}, u32[]{:S(2)}, u32[]{:S(2)}) collective-permute-start(bf16[64,1024]{1,0:T(8,128)(2,1)S(1)} %get-tuple-element.120.refs_0_), channel_id=1, source_target_pairs={{0,24},{4,28},{8,16},{12,20},{16,8},{20,12},{24,0},{28,4},{1,25},{... | collective-permute-start | bytes 393224 | tf_op jit(solution)/shard_map/ppermute | solution.py:27
  47.3 0.1 collective-permute-start.14
  47.3 2.5 %late.1 = (f32[256,2048]{1,0:T(8,128)S(1)}, f32[256,2048]{1,0:T(8,128)S(1)}, f32[8,128]{1,0:T(8,128)S(1)}) custom-call(bf16[128,1024]{1,0:T(8,128)(2,1)S(1)} %stack.1.refs_0_.refs_1_, bf16[128,1024]{1,0:T(8,128)(2,1)S(1)} %collective-permute-done.10.refs_1_.refs_2_, ...), custom_call_target="tpu_custom_call", output_to_operand_aliasing={{0}: (7, {}), {1}: (8, {})} | custom-call | bytes 8388608 | tf_op jit(solution)/shard_map/late/pallas_call | solution.py:297
  50.0 1.5 %collective-permute-start.22 = (bf16[64,1024]{1,0:T(8,128)(2,1)S(1)}, bf16[64,1024]{1,0:T(8,128)(2,1)S(1)}, u32[]{:S(2)}, u32[]{:S(2)}) collective-permute-start(bf16[64,1024]{1,0:T(8,128)(2,1)S(1)} %pick.3.refs_0_), channel_id=1, source_target_pairs={{0,16},{4,20},{8,24},{12,28},{16,0},{20,4},{24,8},{28,12},{1,17},{... | collective-permute-start | bytes 393224 | tf_op jit(solution)/shard_map/ppermute | solution.py:27
  51.4 1.2 %collective-permute-start.21 = (bf16[64,1024]{1,0:T(8,128)(2,1)S(1)}, bf16[64,1024]{1,0:T(8,128)(2,1)S(1)}, u32[]{:S(2)}, u32[]{:S(2)}) collective-permute-start(bf16[64,1024]{1,0:T(8,128)(2,1)S(1)} %pick.3.refs_0_), channel_id=1, source_target_pairs={{0,24},{4,28},{8,16},{12,20},{16,8},{20,12},{24,0},{28,4},{1,25},{... | collective-permute-start | bytes 393224 | tf_op jit(solution)/shard_map/ppermute | solution.py:27
  52.6 0.1 collective-permute-start.20
  52.7 5.2 %collective-permute-start.23 = (f32[128,1024]{1,0:T(8,128)S(1)}, f32[128,1024]{1,0:T(8,128)S(1)}, u32[]{:S(2)}, u32[]{:S(2)}) collective-permute-start(f32[128,1024]{1,0:T(8,128)S(1)} %get-tuple-element.129), channel_id=1, source_target_pairs={{0,4},{4,0},{8,12},{12,8},{16,20},{20,16},{24,28},{28,24},{1,5},{5... | collective-permute-start | bytes 1572872 | tf_op jit(solution)/shard_map/ppermute | solution.py:27
  57.9 0.8 %hidden.5.refs_2_ = bf16[128,2048]{1,0:T(8,128)(2,1)S(1)} custom-call(bf16[64,1024]{1,0:T(8,128)(2,1)S(1)} %collective-permute-done.15.refs_0_, bf16[64,1024]{1,0:T(8,128)(2,1)S(1)} %collective-permute-done.16.refs_1_, f32[1,1024]{1,0:T(1,128)S(1)} %get-tuple-element.76.refs_4_.refs_3_.refs_2_, bf16[1024,2048]{1,0:T(8,128)(2,1)S(1)} %get-tuple-element.88.refs_3_, ...), custom_call_target="tpu_custom_call" | custom-call | bytes 8388608 | tf_op jit(solution)/shard_map/hidden/pallas_call | solution.py:297
  58.7 0.1 collective-permute-start.18
  58.8 0.8 %hidden.4.refs_1_ = bf16[128,2048]{1,0:T(8,128)(2,1)S(1)} custom-call(bf16[64,1024]{1,0:T(8,128)(2,1)S(1)} %get-tuple-element.120.refs_0_, bf16[64,1024]{1,0:T(8,128)(2,1)S(1)} %collective-permute-done.14.refs_1_, f32[1,1024]{1,0:T(1,128)S(1)} %get-tuple-element.76.refs_4_.refs_3_.refs_2_, bf16[1024,2048]{1,0:T(8,128)(2,1)S(1)} %get-tuple-element.88.refs_3_, ...), custom_call_target="tpu_custom_call" | custom-call | bytes 8388608 | tf_op jit(solution)/shard_map/hidden/pallas_call | solution.py:297
  59.6 0.7 %collective-permute-start.17 = (bf16[128,2048]{1,0:T(8,128)(2,1)S(1)}, bf16[128,2048]{1,0:T(8,128)(2,1)S(1)}, u32[]{:S(2)}, u32[]{:S(2)}) collective-permute-start(bf16[128,2048]{1,0:T(8,128)(2,1)S(1)} %hidden.4.refs_1_), channel_id=1, source_target_pairs={{0,4},{4,0},{8,12},{12,8},{16,20},{20,16},{24,28},{28,24},{1,5},{5... | collective-permute-start | bytes 1572872 | tf_op jit(solution)/shard_map/ppermute | solution.py:27
  60.3 0.8 %hidden.7.refs_6_ = bf16[128,2048]{1,0:T(8,128)(2,1)S(1)} custom-call(bf16[64,1024]{1,0:T(8,128)(2,1)S(1)} %collective-permute-done.21.refs_0_, bf16[64,1024]{1,0:T(8,128)(2,1)S(1)} %collective-permute-done.22.refs_1_, f32[1,1024]{1,0:T(1,128)S(1)} %get-tuple-element.76.refs_4_.refs_3_.refs_2_, bf16[1024,2048]{1,0:T(8,128)(2,1)S(1)} %get-tuple-element.88.refs_3_, ...), custom_call_target="tpu_custom_call" | custom-call | bytes 8388608 | tf_op jit(solution)/shard_map/hidden/pallas_call | solution.py:297
  61.0 2.0 %collective-permute-start.25 = (bf16[128,2048]{1,0:T(8,128)(2,1)S(1)}, bf16[128,2048]{1,0:T(8,128)(2,1)S(1)}, u32[]{:S(2)}, u32[]{:S(2)}) collective-permute-start(bf16[128,2048]{1,0:T(8,128)(2,1)S(1)} %hidden.7.refs_6_), channel_id=1, source_target_pairs={{0,4},{4,0},{8,12},{12,8},{16,20},{20,16},{24,28},{28,24},{1,5},{5... | collective-permute-start | bytes 1572872 | tf_op jit(solution)/shard_map/ppermute | solution.py:27
  63.0 0.8 %hidden.6.refs_5_ = bf16[128,2048]{1,0:T(8,128)(2,1)S(1)} custom-call(bf16[64,1024]{1,0:T(8,128)(2,1)S(1)} %pick.3.refs_0_, bf16[64,1024]{1,0:T(8,128)(2,1)S(1)} %collective-permute-done.20.refs_1_, f32[1,1024]{1,0:T(1,128)S(1)} %get-tuple-element.76.refs_4_.refs_3_.refs_2_, bf16[1024,2048]{1,0:T(8,128)(2,1)S(1)} %get-tuple-element.88.refs_3_, ...), custom_call_target="tpu_custom_call" | custom-call | bytes 8388608 | tf_op jit(solution)/shard_map/hidden/pallas_call | solution.py:297
  63.8 0.1 collective-permute-start.24
  63.9 1.9 %partial.1 = (f32[256,2048]{1,0:T(8,128)S(1)}, f32[128,1024]{1,0:T(8,128)}) custom-call(s32[2]{0:T(128)S(4)} %get-tuple-element.86.refs_0_, bf16[128,2048]{1,0:T(8,128)(2,1)S(1)} %hidden.4.refs_1_, bf16[128,2048]{1,0:T(8,128)(2,1)S(1)} %hidden.5.refs_2_, bf16[128,2048]{1,0:T(8,128)(2,1)S(1)} %collective-permute-done.17.refs_3_, ...), custom_call_target="tpu_custom_call" | custom-call | bytes 8388608 | tf_op jit(solution)/shard_map/partial/pallas_call | solution.py:297
  65.8 1.7 %square.1 = f32[256,2048]{1,0:T(8,128)} custom-call(s32[2]{0:T(128)S(4)} %get-tuple-element.86.refs_0_, bf16[128,2048]{1,0:T(8,128)(2,1)S(1)} %collective-permute-done.24.refs_1_, bf16[128,2048]{1,0:T(8,128)(2,1)S(1)} %collective-permute-done.25.refs_2_, f32[256,2048]{1,0:T(8,128)S(1)} %get-tuple-element.131.refs_3_, ...), custom_call_target="tpu_custom_call" | custom-call | bytes 8388608 | tf_op jit(solution)/shard_map/square/pallas_call | solution.py:297
  (34 shorter events, 0.2 us)
Async XLA Ops:
  0.8 8.3 %collective-permute-start.1 = (bf16[64,1024]{1,0:T(8,128)(2,1)S(1)}, bf16[64,1024]{1,0:T(8,128)(2,1)S(1)}, u32[]{:S(2)}, u32[]{:S(2)}) collective-permute-start(bf16[64,1024]{1,0:T(8,128)(2,1)S(1)} %get-tuple-element.82), channel_id=1, source_target_pairs={{0,1},{4,5},{8,9},{12,13},{16,17},{20,21},{24,25},{28,29}} | collective-permute-start | bytes 393224 | tf_op jit(solution)/shard_map/ppermute | solution.py:22
  5.8 6.4 %collective-permute-start = (bf16[64,1024]{1,0:T(8,128)(2,1)S(1)}, bf16[64,1024]{1,0:T(8,128)(2,1)S(1)}, u32[]{:S(2)}, u32[]{:S(2)}) collective-permute-start(bf16[64,1024]{1,0:T(8,128)(2,1)S(1)} %get-tuple-element.81), channel_id=1, source_target_pairs={{0,1},{4,5},{8,9},{12,13},{16,17},{20,21},{24,25},{28,29}} | collective-permute-start | bytes 393224 | tf_op jit(solution)/shard_map/ppermute | solution.py:22
  10.8 7.4 %collective-permute-start.2 = (bf16[64,1024]{1,0:T(8,128)(2,1)S(1)}, bf16[64,1024]{1,0:T(8,128)(2,1)S(1)}, u32[]{:S(2)}, u32[]{:S(2)}) collective-permute-start(bf16[64,1024]{1,0:T(8,128)(2,1)S(1)} %get-tuple-element.89), channel_id=1, source_target_pairs={{1,2},{5,6},{9,10},{13,14},{17,18},{21,22},{25,26},{29,30}} | collective-permute-start | bytes 393224 | tf_op jit(solution)/shard_map/ppermute | solution.py:22
  12.1 3.1 %copy-start = (s32[8]{0:T(128)S(1)}, s32[8]{0:T(128)}, u32[]{:S(2)}) copy-start(s32[8]{0:T(128)} %refs_0_.5) | copy-start | bytes 100
  13.9 5.0 %collective-permute-start.4 = (bf16[64,1024]{1,0:T(8,128)(2,1)S(1)}, bf16[64,1024]{1,0:T(8,128)(2,1)S(1)}, u32[]{:S(2)}, u32[]{:S(2)}) collective-permute-start(bf16[64,1024]{1,0:T(8,128)(2,1)S(1)} %get-tuple-element.92), channel_id=1, source_target_pairs={{1,2},{5,6},{9,10},{13,14},{17,18},{21,22},{25,26},{29,30}} | collective-permute-start | bytes 393224 | tf_op jit(solution)/shard_map/ppermute | solution.py:22
  18.2 1.4 %collective-permute-start.3 = (bf16[64,1024]{1,0:T(8,128)(2,1)S(1)}, bf16[64,1024]{1,0:T(8,128)(2,1)S(1)}, u32[]{:S(2)}, u32[]{:S(2)}) collective-permute-start(bf16[64,1024]{1,0:T(8,128)(2,1)S(1)} %get-tuple-element.91), channel_id=1, source_target_pairs={{2,3},{6,7},{10,11},{14,15},{18,19},{22,23},{26,27},{30,31}} | collective-permute-start | bytes 393224 | tf_op jit(solution)/shard_map/ppermute | solution.py:22
  18.9 2.7 %collective-permute-start.6 = (bf16[64,1024]{1,0:T(8,128)(2,1)S(1)}, bf16[64,1024]{1,0:T(8,128)(2,1)S(1)}, u32[]{:S(2)}, u32[]{:S(2)}) collective-permute-start(bf16[64,1024]{1,0:T(8,128)(2,1)S(1)} %get-tuple-element.101), channel_id=1, source_target_pairs={{2,3},{6,7},{10,11},{14,15},{18,19},{22,23},{26,27},{30,31}} | collective-permute-start | bytes 393224 | tf_op jit(solution)/shard_map/ppermute | solution.py:22
  20.9 5.3 %collective-permute-start.5 = (bf16[64,1024]{1,0:T(8,128)(2,1)S(1)}, bf16[64,1024]{1,0:T(8,128)(2,1)S(1)}, u32[]{:S(2)}, u32[]{:S(2)}) collective-permute-start(bf16[64,1024]{1,0:T(8,128)(2,1)S(1)} %get-tuple-element.100), channel_id=1, source_target_pairs={{3,2},{7,6},{11,10},{15,14},{19,18},{23,22},{27,26},{31,30}} | collective-permute-start | bytes 393224 | tf_op jit(solution)/shard_map/ppermute | solution.py:22
  22.8 4.8 %collective-permute-start.8 = (bf16[64,1024]{1,0:T(8,128)(2,1)S(1)}, bf16[64,1024]{1,0:T(8,128)(2,1)S(1)}, u32[]{:S(2)}, u32[]{:S(2)}) collective-permute-start(bf16[64,1024]{1,0:T(8,128)(2,1)S(1)} %get-tuple-element.110), channel_id=1, source_target_pairs={{3,2},{7,6},{11,10},{15,14},{19,18},{23,22},{27,26},{31,30}} | collective-permute-start | bytes 393224 | tf_op jit(solution)/shard_map/ppermute | solution.py:22
  23.5 16.1 %collective-permute-start.12 = (bf16[128,1024]{1,0:T(8,128)(2,1)S(1)}, bf16[128,1024]{1,0:T(8,128)(2,1)S(1)}, u32[]{:S(2)}, u32[]{:S(2)}) collective-permute-start(bf16[128,1024]{1,0:T(8,128)(2,1)S(1)} %stack.1.refs_0_.refs_1_), channel_id=1, source_target_pairs={{0,8},{4,12},{8,0},{12,4},{16,24},{20,28},{24,16},{28,20},{1,9},{5... | collective-permute-start | bytes 786440 | tf_op jit(solution)/shard_map/ppermute | solution.py:27
  25.0 14.5 %collective-permute-start.11 = (bf16[128,1024]{1,0:T(8,128)(2,1)S(1)}, bf16[128,1024]{1,0:T(8,128)(2,1)S(1)}, u32[]{:S(2)}, u32[]{:S(2)}) collective-permute-start(bf16[128,1024]{1,0:T(8,128)(2,1)S(1)} %stack.1.refs_0_.refs_1_), channel_id=1, source_target_pairs={{0,16},{4,20},{8,24},{12,28},{16,0},{20,4},{24,8},{28,12},{1,17},{... | collective-permute-start | bytes 786440 | tf_op jit(solution)/shard_map/ppermute | solution.py:27
  26.3 13.3 %collective-permute-start.10 = (bf16[128,1024]{1,0:T(8,128)(2,1)S(1)}, bf16[128,1024]{1,0:T(8,128)(2,1)S(1)}, u32[]{:S(2)}, u32[]{:S(2)}) collective-permute-start(bf16[128,1024]{1,0:T(8,128)(2,1)S(1)} %stack.1.refs_0_.refs_1_), channel_id=1, source_target_pairs={{0,24},{4,28},{8,16},{12,20},{16,8},{20,12},{24,0},{28,4},{1,25},{... | collective-permute-start | bytes 786440 | tf_op jit(solution)/shard_map/ppermute | solution.py:27
  26.3 10.2 %collective-permute-start.7 = (bf16[64,1024]{1,0:T(8,128)(2,1)S(1)}, bf16[64,1024]{1,0:T(8,128)(2,1)S(1)}, u32[]{:S(2)}, u32[]{:S(2)}) collective-permute-start(bf16[64,1024]{1,0:T(8,128)(2,1)S(1)} %get-tuple-element.109), channel_id=1, source_target_pairs={{2,1},{6,5},{10,9},{14,13},{18,17},{22,21},{26,25},{30,29}} | collective-permute-start | bytes 393224 | tf_op jit(solution)/shard_map/ppermute | solution.py:22
  27.6 12.4 %collective-permute-start.13 = (bf16[64,1024]{1,0:T(8,128)(2,1)S(1)}, bf16[64,1024]{1,0:T(8,128)(2,1)S(1)}, u32[]{:S(2)}, u32[]{:S(2)}) collective-permute-start(bf16[64,1024]{1,0:T(8,128)(2,1)S(1)} %get-tuple-element.116), channel_id=1, source_target_pairs={{2,1},{6,5},{10,9},{14,13},{18,17},{22,21},{26,25},{30,29}} | collective-permute-start | bytes 393224 | tf_op jit(solution)/shard_map/ppermute | solution.py:22
  38.2 5.4 %collective-permute-start.9 = (bf16[64,1024]{1,0:T(8,128)(2,1)S(1)}, bf16[64,1024]{1,0:T(8,128)(2,1)S(1)}, u32[]{:S(2)}, u32[]{:S(2)}) collective-permute-start(bf16[64,1024]{1,0:T(8,128)(2,1)S(1)} %get-tuple-element.113), channel_id=1, source_target_pairs={{1,0},{5,4},{9,8},{13,12},{17,16},{21,20},{25,24},{29,28}} | collective-permute-start | bytes 393224 | tf_op jit(solution)/shard_map/ppermute | solution.py:22
  41.7 8.2 %collective-permute-start.19 = (bf16[64,1024]{1,0:T(8,128)(2,1)S(1)}, bf16[64,1024]{1,0:T(8,128)(2,1)S(1)}, u32[]{:S(2)}, u32[]{:S(2)}) collective-permute-start(bf16[64,1024]{1,0:T(8,128)(2,1)S(1)} %get-tuple-element.126), channel_id=1, source_target_pairs={{1,0},{5,4},{9,8},{13,12},{17,16},{21,20},{25,24},{29,28}} | collective-permute-start | bytes 393224 | tf_op jit(solution)/shard_map/ppermute | solution.py:22
  43.7 8.9 %collective-permute-start.16 = (bf16[64,1024]{1,0:T(8,128)(2,1)S(1)}, bf16[64,1024]{1,0:T(8,128)(2,1)S(1)}, u32[]{:S(2)}, u32[]{:S(2)}) collective-permute-start(bf16[64,1024]{1,0:T(8,128)(2,1)S(1)} %get-tuple-element.120.refs_0_), channel_id=1, source_target_pairs={{0,16},{4,20},{8,24},{12,28},{16,0},{20,4},{24,8},{28,12},{1,17},{... | collective-permute-start | bytes 393224 | tf_op jit(solution)/shard_map/ppermute | solution.py:27
  46.1 6.6 %collective-permute-start.15 = (bf16[64,1024]{1,0:T(8,128)(2,1)S(1)}, bf16[64,1024]{1,0:T(8,128)(2,1)S(1)}, u32[]{:S(2)}, u32[]{:S(2)}) collective-permute-start(bf16[64,1024]{1,0:T(8,128)(2,1)S(1)} %get-tuple-element.120.refs_0_), channel_id=1, source_target_pairs={{0,24},{4,28},{8,16},{12,20},{16,8},{20,12},{24,0},{28,4},{1,25},{... | collective-permute-start | bytes 393224 | tf_op jit(solution)/shard_map/ppermute | solution.py:27
  47.3 11.4 %collective-permute-start.14 = (bf16[64,1024]{1,0:T(8,128)(2,1)S(1)}, bf16[64,1024]{1,0:T(8,128)(2,1)S(1)}, u32[]{:S(2)}, u32[]{:S(2)}) collective-permute-start(bf16[64,1024]{1,0:T(8,128)(2,1)S(1)} %get-tuple-element.120.refs_0_), channel_id=1, source_target_pairs={{0,8},{4,12},{8,0},{12,4},{16,24},{20,28},{24,16},{28,20},{1,9},{5... | collective-permute-start | bytes 393224 | tf_op jit(solution)/shard_map/ppermute | solution.py:27
  50.0 9.6 %collective-permute-start.22 = (bf16[64,1024]{1,0:T(8,128)(2,1)S(1)}, bf16[64,1024]{1,0:T(8,128)(2,1)S(1)}, u32[]{:S(2)}, u32[]{:S(2)}) collective-permute-start(bf16[64,1024]{1,0:T(8,128)(2,1)S(1)} %pick.3.refs_0_), channel_id=1, source_target_pairs={{0,16},{4,20},{8,24},{12,28},{16,0},{20,4},{24,8},{28,12},{1,17},{... | collective-permute-start | bytes 393224 | tf_op jit(solution)/shard_map/ppermute | solution.py:27
  51.4 8.9 %collective-permute-start.21 = (bf16[64,1024]{1,0:T(8,128)(2,1)S(1)}, bf16[64,1024]{1,0:T(8,128)(2,1)S(1)}, u32[]{:S(2)}, u32[]{:S(2)}) collective-permute-start(bf16[64,1024]{1,0:T(8,128)(2,1)S(1)} %pick.3.refs_0_), channel_id=1, source_target_pairs={{0,24},{4,28},{8,16},{12,20},{16,8},{20,12},{24,0},{28,4},{1,25},{... | collective-permute-start | bytes 393224 | tf_op jit(solution)/shard_map/ppermute | solution.py:27
  52.6 10.5 %collective-permute-start.20 = (bf16[64,1024]{1,0:T(8,128)(2,1)S(1)}, bf16[64,1024]{1,0:T(8,128)(2,1)S(1)}, u32[]{:S(2)}, u32[]{:S(2)}) collective-permute-start(bf16[64,1024]{1,0:T(8,128)(2,1)S(1)} %pick.3.refs_0_), channel_id=1, source_target_pairs={{0,8},{4,12},{8,0},{12,4},{16,24},{20,28},{24,16},{28,20},{1,9},{5... | collective-permute-start | bytes 393224 | tf_op jit(solution)/shard_map/ppermute | solution.py:27
  52.7 11.2 %collective-permute-start.23 = (f32[128,1024]{1,0:T(8,128)S(1)}, f32[128,1024]{1,0:T(8,128)S(1)}, u32[]{:S(2)}, u32[]{:S(2)}) collective-permute-start(f32[128,1024]{1,0:T(8,128)S(1)} %get-tuple-element.129), channel_id=1, source_target_pairs={{0,4},{4,0},{8,12},{12,8},{16,20},{20,16},{24,28},{28,24},{1,5},{5... | collective-permute-start | bytes 1572872 | tf_op jit(solution)/shard_map/ppermute | solution.py:27
  58.7 5.2 %collective-permute-start.18 = (bf16[128,2048]{1,0:T(8,128)(2,1)S(1)}, bf16[128,2048]{1,0:T(8,128)(2,1)S(1)}, u32[]{:S(2)}, u32[]{:S(2)}) collective-permute-start(bf16[128,2048]{1,0:T(8,128)(2,1)S(1)} %hidden.5.refs_2_), channel_id=1, source_target_pairs={{0,4},{4,0},{8,12},{12,8},{16,20},{20,16},{24,28},{28,24},{1,5},{5... | collective-permute-start | bytes 1572872 | tf_op jit(solution)/shard_map/ppermute | solution.py:27
  59.6 4.3 %collective-permute-start.17 = (bf16[128,2048]{1,0:T(8,128)(2,1)S(1)}, bf16[128,2048]{1,0:T(8,128)(2,1)S(1)}, u32[]{:S(2)}, u32[]{:S(2)}) collective-permute-start(bf16[128,2048]{1,0:T(8,128)(2,1)S(1)} %hidden.4.refs_1_), channel_id=1, source_target_pairs={{0,4},{4,0},{8,12},{12,8},{16,20},{20,16},{24,28},{28,24},{1,5},{5... | collective-permute-start | bytes 1572872 | tf_op jit(solution)/shard_map/ppermute | solution.py:27
  61.0 4.8 %collective-permute-start.25 = (bf16[128,2048]{1,0:T(8,128)(2,1)S(1)}, bf16[128,2048]{1,0:T(8,128)(2,1)S(1)}, u32[]{:S(2)}, u32[]{:S(2)}) collective-permute-start(bf16[128,2048]{1,0:T(8,128)(2,1)S(1)} %hidden.7.refs_6_), channel_id=1, source_target_pairs={{0,4},{4,0},{8,12},{12,8},{16,20},{20,16},{24,28},{28,24},{1,5},{5... | collective-permute-start | bytes 1572872 | tf_op jit(solution)/shard_map/ppermute | solution.py:27
  63.8 2.0 %collective-permute-start.24 = (bf16[128,2048]{1,0:T(8,128)(2,1)S(1)}, bf16[128,2048]{1,0:T(8,128)(2,1)S(1)}, u32[]{:S(2)}, u32[]{:S(2)}) collective-permute-start(bf16[128,2048]{1,0:T(8,128)(2,1)S(1)} %hidden.6.refs_5_), channel_id=1, source_target_pairs={{0,4},{4,0},{8,12},{12,8},{16,20},{20,16},{24,28},{28,24},{1,5},{5... | collective-permute-start | bytes 1572872 | tf_op jit(solution)/shard_map/ppermute | solution.py:27

commit v8 on v7

--- a/solution.py
+++ b/solution.py
@@ -182,27 +182,27 @@
     choose(whole, batch, sections - 1, list(enumerate(later)), chosen)
 
 
-def take_slopes(section, count, *refs):
-    batches = (len(refs) - count - 1) // 2
+def take_slopes(section, count, which, *refs):
+    batches = len(which)
     blocks, weight_in, known, slopes = refs[:count], refs[count], refs[count + 1 : -batches], refs[-batches:]
     part = known[0].shape[0]
 
     @pl.when(section(lax.axis_index("section")))
     def _():
         size = (count - 1) * part
-        others = [block[batch * part : (batch + 1) * part, :] for batch in range(batches) for block in blocks[1:]]
+        others = [block[batch * part : (batch + 1) * part, :] for batch in which for block in blocks[1:]]
         others = jnp.concatenate(others, axis=0)
         for cols in tiles(weight_in.shape[1], 256):
             values = gelu_slope(dot(others, weight_in[:, cols]))
-            for batch, slope in enumerate(slopes):
-                slope[part:, cols] = values[batch * size : (batch + 1) * size, :]
-        for batch, slope in enumerate(slopes):
-            slope[:part, :] = known[batch][...]
+            for index, slope in enumerate(slopes):
+                slope[part:, cols] = values[index * size : (index + 1) * size, :]
+        for index, slope in enumerate(slopes):
+            slope[:part, :] = known[index][...]
 
 
 def slopes_kernel(count, batches, late, owned, *refs):
     sums, slopes, rows = refs[count + 1 + batches :][:2], refs[-1 - batches : -1], refs[-1]
-    take_slopes(lambda section: section != late, count, *refs[: count + 1 + batches], *slopes)
+    take_slopes(lambda section: section != late, count, range(batches), *refs[: count + 1 + batches], *slopes)
     blocks = refs[:count]
     height = blocks[0].shape[0]
     for index, block in enumerate(blocks):
@@ -212,8 +212,8 @@
             total[:, cols] = value
 
 
-def late_kernel(count, batches, late, *refs):
-    take_slopes(lambda section: section == late, count, *refs[: count + 1 + batches], *refs[-batches:])
+def late_kernel(count, batch, late, *refs):
+    take_slopes(lambda section: section == late, count, [batch], *refs[: count + 2], refs[-1])
 
 
 def arrived_kernel(*refs):
@@ -387,7 +387,7 @@
         aliases={len(far) + index: index for index in range(len(far))},
     )
     paired = owners in (2, 4, 8) and not (width // owners % 128 or width_hidden // owners % 128)
-    masks = range(owners - 2, 0, -2)
+    masks = range(2, owners, 2)
     gain, given, weight_in, weight_out, scales, asked = [pinned(value) for value in near]
     for step in range(sections - 1):
         for m in batches:
@@ -478,17 +478,16 @@
             [asked, *returned[m]],
             [block],
             name="pick",
-            ordered=m == 0,
         )
         cotangents.append(cotangent)
-        if paired and m == 0:
-            slopes = call(
-                functools.partial(late_kernel, count, batch_count, 1),
-                [*to_slopes, *[pinned(value) for value in slopes]],
-                [shape((count * row_count, width_hidden), F32)] * batch_count,
+        if paired:
+            slopes[m] = call(
+                functools.partial(late_kernel, count, m, 1),
+                [*to_slopes[: count + 1], to_slopes[count + 1 + m], pinned(slopes[m])],
+                [shape((count * row_count, width_hidden), F32)],
                 name="late",
-                aliases={len(to_slopes) + n: n for n in batches},
-                )
+                aliases={count + 2: 0},
+            )[0]
     for m in batches:
         cotangent = cotangents[m]
         order = [mask for mask in masks if paired]

time: 68.1 us -> 68.4 us (level)
  starting transfers between devices: 30.3 us -> 29.6 us
    pallas_call x28 -> x29, Pallas kernels: 26.1 us -> 26.6 us  [__call__(): pl.pallas_call(body, in_specs=(specs or [IN_VMEM] * count) + [IN_VMEM] *...]
  transfers between devices with their start and end apart: 26 -> 26, of which waited for: 3 -> 3; matrix products, arithmetic and copies ran while one was open for 0% -> 0% of each run, Pallas kernels for 36% -> 37%
where the time goes in v8:
time: 68.4 us; the launch traced here: 67.5 us
  starting transfers between devices  29.6 us (43%)
  Pallas kernels  26.6 us (39%)
  waiting for transfers between devices  9.99 us (15%)
  between operations  1.26 us (2%)
    pallas_call x29, Pallas kernels, __call__(): pl.pallas_call(body, in_specs=(specs or [IN_VMEM] * count) + [IN_VMEM] *...  26.6 us
    ppermute x14, starting transfers between devices, swapped(): lax.ppermute(value, axis, [(source, source ^ mask) for source in range(co...  16.6 us
    ppermute x12, starting transfers between devices, hop(): return lax.ppermute(value, 'section', [(source, source + steps)])  13 us
    ppermute x12, waiting for transfers between devices, hop(): return lax.ppermute(value, 'section', [(source, source + steps)])  9.96 us
  transfers between devices with their start and end apart: 26, of which 3 were waited for; matrix products, arithmetic and copies ran while one was open for 0% of the time, Pallas kernels for 37%

profile of v8, /device:TPU:9, one launch (start us, length us, event | category | flops | bytes accessed | tf_op | source)
XLA Modules:
  0.0 67.5 jit_solution(4422682585159858957)
XLA Ops:
  0.6 0.1 first.1
  0.8 1.3 %collective-permute-start.1 = (bf16[64,1024]{1,0:T(8,128)(2,1)S(1)}, bf16[64,1024]{1,0:T(8,128)(2,1)S(1)}, u32[]{:S(2)}, u32[]{:S(2)}) collective-permute-start(bf16[64,1024]{1,0:T(8,128)(2,1)S(1)} %get-tuple-element.85), channel_id=1, source_target_pairs={{0,1},{4,5},{8,9},{12,13},{16,17},{20,21},{24,25},{28,29}} | collective-permute-start | bytes 393224 | tf_op jit(solution)/shard_map/ppermute | solution.py:22
  2.1 3.7 %load.1 = (f32[1,1024]{1,0:T(1,128)S(1)}, bf16[2,64,1024]{2,1,0:T(8,128)(2,1)S(1)}, bf16[1024,2048]{1,0:T(8,128)(2,1)S(1)}, bf16[2048,1024]{1,0:T(8,128)(2,1)S(1...) custom-call(f32[1,1024]{1,0:T(1,128)} %refs_0_.4, ...), custom_call_target="tpu_custom_call", output_to_operand_aliasing={{0}: (6, {}), {1}: (7, {}), {2}: (8, {}), {3}: (9, {}), {4}... | custom-call | bytes 8388608 | tf_op jit(solution)/shard_map/load/pallas_call | solution.py:297
  5.8 1.3 %collective-permute-start = (bf16[64,1024]{1,0:T(8,128)(2,1)S(1)}, bf16[64,1024]{1,0:T(8,128)(2,1)S(1)}, u32[]{:S(2)}, u32[]{:S(2)}) collective-permute-start(bf16[64,1024]{1,0:T(8,128)(2,1)S(1)} %get-tuple-element.84), channel_id=1, source_target_pairs={{0,1},{4,5},{8,9},{12,13},{16,17},{20,21},{24,25},{28,29}} | collective-permute-start | bytes 393224 | tf_op jit(solution)/shard_map/ppermute | solution.py:22
  7.1 2.0 %collective-permute-done.1.refs_0_.refs_1_ = bf16[64,1024]{1,0:T(8,128)(2,1)S(1)} collective-permute-done((bf16[64,1024]{1,0:T(8,128)(2,1)S(1)}, bf16[64,1024]{1,0:T(8,128)(2,1)S(1)}, u32[]{:S(2)}, u32[]{:S(2)}) %collective-permute-start.1) | collective-permute-done | bytes 131104 | tf_op jit(solution)/shard_map/ppermute | solution.py:22
  9.0 1.8 %forward.6 = (bf16[64,1024]{1,0:T(8,128)(2,1)S(1)}, f32[8,128]{1,0:T(8,128)S(1)}) custom-call(bf16[64,1024]{1,0:T(8,128)(2,1)S(1)} %collective-permute-done.1.refs_0_.refs_1_, f32[1,1024]{1,0:T(1,128)S(1)} %get-tuple-element.82.refs_1_.refs_4_, bf16[1024,2048]{1,0:T(8,128)(2,1)S(1)} %get-tuple-element.77.refs_2_.refs_1_.refs_5_.refs_4_, ...), custom_call_target="tpu_custom_call" | custom-call | flops 536870912 | bytes 8388608 | tf_op jit(solution)/shard_map/forward/pallas_call | solution.py:297
  10.8 1.3 %collective-permute-start.2 = (bf16[64,1024]{1,0:T(8,128)(2,1)S(1)}, bf16[64,1024]{1,0:T(8,128)(2,1)S(1)}, u32[]{:S(2)}, u32[]{:S(2)}) collective-permute-start(bf16[64,1024]{1,0:T(8,128)(2,1)S(1)} %get-tuple-element.92), channel_id=1, source_target_pairs={{1,2},{5,6},{9,10},{13,14},{17,18},{21,22},{25,26},{29,30}} | collective-permute-start | bytes 393224 | tf_op jit(solution)/shard_map/ppermute | solution.py:22
  12.1 1.8 %forward.7 = (bf16[64,1024]{1,0:T(8,128)(2,1)S(1)}, f32[8,128]{1,0:T(8,128)S(1)}) custom-call(bf16[64,1024]{1,0:T(8,128)(2,1)S(1)} %collective-permute-done.refs_0_.refs_1_, f32[1,1024]{1,0:T(1,128)S(1)} %get-tuple-element.82.refs_1_.refs_4_, bf16[1024,2048]{1,0:T(8,128)(2,1)S(1)} %get-tuple-element.77.refs_2_.refs_1_.refs_5_.refs_4_, ...), custom_call_target="tpu_custom_call" | custom-call | flops 536870912 | bytes 8388608 | tf_op jit(solution)/shard_map/forward/pallas_call | solution.py:297
  13.9 1.3 %collective-permute-start.4 = (bf16[64,1024]{1,0:T(8,128)(2,1)S(1)}, bf16[64,1024]{1,0:T(8,128)(2,1)S(1)}, u32[]{:S(2)}, u32[]{:S(2)}) collective-permute-start(bf16[64,1024]{1,0:T(8,128)(2,1)S(1)} %get-tuple-element.95), channel_id=1, source_target_pairs={{1,2},{5,6},{9,10},{13,14},{17,18},{21,22},{25,26},{29,30}} | collective-permute-start | bytes 393224 | tf_op jit(solution)/shard_map/ppermute | solution.py:22
  15.2 3.0 %turn.1 = (bf16[2048,1024]{1,0:T(8,128)(2,1)S(1)}, bf16[1024,2048]{1,0:T(8,128)(2,1)S(1)}, s32[2]{0:T(128)S(4)}, f32[64,2048]{1,0:T(8,128)S(1)}, f32[64,2048]{1,0:T(8,128)S(1)}, /*index=5*/f32[8,128]{1,0:T(8,128)S(1)}) custom-call(s32[8]{0:T(128)S(1)} %copy-done, bf16[1024,2048]{1,0:T(8,128)(2,1)S(1)} %get-tuple-element.77.refs_2_.refs_1_.refs_5_.refs_4_, ...), custom_call_target="tpu_custom_call" | custom-call | bytes 8388608 | tf_op jit(solution)/shard_map/turn/pallas_call | solution.py:297
  18.2 0.7 collective-permute-start.3
  18.9 0.7 collective-permute-start.6
  19.6 1.1 %save.2 = (bf16[64,1024]{1,0:T(8,128)(2,1)S(1)}, f32[64,1024]{1,0:T(8,128)S(1)}, f32[64,1]{1,0:T(8,128)S(1)}, f32[64,2048]{1,0:T(8,128)S(1)}, f32[8,128]{1,0:T(8,128)S(1)}) custom-call(bf16[2,64,1024]{2,1,0:T(8,128)(2,1)S(1)} %get-tuple-element.81.refs_0_, bf16[64,1024]{1,0:T(8,128)(2,1)S(1)} %collective-permute-done.1.refs_0_.refs_1_, ...), custom_call_target="tpu_custom_call" | custom-call | flops 268435456 | bytes 8388608 | tf_op jit(solution)/shard_map/save/pallas_call | solution.py:297
  20.7 0.2 backward.6
  20.9 0.7 collective-permute-start.5
  21.6 1.1 %save.3 = (bf16[64,1024]{1,0:T(8,128)(2,1)S(1)}, f32[64,1024]{1,0:T(8,128)S(1)}, f32[64,1]{1,0:T(8,128)S(1)}, f32[64,2048]{1,0:T(8,128)S(1)}, f32[8,128]{1,0:T(8,128)S(1)}) custom-call(bf16[2,64,1024]{2,1,0:T(8,128)(2,1)S(1)} %get-tuple-element.81.refs_0_, bf16[64,1024]{1,0:T(8,128)(2,1)S(1)} %collective-permute-done.refs_0_.refs_1_, ...), custom_call_target="tpu_custom_call" | custom-call | flops 268435456 | bytes 8388608 | tf_op jit(solution)/shard_map/save/pallas_call | solution.py:297
  22.8 0.7 collective-permute-start.8
  23.5 2.5 %collective-permute-start.12 = (bf16[128,1024]{1,0:T(8,128)(2,1)S(1)}, bf16[128,1024]{1,0:T(8,128)(2,1)S(1)}, u32[]{:S(2)}, u32[]{:S(2)}) collective-permute-start(bf16[128,1024]{1,0:T(8,128)(2,1)S(1)} %stack.1.refs_0_.refs_1_), channel_id=1, source_target_pairs={{0,24},{4,28},{8,16},{12,20},{16,8},{20,12},{24,0},{28,4},{1,25},{... | collective-permute-start | bytes 786440 | tf_op jit(solution)/shard_map/ppermute | solution.py:27
  26.0 0.2 collective-permute-start.11
  26.2 0.1 collective-permute-start.10
  26.3 1.3 %collective-permute-start.7 = (bf16[64,1024]{1,0:T(8,128)(2,1)S(1)}, bf16[64,1024]{1,0:T(8,128)(2,1)S(1)}, u32[]{:S(2)}, u32[]{:S(2)}) collective-permute-start(bf16[64,1024]{1,0:T(8,128)(2,1)S(1)} %get-tuple-element.112), channel_id=1, source_target_pairs={{2,1},{6,5},{10,9},{14,13},{18,17},{22,21},{26,25},{30,29}} | collective-permute-start | bytes 393224 | tf_op jit(solution)/shard_map/ppermute | solution.py:22
  27.7 1.3 %collective-permute-start.13 = (bf16[64,1024]{1,0:T(8,128)(2,1)S(1)}, bf16[64,1024]{1,0:T(8,128)(2,1)S(1)}, u32[]{:S(2)}, u32[]{:S(2)}) collective-permute-start(bf16[64,1024]{1,0:T(8,128)(2,1)S(1)} %get-tuple-element.119), channel_id=1, source_target_pairs={{2,1},{6,5},{10,9},{14,13},{18,17},{22,21},{26,25},{30,29}} | collective-permute-start | bytes 393224 | tf_op jit(solution)/shard_map/ppermute | solution.py:22
  29.0 7.5 %collective-permute-done.7.refs_0_.refs_2_ = bf16[64,1024]{1,0:T(8,128)(2,1)S(1)} collective-permute-done((bf16[64,1024]{1,0:T(8,128)(2,1)S(1)}, bf16[64,1024]{1,0:T(8,128)(2,1)S(1)}, u32[]{:S(2)}, u32[]{:S(2)}) %collective-permute-start.7) | collective-permute-done | bytes 131104 | tf_op jit(solution)/shard_map/ppermute | solution.py:22
  36.5 1.7 %backward.10 = (bf16[64,1024]{1,0:T(8,128)(2,1)S(1)}, f32[8,128]{1,0:T(8,128)S(1)}) custom-call(bf16[64,1024]{1,0:T(8,128)(2,1)S(1)} %collective-permute-done.7.refs_0_.refs_2_, f32[1,1024]{1,0:T(1,128)S(1)} %get-tuple-element.82.refs_1_.refs_4_, bf16[2048,1024]{1,0:T(8,128)(2,1)S(1)} %get-tuple-element.90.refs_2_, ...), custom_call_target="tpu_custom_call" | custom-call | flops 536870912 | bytes 8388608 | tf_op jit(solution)/shard_map/backward/pallas_call | solution.py:297
  38.2 1.3 %collective-permute-start.9 = (bf16[64,1024]{1,0:T(8,128)(2,1)S(1)}, bf16[64,1024]{1,0:T(8,128)(2,1)S(1)}, u32[]{:S(2)}, u32[]{:S(2)}) collective-permute-start(bf16[64,1024]{1,0:T(8,128)(2,1)S(1)} %get-tuple-element.116), channel_id=1, source_target_pairs={{1,0},{5,4},{9,8},{13,12},{17,16},{21,20},{25,24},{29,28}} | collective-permute-start | bytes 393224 | tf_op jit(solution)/shard_map/ppermute | solution.py:22
  39.5 0.4 collective-permute-done.13.refs_0_.refs_2_
  40.0 1.7 %backward.11 = (bf16[64,1024]{1,0:T(8,128)(2,1)S(1)}, f32[8,128]{1,0:T(8,128)S(1)}) custom-call(bf16[64,1024]{1,0:T(8,128)(2,1)S(1)} %collective-permute-done.13.refs_0_.refs_2_, f32[1,1024]{1,0:T(1,128)S(1)} %get-tuple-element.82.refs_1_.refs_4_, bf16[2048,1024]{1,0:T(8,128)(2,1)S(1)} %get-tuple-element.90.refs_2_, ...), custom_call_target="tpu_custom_call" | custom-call | flops 536870912 | bytes 8388608 | tf_op jit(solution)/shard_map/backward/pallas_call | solution.py:297
  41.7 1.3 %collective-permute-start.15 = (bf16[64,1024]{1,0:T(8,128)(2,1)S(1)}, bf16[64,1024]{1,0:T(8,128)(2,1)S(1)}, u32[]{:S(2)}, u32[]{:S(2)}) collective-permute-start(bf16[64,1024]{1,0:T(8,128)(2,1)S(1)} %get-tuple-element.128), channel_id=1, source_target_pairs={{1,0},{5,4},{9,8},{13,12},{17,16},{21,20},{25,24},{29,28}} | collective-permute-start | bytes 393224 | tf_op jit(solution)/shard_map/ppermute | solution.py:22
  43.0 0.6 slopes.1
  43.6 2.5 %collective-permute-start.17 = (bf16[64,1024]{1,0:T(8,128)(2,1)S(1)}, bf16[64,1024]{1,0:T(8,128)(2,1)S(1)}, u32[]{:S(2)}, u32[]{:S(2)}) collective-permute-start(bf16[64,1024]{1,0:T(8,128)(2,1)S(1)} %get-tuple-element.123.refs_0_), channel_id=1, source_target_pairs={{0,16},{4,20},{8,24},{12,28},{16,0},{20,4},{24,8},{28,12},{1,17},{... | collective-permute-start | bytes 393224 | tf_op jit(solution)/shard_map/ppermute | solution.py:27
  46.1 1.2 %collective-permute-start.16 = (bf16[64,1024]{1,0:T(8,128)(2,1)S(1)}, bf16[64,1024]{1,0:T(8,128)(2,1)S(1)}, u32[]{:S(2)}, u32[]{:S(2)}) collective-permute-start(bf16[64,1024]{1,0:T(8,128)(2,1)S(1)} %get-tuple-element.123.refs_0_), channel_id=1, source_target_pairs={{0,8},{4,12},{8,0},{12,4},{16,24},{20,28},{24,16},{28,20},{1,9},{5... | collective-permute-start | bytes 393224 | tf_op jit(solution)/shard_map/ppermute | solution.py:27
  47.4 1.4 %late.2 = (f32[256,2048]{1,0:T(8,128)S(1)}, f32[8,128]{1,0:T(8,128)S(1)}) custom-call(bf16[128,1024]{1,0:T(8,128)(2,1)S(1)} %stack.1.refs_0_.refs_1_, bf16[128,1024]{1,0:T(8,128)(2,1)S(1)} %collective-permute-done.10.refs_1_.refs_2_, bf16[128,1024]{1,0:T(8,128)(2,1)S(1)} %collective-permute-done.11.refs_2_.refs_3_, ...), custom_call_target="tpu_custom_call", output_to_operand_aliasing={{0}: (6, {})} | custom-call | bytes 8388608 | tf_op jit(solution)/shard_map/late/pallas_call | solution.py:297
  48.9 0.3 pick.3
  49.1 1.4 %collective-permute-start.22 = (bf16[64,1024]{1,0:T(8,128)(2,1)S(1)}, bf16[64,1024]{1,0:T(8,128)(2,1)S(1)}, u32[]{:S(2)}, u32[]{:S(2)}) collective-permute-start(bf16[64,1024]{1,0:T(8,128)(2,1)S(1)} %get-tuple-element.132.refs_0_), channel_id=1, source_target_pairs={{0,16},{4,20},{8,24},{12,28},{16,0},{20,4},{24,8},{28,12},{1,17},{... | collective-permute-start | bytes 393224 | tf_op jit(solution)/shard_map/ppermute | solution.py:27
  50.6 1.2 %collective-permute-start.21 = (bf16[64,1024]{1,0:T(8,128)(2,1)S(1)}, bf16[64,1024]{1,0:T(8,128)(2,1)S(1)}, u32[]{:S(2)}, u32[]{:S(2)}) collective-permute-start(bf16[64,1024]{1,0:T(8,128)(2,1)S(1)} %get-tuple-element.132.refs_0_), channel_id=1, source_target_pairs={{0,8},{4,12},{8,0},{12,4},{16,24},{20,28},{24,16},{28,20},{1,9},{5... | collective-permute-start | bytes 393224 | tf_op jit(solution)/shard_map/ppermute | solution.py:27
  51.8 0.1 collective-permute-start.20
  51.8 1.4 %late.3 = (f32[256,2048]{1,0:T(8,128)S(1)}, f32[8,128]{1,0:T(8,128)S(1)}) custom-call(bf16[128,1024]{1,0:T(8,128)(2,1)S(1)} %stack.1.refs_0_.refs_1_, bf16[128,1024]{1,0:T(8,128)(2,1)S(1)} %collective-permute-done.10.refs_1_.refs_2_, bf16[128,1024]{1,0:T(8,128)(2,1)S(1)} %collective-permute-done.11.refs_2_.refs_3_, ...), custom_call_target="tpu_custom_call", output_to_operand_aliasing={{0}: (6, {})} | custom-call | bytes 8388608 | tf_op jit(solution)/shard_map/late/pallas_call | solution.py:297
  53.3 5.5 %collective-permute-start.23 = (f32[128,1024]{1,0:T(8,128)S(1)}, f32[128,1024]{1,0:T(8,128)S(1)}, u32[]{:S(2)}, u32[]{:S(2)}) collective-permute-start(f32[128,1024]{1,0:T(8,128)S(1)} %get-tuple-element.135), channel_id=1, source_target_pairs={{0,4},{4,0},{8,12},{12,8},{16,20},{20,16},{24,28},{28,24},{1,5},{5... | collective-permute-start | bytes 1572872 | tf_op jit(solution)/shard_map/ppermute | solution.py:27
  58.8 0.8 %hidden.5.refs_2_ = bf16[128,2048]{1,0:T(8,128)(2,1)S(1)} custom-call(bf16[64,1024]{1,0:T(8,128)(2,1)S(1)} %collective-permute-done.16.refs_0_, bf16[64,1024]{1,0:T(8,128)(2,1)S(1)} %collective-permute-done.17.refs_1_, f32[1,1024]{1,0:T(1,128)S(1)} %get-tuple-element.79.refs_4_.refs_3_.refs_2_, bf16[1024,2048]{1,0:T(8,128)(2,1)S(1)} %get-tuple-element.91.refs_3_, ...), custom_call_target="tpu_custom_call" | custom-call | bytes 8388608 | tf_op jit(solution)/shard_map/hidden/pallas_call | solution.py:297
  59.6 0.1 collective-permute-start.19
  59.7 0.8 %hidden.4.refs_1_ = bf16[128,2048]{1,0:T(8,128)(2,1)S(1)} custom-call(bf16[64,1024]{1,0:T(8,128)(2,1)S(1)} %get-tuple-element.123.refs_0_, bf16[64,1024]{1,0:T(8,128)(2,1)S(1)} %collective-permute-done.14.refs_1_, f32[1,1024]{1,0:T(1,128)S(1)} %get-tuple-element.79.refs_4_.refs_3_.refs_2_, bf16[1024,2048]{1,0:T(8,128)(2,1)S(1)} %get-tuple-element.91.refs_3_, ...), custom_call_target="tpu_custom_call" | custom-call | bytes 8388608 | tf_op jit(solution)/shard_map/hidden/pallas_call | solution.py:297
  60.5 0.6 collective-permute-start.18
  61.0 0.8 %hidden.7.refs_6_ = bf16[128,2048]{1,0:T(8,128)(2,1)S(1)} custom-call(bf16[64,1024]{1,0:T(8,128)(2,1)S(1)} %collective-permute-done.21.refs_0_, bf16[64,1024]{1,0:T(8,128)(2,1)S(1)} %collective-permute-done.22.refs_1_, f32[1,1024]{1,0:T(1,128)S(1)} %get-tuple-element.79.refs_4_.refs_3_.refs_2_, bf16[1024,2048]{1,0:T(8,128)(2,1)S(1)} %get-tuple-element.91.refs_3_, ...), custom_call_target="tpu_custom_call" | custom-call | bytes 8388608 | tf_op jit(solution)/shard_map/hidden/pallas_call | solution.py:297
  61.8 0.1 collective-permute-start.25
  61.9 0.8 %hidden.6.refs_5_ = bf16[128,2048]{1,0:T(8,128)(2,1)S(1)} custom-call(bf16[64,1024]{1,0:T(8,128)(2,1)S(1)} %get-tuple-element.132.refs_0_, bf16[64,1024]{1,0:T(8,128)(2,1)S(1)} %collective-permute-done.20.refs_1_, f32[1,1024]{1,0:T(1,128)S(1)} %get-tuple-element.79.refs_4_.refs_3_.refs_2_, bf16[1024,2048]{1,0:T(8,128)(2,1)S(1)} %get-tuple-element.91.refs_3_, ...), custom_call_target="tpu_custom_call" | custom-call | bytes 8388608 | tf_op jit(solution)/shard_map/hidden/pallas_call | solution.py:297
  62.7 1.0 %collective-permute-start.24 = (bf16[128,2048]{1,0:T(8,128)(2,1)S(1)}, bf16[128,2048]{1,0:T(8,128)(2,1)S(1)}, u32[]{:S(2)}, u32[]{:S(2)}) collective-permute-start(bf16[128,2048]{1,0:T(8,128)(2,1)S(1)} %hidden.6.refs_5_), channel_id=1, source_target_pairs={{0,4},{4,0},{8,12},{12,8},{16,20},{20,16},{24,28},{28,24},{1,5},{5... | collective-permute-start | bytes 1572872 | tf_op jit(solution)/shard_map/ppermute | solution.py:27
  63.7 1.9 %partial.1 = (f32[256,2048]{1,0:T(8,128)S(1)}, f32[128,1024]{1,0:T(8,128)}) custom-call(s32[2]{0:T(128)S(4)} %get-tuple-element.89.refs_0_, bf16[128,2048]{1,0:T(8,128)(2,1)S(1)} %hidden.4.refs_1_, bf16[128,2048]{1,0:T(8,128)(2,1)S(1)} %hidden.5.refs_2_, bf16[128,2048]{1,0:T(8,128)(2,1)S(1)} %collective-permute-done.18.refs_3_, ...), custom_call_target="tpu_custom_call" | custom-call | bytes 8388608 | tf_op jit(solution)/shard_map/partial/pallas_call | solution.py:297
  65.6 1.7 %square.1 = f32[256,2048]{1,0:T(8,128)} custom-call(s32[2]{0:T(128)S(4)} %get-tuple-element.89.refs_0_, bf16[128,2048]{1,0:T(8,128)(2,1)S(1)} %collective-permute-done.24.refs_1_, bf16[128,2048]{1,0:T(8,128)(2,1)S(1)} %collective-permute-done.25.refs_2_, f32[256,2048]{1,0:T(8,128)S(1)} %get-tuple-element.137.refs_3_, ...), custom_call_target="tpu_custom_call" | custom-call | bytes 8388608 | tf_op jit(solution)/shard_map/square/pallas_call | solution.py:297
  (35 shorter events, 0.3 us)
Async XLA Ops:
  0.8 8.3 %collective-permute-start.1 = (bf16[64,1024]{1,0:T(8,128)(2,1)S(1)}, bf16[64,1024]{1,0:T(8,128)(2,1)S(1)}, u32[]{:S(2)}, u32[]{:S(2)}) collective-permute-start(bf16[64,1024]{1,0:T(8,128)(2,1)S(1)} %get-tuple-element.85), channel_id=1, source_target_pairs={{0,1},{4,5},{8,9},{12,13},{16,17},{20,21},{24,25},{28,29}} | collective-permute-start | bytes 393224 | tf_op jit(solution)/shard_map/ppermute | solution.py:22
  5.8 6.4 %collective-permute-start = (bf16[64,1024]{1,0:T(8,128)(2,1)S(1)}, bf16[64,1024]{1,0:T(8,128)(2,1)S(1)}, u32[]{:S(2)}, u32[]{:S(2)}) collective-permute-start(bf16[64,1024]{1,0:T(8,128)(2,1)S(1)} %get-tuple-element.84), channel_id=1, source_target_pairs={{0,1},{4,5},{8,9},{12,13},{16,17},{20,21},{24,25},{28,29}} | collective-permute-start | bytes 393224 | tf_op jit(solution)/shard_map/ppermute | solution.py:22
  10.8 7.4 %collective-permute-start.2 = (bf16[64,1024]{1,0:T(8,128)(2,1)S(1)}, bf16[64,1024]{1,0:T(8,128)(2,1)S(1)}, u32[]{:S(2)}, u32[]{:S(2)}) collective-permute-start(bf16[64,1024]{1,0:T(8,128)(2,1)S(1)} %get-tuple-element.92), channel_id=1, source_target_pairs={{1,2},{5,6},{9,10},{13,14},{17,18},{21,22},{25,26},{29,30}} | collective-permute-start | bytes 393224 | tf_op jit(solution)/shard_map/ppermute | solution.py:22
  12.1 3.1 %copy-start = (s32[8]{0:T(128)S(1)}, s32[8]{0:T(128)}, u32[]{:S(2)}) copy-start(s32[8]{0:T(128)} %refs_0_.5) | copy-start | bytes 100
  13.9 5.0 %collective-permute-start.4 = (bf16[64,1024]{1,0:T(8,128)(2,1)S(1)}, bf16[64,1024]{1,0:T(8,128)(2,1)S(1)}, u32[]{:S(2)}, u32[]{:S(2)}) collective-permute-start(bf16[64,1024]{1,0:T(8,128)(2,1)S(1)} %get-tuple-element.95), channel_id=1, source_target_pairs={{1,2},{5,6},{9,10},{13,14},{17,18},{21,22},{25,26},{29,30}} | collective-permute-start | bytes 393224 | tf_op jit(solution)/shard_map/ppermute | solution.py:22
  18.2 1.4 %collective-permute-start.3 = (bf16[64,1024]{1,0:T(8,128)(2,1)S(1)}, bf16[64,1024]{1,0:T(8,128)(2,1)S(1)}, u32[]{:S(2)}, u32[]{:S(2)}) collective-permute-start(bf16[64,1024]{1,0:T(8,128)(2,1)S(1)} %get-tuple-element.94), channel_id=1, source_target_pairs={{2,3},{6,7},{10,11},{14,15},{18,19},{22,23},{26,27},{30,31}} | collective-permute-start | bytes 393224 | tf_op jit(solution)/shard_map/ppermute | solution.py:22
  18.9 2.7 %collective-permute-start.6 = (bf16[64,1024]{1,0:T(8,128)(2,1)S(1)}, bf16[64,1024]{1,0:T(8,128)(2,1)S(1)}, u32[]{:S(2)}, u32[]{:S(2)}) collective-permute-start(bf16[64,1024]{1,0:T(8,128)(2,1)S(1)} %get-tuple-element.104), channel_id=1, source_target_pairs={{2,3},{6,7},{10,11},{14,15},{18,19},{22,23},{26,27},{30,31}} | collective-permute-start | bytes 393224 | tf_op jit(solution)/shard_map/ppermute | solution.py:22
  20.9 5.4 %collective-permute-start.5 = (bf16[64,1024]{1,0:T(8,128)(2,1)S(1)}, bf16[64,1024]{1,0:T(8,128)(2,1)S(1)}, u32[]{:S(2)}, u32[]{:S(2)}) collective-permute-start(bf16[64,1024]{1,0:T(8,128)(2,1)S(1)} %get-tuple-element.103), channel_id=1, source_target_pairs={{3,2},{7,6},{11,10},{15,14},{19,18},{23,22},{27,26},{31,30}} | collective-permute-start | bytes 393224 | tf_op jit(solution)/shard_map/ppermute | solution.py:22
  22.8 4.9 %collective-permute-start.8 = (bf16[64,1024]{1,0:T(8,128)(2,1)S(1)}, bf16[64,1024]{1,0:T(8,128)(2,1)S(1)}, u32[]{:S(2)}, u32[]{:S(2)}) collective-permute-start(bf16[64,1024]{1,0:T(8,128)(2,1)S(1)} %get-tuple-element.113), channel_id=1, source_target_pairs={{3,2},{7,6},{11,10},{15,14},{19,18},{23,22},{27,26},{31,30}} | collective-permute-start | bytes 393224 | tf_op jit(solution)/shard_map/ppermute | solution.py:22
  23.5 16.0 %collective-permute-start.12 = (bf16[128,1024]{1,0:T(8,128)(2,1)S(1)}, bf16[128,1024]{1,0:T(8,128)(2,1)S(1)}, u32[]{:S(2)}, u32[]{:S(2)}) collective-permute-start(bf16[128,1024]{1,0:T(8,128)(2,1)S(1)} %stack.1.refs_0_.refs_1_), channel_id=1, source_target_pairs={{0,24},{4,28},{8,16},{12,20},{16,8},{20,12},{24,0},{28,4},{1,25},{... | collective-permute-start | bytes 786440 | tf_op jit(solution)/shard_map/ppermute | solution.py:27
  26.0 13.6 %collective-permute-start.11 = (bf16[128,1024]{1,0:T(8,128)(2,1)S(1)}, bf16[128,1024]{1,0:T(8,128)(2,1)S(1)}, u32[]{:S(2)}, u32[]{:S(2)}) collective-permute-start(bf16[128,1024]{1,0:T(8,128)(2,1)S(1)} %stack.1.refs_0_.refs_1_), channel_id=1, source_target_pairs={{0,16},{4,20},{8,24},{12,28},{16,0},{20,4},{24,8},{28,12},{1,17},{... | collective-permute-start | bytes 786440 | tf_op jit(solution)/shard_map/ppermute | solution.py:27
  26.2 13.3 %collective-permute-start.10 = (bf16[128,1024]{1,0:T(8,128)(2,1)S(1)}, bf16[128,1024]{1,0:T(8,128)(2,1)S(1)}, u32[]{:S(2)}, u32[]{:S(2)}) collective-permute-start(bf16[128,1024]{1,0:T(8,128)(2,1)S(1)} %stack.1.refs_0_.refs_1_), channel_id=1, source_target_pairs={{0,8},{4,12},{8,0},{12,4},{16,24},{20,28},{24,16},{28,20},{1,9},{5... | collective-permute-start | bytes 786440 | tf_op jit(solution)/shard_map/ppermute | solution.py:27
  26.3 10.1 %collective-permute-start.7 = (bf16[64,1024]{1,0:T(8,128)(2,1)S(1)}, bf16[64,1024]{1,0:T(8,128)(2,1)S(1)}, u32[]{:S(2)}, u32[]{:S(2)}) collective-permute-start(bf16[64,1024]{1,0:T(8,128)(2,1)S(1)} %get-tuple-element.112), channel_id=1, source_target_pairs={{2,1},{6,5},{10,9},{14,13},{18,17},{22,21},{26,25},{30,29}} | collective-permute-start | bytes 393224 | tf_op jit(solution)/shard_map/ppermute | solution.py:22
  27.7 12.3 %collective-permute-start.13 = (bf16[64,1024]{1,0:T(8,128)(2,1)S(1)}, bf16[64,1024]{1,0:T(8,128)(2,1)S(1)}, u32[]{:S(2)}, u32[]{:S(2)}) collective-permute-start(bf16[64,1024]{1,0:T(8,128)(2,1)S(1)} %get-tuple-element.119), channel_id=1, source_target_pairs={{2,1},{6,5},{10,9},{14,13},{18,17},{22,21},{26,25},{30,29}} | collective-permute-start | bytes 393224 | tf_op jit(solution)/shard_map/ppermute | solution.py:22
  38.2 5.4 %collective-permute-start.9 = (bf16[64,1024]{1,0:T(8,128)(2,1)S(1)}, bf16[64,1024]{1,0:T(8,128)(2,1)S(1)}, u32[]{:S(2)}, u32[]{:S(2)}) collective-permute-start(bf16[64,1024]{1,0:T(8,128)(2,1)S(1)} %get-tuple-element.116), channel_id=1, source_target_pairs={{1,0},{5,4},{9,8},{13,12},{17,16},{21,20},{25,24},{29,28}} | collective-permute-start | bytes 393224 | tf_op jit(solution)/shard_map/ppermute | solution.py:22
  41.7 7.1 %collective-permute-start.15 = (bf16[64,1024]{1,0:T(8,128)(2,1)S(1)}, bf16[64,1024]{1,0:T(8,128)(2,1)S(1)}, u32[]{:S(2)}, u32[]{:S(2)}) collective-permute-start(bf16[64,1024]{1,0:T(8,128)(2,1)S(1)} %get-tuple-element.128), channel_id=1, source_target_pairs={{1,0},{5,4},{9,8},{13,12},{17,16},{21,20},{25,24},{29,28}} | collective-permute-start | bytes 393224 | tf_op jit(solution)/shard_map/ppermute | solution.py:22
  43.6 8.1 %collective-permute-start.17 = (bf16[64,1024]{1,0:T(8,128)(2,1)S(1)}, bf16[64,1024]{1,0:T(8,128)(2,1)S(1)}, u32[]{:S(2)}, u32[]{:S(2)}) collective-permute-start(bf16[64,1024]{1,0:T(8,128)(2,1)S(1)} %get-tuple-element.123.refs_0_), channel_id=1, source_target_pairs={{0,16},{4,20},{8,24},{12,28},{16,0},{20,4},{24,8},{28,12},{1,17},{... | collective-permute-start | bytes 393224 | tf_op jit(solution)/shard_map/ppermute | solution.py:27
  46.1 7.1 %collective-permute-start.16 = (bf16[64,1024]{1,0:T(8,128)(2,1)S(1)}, bf16[64,1024]{1,0:T(8,128)(2,1)S(1)}, u32[]{:S(2)}, u32[]{:S(2)}) collective-permute-start(bf16[64,1024]{1,0:T(8,128)(2,1)S(1)} %get-tuple-element.123.refs_0_), channel_id=1, source_target_pairs={{0,8},{4,12},{8,0},{12,4},{16,24},{20,28},{24,16},{28,20},{1,9},{5... | collective-permute-start | bytes 393224 | tf_op jit(solution)/shard_map/ppermute | solution.py:27
  47.3 12.2 %collective-permute-start.14 = (bf16[64,1024]{1,0:T(8,128)(2,1)S(1)}, bf16[64,1024]{1,0:T(8,128)(2,1)S(1)}, u32[]{:S(2)}, u32[]{:S(2)}) collective-permute-start(bf16[64,1024]{1,0:T(8,128)(2,1)S(1)} %get-tuple-element.123.refs_0_), channel_id=1, source_target_pairs={{0,24},{4,28},{8,16},{12,20},{16,8},{20,12},{24,0},{28,4},{1,25},{... | collective-permute-start | bytes 393224 | tf_op jit(solution)/shard_map/ppermute | solution.py:27
  49.1 11.3 %collective-permute-start.22 = (bf16[64,1024]{1,0:T(8,128)(2,1)S(1)}, bf16[64,1024]{1,0:T(8,128)(2,1)S(1)}, u32[]{:S(2)}, u32[]{:S(2)}) collective-permute-start(bf16[64,1024]{1,0:T(8,128)(2,1)S(1)} %get-tuple-element.132.refs_0_), channel_id=1, source_target_pairs={{0,16},{4,20},{8,24},{12,28},{16,0},{20,4},{24,8},{28,12},{1,17},{... | collective-permute-start | bytes 393224 | tf_op jit(solution)/shard_map/ppermute | solution.py:27
  50.6 10.5 %collective-permute-start.21 = (bf16[64,1024]{1,0:T(8,128)(2,1)S(1)}, bf16[64,1024]{1,0:T(8,128)(2,1)S(1)}, u32[]{:S(2)}, u32[]{:S(2)}) collective-permute-start(bf16[64,1024]{1,0:T(8,128)(2,1)S(1)} %get-tuple-element.132.refs_0_), channel_id=1, source_target_pairs={{0,8},{4,12},{8,0},{12,4},{16,24},{20,28},{24,16},{28,20},{1,9},{5... | collective-permute-start | bytes 393224 | tf_op jit(solution)/shard_map/ppermute | solution.py:27
  51.8 10.1 %collective-permute-start.20 = (bf16[64,1024]{1,0:T(8,128)(2,1)S(1)}, bf16[64,1024]{1,0:T(8,128)(2,1)S(1)}, u32[]{:S(2)}, u32[]{:S(2)}) collective-permute-start(bf16[64,1024]{1,0:T(8,128)(2,1)S(1)} %get-tuple-element.132.refs_0_), channel_id=1, source_target_pairs={{0,24},{4,28},{8,16},{12,20},{16,8},{20,12},{24,0},{28,4},{1,25},{... | collective-permute-start | bytes 393224 | tf_op jit(solution)/shard_map/ppermute | solution.py:27
  53.3 10.4 %collective-permute-start.23 = (f32[128,1024]{1,0:T(8,128)S(1)}, f32[128,1024]{1,0:T(8,128)S(1)}, u32[]{:S(2)}, u32[]{:S(2)}) collective-permute-start(f32[128,1024]{1,0:T(8,128)S(1)} %get-tuple-element.135), channel_id=1, source_target_pairs={{0,4},{4,0},{8,12},{12,8},{16,20},{20,16},{24,28},{28,24},{1,5},{5... | collective-permute-start | bytes 1572872 | tf_op jit(solution)/shard_map/ppermute | solution.py:27
  59.6 4.1 %collective-permute-start.19 = (bf16[128,2048]{1,0:T(8,128)(2,1)S(1)}, bf16[128,2048]{1,0:T(8,128)(2,1)S(1)}, u32[]{:S(2)}, u32[]{:S(2)}) collective-permute-start(bf16[128,2048]{1,0:T(8,128)(2,1)S(1)} %hidden.5.refs_2_), channel_id=1, source_target_pairs={{0,4},{4,0},{8,12},{12,8},{16,20},{20,16},{24,28},{28,24},{1,5},{5... | collective-permute-start | bytes 1572872 | tf_op jit(solution)/shard_map/ppermute | solution.py:27
  60.5 3.2 %collective-permute-start.18 = (bf16[128,2048]{1,0:T(8,128)(2,1)S(1)}, bf16[128,2048]{1,0:T(8,128)(2,1)S(1)}, u32[]{:S(2)}, u32[]{:S(2)}) collective-permute-start(bf16[128,2048]{1,0:T(8,128)(2,1)S(1)} %hidden.4.refs_1_), channel_id=1, source_target_pairs={{0,4},{4,0},{8,12},{12,8},{16,20},{20,16},{24,28},{28,24},{1,5},{5... | collective-permute-start | bytes 1572872 | tf_op jit(solution)/shard_map/ppermute | solution.py:27
  61.8 3.8 %collective-permute-start.25 = (bf16[128,2048]{1,0:T(8,128)(2,1)S(1)}, bf16[128,2048]{1,0:T(8,128)(2,1)S(1)}, u32[]{:S(2)}, u32[]{:S(2)}) collective-permute-start(bf16[128,2048]{1,0:T(8,128)(2,1)S(1)} %hidden.7.refs_6_), channel_id=1, source_target_pairs={{0,4},{4,0},{8,12},{12,8},{16,20},{20,16},{24,28},{28,24},{1,5},{5... | collective-permute-start | bytes 1572872 | tf_op jit(solution)/shard_map/ppermute | solution.py:27
  62.7 2.9 %collective-permute-start.24 = (bf16[128,2048]{1,0:T(8,128)(2,1)S(1)}, bf16[128,2048]{1,0:T(8,128)(2,1)S(1)}, u32[]{:S(2)}, u32[]{:S(2)}) collective-permute-start(bf16[128,2048]{1,0:T(8,128)(2,1)S(1)} %hidden.6.refs_5_), channel_id=1, source_target_pairs={{0,4},{4,0},{8,12},{12,8},{16,20},{20,16},{24,28},{28,24},{1,5},{5... | collective-permute-start | bytes 1572872 | tf_op jit(solution)/shard_map/ppermute | solution.py:27
